TPU v7x, 32 devices: a whole 2x2x4 slice. The times are simulated.
32 devices in a mesh: gx: 8 (over z, y), gy: 4 (over x, core).
Axes of the slice: x: 2, y: 2, z: 4, core: 2. Of those that a mesh axis runs over, the one named last changes fastest.
Arguments:
- populations: float32 [4, 16, 19, 4096], P('gy', 'gx'), may hold values from 0 to 0.67
- solid_mask: int32 [4, 16, 4096], P('gy', 'gx'), may hold values from 0 to 1, as said below
- slot_blocks: int32 [4, 16], P('gy', 'gx'), may hold values from 0 to 15, as said below
- swap_slots: int32 [4, 8, 3, 2], P('gy', 'gx'), may hold values from 0 to 1, as said below
Outputs:
- moved_populations: float32 [4, 16, 19, 4096], P('gy', 'gx')
Inputs may be any that keep to these rules, and one draw needn't show every extreme that they name: `slot_blocks`: each slab's row is a permutation of its 16 block numbers. `swap_slots`: for each slab, owner and round, 2 distinct slot numbers of that owner. `solid_mask`: every block is either rock throughout or holds fluid cells.
All inputs are finite; a program needn't handle non-finite values.
Results may differ from a plain program's by a relative error of at most 0.0003.
Values sent between devices are 32-bit elements; how exact they have to be, the bound alone decides.
No kernel may reach another device: no remote copies, remote signals or barrier semaphores. Data moves between devices by JAX's collectives and lax.ppermute only.
A program may use at most 64 MiB of HBM per device.

v0:
```python
import jax
import jax.numpy as jnp
import numpy as np
from jax import lax
from jax.sharding import PartitionSpec as P

B = 16
NB = 2
STEPS = 2


VELOCITIES = (
    (0, 0, 0),
    (1, 0, 0),
    (-1, 0, 0),
    (0, 1, 0),
    (0, -1, 0),
    (0, 0, 1),
    (0, 0, -1),
    (1, 1, 0),
    (-1, -1, 0),
    (1, -1, 0),
    (-1, 1, 0),
    (1, 0, 1),
    (-1, 0, -1),
    (1, 0, -1),
    (-1, 0, 1),
    (0, 1, 1),
    (0, -1, -1),
    (0, 1, -1),
    (0, -1, 1),
)
OPPOSITE = (0, 2, 1, 4, 3, 6, 5, 8, 7, 10, 9, 12, 11, 14, 13, 16, 15, 18, 17)
WEIGHTS = (1.0 / 3.0,) + (1.0 / 18.0,) * 6 + (1.0 / 36.0,) * 12
RATES = (0.0, 0.0, 0.0, 0.0) + (1.25,) * 6 + (1.5,) * 6 + (1.3,) * 3


def swapped(value, axis, apart):
    mask = 2**apart
    pairs = [(source, source ^ mask) for source in range(lax.axis_size(axis))]
    return lax.ppermute(value, axis, pairs)


def passed_along(value, axis, steps):
    count = lax.axis_size(axis)
    pairs = [(source, (source + steps) % count) for source in range(count)]
    return lax.ppermute(value, axis, pairs)


def device_tables():
    velocity = jnp.asarray(VELOCITIES, dtype=jnp.float32)
    x_part = velocity[:, 0]
    y_part = velocity[:, 1]
    z_part = velocity[:, 2]
    polynomials = jnp.stack(
        [
            jnp.ones((19,), jnp.float32),
            x_part,
            y_part,
            z_part,
            x_part * x_part,
            y_part * y_part,
            z_part * z_part,
            x_part * y_part,
            x_part * z_part,
            y_part * z_part,
            x_part * x_part * y_part,
            x_part * x_part * z_part,
            y_part * y_part * x_part,
            y_part * y_part * z_part,
            z_part * z_part * x_part,
            z_part * z_part * y_part,
            x_part * x_part * y_part * y_part,
            x_part * x_part * z_part * z_part,
            y_part * y_part * z_part * z_part,
        ]
    )
    rates = jnp.asarray(RATES, dtype=jnp.float32)
    scaled = rates[:, None] * polynomials
    gram = jnp.dot(polynomials, polynomials.T, precision=lax.Precision.HIGHEST)
    lower = jnp.linalg.cholesky(gram)
    solved = jax.scipy.linalg.cho_solve((lower, True), scaled)
    relaxation = jnp.dot(polynomials.T, solved, precision=lax.Precision.HIGHEST)
    weights = jnp.asarray(WEIGHTS, dtype=jnp.float32)
    reverse_table = jnp.asarray(np.eye(19, dtype=np.float32)[np.array(OPPOSITE, dtype=np.int32)])
    return (relaxation, velocity, weights, reverse_table)


def direction_sets(axis_number):
    plus_index = np.array(
        [index for index in range(19) if VELOCITIES[index][axis_number] == 1], dtype=np.int32
    )
    minus_index = np.array(
        [index for index in range(19) if VELOCITIES[index][axis_number] == -1], dtype=np.int32
    )
    plus_mask = np.array([VELOCITIES[index][axis_number] == 1 for index in range(19)])
    minus_mask = np.array([VELOCITIES[index][axis_number] == -1 for index in range(19)])
    return (
        plus_index,
        minus_index,
        plus_mask[None, :, None, None],
        minus_mask[None, :, None, None],
    )


def bounce_back(current, tables):
    return jnp.einsum("ij,...jc->...ic", tables[3], current, precision=lax.Precision.HIGHEST)


def collide(current, fluid_cells, tables):
    relaxation, velocity, weights, reverse_table = tables
    density = jnp.sum(current, axis=-2)
    momentum = jnp.einsum("iv,...ic->...vc", velocity, current, precision=lax.Precision.HIGHEST)
    projected = jnp.einsum("iv,...vc->...ic", velocity, momentum, precision=lax.Precision.HIGHEST)
    squared = jnp.sum(momentum * momentum, axis=-2)
    equilibrium = weights[:, None] * (
        density[..., None, :]
        + 3.0 * projected
        + 4.5 * projected * projected
        - 1.5 * squared[..., None, :]
    )
    relaxed = current - jnp.einsum(
        "ij,...jc->...ic", relaxation, current - equilibrium, precision=lax.Precision.HIGHEST
    )
    bounced = bounce_back(current, tables)
    return jnp.where(fluid_cells[..., None, :] > 0, relaxed, bounced)


def widen(face_five, chosen_index):
    filled = jnp.zeros((face_five.shape[0], 19) + face_five.shape[2:], jnp.float32)
    return filled.at[:, chosen_index].set(face_five)


def stream_x(lattice_state, faces_from):
    plus_index, minus_index, plus_mask, minus_mask = direction_sets(0)
    side_cells = lattice_state.shape[2]
    high_face = lattice_state[:, :, side_cells - 1, :][:, plus_index]
    low_face = lattice_state[:, :, 0, :][:, minus_index]
    from_below, from_above = faces_from(high_face, low_face)
    wide_below = widen(from_below, plus_index)
    wide_above = widen(from_above, minus_index)
    moved_up = jnp.concatenate([wide_below[:, :, None, :], lattice_state[:, :, :-1, :]], axis=2)
    moved_down = jnp.concatenate([lattice_state[:, :, 1:, :], wide_above[:, :, None, :]], axis=2)
    return jnp.where(plus_mask, moved_up, jnp.where(minus_mask, moved_down, lattice_state))


def stream_y(lattice_state, faces_from):
    plus_index, minus_index, plus_mask, minus_mask = direction_sets(1)
    slot_count, side_cells, plane_cells = (
        lattice_state.shape[0],
        lattice_state.shape[2],
        lattice_state.shape[3],
    )
    high_face = lattice_state[:, plus_index][:, :, :, plane_cells - side_cells :].reshape(
        slot_count, 5, plane_cells
    )
    low_face = lattice_state[:, minus_index][:, :, :, :side_cells].reshape(
        slot_count, 5, plane_cells
    )
    from_below, from_above = faces_from(high_face, low_face)
    wide_below = jnp.tile(
        widen(from_below.reshape(slot_count, 5, side_cells, side_cells), plus_index),
        (1, 1, 1, side_cells),
    )
    wide_above = jnp.tile(
        widen(from_above.reshape(slot_count, 5, side_cells, side_cells), minus_index),
        (1, 1, 1, side_cells),
    )
    place = jnp.arange(plane_cells)
    moved_up = jnp.where(
        place < side_cells, wide_below, jnp.roll(lattice_state, side_cells, axis=3)
    )
    moved_down = jnp.where(
        place >= plane_cells - side_cells, wide_above, jnp.roll(lattice_state, -side_cells, axis=3)
    )
    return jnp.where(plus_mask, moved_up, jnp.where(minus_mask, moved_down, lattice_state))


def stream_z(lattice_state, faces_from):
    plus_index, minus_index, plus_mask, minus_mask = direction_sets(2)
    slot_count, side_cells, plane_cells = (
        lattice_state.shape[0],
        lattice_state.shape[2],
        lattice_state.shape[3],
    )
    high_face = lattice_state[:, plus_index][:, :, :, side_cells - 1 :: side_cells].reshape(
        slot_count, 5, plane_cells
    )
    low_face = lattice_state[:, minus_index][:, :, :, 0::side_cells].reshape(
        slot_count, 5, plane_cells
    )
    from_below, from_above = faces_from(high_face, low_face)
    wide_below = jnp.repeat(
        widen(from_below.reshape(slot_count, 5, side_cells, side_cells), plus_index),
        side_cells,
        axis=3,
    )
    wide_above = jnp.repeat(
        widen(from_above.reshape(slot_count, 5, side_cells, side_cells), minus_index),
        side_cells,
        axis=3,
    )
    column_place = jnp.arange(plane_cells) % side_cells
    moved_up = jnp.where(column_place == 0, wide_below, jnp.roll(lattice_state, 1, axis=3))
    moved_down = jnp.where(
        column_place == side_cells - 1, wide_above, jnp.roll(lattice_state, -1, axis=3)
    )
    return jnp.where(plus_mask, moved_up, jnp.where(minus_mask, moved_down, lattice_state))


def shards(populations, solid_mask, slot_blocks, swap_slots):
    tables = device_tables()
    current = populations[0]
    fluid_cells = solid_mask[0]
    blocks = slot_blocks[0]
    swap_lists = swap_slots[0, 0]
    for round_bit in range(3):
        chosen = swap_lists[round_bit]
        parcel = (
            current[chosen],
            fluid_cells[chosen].astype(jnp.float32),
            blocks[chosen].astype(jnp.float32),
        )
        arrived = swapped((parcel[0], parcel[1], parcel[2]), "gx", round_bit)
        current = current.at[chosen].set(arrived[0])
        fluid_cells = fluid_cells.at[chosen].set(arrived[1].astype(jnp.int32))
        blocks = blocks.at[chosen].set(arrived[2].astype(jnp.int32))
    owners = lax.axis_size("gx")
    slot_count = current.shape[0]
    cell_count = current.shape[2]
    slab_map = lax.all_gather(blocks, "gx", axis=0, tiled=True)
    slab_slots = jnp.argsort(slab_map)
    row_block = blocks // NB
    column_block = blocks % NB
    below_y = (row_block - 1) % owners * NB + column_block
    above_y = (row_block + 1) % owners * NB + column_block
    below_z = row_block * NB + (column_block - 1) % NB
    above_z = row_block * NB + (column_block + 1) % NB

    def collect(face_pair):
        return (
            lax.all_gather(face_pair[0], "gx", axis=0, tiled=True),
            lax.all_gather(face_pair[1], "gx", axis=0, tiled=True),
        )

    def within_slab(below, above):

        def faces_from(high_face, low_face):
            got_high, got_low = collect((high_face, low_face))
            return (got_high[slab_slots[below]], got_low[slab_slots[above]])

        return faces_from

    def across_slabs(high_face, low_face):
        got_high, got_low = collect((high_face, low_face))
        ordered_high = got_high[slab_slots]
        ordered_low = got_low[slab_slots]
        from_lower_slab = passed_along(ordered_high, "gy", 1)
        from_upper_slab = passed_along(ordered_low, "gy", -1)
        return (from_lower_slab[blocks], from_upper_slab[blocks])

    for step_index in range(STEPS):
        collided = collide(current, fluid_cells, tables)
        lattice_state = collided.reshape(slot_count, 19, B, cell_count // B)
        lattice_state = stream_x(lattice_state, across_slabs)
        lattice_state = stream_y(lattice_state, within_slab(below_y, above_y))
        lattice_state = stream_z(lattice_state, within_slab(below_z, above_z))
        current = lattice_state.reshape(slot_count, 19, cell_count)
    return current[None]


def solution(mesh):
    return jax.shard_map(
        shards,
        mesh=mesh,
        in_specs=(
            P("gy", "gx", None, None),
            P("gy", "gx", None),
            P("gy", "gx"),
            P("gy", "gx", None, None),
        ),
        out_specs=P("gy", "gx", None, None),
        check_vma=False,
    )
```

profile of v0, /device:TPU:0, one launch (start us, length us, event | category | flops | bytes accessed | tf_op | source)
XLA Modules:
  0.0 669.3 jit_solution(17034830228773938820)
XLA Ops:
  3.2 3.0 collective-permute-start.6
  14.2 2.4 cholesky.16
  27.3 2.6 collective-permute-start.8
  32.6 11.6 %all-reduce = s32[16]{0:T(128)S(1)} all-reduce(s32[16]{0:T(128)S(1)} %dynamic-update-slice.3), channel_id=1, replica_groups=mesh['gx'=8,'gy'=4] {'gx'}, use_global_device_ids=true, to_apply=%add | all-reduce | flops 16 | bytes 128
  55.0 7.0 %collective-permute-done.1 = f32[2,4096]{1,0:T(2,128)S(1)} collective-permute-done((f32[2,4096]{1,0:T(2,128)S(1)}, f32[2,4096]{1,0:T(2,128)S(1)}, u32[]{:S(2)}, u32[]{:S(2)}) %collective-permute-start.1) | collective-permute-done | bytes 32800 | tf_op jit(solution)/shard_map/ppermute | solution.py:41
  63.8 10.8 %collective-permute-done.2 = f32[2,4096]{1,0:T(2,128)S(1)} collective-permute-done((f32[2,4096]{1,0:T(2,128)S(1)}, f32[2,4096]{1,0:T(2,128)S(1)}, u32[]{:S(2)}, u32[]{:S(2)}) %collective-permute-start.2) | collective-permute-done | bytes 32800 | tf_op jit(solution)/shard_map/ppermute | solution.py:41
  77.6 16.5 %collective-permute-done.5 = f32[2,19,4096]{2,0,1:T(2,128)S(1)} collective-permute-done((f32[2,19,4096]{2,0,1:T(2,128)S(1)}, f32[2,19,4096]{2,0,1:T(2,128)S(1)}, u32[]{:S(2)}, u32[]{:S(2)}) %collective-permute-start.5) | collective-permute-done | bytes 622624 | tf_op jit(solution)/shard_map/ppermute | solution.py:41
  100.1 30.6 %all-gather.1 = f32[16,5,256]{2,1,0:T(8,128)S(1)} all-gather(f32[2,5,256]{2,1,0:T(8,128)S(1)} %copy.194), channel_id=3, replica_groups=mesh['gx'=8,'gy'=4] {'gx'}, dimensions={0}, use_global_device_ids=true | all-gather | bytes 92160 | tf_op jit(solution)/shard_map/all_gather | solution.py:243
  130.7 30.5 %all-gather = f32[16,5,256]{2,1,0:T(8,128)S(1)} all-gather(f32[2,5,256]{2,1,0:T(8,128)S(1)} %copy.191), channel_id=2, replica_groups=mesh['gx'=8,'gy'=4] {'gx'}, dimensions={0}, use_global_device_ids=true | all-gather | bytes 92160 | tf_op jit(solution)/shard_map/all_gather | solution.py:242
  174.1 30.5 %all_gather.42 = f32[16,5,256]{2,1,0:T(8,128)S(1)} all-gather(f32[2,5,256]{2,1,0:T(8,128)S(1)} %copy.197), channel_id=1, replica_groups=mesh['gx'=8,'gy'=4] {'gx'}, dimensions={0}, use_global_device_ids=true | all-gather | bytes 92160 | tf_op jit(solution)/shard_map/all_gather | solution.py:242
  206.1 2.6 tile.44
  208.7 5.3 tile.48
  214.0 4.8 reshape.1068
  219.5 30.5 %all_gather.43 = f32[16,5,256]{2,1,0:T(8,128)S(1)} all-gather(f32[2,5,256]{2,1,0:T(8,128)S(1)} %copy.202), channel_id=1, replica_groups=mesh['gx'=8,'gy'=4] {'gx'}, dimensions={0}, use_global_device_ids=true | all-gather | bytes 92160 | tf_op jit(solution)/shard_map/all_gather | solution.py:243
  251.6 2.6 tile.46
  254.2 5.3 tile.49
  259.5 4.8 reshape.1069
  264.3 3.3 select_select_fusion.2
  273.5 31.0 %all_gather.45 = f32[16,5,256]{2,1,0:T(8,128)S(1)} all-gather(f32[2,5,256]{2,1,0:T(8,128)S(1)} %copy.212), channel_id=1, replica_groups=mesh['gx'=8,'gy'=4] {'gx'}, dimensions={0}, use_global_device_ids=true | all-gather | bytes 92160 | tf_op jit(solution)/shard_map/all_gather | solution.py:243
  311.6 30.5 %all_gather.44 = f32[16,5,256]{2,1,0:T(8,128)S(1)} all-gather(f32[2,5,256]{2,1,0:T(8,128)S(1)} %copy.207), channel_id=1, replica_groups=mesh['gx'=8,'gy'=4] {'gx'}, dimensions={0}, use_global_device_ids=true | all-gather | bytes 92160 | tf_op jit(solution)/shard_map/all_gather | solution.py:242
  348.3 2.3 concatenate.69
  352.8 2.3 concatenate.71
  355.2 3.8 broadcast_in_dim.380
  359.0 5.3 reshape.532
  364.3 3.8 broadcast_in_dim.389
  368.2 5.4 reshape.535
  373.7 7.3 %fusion.24 = f32[2,19,4096]{2,1,0:T(8,128)S(1)} fusion(f32[2,19,4096]{2,0,1:T(2,128)S(1)} %concatenate.74, f32[2,19,4096]{2,1,0:T(8,128)S(1)} %fusion.7, f32[2,19,4096]{2,0,1:T(2,128)S(1)} %concatenate.75, f32[2,19,4096]{2,0,1:T(2,128)S(1)} %concatenate.73, f32[2,19,4096]{2,0,1:T(2,128)} %tile.49, f32[2,19,4096]{2,0,1:T(2,128)S(1)} %concatenate.72, ...), kind=kLoop, calls=%fused_computation.104 | loop fusion | flops 1556480 | bytes 7487602 | tf_op jit(solution)/shard_map/jit(_where)/select_n | solution.py:208
  386.1 30.6 %all-gather.3 = f32[16,5,256]{2,1,0:T(8,128)S(1)} all-gather(f32[2,5,256]{2,1,0:T(8,128)S(1)} %copy.227), channel_id=5, replica_groups=mesh['gx'=8,'gy'=4] {'gx'}, dimensions={0}, use_global_device_ids=true | all-gather | bytes 92160 | tf_op jit(solution)/shard_map/all_gather | solution.py:243
  417.4 30.5 %all-gather.2 = f32[16,5,256]{2,1,0:T(8,128)S(1)} all-gather(f32[2,5,256]{2,1,0:T(8,128)S(1)} %copy.224), channel_id=4, replica_groups=mesh['gx'=8,'gy'=4] {'gx'}, dimensions={0}, use_global_device_ids=true | all-gather | bytes 92160 | tf_op jit(solution)/shard_map/all_gather | solution.py:242
  461.4 30.5 %all_gather.48 = f32[16,5,256]{2,1,0:T(8,128)S(1)} all-gather(f32[2,5,256]{2,1,0:T(8,128)S(1)} %copy.230), channel_id=1, replica_groups=mesh['gx'=8,'gy'=4] {'gx'}, dimensions={0}, use_global_device_ids=true | all-gather | bytes 92160 | tf_op jit(solution)/shard_map/all_gather | solution.py:242
  493.7 2.6 tile.50
  496.3 5.3 tile.54
  501.7 4.8 reshape.1071
  506.6 30.5 %all_gather.49 = f32[16,5,256]{2,1,0:T(8,128)S(1)} all-gather(f32[2,5,256]{2,1,0:T(8,128)S(1)} %copy.235), channel_id=1, replica_groups=mesh['gx'=8,'gy'=4] {'gx'}, dimensions={0}, use_global_device_ids=true | all-gather | bytes 92160 | tf_op jit(solution)/shard_map/all_gather | solution.py:243
  538.8 2.6 tile.52
  541.4 5.3 tile.55
  546.7 4.8 reshape.1072
  551.5 3.3 select_select_fusion
  561.4 2.7 slice.178
  564.2 30.5 %all_gather.51 = f32[16,5,256]{2,1,0:T(8,128)S(1)} all-gather(f32[2,5,256]{2,1,0:T(8,128)S(1)} %copy.245), channel_id=1, replica_groups=mesh['gx'=8,'gy'=4] {'gx'}, dimensions={0}, use_global_device_ids=true | all-gather | bytes 92160 | tf_op jit(solution)/shard_map/all_gather | solution.py:243
  598.0 30.5 %all_gather.50 = f32[16,5,256]{2,1,0:T(8,128)S(1)} all-gather(f32[2,5,256]{2,1,0:T(8,128)S(1)} %copy.240), channel_id=1, replica_groups=mesh['gx'=8,'gy'=4] {'gx'}, dimensions={0}, use_global_device_ids=true | all-gather | bytes 92160 | tf_op jit(solution)/shard_map/all_gather | solution.py:242
  634.9 2.3 concatenate.81
  639.4 2.3 concatenate.83
  641.7 3.8 broadcast_in_dim.413
  645.5 5.3 reshape.543
  650.8 3.8 broadcast_in_dim.418
  654.6 5.6 reshape.546
  660.2 7.3 %fusion.20 = f32[1,2,19,4096]{3,2,1,0:T(8,128)S(1)} fusion(f32[2,19,4096]{2,0,1:T(2,128)S(1)} %concatenate.86, f32[2,19,4096]{2,1,0:T(8,128)S(1)} %fusion.4, f32[2,19,4096]{2,0,1:T(2,128)S(1)} %concatenate.87, f32[2,19,4096]{2,0,1:T(2,128)S(1)} %concatenate.85, f32[2,19,4096]{2,0,1:T(2,128)} %tile.55, f32[2,19,4096]{2,0,1:T(2,128)S(1)} %concatenate.84, ...), kind=kLoop, calls=%fused_computation.94 | loop fusion | flops 1556480 | bytes 7487602 | tf_op jit(solution)/shard_map/jit(_where)/select_n | solution.py:208
  (366 shorter events, 124.6 us)
Async XLA Ops:
  0.0 12.2 %copy-start.26 = (s32[5]{0:T(128)S(1)}, s32[5]{0:T(128)}, u32[]{:S(2)}) copy-start(s32[5]{0:T(128)} %constant.240) | copy-start | bytes 64
  0.0 12.8 %copy-start.32 = (s32[5]{0:T(128)S(1)}, s32[5]{0:T(128)}, u32[]{:S(2)}) copy-start(s32[5]{0:T(128)} %constant.241) | copy-start | bytes 64
  0.0 12.8 %copy-start.41 = (s32[5]{0:T(128)S(1)}, s32[5]{0:T(128)}, u32[]{:S(2)}) copy-start(s32[5]{0:T(128)} %constant.242) | copy-start | bytes 64
  0.0 12.9 %copy-start.39 = (s32[5]{0:T(128)S(1)}, s32[5]{0:T(128)}, u32[]{:S(2)}) copy-start(s32[5]{0:T(128)} %constant.247) | copy-start | bytes 64
  0.0 12.9 %copy-start.30 = (s32[5]{0:T(128)S(1)}, s32[5]{0:T(128)}, u32[]{:S(2)}) copy-start(s32[5]{0:T(128)} %constant.250) | copy-start | bytes 64
  0.0 12.9 %copy-start.28 = (s32[5]{0:T(128)S(1)}, s32[5]{0:T(128)}, u32[]{:S(2)}) copy-start(s32[5]{0:T(128)} %constant.253) | copy-start | bytes 64
  0.0 19.4 %copy-start.8 = (f32[19,19]{1,0:T(8,128)S(1)}, f32[19,19]{1,0:T(8,128)}, u32[]{:S(2)}) copy-start(f32[19,19]{1,0:T(8,128)} %constant.233) | copy-start | bytes 4336
  0.0 19.8 %copy-start.47 = (u32[32]{0:T(128)S(1)}, u32[32]{0:T(128)}, u32[]{:S(2)}) copy-start(u32[32]{0:T(128)} %constant.266) | copy-start | bytes 388
  0.1 21.0 %copy-start.7 = (f32[19,19]{1,0:T(8,128)S(1)}, f32[19,19]{1,0:T(8,128)}, u32[]{:S(2)}) copy-start(f32[19,19]{1,0:T(8,128)} %constant.228) | copy-start | bytes 4336
  3.2 18.0 %collective-permute-start.6 = (f32[2]{0:T(128)S(1)}, f32[2]{0:T(128)S(1)}, u32[]{:S(2)}, u32[]{:S(2)}) collective-permute-start(f32[2]{0:T(128)S(1)} %convert_element_type.42), channel_id=1, source_target_pairs={{0,4},{4,0},{8,12},{12,8},{16,20},{20,16},{24,28},{28,24},{1,5},{5... | collective-permute-start | bytes 32 | tf_op jit(solution)/shard_map/ppermute | solution.py:41
  6.8 44.7 %collective-permute-start = (f32[2,4096]{1,0:T(2,128)S(1)}, f32[2,4096]{1,0:T(2,128)S(1)}, u32[]{:S(2)}, u32[]{:S(2)}) collective-permute-start(f32[2,4096]{1,0:T(2,128)S(1)} %convert_element_type.36), channel_id=1, source_target_pairs={{0,4},{4,0},{8,12},{12,8},{16,20},{20,16},{24,28},{28,24},{1,5},{5... | collective-permute-start | bytes 98312 | tf_op jit(solution)/shard_map/ppermute | solution.py:41
  9.4 39.3 %collective-permute-start.3 = (f32[2,19,4096]{2,0,1:T(2,128)S(1)}, f32[2,19,4096]{2,0,1:T(2,128)S(1)}, u32[]{:S(2)}, u32[]{:S(2)}) collective-permute-start(f32[2,19,4096]{2,0,1:T(2,128)S(1)} %copy.184), channel_id=1, source_target_pairs={{0,4},{4,0},{8,12},{12,8},{16,20},{20,16},{24,28},{28,24},{1,5},{5... | collective-permute-start | bytes 1867784 | tf_op jit(solution)/shard_map/ppermute | solution.py:41
  11.5 252.8 %copy-start.34 = (pred[256]{0:T(512)(128)(4,1)}, pred[256]{0:T(512)(128)(4,1)S(1)}, u32[]{:S(2)}) copy-start(pred[256]{0:T(512)(128)(4,1)S(1)} %get-tuple-element.59) | copy-start | bytes 772
  12.8 160.5 %copy-start.20 = (s32[1024]{0:T(1024)}, s32[1024]{0:T(1024)S(1)}, u32[]{:S(2)}) copy-start(s32[1024]{0:T(1024)S(1)} %pad_clamp_fusion.11) | copy-start | bytes 12292
  12.9 86.0 %copy-start.23 = (s32[1024]{0:T(1024)}, s32[1024]{0:T(1024)S(1)}, u32[]{:S(2)}) copy-start(s32[1024]{0:T(1024)S(1)} %pad_clamp_fusion.15) | copy-start | bytes 12292
  12.9 86.6 %copy-start.22 = (s32[1024]{0:T(1024)}, s32[1024]{0:T(1024)S(1)}, u32[]{:S(2)}) copy-start(s32[1024]{0:T(1024)S(1)} %pad_clamp_fusion.12) | copy-start | bytes 12292
  12.9 205.9 %copy-start.21 = (s32[1024]{0:T(1024)}, s32[1024]{0:T(1024)S(1)}, u32[]{:S(2)}) copy-start(s32[1024]{0:T(1024)S(1)} %pad_clamp_fusion.8) | copy-start | bytes 12292
  13.0 259.1 %copy-start.19 = (s32[1024]{0:T(1024)}, s32[1024]{0:T(1024)S(1)}, u32[]{:S(2)}) copy-start(s32[1024]{0:T(1024)S(1)} %pad_clamp_fusion.2) | copy-start | bytes 12292
  22.5 3.5 collective-permute-start.7
  27.3 4.4 collective-permute-start.8
  48.1 113.7 %copy-start.10 = (s32[1024]{0:T(1024)}, s32[1024]{0:T(1024)S(1)}, u32[]{:S(2)}) copy-start(s32[1024]{0:T(1024)S(1)} %pad_clamp_fusion.14) | copy-start | bytes 12292
  50.9 24.3 %collective-permute-start.4 = (f32[2,19,4096]{2,0,1:T(2,128)S(1)}, f32[2,19,4096]{2,0,1:T(2,128)S(1)}, u32[]{:S(2)}, u32[]{:S(2)}) collective-permute-start(f32[2,19,4096]{2,0,1:T(2,128)S(1)} %copy.186), channel_id=1, source_target_pairs={{0,8},{4,12},{8,0},{12,4},{16,24},{20,28},{24,16},{28,20},{1,9},{5... | collective-permute-start | bytes 1867784 | tf_op jit(solution)/shard_map/ppermute | solution.py:41
  51.4 116.7 %copy-start.9 = (s32[1024]{0:T(1024)}, s32[1024]{0:T(1024)S(1)}, u32[]{:S(2)}) copy-start(s32[1024]{0:T(1024)S(1)} %pad_clamp_fusion.13) | copy-start | bytes 12292
  51.5 153.1 %copy-start.24 = (s32[1024]{0:T(1024)}, s32[1024]{0:T(1024)S(1)}, u32[]{:S(2)}) copy-start(s32[1024]{0:T(1024)S(1)} %pad_clamp_fusion.9) | copy-start | bytes 12292
  52.8 9.3 %collective-permute-start.1 = (f32[2,4096]{1,0:T(2,128)S(1)}, f32[2,4096]{1,0:T(2,128)S(1)}, u32[]{:S(2)}, u32[]{:S(2)}) collective-permute-start(f32[2,4096]{1,0:T(2,128)S(1)} %convert_element_type.38), channel_id=1, source_target_pairs={{0,8},{4,12},{8,0},{12,4},{16,24},{20,28},{24,16},{28,20},{1,9},{5... | collective-permute-start | bytes 98312 | tf_op jit(solution)/shard_map/ppermute | solution.py:41
  63.3 11.2 %collective-permute-start.2 = (f32[2,4096]{1,0:T(2,128)S(1)}, f32[2,4096]{1,0:T(2,128)S(1)}, u32[]{:S(2)}, u32[]{:S(2)}) collective-permute-start(f32[2,4096]{1,0:T(2,128)S(1)} %convert_element_type.40), channel_id=1, source_target_pairs={{0,16},{4,20},{8,24},{12,28},{16,0},{20,4},{24,8},{28,12},{1,17},{... | collective-permute-start | bytes 98312 | tf_op jit(solution)/shard_map/ppermute | solution.py:41
  63.8 186.3 %copy-start.25 = (s32[1024]{0:T(1024)}, s32[1024]{0:T(1024)S(1)}, u32[]{:S(2)}) copy-start(s32[1024]{0:T(1024)S(1)} %pad_clamp_fusion.6) | copy-start | bytes 12292
  75.2 20.0 %copy-start.5 = (f32[19,3,1]{0,1,2:T(4,128)S(1)}, f32[19,3,1]{0,1,2:T(4,128)}, u32[]{:S(2)}) copy-start(f32[19,3,1]{0,1,2:T(4,128)} %constant.270) | copy-start | bytes 688
  75.6 21.1 %copy-start = (f32[19,19,1]{1,0,2:T(8,128)S(1)}, f32[19,19,1]{1,0,2:T(8,128)}, u32[]{:S(2)}) copy-start(f32[19,19,1]{1,0,2:T(8,128)} %constant.271) | copy-start | bytes 4336
  76.4 21.2 %copy-start.45 = (f32[19]{0:T(128)S(1)}, f32[19]{0:T(128)}, u32[]{:S(2)}) copy-start(f32[19]{0:T(128)} %constant.182.clone) | copy-start | bytes 232
  77.5 16.6 %collective-permute-start.5 = (f32[2,19,4096]{2,0,1:T(2,128)S(1)}, f32[2,19,4096]{2,0,1:T(2,128)S(1)}, u32[]{:S(2)}, u32[]{:S(2)}) collective-permute-start(f32[2,19,4096]{2,0,1:T(2,128)S(1)} %copy.188), channel_id=1, source_target_pairs={{0,16},{4,20},{8,24},{12,28},{16,0},{20,4},{24,8},{28,12},{1,17},{... | collective-permute-start | bytes 1867784 | tf_op jit(solution)/shard_map/ppermute | solution.py:41
  97.8 71.7 %copy-start.11 = (pred[19]{0:T(512)(128)(4,1)S(1)}, pred[19]{0:T(512)(128)(4,1)}, u32[]{:S(2)}) copy-start(pred[19]{0:T(512)(128)(4,1)} %constant.234) | copy-start | bytes 61
  97.8 71.7 %copy-start.13 = (pred[19]{0:T(512)(128)(4,1)S(1)}, pred[19]{0:T(512)(128)(4,1)}, u32[]{:S(2)}) copy-start(pred[19]{0:T(512)(128)(4,1)} %constant.205) | copy-start | bytes 61
  162.4 4.4 collective-permute-start.9
  162.4 5.7 collective-permute-start.10
  254.2 10.1 %copy-start.15 = (pred[19]{0:T(512)(128)(4,1)S(1)}, pred[19]{0:T(512)(128)(4,1)}, u32[]{:S(2)}) copy-start(pred[19]{0:T(512)(128)(4,1)} %constant.236) | copy-start | bytes 61
  254.2 10.1 %copy-start.17 = (pred[19]{0:T(512)(128)(4,1)S(1)}, pred[19]{0:T(512)(128)(4,1)}, u32[]{:S(2)}) copy-start(pred[19]{0:T(512)(128)(4,1)} %constant.203) | copy-start | bytes 61
  254.2 10.1 %copy-start.37 = (pred[256]{0:T(512)(128)(4,1)S(1)}, pred[256]{0:T(512)(128)(4,1)}, u32[]{:S(2)}) copy-start(pred[256]{0:T(512)(128)(4,1)} %copy-done.36) | copy-start | bytes 772
  382.8 70.9 %copy-start.42 = (s32[5]{0:T(128)S(1)}, s32[5]{0:T(128)}, u32[]{:S(2)}) copy-start(s32[5]{0:T(128)} %constant.242) | copy-start | bytes 64
  382.8 72.4 %copy-start.40 = (s32[5]{0:T(128)S(1)}, s32[5]{0:T(128)}, u32[]{:S(2)}) copy-start(s32[5]{0:T(128)} %constant.247) | copy-start | bytes 64
  448.6 4.4 collective-permute-start.11
  448.7 5.9 collective-permute-start.12
  451.5 41.2 %copy-start.33 = (s32[5]{0:T(128)S(1)}, s32[5]{0:T(128)}, u32[]{:S(2)}) copy-start(s32[5]{0:T(128)} %constant.241) | copy-start | bytes 64
  496.3 41.6 %copy-start.31 = (s32[5]{0:T(128)S(1)}, s32[5]{0:T(128)}, u32[]{:S(2)}) copy-start(s32[5]{0:T(128)} %constant.250) | copy-start | bytes 64
  541.4 10.1 %copy-start.35 = (pred[256]{0:T(512)(128)(4,1)S(1)}, pred[256]{0:T(512)(128)(4,1)}, u32[]{:S(2)}) copy-start(pred[256]{0:T(512)(128)(4,1)} %copy-done.34) | copy-start | bytes 772
  541.4 10.1 %copy-start.38 = (pred[256]{0:T(512)(128)(4,1)S(1)}, pred[256]{0:T(512)(128)(4,1)}, u32[]{:S(2)}) copy-start(pred[256]{0:T(512)(128)(4,1)} %copy-done.36) | copy-start | bytes 772
  554.7 40.8 %copy-start.29 = (s32[5]{0:T(128)S(1)}, s32[5]{0:T(128)}, u32[]{:S(2)}) copy-start(s32[5]{0:T(128)} %constant.253) | copy-start | bytes 64
  556.9 72.5 %copy-start.27 = (s32[5]{0:T(128)S(1)}, s32[5]{0:T(128)}, u32[]{:S(2)}) copy-start(s32[5]{0:T(128)} %constant.240) | copy-start | bytes 64
  (13 other events, 108.3 us)
where the time goes:
time: 680 us; the launch traced here: 669 us
  blocking collectives  378 us (56%)
  local copies, waits for them, and re-layouts  180 us (26%)
  other arithmetic  44 us (6%)
  waiting for transfers between devices  41 us (6%)
  starting transfers between devices  15.7 us (2%)
    all_gather x6, blocking collectives, collect(): lax.all_gather(face_pair[1], 'gx', axis=0, tiled=True)  184 us
    all_gather x6, blocking collectives, collect(): lax.all_gather(face_pair[0], 'gx', axis=0, tiled=True)  183 us
    ppermute x9, waiting for transfers between devices, swapped(): return lax.ppermute(value, axis, pairs)  38.2 us
    another operation x6, local copies, waits for them, and re-layouts, stream_y(): jnp.tile(widen(from_below.reshape(slot_count, 5, side_cells, side_cells),...  25.4 us
    another operation x6, local copies, waits for them, and re-layouts, stream_y(): jnp.tile(widen(from_above.reshape(slot_count, 5, side_cells, side_cells),...  25.4 us
    scatter x20, local copies, waits for them, and re-layouts, widen(): return filled.at[:, chosen_index].set(face_five)  15.3 us
    select_n x2, other arithmetic, stream_z(): jnp.where(plus_mask, moved_up, jnp.where(minus_mask, moved_down, lattice_...  14.5 us
  transfers between devices with their start and end apart: 13, of which 7 were waited for; matrix products, arithmetic and copies ran while one was open for 5% of the time, Pallas kernels for 0%

commit v1 on v0

v1 whole, which is shorter than its diff:
```python
import jax
import jax.numpy as jnp
from jax import lax
from jax.experimental import pallas as pl
from jax.experimental.pallas import tpu as pltpu
from jax.sharding import PartitionSpec as P

B = 16
NB = 2
LANES = 128
PLANE_ROWS = B * B // LANES
HALF = LANES // B

VELOCITIES = (
    (0, 0, 0),
    (1, 0, 0),
    (-1, 0, 0),
    (0, 1, 0),
    (0, -1, 0),
    (0, 0, 1),
    (0, 0, -1),
    (1, 1, 0),
    (-1, -1, 0),
    (1, -1, 0),
    (-1, 1, 0),
    (1, 0, 1),
    (-1, 0, -1),
    (1, 0, -1),
    (-1, 0, 1),
    (0, 1, 1),
    (0, -1, -1),
    (0, 1, -1),
    (0, -1, 1),
)
OPPOSITE = (0, 2, 1, 4, 3, 6, 5, 8, 7, 10, 9, 12, 11, 14, 13, 16, 15, 18, 17)
Q = len(VELOCITIES)
UPWARD = tuple(p for p in range(Q) if VELOCITIES[p][0] == 1)
DOWNWARD = tuple(p for p in range(Q) if VELOCITIES[p][0] == -1)

VMEM_SPEC = pl.BlockSpec(memory_space=pltpu.VMEM)
SMEM_SPEC = pl.BlockSpec(memory_space=pltpu.SMEM)
PARAMS = pltpu.CompilerParams(vmem_limit_bytes=40 * 1024 * 1024)


def snake(place):
    pair = place // 2
    return 2 * pair + (place % 2 if pair % 2 == 0 else 1 - place % 2)


def owner_at(place, slab, owners):
    return snake(place if slab % 2 == 0 else owners - 1 - place)


def dynamic_owner(place, odd_slab, owners):
    return jnp.where(odd_slab == 1, snake(owners - 1 - place), snake(place))


def ring_pairs(owners, slabs, step):
    pairs = []
    for slab in range(slabs):
        for place in range(owners):
            target = slab * owners + place + step
            there, seat = (target // owners) % slabs, target % owners
            pairs.append(
                (
                    owner_at(place, slab, owners) * slabs + slab,
                    owner_at(seat, there, owners) * slabs + there,
                )
            )
    return pairs


def collide(f, fluid):
    def pair(p):
        return f[p] + f[p + 1], f[p] - f[p + 1]

    sx, dx = pair(1)
    sy, dy = pair(3)
    sz, dz = pair(5)
    sxy_a, dxy_a = pair(7)
    sxy_b, dxy_b = pair(9)
    sxz_a, dxz_a = pair(11)
    sxz_b, dxz_b = pair(13)
    syz_a, dyz_a = pair(15)
    syz_b, dyz_b = pair(17)
    axy, bxy = sxy_a + sxy_b, sxy_a - sxy_b
    axz, bxz = sxz_a + sxz_b, sxz_a - sxz_b
    ayz, byz = syz_a + syz_b, syz_a - syz_b
    rho = f[0] + sx + sy + sz + axy + axz + ayz
    ox = dxy_a + dxy_b + dxz_a + dxz_b
    oy = dxy_a - dxy_b + dyz_a + dyz_b
    oz = dxz_a - dxz_b + dyz_a - dyz_b
    jx, jy, jz = dx + ox, dy + oy, dz + oz
    jxx, jyy, jzz = jx * jx, jy * jy, jz * jz
    base = rho * (1.3 / 9.0)
    wide = 1.3 / 3.0
    thin = 1.3 / 6.0
    axy1 = base - 0.3 * axy + wide * (jxx + jyy) - thin * jzz
    axz1 = base - 0.3 * axz + wide * (jxx + jzz) - thin * jyy
    ayz1 = base - 0.3 * ayz + wide * (jyy + jzz) - thin * jxx
    bxy1 = 1.25 * (jx * jy) - 0.25 * bxy
    bxz1 = 1.25 * (jx * jz) - 0.25 * bxz
    byz1 = 1.25 * (jy * jz) - 0.25 * byz
    third = rho * (1.25 / 3.0)
    sx1 = third + 1.25 * jxx - 0.25 * (sx + axy + axz) - axy1 - axz1
    sy1 = third + 1.25 * jyy - 0.25 * (sy + axy + ayz) - axy1 - ayz1
    sz1 = third + 1.25 * jzz - 0.25 * (sz + axz + ayz) - axz1 - ayz1
    rest = rho - sx1 - sy1 - sz1 - axy1 - axz1 - ayz1

    def split(even, odd):
        return 0.5 * (even + odd), 0.5 * (even - odd)

    def diagonal(a1, b1, d_a, d_b, j_first, j_second):
        plus = 0.25 * (j_first + j_second) - 0.5 * d_a
        minus = 0.25 * (j_first - j_second) - 0.5 * d_b
        return split(0.5 * (a1 + b1), plus) + split(0.5 * (a1 - b1), minus)

    relaxed = (
        (rest,)
        + split(sx1, 0.5 * ox)
        + split(sy1, 0.5 * oy)
        + split(sz1, 0.5 * oz)
        + diagonal(axy1, bxy1, dxy_a, dxy_b, jx, jy)
        + diagonal(axz1, bxz1, dxz_a, dxz_b, jx, jz)
        + diagonal(ayz1, byz1, dyz_a, dyz_b, jy, jz)
    )
    return [jnp.where(fluid, relaxed[p], f[OPPOSITE[p]]) for p in range(Q)]


def shift_y(value, step, lane):
    rows = value.shape[0]
    if step == 1:
        turned = pltpu.roll(value, B, 1)
        return jnp.where(lane < B, pltpu.roll(turned, 1, 0), turned)
    turned = pltpu.roll(value, LANES - B, 1)
    return jnp.where(lane >= LANES - B, pltpu.roll(turned, rows - 1, 0), turned)


def shift_z(value, other, step, lane):
    if step == 1:
        return jnp.where(
            lane % B == 0, pltpu.roll(other, LANES - (B - 1), 1), pltpu.roll(value, 1, 1)
        )
    return jnp.where(
        lane % B == B - 1, pltpu.roll(other, B - 1, 1), pltpu.roll(value, LANES - 1, 1)
    )


def collide_and_pass(take, fluid_at, planes, rows, post, body, high, low):
    for i in range(planes):
        for kz in range(NB):
            after = collide([take(p, i, kz) for p in range(Q)], fluid_at(i, kz))
            for p in range(Q):
                post[p, i, kz] = after[p]
    lane = lax.broadcasted_iota(jnp.int32, (rows, LANES), 1)
    for i in range(planes):
        for p in range(Q):
            cx, cy, cz = VELOCITIES[p]
            pair = [post[p, i, kz] for kz in range(NB)]
            if cy:
                pair = [shift_y(value, cy, lane) for value in pair]
            if cz:
                pair = [shift_z(pair[kz], pair[1 - kz], cz, lane) for kz in range(NB)]
            for kz in range(NB):
                if cx == 1 and i == planes - 1:
                    high[UPWARD.index(p), kz] = pair[kz]
                elif cx == -1 and i == 0:
                    low[DOWNWARD.index(p), kz] = pair[kz]
                else:
                    body[p, i + cx, kz] = pair[kz]


def taker(planes, body, from_below, from_above):
    def take(p, i, kz, rows=slice(None)):
        cx = VELOCITIES[p][0]
        if cx == 1 and i == 0:
            return from_below[UPWARD.index(p), kz, rows]
        if cx == -1 and i == planes - 1:
            return from_above[DOWNWARD.index(p), kz, rows]
        return body[p, i, kz, rows]

    return take


def build(mesh):
    owners, slabs = mesh.shape["gx"], mesh.shape["gy"]
    planes = B // owners
    count = planes * PLANE_ROWS
    rows = owners * PLANE_ROWS
    slot_rows_in = (Q + 1) * count
    head = NB * slot_rows_in
    rows_in = head + 8
    slot_rows_out = Q * count
    rows_out = NB * slot_rows_out
    blocks = NB * owners
    f32 = jnp.float32

    def pack_kernel(odd_ref, pops, mask, slots, swaps, out):
        odd = odd_ref[0]
        lane = lax.broadcasted_iota(jnp.int32, (8, LANES), 1)
        header = jnp.zeros((8, LANES), jnp.int32)
        for t in range(NB):
            header = jnp.where(lane == t, slots[0, t], header)
        for r in range(3):
            header = jnp.where(lane == NB + r, swaps[0, 0, r, 0], header)
        header = header.astype(f32)
        for place in range(owners):
            d = dynamic_owner(place, odd, owners)
            for t in range(NB):
                for c in range(count):
                    cells = pl.ds((place * count + c) * LANES, LANES)
                    for p0 in range(0, Q, 8):
                        n = min(8, Q - p0)
                        out[d, pl.ds(t * slot_rows_in + p0 * count + c, n, stride=count), :] = pops[
                            t, p0 : p0 + n, cells
                        ]
                    out[d, pl.ds(t * slot_rows_in + Q * count + c, 1), :] = mask[
                        t : t + 1, cells
                    ].astype(f32)
            out[d, pl.ds(head, 8), :] = header

    def first_kernel(got, body, fluid, high, low, final, lattice, post, table, inverse, sem):
        copies = [
            pltpu.make_async_copy(got.at[g, pl.ds(head, 1), :], table.at[pl.ds(g, 1), :], sem.at[g])
            for g in range(owners)
        ]
        for copy in copies:
            copy.start()
        for copy in copies:
            copy.wait()
        held = [
            [table[g, t].astype(jnp.int32) for t in range(NB)] for g in range(owners)
        ]
        first = [
            [table[g, NB + r].astype(jnp.int32) for r in range(3)] for g in range(owners)
        ]
        for g in range(owners):
            for t in range(NB):
                inverse[held[g][t]] = g * NB + t
        for g in range(owners):
            flip = first[g][2] + first[g ^ 4][2] + first[g ^ 4][1]
            flip = flip + first[g ^ 6][1] + first[g ^ 6][0] + first[g ^ 7][0]
            crossed = flip % 2 == 1
            one, two = held[g ^ 7]
            final[g * NB] = jnp.where(crossed, two, one)
            final[g * NB + 1] = jnp.where(crossed, one, two)
        for b in range(blocks):
            ky, kz = b // NB, b % NB
            q = inverse[b]
            g, t = q // NB, q % NB
            for v in range(slot_rows_in // 8):
                start = pl.multiple_of(t * slot_rows_in + 8 * v, 8)
                chunk = got[g, pl.ds(start, 8), :]
                for r in range(0, 8, PLANE_ROWS):
                    p, c = (8 * v + r) // count, (8 * v + r) % count
                    lattice[p, c // PLANE_ROWS, kz, pl.ds(ky * PLANE_ROWS, PLANE_ROWS), :] = chunk[
                        r : r + PLANE_ROWS
                    ]
        fluid[...] = lattice[Q]
        collide_and_pass(
            lambda p, i, kz: lattice[p, i, kz],
            lambda i, kz: lattice[Q, i, kz] > 0.5,
            planes,
            rows,
            post,
            body,
            high,
            low,
        )

    def second_kernel(body_in, fluid, from_below, from_above, body, high, low, post):
        collide_and_pass(
            taker(planes, body_in, from_below, from_above),
            lambda i, kz: fluid[i, kz] > 0.5,
            planes,
            rows,
            post,
            body,
            high,
            low,
        )

    def sort_kernel(final, body, from_below, from_above, out):
        take = taker(planes, body, from_below, from_above)
        for g in range(owners):
            for t in range(NB):
                b = final[g * NB + t]
                kz = b % NB
                place = pl.ds(pl.multiple_of((b // NB) * PLANE_ROWS, PLANE_ROWS), PLANE_ROWS)
                for p in range(Q):
                    for i in range(planes):
                        at = t * slot_rows_out + p * count + i * PLANE_ROWS
                        out[g, pl.ds(at, PLANE_ROWS), :] = take(p, i, kz, place)

    def unpack_kernel(odd_ref, got, out):
        odd = odd_ref[0]
        for place in range(owners):
            g = dynamic_owner(place, odd, owners)
            for t in range(NB):
                for c in range(count):
                    cells = pl.ds((place * count + c) * LANES, LANES)
                    for p0 in range(0, Q, 8):
                        n = min(8, Q - p0)
                        out[0, t, p0 : p0 + n, cells] = got[
                            g, pl.ds(t * slot_rows_out + p0 * count + c, n, stride=count), :
                        ]

    def shape(*dims, dtype=f32):
        return jax.ShapeDtypeStruct(dims, dtype)

    body_shape = shape(Q, planes, NB, rows, LANES)
    face_shape = shape(len(UPWARD), NB, rows, LANES)
    post_scratch = pltpu.VMEM((Q, planes, NB, rows, LANES), f32)
    up_pairs = ring_pairs(owners, slabs, 1)
    down_pairs = ring_pairs(owners, slabs, -1)

    def shards(populations, solid_mask, slot_blocks, swap_slots):
        odd = (lax.axis_index("gy") % 2).astype(jnp.int32).reshape(1)
        packed = pl.pallas_call(
            pack_kernel,
            out_shape=shape(owners, rows_in, LANES),
            in_specs=[SMEM_SPEC, VMEM_SPEC, VMEM_SPEC, SMEM_SPEC, SMEM_SPEC],
            out_specs=VMEM_SPEC,
            compiler_params=PARAMS,
            name="pack",
        )(odd, populations[0], solid_mask[0], slot_blocks, swap_slots)
        got = lax.all_to_all(packed, "gx", 0, 0, tiled=True)
        body, fluid, high, low, final = pl.pallas_call(
            first_kernel,
            out_shape=(
                body_shape,
                shape(planes, NB, rows, LANES),
                face_shape,
                face_shape,
                shape(blocks, dtype=jnp.int32),
            ),
            in_specs=[VMEM_SPEC],
            out_specs=(VMEM_SPEC, VMEM_SPEC, VMEM_SPEC, VMEM_SPEC, SMEM_SPEC),
            scratch_shapes=[
                pltpu.VMEM((Q + 1, planes, NB, rows, LANES), f32),
                post_scratch,
                pltpu.SMEM((owners, LANES), f32),
                pltpu.SMEM((blocks,), jnp.int32),
                pltpu.SemaphoreType.DMA((owners,)),
            ],
            compiler_params=PARAMS,
            name="first_step",
        )(got)
        from_below = lax.ppermute(high, ("gx", "gy"), up_pairs)
        from_above = lax.ppermute(low, ("gx", "gy"), down_pairs)
        body, high, low = pl.pallas_call(
            second_kernel,
            out_shape=(body_shape, face_shape, face_shape),
            in_specs=[VMEM_SPEC] * 4,
            out_specs=(VMEM_SPEC,) * 3,
            scratch_shapes=[post_scratch],
            compiler_params=PARAMS,
            name="second_step",
        )(body, fluid, from_below, from_above)
        from_below = lax.ppermute(high, ("gx", "gy"), up_pairs)
        from_above = lax.ppermute(low, ("gx", "gy"), down_pairs)
        sorted_pieces = pl.pallas_call(
            sort_kernel,
            out_shape=shape(owners, rows_out, LANES),
            in_specs=[SMEM_SPEC, VMEM_SPEC, VMEM_SPEC, VMEM_SPEC],
            out_specs=VMEM_SPEC,
            compiler_params=PARAMS,
            name="sort_blocks",
        )(final, body, from_below, from_above)
        home = lax.all_to_all(sorted_pieces, "gx", 0, 0, tiled=True)
        return pl.pallas_call(
            unpack_kernel,
            out_shape=shape(1, NB, Q, B * B * B),
            in_specs=[SMEM_SPEC, VMEM_SPEC],
            out_specs=VMEM_SPEC,
            compiler_params=PARAMS,
            name="unpack",
        )(odd, home)

    return shards


def solution(mesh):
    return jax.shard_map(
        build(mesh),
        mesh=mesh,
        in_specs=(
            P("gy", "gx", None, None),
            P("gy", "gx", None),
            P("gy", "gx"),
            P("gy", "gx", None, None),
        ),
        out_specs=P("gy", "gx", None, None),
        check_vma=False,
    )
```

time: 680 us -> 65.4 us (0.10); the launches traced: 669 us -> 65.2 us
  blocking collectives: 378 us -> 45.7 us
  local copies, waits for them, and re-layouts: 180 us -> 4.17 us
  other arithmetic: 44 us -> 0 us
  waiting for transfers between devices: 41 us -> 7.19 us
  starting transfers between devices: 15.7 us -> 3.6 us
    all_gather x12 -> x0, blocking collectives: 367 us -> none  [the longest x6 184 us: collect(): lax.all_gather(face_pair[1], 'gx', axis=0, tiled=True)]
    another operation x24 -> x0, local copies, waits for them, and re-layouts: 51.8 us -> none  [the longest x6 25.4 us: stream_y(): jnp.tile(widen(from_below.reshape(slot_count, 5, side_cells, side_cells),...]
    all_to_all x0 -> x2, blocking collectives: none -> 45.7 us  [the longest x1 25.4 us: shards(): got = lax.all_to_all(packed, 'gx', 0, 0, tiled=True)]
    ppermute x13 -> x4, waiting for transfers between devices: 41 us -> 7.19 us  [the longest x2 4.24 us: shards(): from_below = lax.ppermute(high, ('gx', 'gy'), up_pairs)]
    gather x60 -> x0, local copies, waits for them, and re-layouts: 28 us -> none  [the longest x20 7.73 us: faces_from(): return (got_high[slab_slots[below]], got_low[slab_slots[above]])]
    select_n x16 -> x0, other arithmetic: 24.2 us -> none  [the longest x2 14.5 us: stream_z(): jnp.where(plus_mask, moved_up, jnp.where(minus_mask, moved_down, lattice_...]
    reshape x30 -> x0, local copies, waits for them, and re-layouts: 23.5 us -> none  [the longest x2 11 us: stream_z(): jnp.repeat(widen(from_above.reshape(slot_count, 5, side_cells, side_cells...]
    scatter x26 -> x0, local copies, waits for them, and re-layouts: 19.2 us -> none  [the longest x20 15.3 us: widen(): return filled.at[:, chosen_index].set(face_five)]
  transfers between devices with their start and end apart: 13 -> 4, of which waited for: 7 -> 4; matrix products, arithmetic and copies ran while one was open for 5% -> 0% of each run, Pallas kernels for 0% -> 0%
where the time goes in v1:
time: 65.4 us; the launch traced here: 65.2 us
  blocking collectives  45.7 us (70%)
  waiting for transfers between devices  7.19 us (11%)
  Pallas kernels  4.39 us (7%)
  local copies, waits for them, and re-layouts  4.17 us (6%)
  starting transfers between devices  3.6 us (6%)
    all_to_all x1, blocking collectives, shards(): got = lax.all_to_all(packed, 'gx', 0, 0, tiled=True)  25.4 us
    all_to_all x1, blocking collectives, shards(): home = lax.all_to_all(sorted_pieces, 'gx', 0, 0, tiled=True)  20.4 us
    ppermute x2, waiting for transfers between devices, shards(): from_below = lax.ppermute(high, ('gx', 'gy'), up_pairs)  4.24 us
    ppermute x2, waiting for transfers between devices, shards(): from_above = lax.ppermute(low, ('gx', 'gy'), down_pairs)  2.95 us
    unnamed x8, local copies, waits for them, and re-layouts  2.86 us
    pallas_call x1, Pallas kernels, shards(): pl.pallas_call(first_kernel, out_shape=(body_shape, shape(planes, NB, row...  2.1 us
    ppermute x2, starting transfers between devices, shards(): from_below = lax.ppermute(high, ('gx', 'gy'), up_pairs)  1.91 us
    ppermute x2, starting transfers between devices, shards(): from_above = lax.ppermute(low, ('gx', 'gy'), down_pairs)  1.69 us
  transfers between devices with their start and end apart: 4, of which 4 were waited for; matrix products, arithmetic and copies ran while one was open for 0% of the time, Pallas kernels for 0%

profile of v1, /device:TPU:0, one launch (start us, length us, event | category | flops | bytes accessed | tf_op | source)
XLA Modules:
  0.0 65.2 jit_solution(18299081351240421415)
XLA Ops:
  0.0 0.0 copy-start.2
  0.0 0.7 %copy-done.2 = s32[1,1,3,2]{2,3,1,0:T(2,128)S(1)} copy-done((s32[1,1,3,2]{2,3,1,0:T(2,128)S(1)}, s32[1,1,3,2]{2,3,1,0:T(2,128)}, u32[]{:S(2)}) %copy-start.2) | copy-done | bytes 48
  0.7 0.1 copy.6.swaps
  0.8 0.0 copy-start
  0.8 1.4 %copy.9 = f32[1,2,19,4096]{3,2,1,0:T(8,128)S(1)} copy(f32[1,2,19,4096]{3,1,2,0:T(2,128)} %param.4) | data formatting | bytes 1245184 | tf_op args[0]
  2.2 0.0 copy-start.1
  2.2 0.0 copy-done
  2.3 0.6 copy-done.1
  2.9 0.7 %pack.1 = f32[8,168,128]{2,1,0:T(8,128)S(1)} custom-call(s32[1]{0:T(128)} %bitcast.odd_ref, f32[2,19,4096]{2,1,0:T(8,128)S(1)} %bitcast.5, s32[2,4096]{1,0:T(2,128)S(1)} %bitcast.6, s32[1,2]{1,0:T(1,128)S(1)} %copy-done.1, s32[1,1,3,2]{3,2,1,0:T(4,128)S(1)} %copy.6.swaps), custom_call_target="tpu_custom_call" | custom-call | tf_op jit(solution)/shard_map/pack/pallas_call | solution.py:319
  3.6 25.4 %all_to_all.10.got = f32[8,168,128]{2,1,0:T(8,128)S(1)} all-to-all(f32[8,168,128]{2,1,0:T(8,128)S(1)} %pack.1), channel_id=1, replica_groups=mesh['gx'=8,'gy'=4] {'gx'}, dimensions={0} | all-to-all | bytes 1376256 | tf_op jit(solution)/shard_map/all_to_all | solution.py:327
  28.9 2.1 %first_step.1 = (f32[19,2,2,16,128]{4,3,2,1,0:T(8,128)S(1)}, f32[2,2,16,128]{3,2,1,0:T(8,128)S(1)}, f32[5,2,16,128]{3,2,1,0:T(8,128)S(1)}, f32[5,2,16,128]{3,2,1,0:T(8,128)S(1)}, s32[16]{0:T(128)S(1)}) custom-call(f32[8,168,128]{2,1,0:T(8,128)S(1)} %all_to_all.10.got), custom_call_target="tpu_custom_call" | custom-call | tf_op jit(solution)/shard_map/first_step/pallas_call | solution.py:328
  31.0 1.3 %collective-permute-start = (f32[5,2,16,128]{3,2,1,0:T(8,128)S(1)}, f32[5,2,16,128]{3,2,1,0:T(8,128)S(1)}, u32[]{:S(2)}, u32[]{:S(2)}) collective-permute-start(f32[5,2,16,128]{3,2,1,0:T(8,128)S(1)} %get-tuple-element.16), channel_id=1, source_target_pairs={{0,4},{4,12},{12,8},{8,16},{16,20},{20,28},{28,24},{24,25},{25,29}... | collective-permute-start | bytes 245768 | tf_op jit(solution)/shard_map/ppermute | solution.py:349
  32.3 0.5 collective-permute-start.1
  32.8 2.1 %collective-permute-done.from_below = f32[5,2,16,128]{3,2,1,0:T(8,128)S(1)} collective-permute-done((f32[5,2,16,128]{3,2,1,0:T(8,128)S(1)}, f32[5,2,16,128]{3,2,1,0:T(8,128)S(1)}, u32[]{:S(2)}, u32[]{:S(2)}) %collective-permute-start) | collective-permute-done | bytes 81952 | tf_op jit(solution)/shard_map/ppermute | solution.py:349
  34.9 1.8 %collective-permute-done.1.from_above = f32[5,2,16,128]{3,2,1,0:T(8,128)S(1)} collective-permute-done((f32[5,2,16,128]{3,2,1,0:T(8,128)S(1)}, f32[5,2,16,128]{3,2,1,0:T(8,128)S(1)}, u32[]{:S(2)}, u32[]{:S(2)}) %collective-permute-start.1) | collective-permute-done | bytes 81952 | tf_op jit(solution)/shard_map/ppermute | solution.py:350
  36.7 0.7 %second_step.1 = (f32[19,2,2,16,128]{4,3,2,1,0:T(8,128)S(1)}, f32[5,2,16,128]{3,2,1,0:T(8,128)S(1)}, f32[5,2,16,128]{3,2,1,0:T(8,128)S(1)}) custom-call(f32[19,2,2,16,128]{4,3,2,1,0:T(8,128)S(1)} %get-tuple-element.14.body_in, f32[2,2,16,128]{3,2,1,0:T(8,128)S(1)} %get-tuple-element.15.fluid, f32[5,2,16,128]{3,2,1,0:T(8,128)S(1)} %collective-permute-done.from_below, ...), custom_call_target="tpu_custom_call" | custom-call | tf_op jit(solution)/shard_map/second_step/pallas_call | solution.py:351
  37.4 0.6 collective-permute-start.2
  38.1 1.2 %collective-permute-start.3 = (f32[5,2,16,128]{3,2,1,0:T(8,128)S(1)}, f32[5,2,16,128]{3,2,1,0:T(8,128)S(1)}, u32[]{:S(2)}, u32[]{:S(2)}) collective-permute-start(f32[5,2,16,128]{3,2,1,0:T(8,128)S(1)} %get-tuple-element.20), channel_id=1, source_target_pairs={{0,3},{4,0},{12,4},{8,12},{16,8},{20,16},{28,20},{24,28},{25,24},{... | collective-permute-start | bytes 245768 | tf_op jit(solution)/shard_map/ppermute | solution.py:361
  39.2 2.1 %collective-permute-done.2.from_below = f32[5,2,16,128]{3,2,1,0:T(8,128)S(1)} collective-permute-done((f32[5,2,16,128]{3,2,1,0:T(8,128)S(1)}, f32[5,2,16,128]{3,2,1,0:T(8,128)S(1)}, u32[]{:S(2)}, u32[]{:S(2)}) %collective-permute-start.2) | collective-permute-done | bytes 81952 | tf_op jit(solution)/shard_map/ppermute | solution.py:360
  41.3 1.2 %collective-permute-done.3.from_above = f32[5,2,16,128]{3,2,1,0:T(8,128)S(1)} collective-permute-done((f32[5,2,16,128]{3,2,1,0:T(8,128)S(1)}, f32[5,2,16,128]{3,2,1,0:T(8,128)S(1)}, u32[]{:S(2)}, u32[]{:S(2)}) %collective-permute-start.3) | collective-permute-done | bytes 81952 | tf_op jit(solution)/shard_map/ppermute | solution.py:361
  42.5 0.9 %sort_blocks.1 = f32[8,152,128]{2,1,0:T(8,128)S(1)} custom-call(s32[16]{0:T(128)S(1)} %get-tuple-element.13.final, f32[19,2,2,16,128]{4,3,2,1,0:T(8,128)S(1)} %get-tuple-element.18.body, f32[5,2,16,128]{3,2,1,0:T(8,128)S(1)} %collective-permute-done.2.from_below, f32[5,2,16,128]{3,2,1,0:T(8,128)S(1)} %collective-permute-done.3.from_above), custom_call_target="tpu_custom_call" | custom-call | tf_op jit(solution)/shard_map/sort_blocks/pallas_call | solution.py:362
  43.4 20.4 %all_to_all.11.got = f32[8,152,128]{2,1,0:T(8,128)S(1)} all-to-all(f32[8,152,128]{2,1,0:T(8,128)S(1)} %sort_blocks.1), channel_id=1, replica_groups=mesh['gx'=8,'gy'=4] {'gx'}, dimensions={0} | all-to-all | bytes 1245184 | tf_op jit(solution)/shard_map/all_to_all | solution.py:370
  63.8 0.1 unpack.1
  63.9 1.3 %copy.7 = f32[1,2,19,4096]{3,1,2,0:T(2,128)} copy(f32[1,2,19,4096]{3,2,1,0:T(8,128)S(1)} %unpack.1) | data formatting | bytes 1245184 | tf_op jit(solution)/shard_map/unpack/pallas_call | solution.py:371
Async XLA Ops:
  0.0 0.7 %copy-start.2 = (s32[1,1,3,2]{2,3,1,0:T(2,128)S(1)}, s32[1,1,3,2]{2,3,1,0:T(2,128)}, u32[]{:S(2)}) copy-start(s32[1,1,3,2]{2,3,1,0:T(2,128)} %param.7) | copy-start | bytes 76
  0.8 1.5 %copy-start = (s32[1,2,4096]{2,1,0:T(2,128)S(1)}, s32[1,2,4096]{2,1,0:T(2,128)}, u32[]{:S(2)}) copy-start(s32[1,2,4096]{2,1,0:T(2,128)} %param.5) | copy-start | bytes 98308
  2.2 0.7 %copy-start.1 = (s32[1,2]{1,0:T(1,128)S(1)}, s32[1,2]{1,0:T(1,128)}, u32[]{:S(2)}) copy-start(s32[1,2]{1,0:T(1,128)} %slots.1) | copy-start | bytes 28
  31.0 3.9 %collective-permute-start = (f32[5,2,16,128]{3,2,1,0:T(8,128)S(1)}, f32[5,2,16,128]{3,2,1,0:T(8,128)S(1)}, u32[]{:S(2)}, u32[]{:S(2)}) collective-permute-start(f32[5,2,16,128]{3,2,1,0:T(8,128)S(1)} %get-tuple-element.16), channel_id=1, source_target_pairs={{0,4},{4,12},{12,8},{8,16},{16,20},{20,28},{28,24},{24,25},{25,29}... | collective-permute-start | bytes 245768 | tf_op jit(solution)/shard_map/ppermute | solution.py:349
  32.3 4.4 %collective-permute-start.1 = (f32[5,2,16,128]{3,2,1,0:T(8,128)S(1)}, f32[5,2,16,128]{3,2,1,0:T(8,128)S(1)}, u32[]{:S(2)}, u32[]{:S(2)}) collective-permute-start(f32[5,2,16,128]{3,2,1,0:T(8,128)S(1)} %get-tuple-element.17), channel_id=1, source_target_pairs={{0,3},{4,0},{12,4},{8,12},{16,8},{20,16},{28,20},{24,28},{25,24},{... | collective-permute-start | bytes 245768 | tf_op jit(solution)/shard_map/ppermute | solution.py:350
  37.4 3.9 %collective-permute-start.2 = (f32[5,2,16,128]{3,2,1,0:T(8,128)S(1)}, f32[5,2,16,128]{3,2,1,0:T(8,128)S(1)}, u32[]{:S(2)}, u32[]{:S(2)}) collective-permute-start(f32[5,2,16,128]{3,2,1,0:T(8,128)S(1)} %get-tuple-element.19), channel_id=1, source_target_pairs={{0,4},{4,12},{12,8},{8,16},{16,20},{20,28},{28,24},{24,25},{25,29}... | collective-permute-start | bytes 245768 | tf_op jit(solution)/shard_map/ppermute | solution.py:360
  38.1 4.4 %collective-permute-start.3 = (f32[5,2,16,128]{3,2,1,0:T(8,128)S(1)}, f32[5,2,16,128]{3,2,1,0:T(8,128)S(1)}, u32[]{:S(2)}, u32[]{:S(2)}) collective-permute-start(f32[5,2,16,128]{3,2,1,0:T(8,128)S(1)} %get-tuple-element.20), channel_id=1, source_target_pairs={{0,3},{4,0},{12,4},{8,12},{16,8},{20,16},{28,20},{24,28},{25,24},{... | collective-permute-start | bytes 245768 | tf_op jit(solution)/shard_map/ppermute | solution.py:361

commit v2 on v1

v2 whole, which is shorter than its diff:
```python
import jax
import jax.numpy as jnp
from jax import lax
from jax.experimental import pallas as pl
from jax.experimental.pallas import tpu as pltpu
from jax.sharding import PartitionSpec as P

B = 16
NB = 2
LANES = 128
PLANE_ROWS = B * B // LANES
PLANE = PLANE_ROWS * NB
WHOLE = B * PLANE

VELOCITIES = (
    (0, 0, 0),
    (1, 0, 0),
    (-1, 0, 0),
    (0, 1, 0),
    (0, -1, 0),
    (0, 0, 1),
    (0, 0, -1),
    (1, 1, 0),
    (-1, -1, 0),
    (1, -1, 0),
    (-1, 1, 0),
    (1, 0, 1),
    (-1, 0, -1),
    (1, 0, -1),
    (-1, 0, 1),
    (0, 1, 1),
    (0, -1, -1),
    (0, 1, -1),
    (0, -1, 1),
)
OPPOSITE = (0, 2, 1, 4, 3, 6, 5, 8, 7, 10, 9, 12, 11, 14, 13, 16, 15, 18, 17)
Q = len(VELOCITIES)
UPWARD = tuple(p for p in range(Q) if VELOCITIES[p][0] == 1)
DOWNWARD = tuple(p for p in range(Q) if VELOCITIES[p][0] == -1)

VMEM_SPEC = pl.BlockSpec(memory_space=pltpu.VMEM)
PARAMS = pltpu.CompilerParams(vmem_limit_bytes=40 * 1024 * 1024)


def dynamic_place(owner, odd_slab, owners):
    pair, core = owner // 2, owner % 2
    forward = 2 * pair + jnp.where(pair % 2 == 0, core, 1 - core)
    return jnp.where(odd_slab == 1, owners - 1 - forward, forward)


def collide(f, fluid):
    def pair(p):
        return f[p] + f[p + 1], f[p] - f[p + 1]

    sx, dx = pair(1)
    sy, dy = pair(3)
    sz, dz = pair(5)
    sxy_a, dxy_a = pair(7)
    sxy_b, dxy_b = pair(9)
    sxz_a, dxz_a = pair(11)
    sxz_b, dxz_b = pair(13)
    syz_a, dyz_a = pair(15)
    syz_b, dyz_b = pair(17)
    axy, bxy = sxy_a + sxy_b, sxy_a - sxy_b
    axz, bxz = sxz_a + sxz_b, sxz_a - sxz_b
    ayz, byz = syz_a + syz_b, syz_a - syz_b
    rho = f[0] + sx + sy + sz + axy + axz + ayz
    ox = dxy_a + dxy_b + dxz_a + dxz_b
    oy = dxy_a - dxy_b + dyz_a + dyz_b
    oz = dxz_a - dxz_b + dyz_a - dyz_b
    jx, jy, jz = dx + ox, dy + oy, dz + oz
    jxx, jyy, jzz = jx * jx, jy * jy, jz * jz
    base = rho * (1.3 / 9.0)
    wide = 1.3 / 3.0
    thin = 1.3 / 6.0
    axy1 = base - 0.3 * axy + wide * (jxx + jyy) - thin * jzz
    axz1 = base - 0.3 * axz + wide * (jxx + jzz) - thin * jyy
    ayz1 = base - 0.3 * ayz + wide * (jyy + jzz) - thin * jxx
    bxy1 = 1.25 * (jx * jy) - 0.25 * bxy
    bxz1 = 1.25 * (jx * jz) - 0.25 * bxz
    byz1 = 1.25 * (jy * jz) - 0.25 * byz
    third = rho * (1.25 / 3.0)
    sx1 = third + 1.25 * jxx - 0.25 * (sx + axy + axz) - axy1 - axz1
    sy1 = third + 1.25 * jyy - 0.25 * (sy + axy + ayz) - axy1 - ayz1
    sz1 = third + 1.25 * jzz - 0.25 * (sz + axz + ayz) - axz1 - ayz1
    rest = rho - sx1 - sy1 - sz1 - axy1 - axz1 - ayz1

    def split(even, odd):
        return 0.5 * (even + odd), 0.5 * (even - odd)

    def diagonal(a1, b1, d_a, d_b, j_first, j_second):
        plus = 0.25 * (j_first + j_second) - 0.5 * d_a
        minus = 0.25 * (j_first - j_second) - 0.5 * d_b
        return split(0.5 * (a1 + b1), plus) + split(0.5 * (a1 - b1), minus)

    relaxed = (
        (rest,)
        + split(sx1, 0.5 * ox)
        + split(sy1, 0.5 * oy)
        + split(sz1, 0.5 * oz)
        + diagonal(axy1, bxy1, dxy_a, dxy_b, jx, jy)
        + diagonal(axz1, bxz1, dxz_a, dxz_b, jx, jz)
        + diagonal(ayz1, byz1, dyz_a, dyz_b, jy, jz)
    )
    return [jnp.where(fluid, relaxed[p], f[OPPOSITE[p]]) for p in range(Q)]


def shift_y(value, step, lane):
    rows = value.shape[0]
    if step == 1:
        turned = pltpu.roll(value, B, 1)
        return jnp.where(lane < B, pltpu.roll(turned, 1, 0), turned)
    turned = pltpu.roll(value, LANES - B, 1)
    return jnp.where(lane >= LANES - B, pltpu.roll(turned, rows - 1, 0), turned)


def shift_z(value, other, step, lane):
    if step == 1:
        return jnp.where(
            lane % B == 0, pltpu.roll(other, LANES - (B - 1), 1), pltpu.roll(value, 1, 1)
        )
    return jnp.where(
        lane % B == B - 1, pltpu.roll(other, B - 1, 1), pltpu.roll(value, LANES - 1, 1)
    )


def build(mesh):
    owners, slabs = mesh.shape["gx"], mesh.shape["gy"]
    planes = B // owners
    share = planes * PLANE
    rows = owners * PLANE_ROWS
    head = (Q + 1) * share
    rows_in = head + 8
    rows_out = Q * share
    faces = len(UPWARD) * PLANE
    rows_hop = faces + 4
    f32 = jnp.float32

    def position():
        me = lax.axis_index("gx")
        return me, lax.axis_index("gy") % 2

    def edge_kernel(pops, mask, slots, swaps, up, down):
        for start, out, chosen, inside in (
            (WHOLE - 8, up, UPWARD, 8 - PLANE),
            (0, down, DOWNWARD, 0),
        ):
            f = [pops[pl.ds(p * WHOLE + start, 8), :] for p in range(Q)]
            after = collide(f, mask[pl.ds(start, 8), :] > 0)
            for n, p in enumerate(chosen):
                out[pl.ds(n * PLANE, PLANE), :] = after[p][inside : inside + PLANE]
            out[pl.ds(faces, 4), :] = jnp.zeros((4, LANES), f32)
            out[pl.ds(faces, 1), 0:NB] = slots[...].astype(f32)
            out[pl.ds(faces + 1, 1), 0:3] = swaps[0:1].astype(f32)

    def collide_kernel(pops, mask, post):
        for start in range(0, WHOLE, 8):
            f = [pops[pl.ds(p * WHOLE + start, 8), :] for p in range(Q)]
            after = collide(f, mask[pl.ds(start, 8), :] > 0)
            for p in range(Q):
                post[p, pl.ds(8 + start, 8), :] = after[p]

    def pack_kernel(post, mask, slots, swaps, below, above, *outs):
        me, odd = position()
        own = jnp.zeros((4, LANES), f32)
        for d in range(owners):
            out = outs[d]
            place = dynamic_place(me ^ d, odd, owners)
            here = pl.multiple_of(place * share, min(share, 8))
            for p in range(Q):
                cx = VELOCITIES[p][0]
                out[pl.ds(p * share, share), :] = post[p, pl.ds(8 + here - cx * PLANE, share), :]
            out[pl.ds(Q * share, share), :] = mask[pl.ds(here, share), :].astype(f32)
            out[pl.ds(head, 4), :] = own
            out[pl.ds(head, 1), 0:NB] = slots[...].astype(f32)
            out[pl.ds(head + 1, 1), 0:3] = swaps[0:1].astype(f32)
            out[pl.ds(head + 2, 2), :] = below[pl.ds(faces, 2), :]
            out[pl.ds(head + 4, 2), :] = above[pl.ds(faces, 2), :]
            out[pl.ds(head + 6, 2), :] = own[0:2]

            @pl.when(place == 0)
            def _():
                for n, p in enumerate(UPWARD):
                    out[pl.ds(p * share, PLANE), :] = below[pl.ds(n * PLANE, PLANE), :]

            @pl.when(place == owners - 1)
            def _():
                for n, p in enumerate(DOWNWARD):
                    out[pl.ds(p * share + share - PLANE, PLANE), :] = above[
                        pl.ds(n * PLANE, PLANE), :
                    ]

    def middle_kernel(*refs):
        got, outs = refs[:owners], refs[owners : 2 * owners]
        lattice, ready, table, sem = refs[2 * owners :]
        me, odd = position()
        place = dynamic_place(me, odd, owners)
        first, last = place == 0, place == owners - 1
        copies = [
            pltpu.make_async_copy(got[d].at[pl.ds(head, 8), :], table.at[d], sem.at[d])
            for d in range(owners)
        ]
        for copy in copies:
            copy.start()
        for copy in copies:
            copy.wait()

        def number(d, row, column):
            return table[d, row, column].astype(jnp.int32)

        def held(d, t, which):
            return number(d, 2 * which, t)

        def final(d, t, which):
            def lead(e, r):
                return number(d ^ e, 2 * which + 1, r)

            flip = lead(0, 2) + lead(4, 2) + lead(4, 1) + lead(6, 1) + lead(6, 0) + lead(7, 0)
            one, two = held(d ^ 7, t, which), held(d ^ 7, 1 - t, which)
            return jnp.where(flip % 2 == 1, two, one)

        def seat(b):
            return b % NB, pl.multiple_of((b // NB) * PLANE_ROWS, PLANE_ROWS)

        for d in range(owners):
            for t in range(NB):
                usual = held(d, t, 0)
                at_usual = seat(usual)
                at_below = seat(jnp.where(first, held(d, t, 1), usual))
                at_above = seat(jnp.where(last, held(d, t, 2), usual))
                for p in range(Q + 1):
                    cx = VELOCITIES[p][0] if p < Q else 0
                    for i in range(planes):
                        kz, y = at_usual
                        if cx == 1 and i == 0:
                            kz, y = at_below
                        if cx == -1 and i == planes - 1:
                            kz, y = at_above
                        lattice[p, i, kz, pl.ds(y, PLANE_ROWS), :] = got[d][
                            pl.ds(p * share + i * PLANE + t, PLANE_ROWS, stride=NB), :
                        ]
        lane = lax.broadcasted_iota(jnp.int32, (rows, LANES), 1)

        def passed(pair, p):
            cx, cy, cz = VELOCITIES[p]
            if cy:
                pair = [shift_y(value, cy, lane) for value in pair]
            if cz:
                pair = [shift_z(pair[kz], pair[1 - kz], cz, lane) for kz in range(NB)]
            return pair

        for i in range(planes):
            for p in range(Q):
                pair = passed([lattice[p, i, kz] for kz in range(NB)], p)
                for kz in range(NB):
                    ready[p, i, kz] = pair[kz]
            for kz in range(NB):
                after = collide([ready[p, i, kz] for p in range(Q)], lattice[Q, i, kz] > 0.5)
                for p in range(Q):
                    lattice[p, i, kz] = after[p]
            for p in range(Q):
                pair = passed([lattice[p, i, kz] for kz in range(NB)], p)
                for kz in range(NB):
                    ready[p, i, kz] = pair[kz]
        for d in range(owners):
            for t in range(NB):
                usual = final(d, t, 0)
                at_usual = seat(usual)
                at_below = seat(jnp.where(first, final(d, t, 1), usual))
                at_above = seat(jnp.where(last, final(d, t, 2), usual))
                for p in range(Q):
                    cx = VELOCITIES[p][0]
                    for i in range(planes):
                        kz, y = at_usual
                        if cx == 1 and i == planes - 1:
                            kz, y = at_above
                        if cx == -1 and i == 0:
                            kz, y = at_below
                        outs[d][pl.ds(p * share + i * PLANE + t, PLANE_ROWS, stride=NB), :] = ready[
                            p, i, kz, pl.ds(y, PLANE_ROWS), :
                        ]

    def crossing_kernel(*refs):
        got, up, down = refs[:owners], refs[owners], refs[owners + 1]
        me, odd = position()
        for d in range(owners):
            place = dynamic_place(me ^ d, odd, owners)

            @pl.when(place == owners - 1)
            def _():
                for n, p in enumerate(UPWARD):
                    up[pl.ds(n * PLANE, PLANE), :] = got[d][
                        pl.ds(p * share + share - PLANE, PLANE), :
                    ]

            @pl.when(place == 0)
            def _():
                for n, p in enumerate(DOWNWARD):
                    down[pl.ds(n * PLANE, PLANE), :] = got[d][pl.ds(p * share, PLANE), :]

        for out in (up, down):
            out[pl.ds(faces, 4), :] = jnp.zeros((4, LANES), f32)

    def unpack_kernel(*refs):
        got, main = refs[:owners], refs[owners]
        me, odd = position()
        for d in range(owners):
            place = dynamic_place(me ^ d, odd, owners)
            here = pl.multiple_of(place * share, min(share, 8))
            for p in range(Q):
                cx = VELOCITIES[p][0]
                main[p, pl.ds(8 + here + cx * PLANE, share), :] = got[d][
                    pl.ds(p * share, share), :
                ]

    def finish_kernel(main, below, above, out):
        for p in range(Q):
            out[pl.ds(p * WHOLE, WHOLE), :] = main[p, pl.ds(8, WHOLE), :]
        for n, p in enumerate(UPWARD):
            out[pl.ds(p * WHOLE, PLANE), :] = below[pl.ds(n * PLANE, PLANE), :]
        for n, p in enumerate(DOWNWARD):
            out[pl.ds(p * WHOLE + WHOLE - PLANE, PLANE), :] = above[pl.ds(n * PLANE, PLANE), :]

    def shape(*dims):
        return jax.ShapeDtypeStruct(dims, f32)

    def call(kernel, name, out_shape, inputs, cost, scratch=()):
        outs = jax.tree.map(lambda _: VMEM_SPEC, out_shape)
        return pl.pallas_call(
            kernel,
            out_shape=out_shape,
            in_specs=[VMEM_SPEC] * len(inputs),
            out_specs=outs,
            scratch_shapes=list(scratch),
            compiler_params=PARAMS,
            cost_estimate=pl.CostEstimate(flops=cost, bytes_accessed=cost, transcendentals=0),
            name=name,
        )(*inputs)

    def exchange(parts):
        here = [parts[0]]
        for d in range(1, owners):
            here.append(lax.ppermute(parts[d], "gx", [(g, g ^ d) for g in range(owners)]))
        return here

    def hop(up, down):
        return (
            lax.ppermute(up, "gy", [(s, (s + 1) % slabs) for s in range(slabs)]),
            lax.ppermute(down, "gy", [(s, (s - 1) % slabs) for s in range(slabs)]),
        )

    padded = shape(Q, 8 + WHOLE + 8, LANES)
    work = pltpu.VMEM((Q + 1, planes, NB, rows, LANES), f32)
    small, large = 100_000, 4_000_000

    def shards(populations, solid_mask, slot_blocks, swap_slots):
        tiles = B * B * B // LANES
        pops = populations[0].transpose(1, 0, 2).reshape(Q, NB, tiles, LANES)
        pops = pops.transpose(0, 2, 1, 3).reshape(Q * WHOLE, LANES)
        mask = solid_mask[0].reshape(NB, tiles, LANES).transpose(1, 0, 2).reshape(WHOLE, LANES)
        swaps = swap_slots[0, 0].T
        up, down = call(
            edge_kernel,
            "edge_planes",
            (shape(rows_hop, LANES),) * 2,
            (pops, mask, slot_blocks, swaps),
            small,
        )
        below, above = hop(up, down)
        post = call(collide_kernel, "first_collision", padded, (pops, mask), large)
        parts = call(
            pack_kernel,
            "pack_planes",
            (shape(rows_in, LANES),) * owners,
            (post, mask, slot_blocks, swaps, below, above),
            large,
        )
        got = exchange(parts)
        parts = call(
            middle_kernel,
            "second_step",
            (shape(rows_out, LANES),) * owners,
            got,
            large,
            (
                work,
                work,
                pltpu.SMEM((owners, 8, LANES), f32),
                pltpu.SemaphoreType.DMA((owners,)),
            ),
        )
        home = exchange(parts)
        up, down = call(crossing_kernel, "crossing_planes", (shape(rows_hop, LANES),) * 2, home, small)
        below, above = hop(up, down)
        main = call(unpack_kernel, "unpack_planes", padded, home, large)
        out = call(
            finish_kernel, "finish", shape(Q * WHOLE, LANES), (main, below, above), small
        )
        out = out.reshape(Q, tiles, NB, LANES).transpose(0, 2, 1, 3)
        return out.reshape(Q, NB, B * B * B).transpose(1, 0, 2)[None]

    return shards


def solution(mesh):
    return jax.shard_map(
        build(mesh),
        mesh=mesh,
        in_specs=(
            P("gy", "gx", None, None),
            P("gy", "gx", None),
            P("gy", "gx"),
            P("gy", "gx", None, None),
        ),
        out_specs=P("gy", "gx", None, None),
        check_vma=False,
    )
```

time: 65.4 us -> 57.5 us (0.88); the launches traced: 65.2 us -> 56.4 us
  blocking collectives: 45.7 us -> 0 us
  starting transfers between devices: 3.6 us -> 29.8 us
  waiting for transfers between devices: 7.19 us -> 18.9 us
  local copies, waits for them, and re-layouts: 4.17 us -> 2.51 us
    all_to_all x2 -> x0, blocking collectives: 45.7 us -> none  [the longest x1 25.4 us: shards(): got = lax.all_to_all(packed, 'gx', 0, 0, tiled=True)]
    ppermute x4 -> x18, starting transfers between devices: 3.6 us -> 29.8 us  [the longest x14 25.6 us: exchange(): lax.ppermute(parts[d], 'gx', [(g, g ^ d) for g in range(owners)])]
    ppermute x4 -> x18, waiting for transfers between devices: 7.19 us -> 18.9 us  [the longest x14 16.5 us: exchange(): lax.ppermute(parts[d], 'gx', [(g, g ^ d) for g in range(owners)])]
    pallas_call x1 -> x0, local copies, waits for them, and re-layouts: 1.31 us -> none  [shards(): pl.pallas_call(unpack_kernel, out_shape=shape(1, NB, Q, B * B * B), in_sp...]
    pallas_call x5 -> x7, Pallas kernels: 4.39 us -> 5.04 us  [call(): pl.pallas_call(kernel, out_shape=out_shape, in_specs=[VMEM_SPEC] * len(in...]
  transfers between devices with their start and end apart: 4 -> 18, of which waited for: 4 -> 7; matrix products, arithmetic and copies ran while one was open for 0% -> 0% of each run, Pallas kernels for 0% -> 1%
where the time goes in v2:
time: 57.5 us; the launch traced here: 56.4 us
  starting transfers between devices  29.8 us (52%)
  waiting for transfers between devices  18.9 us (33%)
  Pallas kernels  5.04 us (9%)
  local copies, waits for them, and re-layouts  2.51 us (4%)
    ppermute x14, starting transfers between devices, exchange(): lax.ppermute(parts[d], 'gx', [(g, g ^ d) for g in range(owners)])  25.6 us
    ppermute x14, waiting for transfers between devices, exchange(): lax.ppermute(parts[d], 'gx', [(g, g ^ d) for g in range(owners)])  16.5 us
    pallas_call x7, Pallas kernels, call(): pl.pallas_call(kernel, out_shape=out_shape, in_specs=[VMEM_SPEC] * len(in...  5.04 us
    ppermute x2, starting transfers between devices, hop(): lax.ppermute(down, 'gy', [(s, (s - 1) % slabs) for s in range(slabs)])  3.72 us
    unnamed x8, local copies, waits for them, and re-layouts  2.51 us
    ppermute x2, waiting for transfers between devices, hop(): lax.ppermute(up, 'gy', [(s, (s + 1) % slabs) for s in range(slabs)])  2.32 us
  transfers between devices with their start and end apart: 18, of which 7 were waited for; matrix products, arithmetic and copies ran while one was open for 0% of the time, Pallas kernels for 1%

profile of v2, /device:TPU:0, one launch (start us, length us, event | category | flops | bytes accessed | tf_op | source)
XLA Modules:
  0.0 56.4 jit_solution(5208925982163926216)
XLA Ops:
  0.0 0.0 copy-start.2
  0.0 0.0 copy-start.3
  0.0 0.7 %copy-done.2 = s32[1,1,3,2]{2,3,1,0:T(2,128)S(1)} copy-done((s32[1,1,3,2]{2,3,1,0:T(2,128)S(1)}, s32[1,1,3,2]{2,3,1,0:T(2,128)}, u32[]{:S(2)}) %copy-start.2) | copy-done | bytes 48
  0.7 0.0 copy-done.3
  0.7 1.1 %copy-done = f32[1,2,19,4096]{3,1,2,0:T(2,128)S(1)} copy-done((f32[1,2,19,4096]{3,1,2,0:T(2,128)S(1)}, f32[1,2,19,4096]{3,1,2,0:T(2,128)}, u32[]{:S(2)}) %copy-start) | copy-done | bytes 622616
  1.8 0.8 %copy-done.1 = s32[1,2,4096]{2,1,0:T(2,128)S(1)} copy-done((s32[1,2,4096]{2,1,0:T(2,128)S(1)}, s32[1,2,4096]{2,1,0:T(2,128)}, u32[]{:S(2)}) %copy-start.1) | copy-done | bytes 32792
  2.6 0.5 collective-permute-start
  3.1 2.0 %collective-permute-start.1 = (f32[24,128]{1,0:T(8,128)S(1)}, f32[24,128]{1,0:T(8,128)S(1)}, u32[]{:S(2)}, u32[]{:S(2)}) collective-permute-start(f32[24,128]{1,0:T(8,128)S(1)} %get-tuple-element.26), channel_id=1, source_target_pairs={{0,3},{1,0},{2,1},{3,2},{4,7},{5,4},{6,5},{7,6},{8,11},{9,8},{10,9... | collective-permute-start | bytes 36872 | tf_op jit(solution)/shard_map/ppermute | solution.py:349
  5.1 0.2 first_collision.1.post
  5.3 1.1 %collective-permute-done.below = f32[24,128]{1,0:T(8,128)S(1)} collective-permute-done((f32[24,128]{1,0:T(8,128)S(1)}, f32[24,128]{1,0:T(8,128)S(1)}, u32[]{:S(2)}, u32[]{:S(2)}) %collective-permute-start) | collective-permute-done | bytes 12320 | tf_op jit(solution)/shard_map/ppermute | solution.py:348
  6.4 0.1 collective-permute-done.1.above
  6.5 0.2 pack_planes.1
  6.7 2.3 %collective-permute-start.2 = (f32[168,128]{1,0:T(8,128)S(1)}, f32[168,128]{1,0:T(8,128)S(1)}, u32[]{:S(2)}, u32[]{:S(2)}) collective-permute-start(f32[168,128]{1,0:T(8,128)S(1)} %get-tuple-element.28), channel_id=1, source_target_pairs={{0,4},{4,0},{8,12},{12,8},{16,20},{20,16},{24,28},{28,24},{1,5},{5... | collective-permute-start | bytes 258056 | tf_op jit(solution)/shard_map/ppermute | solution.py:343
  9.0 1.6 %collective-permute-start.3 = (f32[168,128]{1,0:T(8,128)S(1)}, f32[168,128]{1,0:T(8,128)S(1)}, u32[]{:S(2)}, u32[]{:S(2)}) collective-permute-start(f32[168,128]{1,0:T(8,128)S(1)} %get-tuple-element.29), channel_id=1, source_target_pairs={{0,8},{4,12},{8,0},{12,4},{16,24},{20,28},{24,16},{28,20},{1,9},{5... | collective-permute-start | bytes 258056 | tf_op jit(solution)/shard_map/ppermute | solution.py:343
  10.6 0.0 collective-permute-start.4
  10.6 3.0 %collective-permute-start.5 = (f32[168,128]{1,0:T(8,128)S(1)}, f32[168,128]{1,0:T(8,128)S(1)}, u32[]{:S(2)}, u32[]{:S(2)}) collective-permute-start(f32[168,128]{1,0:T(8,128)S(1)} %get-tuple-element.31), channel_id=1, source_target_pairs={{0,16},{4,20},{8,24},{12,28},{16,0},{20,4},{24,8},{28,12},{1,17},{... | collective-permute-start | bytes 258056 | tf_op jit(solution)/shard_map/ppermute | solution.py:343
  13.6 1.3 %collective-permute-start.6 = (f32[168,128]{1,0:T(8,128)S(1)}, f32[168,128]{1,0:T(8,128)S(1)}, u32[]{:S(2)}, u32[]{:S(2)}) collective-permute-start(f32[168,128]{1,0:T(8,128)S(1)} %get-tuple-element.32), channel_id=1, source_target_pairs={{0,20},{4,16},{8,28},{12,24},{16,4},{20,0},{24,12},{28,8},{1,21},{... | collective-permute-start | bytes 258056 | tf_op jit(solution)/shard_map/ppermute | solution.py:343
  14.9 0.0 collective-permute-done.2.refs_1_
  14.9 3.6 %collective-permute-start.7 = (f32[168,128]{1,0:T(8,128)S(1)}, f32[168,128]{1,0:T(8,128)S(1)}, u32[]{:S(2)}, u32[]{:S(2)}) collective-permute-start(f32[168,128]{1,0:T(8,128)S(1)} %get-tuple-element.33), channel_id=1, source_target_pairs={{0,24},{4,28},{8,16},{12,20},{16,8},{20,12},{24,0},{28,4},{1,25},{... | collective-permute-start | bytes 258056 | tf_op jit(solution)/shard_map/ppermute | solution.py:343
  18.5 0.0 collective-permute-done.3.refs_2_
  18.5 0.0 collective-permute-start.8
  18.5 0.8 %collective-permute-done.4.refs_3_ = f32[168,128]{1,0:T(8,128)S(1)} collective-permute-done((f32[168,128]{1,0:T(8,128)S(1)}, f32[168,128]{1,0:T(8,128)S(1)}, u32[]{:S(2)}, u32[]{:S(2)}) %collective-permute-start.4) | collective-permute-done | bytes 86048 | tf_op jit(solution)/shard_map/ppermute | solution.py:343
  19.3 0.0 collective-permute-done.5.refs_4_
  19.3 8.8 %collective-permute-done.6.refs_5_ = f32[168,128]{1,0:T(8,128)S(1)} collective-permute-done((f32[168,128]{1,0:T(8,128)S(1)}, f32[168,128]{1,0:T(8,128)S(1)}, u32[]{:S(2)}, u32[]{:S(2)}) %collective-permute-start.6) | collective-permute-done | bytes 86048 | tf_op jit(solution)/shard_map/ppermute | solution.py:343
  28.0 0.0 collective-permute-done.7.refs_6_
  28.0 0.0 collective-permute-done.8.refs_7_
  28.0 3.4 %second_step.1 = (f32[152,128]{1,0:T(8,128)S(1)}, f32[152,128]{1,0:T(8,128)S(1)}, f32[152,128]{1,0:T(8,128)S(1)}, f32[152,128]{1,0:T(8,128)S(1)}, f32[152,128]{1...) custom-call(f32[168,128]{1,0:T(8,128)S(1)} %get-tuple-element.27.refs_0_, ...), custom_call_target="tpu_custom_call" | custom-call | flops 4000000 | bytes 4000000 | tf_op jit(solution)/shard_map/second_step/pallas_call | solution.py:329
  31.5 1.1 %collective-permute-start.9 = (f32[152,128]{1,0:T(8,128)S(1)}, f32[152,128]{1,0:T(8,128)S(1)}, u32[]{:S(2)}, u32[]{:S(2)}) collective-permute-start(f32[152,128]{1,0:T(8,128)S(1)} %get-tuple-element.36), channel_id=1, source_target_pairs={{0,4},{4,0},{8,12},{12,8},{16,20},{20,16},{24,28},{28,24},{1,5},{5... | collective-permute-start | bytes 233480 | tf_op jit(solution)/shard_map/ppermute | solution.py:343
  32.6 4.1 %collective-permute-start.10 = (f32[152,128]{1,0:T(8,128)S(1)}, f32[152,128]{1,0:T(8,128)S(1)}, u32[]{:S(2)}, u32[]{:S(2)}) collective-permute-start(f32[152,128]{1,0:T(8,128)S(1)} %get-tuple-element.37), channel_id=1, source_target_pairs={{0,8},{4,12},{8,0},{12,4},{16,24},{20,28},{24,16},{28,20},{1,9},{5... | collective-permute-start | bytes 233480 | tf_op jit(solution)/shard_map/ppermute | solution.py:343
  36.7 0.2 collective-permute-start.11
  36.9 3.6 %collective-permute-start.12 = (f32[152,128]{1,0:T(8,128)S(1)}, f32[152,128]{1,0:T(8,128)S(1)}, u32[]{:S(2)}, u32[]{:S(2)}) collective-permute-start(f32[152,128]{1,0:T(8,128)S(1)} %get-tuple-element.39), channel_id=1, source_target_pairs={{0,16},{4,20},{8,24},{12,28},{16,0},{20,4},{24,8},{28,12},{1,17},{... | collective-permute-start | bytes 233480 | tf_op jit(solution)/shard_map/ppermute | solution.py:343
  40.5 0.1 collective-permute-start.13
  40.6 0.0 collective-permute-done.9.refs_1_
  40.6 2.4 %collective-permute-start.14 = (f32[152,128]{1,0:T(8,128)S(1)}, f32[152,128]{1,0:T(8,128)S(1)}, u32[]{:S(2)}, u32[]{:S(2)}) collective-permute-start(f32[152,128]{1,0:T(8,128)S(1)} %get-tuple-element.41), channel_id=1, source_target_pairs={{0,24},{4,28},{8,16},{12,20},{16,8},{20,12},{24,0},{28,4},{1,25},{... | collective-permute-start | bytes 233480 | tf_op jit(solution)/shard_map/ppermute | solution.py:343
  42.9 0.0 collective-permute-done.10.refs_2_
  42.9 2.3 %collective-permute-start.15 = (f32[152,128]{1,0:T(8,128)S(1)}, f32[152,128]{1,0:T(8,128)S(1)}, u32[]{:S(2)}, u32[]{:S(2)}) collective-permute-start(f32[152,128]{1,0:T(8,128)S(1)} %get-tuple-element.42), channel_id=1, source_target_pairs={{0,28},{4,24},{8,20},{12,16},{16,12},{20,8},{24,4},{28,0},{1,29},{... | collective-permute-start | bytes 233480 | tf_op jit(solution)/shard_map/ppermute | solution.py:343
  45.2 0.0 collective-permute-done.11.refs_3_
  45.2 3.8 %collective-permute-done.12.refs_4_ = f32[152,128]{1,0:T(8,128)S(1)} collective-permute-done((f32[152,128]{1,0:T(8,128)S(1)}, f32[152,128]{1,0:T(8,128)S(1)}, u32[]{:S(2)}, u32[]{:S(2)}) %collective-permute-start.12) | collective-permute-done | bytes 77856 | tf_op jit(solution)/shard_map/ppermute | solution.py:343
  49.0 3.1 %collective-permute-done.13.refs_5_ = f32[152,128]{1,0:T(8,128)S(1)} collective-permute-done((f32[152,128]{1,0:T(8,128)S(1)}, f32[152,128]{1,0:T(8,128)S(1)}, u32[]{:S(2)}, u32[]{:S(2)}) %collective-permute-start.13) | collective-permute-done | bytes 77856 | tf_op jit(solution)/shard_map/ppermute | solution.py:343
  52.2 0.0 collective-permute-done.14.refs_6_
  52.2 0.0 collective-permute-done.15.refs_7_
  52.2 0.2 crossing_planes.1
  52.3 0.1 collective-permute-start.16
  52.4 1.7 %collective-permute-start.17 = (f32[24,128]{1,0:T(8,128)S(1)}, f32[24,128]{1,0:T(8,128)S(1)}, u32[]{:S(2)}, u32[]{:S(2)}) collective-permute-start(f32[24,128]{1,0:T(8,128)S(1)} %get-tuple-element.44), channel_id=1, source_target_pairs={{0,3},{1,0},{2,1},{3,2},{4,7},{5,4},{6,5},{7,6},{8,11},{9,8},{10,9... | collective-permute-start | bytes 36872 | tf_op jit(solution)/shard_map/ppermute | solution.py:349
  54.1 0.1 unpack_planes.1.main
  54.3 1.2 %collective-permute-done.16.below = f32[24,128]{1,0:T(8,128)S(1)} collective-permute-done((f32[24,128]{1,0:T(8,128)S(1)}, f32[24,128]{1,0:T(8,128)S(1)}, u32[]{:S(2)}, u32[]{:S(2)}) %collective-permute-start.16) | collective-permute-done | bytes 12320 | tf_op jit(solution)/shard_map/ppermute | solution.py:348
  55.5 0.0 collective-permute-done.17.above
  55.5 0.9 %finish.1 = f32[1216,128]{1,0:T(8,128)} custom-call(f32[19,80,128]{2,1,0:T(8,128)S(1)} %unpack_planes.1.main, f32[24,128]{1,0:T(8,128)S(1)} %collective-permute-done.16.below, f32[24,128]{1,0:T(8,128)S(1)} %collective-permute-done.17.above), custom_call_target="tpu_custom_call" | custom-call | flops 100000 | bytes 100000 | tf_op jit(solution)/shard_map/finish/pallas_call | solution.py:329
  (3 shorter events, 0.0 us)
Async XLA Ops:
  0.0 0.7 %copy-start.2 = (s32[1,1,3,2]{2,3,1,0:T(2,128)S(1)}, s32[1,1,3,2]{2,3,1,0:T(2,128)}, u32[]{:S(2)}) copy-start(s32[1,1,3,2]{2,3,1,0:T(2,128)} %param.7) | copy-start | bytes 76
  0.0 0.7 %copy-start.3 = (s32[1,2]{1,0:T(1,128)S(1)}, s32[1,2]{1,0:T(1,128)}, u32[]{:S(2)}) copy-start(s32[1,2]{1,0:T(1,128)} %slots.3) | copy-start | bytes 28
  0.7 1.1 %copy-start = (f32[1,2,19,4096]{3,1,2,0:T(2,128)S(1)}, f32[1,2,19,4096]{3,1,2,0:T(2,128)}, u32[]{:S(2)}) copy-start(f32[1,2,19,4096]{3,1,2,0:T(2,128)} %param.4) | copy-start | bytes 1867780
  1.8 0.8 %copy-start.1 = (s32[1,2,4096]{2,1,0:T(2,128)S(1)}, s32[1,2,4096]{2,1,0:T(2,128)}, u32[]{:S(2)}) copy-start(s32[1,2,4096]{2,1,0:T(2,128)} %param.5) | copy-start | bytes 98308
  2.6 3.8 %collective-permute-start = (f32[24,128]{1,0:T(8,128)S(1)}, f32[24,128]{1,0:T(8,128)S(1)}, u32[]{:S(2)}, u32[]{:S(2)}) collective-permute-start(f32[24,128]{1,0:T(8,128)S(1)} %get-tuple-element.25), channel_id=1, source_target_pairs={{0,1},{1,2},{2,3},{3,0},{4,5},{5,6},{6,7},{7,4},{8,9},{9,10},{10,1... | collective-permute-start | bytes 36872 | tf_op jit(solution)/shard_map/ppermute | solution.py:348
  3.1 3.4 %collective-permute-start.1 = (f32[24,128]{1,0:T(8,128)S(1)}, f32[24,128]{1,0:T(8,128)S(1)}, u32[]{:S(2)}, u32[]{:S(2)}) collective-permute-start(f32[24,128]{1,0:T(8,128)S(1)} %get-tuple-element.26), channel_id=1, source_target_pairs={{0,3},{1,0},{2,1},{3,2},{4,7},{5,4},{6,5},{7,6},{8,11},{9,8},{10,9... | collective-permute-start | bytes 36872 | tf_op jit(solution)/shard_map/ppermute | solution.py:349
  6.7 8.2 %collective-permute-start.2 = (f32[168,128]{1,0:T(8,128)S(1)}, f32[168,128]{1,0:T(8,128)S(1)}, u32[]{:S(2)}, u32[]{:S(2)}) collective-permute-start(f32[168,128]{1,0:T(8,128)S(1)} %get-tuple-element.28), channel_id=1, source_target_pairs={{0,4},{4,0},{8,12},{12,8},{16,20},{20,16},{24,28},{28,24},{1,5},{5... | collective-permute-start | bytes 258056 | tf_op jit(solution)/shard_map/ppermute | solution.py:343
  9.0 9.5 %collective-permute-start.3 = (f32[168,128]{1,0:T(8,128)S(1)}, f32[168,128]{1,0:T(8,128)S(1)}, u32[]{:S(2)}, u32[]{:S(2)}) collective-permute-start(f32[168,128]{1,0:T(8,128)S(1)} %get-tuple-element.29), channel_id=1, source_target_pairs={{0,8},{4,12},{8,0},{12,4},{16,24},{20,28},{24,16},{28,20},{1,9},{5... | collective-permute-start | bytes 258056 | tf_op jit(solution)/shard_map/ppermute | solution.py:343
  10.6 8.7 %collective-permute-start.4 = (f32[168,128]{1,0:T(8,128)S(1)}, f32[168,128]{1,0:T(8,128)S(1)}, u32[]{:S(2)}, u32[]{:S(2)}) collective-permute-start(f32[168,128]{1,0:T(8,128)S(1)} %get-tuple-element.30), channel_id=1, source_target_pairs={{0,12},{4,8},{8,4},{12,0},{16,28},{20,24},{24,20},{28,16},{1,13},{... | collective-permute-start | bytes 258056 | tf_op jit(solution)/shard_map/ppermute | solution.py:343
  10.6 8.7 %collective-permute-start.5 = (f32[168,128]{1,0:T(8,128)S(1)}, f32[168,128]{1,0:T(8,128)S(1)}, u32[]{:S(2)}, u32[]{:S(2)}) collective-permute-start(f32[168,128]{1,0:T(8,128)S(1)} %get-tuple-element.31), channel_id=1, source_target_pairs={{0,16},{4,20},{8,24},{12,28},{16,0},{20,4},{24,8},{28,12},{1,17},{... | collective-permute-start | bytes 258056 | tf_op jit(solution)/shard_map/ppermute | solution.py:343
  13.6 14.5 %collective-permute-start.6 = (f32[168,128]{1,0:T(8,128)S(1)}, f32[168,128]{1,0:T(8,128)S(1)}, u32[]{:S(2)}, u32[]{:S(2)}) collective-permute-start(f32[168,128]{1,0:T(8,128)S(1)} %get-tuple-element.32), channel_id=1, source_target_pairs={{0,20},{4,16},{8,28},{12,24},{16,4},{20,0},{24,12},{28,8},{1,21},{... | collective-permute-start | bytes 258056 | tf_op jit(solution)/shard_map/ppermute | solution.py:343
  14.9 13.2 %collective-permute-start.7 = (f32[168,128]{1,0:T(8,128)S(1)}, f32[168,128]{1,0:T(8,128)S(1)}, u32[]{:S(2)}, u32[]{:S(2)}) collective-permute-start(f32[168,128]{1,0:T(8,128)S(1)} %get-tuple-element.33), channel_id=1, source_target_pairs={{0,24},{4,28},{8,16},{12,20},{16,8},{20,12},{24,0},{28,4},{1,25},{... | collective-permute-start | bytes 258056 | tf_op jit(solution)/shard_map/ppermute | solution.py:343
  18.5 9.6 %collective-permute-start.8 = (f32[168,128]{1,0:T(8,128)S(1)}, f32[168,128]{1,0:T(8,128)S(1)}, u32[]{:S(2)}, u32[]{:S(2)}) collective-permute-start(f32[168,128]{1,0:T(8,128)S(1)} %get-tuple-element.34), channel_id=1, source_target_pairs={{0,28},{4,24},{8,20},{12,16},{16,12},{20,8},{24,4},{28,0},{1,29},{... | collective-permute-start | bytes 258056 | tf_op jit(solution)/shard_map/ppermute | solution.py:343
  31.5 9.1 %collective-permute-start.9 = (f32[152,128]{1,0:T(8,128)S(1)}, f32[152,128]{1,0:T(8,128)S(1)}, u32[]{:S(2)}, u32[]{:S(2)}) collective-permute-start(f32[152,128]{1,0:T(8,128)S(1)} %get-tuple-element.36), channel_id=1, source_target_pairs={{0,4},{4,0},{8,12},{12,8},{16,20},{20,16},{24,28},{28,24},{1,5},{5... | collective-permute-start | bytes 233480 | tf_op jit(solution)/shard_map/ppermute | solution.py:343
  32.6 10.4 %collective-permute-start.10 = (f32[152,128]{1,0:T(8,128)S(1)}, f32[152,128]{1,0:T(8,128)S(1)}, u32[]{:S(2)}, u32[]{:S(2)}) collective-permute-start(f32[152,128]{1,0:T(8,128)S(1)} %get-tuple-element.37), channel_id=1, source_target_pairs={{0,8},{4,12},{8,0},{12,4},{16,24},{20,28},{24,16},{28,20},{1,9},{5... | collective-permute-start | bytes 233480 | tf_op jit(solution)/shard_map/ppermute | solution.py:343
  36.7 8.6 %collective-permute-start.11 = (f32[152,128]{1,0:T(8,128)S(1)}, f32[152,128]{1,0:T(8,128)S(1)}, u32[]{:S(2)}, u32[]{:S(2)}) collective-permute-start(f32[152,128]{1,0:T(8,128)S(1)} %get-tuple-element.38), channel_id=1, source_target_pairs={{0,12},{4,8},{8,4},{12,0},{16,28},{20,24},{24,20},{28,16},{1,13},{... | collective-permute-start | bytes 233480 | tf_op jit(solution)/shard_map/ppermute | solution.py:343
  36.9 12.1 %collective-permute-start.12 = (f32[152,128]{1,0:T(8,128)S(1)}, f32[152,128]{1,0:T(8,128)S(1)}, u32[]{:S(2)}, u32[]{:S(2)}) collective-permute-start(f32[152,128]{1,0:T(8,128)S(1)} %get-tuple-element.39), channel_id=1, source_target_pairs={{0,16},{4,20},{8,24},{12,28},{16,0},{20,4},{24,8},{28,12},{1,17},{... | collective-permute-start | bytes 233480 | tf_op jit(solution)/shard_map/ppermute | solution.py:343
  40.5 11.6 %collective-permute-start.13 = (f32[152,128]{1,0:T(8,128)S(1)}, f32[152,128]{1,0:T(8,128)S(1)}, u32[]{:S(2)}, u32[]{:S(2)}) collective-permute-start(f32[152,128]{1,0:T(8,128)S(1)} %get-tuple-element.40), channel_id=1, source_target_pairs={{0,20},{4,16},{8,28},{12,24},{16,4},{20,0},{24,12},{28,8},{1,21},{... | collective-permute-start | bytes 233480 | tf_op jit(solution)/shard_map/ppermute | solution.py:343
  40.6 11.6 %collective-permute-start.14 = (f32[152,128]{1,0:T(8,128)S(1)}, f32[152,128]{1,0:T(8,128)S(1)}, u32[]{:S(2)}, u32[]{:S(2)}) collective-permute-start(f32[152,128]{1,0:T(8,128)S(1)} %get-tuple-element.41), channel_id=1, source_target_pairs={{0,24},{4,28},{8,16},{12,20},{16,8},{20,12},{24,0},{28,4},{1,25},{... | collective-permute-start | bytes 233480 | tf_op jit(solution)/shard_map/ppermute | solution.py:343
  42.9 9.2 %collective-permute-start.15 = (f32[152,128]{1,0:T(8,128)S(1)}, f32[152,128]{1,0:T(8,128)S(1)}, u32[]{:S(2)}, u32[]{:S(2)}) collective-permute-start(f32[152,128]{1,0:T(8,128)S(1)} %get-tuple-element.42), channel_id=1, source_target_pairs={{0,28},{4,24},{8,20},{12,16},{16,12},{20,8},{24,4},{28,0},{1,29},{... | collective-permute-start | bytes 233480 | tf_op jit(solution)/shard_map/ppermute | solution.py:343
  52.3 3.2 %collective-permute-start.16 = (f32[24,128]{1,0:T(8,128)S(1)}, f32[24,128]{1,0:T(8,128)S(1)}, u32[]{:S(2)}, u32[]{:S(2)}) collective-permute-start(f32[24,128]{1,0:T(8,128)S(1)} %get-tuple-element.43), channel_id=1, source_target_pairs={{0,1},{1,2},{2,3},{3,0},{4,5},{5,6},{6,7},{7,4},{8,9},{9,10},{10,1... | collective-permute-start | bytes 36872 | tf_op jit(solution)/shard_map/ppermute | solution.py:348
  52.4 3.1 %collective-permute-start.17 = (f32[24,128]{1,0:T(8,128)S(1)}, f32[24,128]{1,0:T(8,128)S(1)}, u32[]{:S(2)}, u32[]{:S(2)}) collective-permute-start(f32[24,128]{1,0:T(8,128)S(1)} %get-tuple-element.44), channel_id=1, source_target_pairs={{0,3},{1,0},{2,1},{3,2},{4,7},{5,4},{6,5},{7,6},{8,11},{9,8},{10,9... | collective-permute-start | bytes 36872 | tf_op jit(solution)/shard_map/ppermute | solution.py:349

commit v3 on v2

--- a/solution.py
+++ b/solution.py
@@ -140,43 +140,59 @@
         me = lax.axis_index("gx")
         return me, lax.axis_index("gy") % 2
 
-    def edge_kernel(pops, mask, slots, swaps, up, down):
-        for start, out, chosen, inside in (
-            (WHOLE - 8, up, UPWARD, 8 - PLANE),
-            (0, down, DOWNWARD, 0),
-        ):
-            f = [pops[pl.ds(p * WHOLE + start, 8), :] for p in range(Q)]
-            after = collide(f, mask[pl.ds(start, 8), :] > 0)
-            for n, p in enumerate(chosen):
-                out[pl.ds(n * PLANE, PLANE), :] = after[p][inside : inside + PLANE]
-            out[pl.ds(faces, 4), :] = jnp.zeros((4, LANES), f32)
-            out[pl.ds(faces, 1), 0:NB] = slots[...].astype(f32)
-            out[pl.ds(faces + 1, 1), 0:3] = swaps[0:1].astype(f32)
-
-    def collide_kernel(pops, mask, post):
+    def edge_kernel(pops, mask, slots, swaps, up, down, own, cells, solid, held, given, sem):
+        ends = (WHOLE - 8, 0)
+        copies = []
+        for n, start in enumerate(ends):
+            copies.append((pops.at[:, pl.ds(start, 8), :], cells.at[n]))
+            copies.append((mask.at[pl.ds(start, 8), :], solid.at[n]))
+        copies += [(slots, held), (swaps, given)]
+        copies = [
+            pltpu.make_async_copy(source, target, sem.at[n])
+            for n, (source, target) in enumerate(copies)
+        ]
+        for copy in copies:
+            copy.start()
+        for copy in copies:
+            copy.wait()
+        own[...] = jnp.zeros((8, LANES), f32)
+        own[0:1, 0:NB] = held[...].astype(f32)
+        own[1:2, 0:3] = given[0:1].astype(f32)
+        for n, (out, chosen, inside) in enumerate(((up, UPWARD, 8 - PLANE), (down, DOWNWARD, 0))):
+            after = collide([cells[n, p] for p in range(Q)], solid[n] > 0)
+            for m, p in enumerate(chosen):
+                out[pl.ds(m * PLANE, PLANE), :] = after[p][inside : inside + PLANE]
+            out[pl.ds(faces, 4), :] = own[0:4]
+
+    def collide_kernel(pops, mask, post, cells, solid, sem):
+        copies = (
+            pltpu.make_async_copy(pops, cells, sem.at[0]),
+            pltpu.make_async_copy(mask, solid, sem.at[1]),
+        )
+        for copy in copies:
+            copy.start()
+        for copy in copies:
+            copy.wait()
         for start in range(0, WHOLE, 8):
-            f = [pops[pl.ds(p * WHOLE + start, 8), :] for p in range(Q)]
-            after = collide(f, mask[pl.ds(start, 8), :] > 0)
+            here = pl.ds(start, 8)
+            after = collide([cells[p, here, :] for p in range(Q)], solid[here, :] > 0)
             for p in range(Q):
                 post[p, pl.ds(8 + start, 8), :] = after[p]
-
-    def pack_kernel(post, mask, slots, swaps, below, above, *outs):
+            post[Q, pl.ds(8 + start, 8), :] = solid[here, :].astype(f32)
+
+    def pack_kernel(post, own, below, above, *outs):
         me, odd = position()
-        own = jnp.zeros((4, LANES), f32)
         for d in range(owners):
             out = outs[d]
             place = dynamic_place(me ^ d, odd, owners)
             here = pl.multiple_of(place * share, min(share, 8))
-            for p in range(Q):
-                cx = VELOCITIES[p][0]
+            for p in range(Q + 1):
+                cx = VELOCITIES[p][0] if p < Q else 0
                 out[pl.ds(p * share, share), :] = post[p, pl.ds(8 + here - cx * PLANE, share), :]
-            out[pl.ds(Q * share, share), :] = mask[pl.ds(here, share), :].astype(f32)
-            out[pl.ds(head, 4), :] = own
-            out[pl.ds(head, 1), 0:NB] = slots[...].astype(f32)
-            out[pl.ds(head + 1, 1), 0:3] = swaps[0:1].astype(f32)
+            out[pl.ds(head, 2), :] = own[0:2]
             out[pl.ds(head + 2, 2), :] = below[pl.ds(faces, 2), :]
             out[pl.ds(head + 4, 2), :] = above[pl.ds(faces, 2), :]
-            out[pl.ds(head + 6, 2), :] = own[0:2]
+            out[pl.ds(head + 6, 2), :] = own[2:4]
 
             @pl.when(place == 0)
             def _():
@@ -324,12 +340,12 @@
     def shape(*dims):
         return jax.ShapeDtypeStruct(dims, f32)
 
-    def call(kernel, name, out_shape, inputs, cost, scratch=()):
+    def call(kernel, name, out_shape, inputs, cost, scratch=(), spec=VMEM_SPEC):
         outs = jax.tree.map(lambda _: VMEM_SPEC, out_shape)
         return pl.pallas_call(
             kernel,
             out_shape=out_shape,
-            in_specs=[VMEM_SPEC] * len(inputs),
+            in_specs=[spec] * len(inputs),
             out_specs=outs,
             scratch_shapes=list(scratch),
             compiler_params=PARAMS,
@@ -338,9 +354,9 @@
         )(*inputs)
 
     def exchange(parts):
-        here = [parts[0]]
-        for d in range(1, owners):
-            here.append(lax.ppermute(parts[d], "gx", [(g, g ^ d) for g in range(owners)]))
+        here = list(parts)
+        for d in reversed(range(1, owners)):
+            here[d] = lax.ppermute(parts[d], "gx", [(g, g ^ d) for g in range(owners)])
         return here
 
     def hop(up, down):
@@ -349,30 +365,53 @@
             lax.ppermute(down, "gy", [(s, (s - 1) % slabs) for s in range(slabs)]),
         )
 
-    padded = shape(Q, 8 + WHOLE + 8, LANES)
+    def padded(count):
+        return shape(count, 8 + WHOLE + 8, LANES)
+
     work = pltpu.VMEM((Q + 1, planes, NB, rows, LANES), f32)
     small, large = 100_000, 4_000_000
 
     def shards(populations, solid_mask, slot_blocks, swap_slots):
         tiles = B * B * B // LANES
         pops = populations[0].transpose(1, 0, 2).reshape(Q, NB, tiles, LANES)
-        pops = pops.transpose(0, 2, 1, 3).reshape(Q * WHOLE, LANES)
+        pops = pops.transpose(0, 2, 1, 3).reshape(Q, WHOLE, LANES)
         mask = solid_mask[0].reshape(NB, tiles, LANES).transpose(1, 0, 2).reshape(WHOLE, LANES)
         swaps = swap_slots[0, 0].T
-        up, down = call(
+        in_place = pl.BlockSpec(memory_space=pl.ANY)
+        up, down, own = call(
             edge_kernel,
             "edge_planes",
-            (shape(rows_hop, LANES),) * 2,
+            (shape(rows_hop, LANES), shape(rows_hop, LANES), shape(8, LANES)),
             (pops, mask, slot_blocks, swaps),
             small,
+            (
+                pltpu.VMEM((2, Q, 8, LANES), f32),
+                pltpu.VMEM((2, 8, LANES), jnp.int32),
+                pltpu.VMEM(slot_blocks.shape, jnp.int32),
+                pltpu.VMEM(swaps.shape, jnp.int32),
+                pltpu.SemaphoreType.DMA((6,)),
+            ),
+            in_place,
         )
         below, above = hop(up, down)
-        post = call(collide_kernel, "first_collision", padded, (pops, mask), large)
+        post = call(
+            collide_kernel,
+            "first_collision",
+            padded(Q + 1),
+            (pops, mask),
+            large,
+            (
+                pltpu.VMEM(pops.shape, f32),
+                pltpu.VMEM(mask.shape, jnp.int32),
+                pltpu.SemaphoreType.DMA((2,)),
+            ),
+            in_place,
+        )
         parts = call(
             pack_kernel,
             "pack_planes",
             (shape(rows_in, LANES),) * owners,
-            (post, mask, slot_blocks, swaps, below, above),
+            (post, own, below, above),
             large,
         )
         got = exchange(parts)
@@ -392,7 +431,7 @@
         home = exchange(parts)
         up, down = call(crossing_kernel, "crossing_planes", (shape(rows_hop, LANES),) * 2, home, small)
         below, above = hop(up, down)
-        main = call(unpack_kernel, "unpack_planes", padded, home, large)
+        main = call(unpack_kernel, "unpack_planes", padded(Q), home, large)
         out = call(
             finish_kernel, "finish", shape(Q * WHOLE, LANES), (main, below, above), small
         )

time: 57.5 us -> 57.5 us (level)
  no operation moved by 1% of the time
where the time goes in v3:
time: 57.5 us; the launch traced here: 56.5 us
  starting transfers between devices  29.9 us (52%)
  waiting for transfers between devices  18.7 us (33%)
  Pallas kernels  5.35 us (9%)
  local copies, waits for them, and re-layouts  2.51 us (4%)
    ppermute x14, starting transfers between devices, exchange(): here[d] = lax.ppermute(parts[d], 'gx', [(g, g ^ d) for g in range(owners)])  25.6 us
    ppermute x14, waiting for transfers between devices, exchange(): here[d] = lax.ppermute(parts[d], 'gx', [(g, g ^ d) for g in range(owners)])  16.5 us
    pallas_call x7, Pallas kernels, call(): pl.pallas_call(kernel, out_shape=out_shape, in_specs=[spec] * len(inputs)...  5.35 us
    ppermute x2, starting transfers between devices, hop(): lax.ppermute(down, 'gy', [(s, (s - 1) % slabs) for s in range(slabs)])  3.72 us
    unnamed x8, local copies, waits for them, and re-layouts  2.51 us
    ppermute x2, waiting for transfers between devices, hop(): lax.ppermute(up, 'gy', [(s, (s + 1) % slabs) for s in range(slabs)])  2.1 us
  transfers between devices with their start and end apart: 18, of which 7 were waited for; matrix products, arithmetic and copies ran while one was open for 0% of the time, Pallas kernels for 1%

profile of v3, /device:TPU:0, one launch (start us, length us, event | category | flops | bytes accessed | tf_op | source)
XLA Modules:
  0.0 56.5 jit_solution(7012104404374365362)
XLA Ops:
  0.0 0.0 copy-start.3
  0.0 0.7 %copy-done.2 = s32[1,1,3,2]{2,3,1,0:T(2,128)S(1)} copy-done((s32[1,1,3,2]{2,3,1,0:T(2,128)S(1)}, s32[1,1,3,2]{2,3,1,0:T(2,128)}, u32[]{:S(2)}) %copy-start.2) | copy-done | bytes 48
  0.7 0.0 copy-done.3
  0.7 1.1 %copy-done = f32[1,2,19,4096]{3,1,2,0:T(2,128)S(1)} copy-done((f32[1,2,19,4096]{3,1,2,0:T(2,128)S(1)}, f32[1,2,19,4096]{3,1,2,0:T(2,128)}, u32[]{:S(2)}) %copy-start) | copy-done | bytes 622616
  1.8 0.8 %copy-done.1 = s32[1,2,4096]{2,1,0:T(2,128)S(1)} copy-done((s32[1,2,4096]{2,1,0:T(2,128)S(1)}, s32[1,2,4096]{2,1,0:T(2,128)}, u32[]{:S(2)}) %copy-start.1) | copy-done | bytes 32792
  2.5 0.1 edge_planes.1
  2.7 0.5 collective-permute-start
  3.2 2.0 %collective-permute-start.1 = (f32[24,128]{1,0:T(8,128)S(1)}, f32[24,128]{1,0:T(8,128)S(1)}, u32[]{:S(2)}, u32[]{:S(2)}) collective-permute-start(f32[24,128]{1,0:T(8,128)S(1)} %get-tuple-element.28), channel_id=1, source_target_pairs={{0,3},{1,0},{2,1},{3,2},{4,7},{5,4},{6,5},{7,6},{8,11},{9,8},{10,9... | collective-permute-start | bytes 36872 | tf_op jit(solution)/shard_map/ppermute | solution.py:365
  5.2 0.5 first_collision.1.post
  5.6 0.9 %collective-permute-done.below = f32[24,128]{1,0:T(8,128)S(1)} collective-permute-done((f32[24,128]{1,0:T(8,128)S(1)}, f32[24,128]{1,0:T(8,128)S(1)}, u32[]{:S(2)}, u32[]{:S(2)}) %collective-permute-start) | collective-permute-done | bytes 12320 | tf_op jit(solution)/shard_map/ppermute | solution.py:364
  6.5 0.1 collective-permute-done.1.above
  6.6 0.2 pack_planes.1
  6.8 2.3 %collective-permute-start.2 = (f32[168,128]{1,0:T(8,128)S(1)}, f32[168,128]{1,0:T(8,128)S(1)}, u32[]{:S(2)}, u32[]{:S(2)}) collective-permute-start(f32[168,128]{1,0:T(8,128)S(1)} %get-tuple-element.30), channel_id=1, source_target_pairs={{0,4},{4,0},{8,12},{12,8},{16,20},{20,16},{24,28},{28,24},{1,5},{5... | collective-permute-start | bytes 258056 | tf_op jit(solution)/shard_map/ppermute | solution.py:359
  9.1 1.6 %collective-permute-start.3 = (f32[168,128]{1,0:T(8,128)S(1)}, f32[168,128]{1,0:T(8,128)S(1)}, u32[]{:S(2)}, u32[]{:S(2)}) collective-permute-start(f32[168,128]{1,0:T(8,128)S(1)} %get-tuple-element.31), channel_id=1, source_target_pairs={{0,8},{4,12},{8,0},{12,4},{16,24},{20,28},{24,16},{28,20},{1,9},{5... | collective-permute-start | bytes 258056 | tf_op jit(solution)/shard_map/ppermute | solution.py:359
  10.7 0.0 collective-permute-start.4
  10.7 3.0 %collective-permute-start.5 = (f32[168,128]{1,0:T(8,128)S(1)}, f32[168,128]{1,0:T(8,128)S(1)}, u32[]{:S(2)}, u32[]{:S(2)}) collective-permute-start(f32[168,128]{1,0:T(8,128)S(1)} %get-tuple-element.33), channel_id=1, source_target_pairs={{0,16},{4,20},{8,24},{12,28},{16,0},{20,4},{24,8},{28,12},{1,17},{... | collective-permute-start | bytes 258056 | tf_op jit(solution)/shard_map/ppermute | solution.py:359
  13.6 1.3 %collective-permute-start.6 = (f32[168,128]{1,0:T(8,128)S(1)}, f32[168,128]{1,0:T(8,128)S(1)}, u32[]{:S(2)}, u32[]{:S(2)}) collective-permute-start(f32[168,128]{1,0:T(8,128)S(1)} %get-tuple-element.34), channel_id=1, source_target_pairs={{0,20},{4,16},{8,28},{12,24},{16,4},{20,0},{24,12},{28,8},{1,21},{... | collective-permute-start | bytes 258056 | tf_op jit(solution)/shard_map/ppermute | solution.py:359
  14.9 0.0 collective-permute-done.2.refs_1_
  14.9 3.6 %collective-permute-start.7 = (f32[168,128]{1,0:T(8,128)S(1)}, f32[168,128]{1,0:T(8,128)S(1)}, u32[]{:S(2)}, u32[]{:S(2)}) collective-permute-start(f32[168,128]{1,0:T(8,128)S(1)} %get-tuple-element.35), channel_id=1, source_target_pairs={{0,24},{4,28},{8,16},{12,20},{16,8},{20,12},{24,0},{28,4},{1,25},{... | collective-permute-start | bytes 258056 | tf_op jit(solution)/shard_map/ppermute | solution.py:359
  18.5 0.0 collective-permute-done.3.refs_2_
  18.5 0.0 collective-permute-start.8
  18.6 0.8 %collective-permute-done.4.refs_3_ = f32[168,128]{1,0:T(8,128)S(1)} collective-permute-done((f32[168,128]{1,0:T(8,128)S(1)}, f32[168,128]{1,0:T(8,128)S(1)}, u32[]{:S(2)}, u32[]{:S(2)}) %collective-permute-start.4) | collective-permute-done | bytes 86048 | tf_op jit(solution)/shard_map/ppermute | solution.py:359
  19.4 0.0 collective-permute-done.5.refs_4_
  19.4 8.8 %collective-permute-done.6.refs_5_ = f32[168,128]{1,0:T(8,128)S(1)} collective-permute-done((f32[168,128]{1,0:T(8,128)S(1)}, f32[168,128]{1,0:T(8,128)S(1)}, u32[]{:S(2)}, u32[]{:S(2)}) %collective-permute-start.6) | collective-permute-done | bytes 86048 | tf_op jit(solution)/shard_map/ppermute | solution.py:359
  28.1 0.0 collective-permute-done.7.refs_6_
  28.1 0.0 collective-permute-done.8.refs_7_
  28.1 3.4 %second_step.1 = (f32[152,128]{1,0:T(8,128)S(1)}, f32[152,128]{1,0:T(8,128)S(1)}, f32[152,128]{1,0:T(8,128)S(1)}, f32[152,128]{1,0:T(8,128)S(1)}, f32[152,128]{1...) custom-call(f32[168,128]{1,0:T(8,128)S(1)} %get-tuple-element.29.refs_0_, ...), custom_call_target="tpu_custom_call" | custom-call | flops 4000000 | bytes 4000000 | tf_op jit(solution)/shard_map/second_step/pallas_call | solution.py:345
  31.5 1.1 %collective-permute-start.9 = (f32[152,128]{1,0:T(8,128)S(1)}, f32[152,128]{1,0:T(8,128)S(1)}, u32[]{:S(2)}, u32[]{:S(2)}) collective-permute-start(f32[152,128]{1,0:T(8,128)S(1)} %get-tuple-element.38), channel_id=1, source_target_pairs={{0,4},{4,0},{8,12},{12,8},{16,20},{20,16},{24,28},{28,24},{1,5},{5... | collective-permute-start | bytes 233480 | tf_op jit(solution)/shard_map/ppermute | solution.py:359
  32.7 4.1 %collective-permute-start.10 = (f32[152,128]{1,0:T(8,128)S(1)}, f32[152,128]{1,0:T(8,128)S(1)}, u32[]{:S(2)}, u32[]{:S(2)}) collective-permute-start(f32[152,128]{1,0:T(8,128)S(1)} %get-tuple-element.39), channel_id=1, source_target_pairs={{0,8},{4,12},{8,0},{12,4},{16,24},{20,28},{24,16},{28,20},{1,9},{5... | collective-permute-start | bytes 233480 | tf_op jit(solution)/shard_map/ppermute | solution.py:359
  36.8 0.2 collective-permute-start.11
  37.0 3.6 %collective-permute-start.12 = (f32[152,128]{1,0:T(8,128)S(1)}, f32[152,128]{1,0:T(8,128)S(1)}, u32[]{:S(2)}, u32[]{:S(2)}) collective-permute-start(f32[152,128]{1,0:T(8,128)S(1)} %get-tuple-element.41), channel_id=1, source_target_pairs={{0,16},{4,20},{8,24},{12,28},{16,0},{20,4},{24,8},{28,12},{1,17},{... | collective-permute-start | bytes 233480 | tf_op jit(solution)/shard_map/ppermute | solution.py:359
  40.6 0.1 collective-permute-start.13
  40.7 0.0 collective-permute-done.9.refs_1_
  40.7 2.4 %collective-permute-start.14 = (f32[152,128]{1,0:T(8,128)S(1)}, f32[152,128]{1,0:T(8,128)S(1)}, u32[]{:S(2)}, u32[]{:S(2)}) collective-permute-start(f32[152,128]{1,0:T(8,128)S(1)} %get-tuple-element.43), channel_id=1, source_target_pairs={{0,24},{4,28},{8,16},{12,20},{16,8},{20,12},{24,0},{28,4},{1,25},{... | collective-permute-start | bytes 233480 | tf_op jit(solution)/shard_map/ppermute | solution.py:359
  43.0 0.0 collective-permute-done.10.refs_2_
  43.0 2.3 %collective-permute-start.15 = (f32[152,128]{1,0:T(8,128)S(1)}, f32[152,128]{1,0:T(8,128)S(1)}, u32[]{:S(2)}, u32[]{:S(2)}) collective-permute-start(f32[152,128]{1,0:T(8,128)S(1)} %get-tuple-element.44), channel_id=1, source_target_pairs={{0,28},{4,24},{8,20},{12,16},{16,12},{20,8},{24,4},{28,0},{1,29},{... | collective-permute-start | bytes 233480 | tf_op jit(solution)/shard_map/ppermute | solution.py:359
  45.3 0.0 collective-permute-done.11.refs_3_
  45.3 3.8 %collective-permute-done.12.refs_4_ = f32[152,128]{1,0:T(8,128)S(1)} collective-permute-done((f32[152,128]{1,0:T(8,128)S(1)}, f32[152,128]{1,0:T(8,128)S(1)}, u32[]{:S(2)}, u32[]{:S(2)}) %collective-permute-start.12) | collective-permute-done | bytes 77856 | tf_op jit(solution)/shard_map/ppermute | solution.py:359
  49.1 3.1 %collective-permute-done.13.refs_5_ = f32[152,128]{1,0:T(8,128)S(1)} collective-permute-done((f32[152,128]{1,0:T(8,128)S(1)}, f32[152,128]{1,0:T(8,128)S(1)}, u32[]{:S(2)}, u32[]{:S(2)}) %collective-permute-start.13) | collective-permute-done | bytes 77856 | tf_op jit(solution)/shard_map/ppermute | solution.py:359
  52.3 0.0 collective-permute-done.14.refs_6_
  52.3 0.0 collective-permute-done.15.refs_7_
  52.3 0.2 crossing_planes.1
  52.4 0.1 collective-permute-start.16
  52.5 1.7 %collective-permute-start.17 = (f32[24,128]{1,0:T(8,128)S(1)}, f32[24,128]{1,0:T(8,128)S(1)}, u32[]{:S(2)}, u32[]{:S(2)}) collective-permute-start(f32[24,128]{1,0:T(8,128)S(1)} %get-tuple-element.46), channel_id=1, source_target_pairs={{0,3},{1,0},{2,1},{3,2},{4,7},{5,4},{6,5},{7,6},{8,11},{9,8},{10,9... | collective-permute-start | bytes 36872 | tf_op jit(solution)/shard_map/ppermute | solution.py:365
  54.2 0.1 unpack_planes.1.main
  54.4 1.2 %collective-permute-done.16.below = f32[24,128]{1,0:T(8,128)S(1)} collective-permute-done((f32[24,128]{1,0:T(8,128)S(1)}, f32[24,128]{1,0:T(8,128)S(1)}, u32[]{:S(2)}, u32[]{:S(2)}) %collective-permute-start.16) | collective-permute-done | bytes 12320 | tf_op jit(solution)/shard_map/ppermute | solution.py:364
  55.6 0.0 collective-permute-done.17.above
  55.6 0.9 %finish.1 = f32[1216,128]{1,0:T(8,128)} custom-call(f32[19,80,128]{2,1,0:T(8,128)S(1)} %unpack_planes.1.main, f32[24,128]{1,0:T(8,128)S(1)} %collective-permute-done.16.below, f32[24,128]{1,0:T(8,128)S(1)} %collective-permute-done.17.above), custom_call_target="tpu_custom_call" | custom-call | flops 100000 | bytes 100000 | tf_op jit(solution)/shard_map/finish/pallas_call | solution.py:345
  (3 shorter events, 0.0 us)
Async XLA Ops:
  0.0 0.7 %copy-start.2 = (s32[1,1,3,2]{2,3,1,0:T(2,128)S(1)}, s32[1,1,3,2]{2,3,1,0:T(2,128)}, u32[]{:S(2)}) copy-start(s32[1,1,3,2]{2,3,1,0:T(2,128)} %param.7) | copy-start | bytes 76
  0.0 0.7 %copy-start.3 = (s32[1,2]{1,0:T(1,128)S(1)}, s32[1,2]{1,0:T(1,128)}, u32[]{:S(2)}) copy-start(s32[1,2]{1,0:T(1,128)} %slots.1) | copy-start | bytes 28
  0.7 1.1 %copy-start = (f32[1,2,19,4096]{3,1,2,0:T(2,128)S(1)}, f32[1,2,19,4096]{3,1,2,0:T(2,128)}, u32[]{:S(2)}) copy-start(f32[1,2,19,4096]{3,1,2,0:T(2,128)} %param.4) | copy-start | bytes 1867780
  1.8 0.8 %copy-start.1 = (s32[1,2,4096]{2,1,0:T(2,128)S(1)}, s32[1,2,4096]{2,1,0:T(2,128)}, u32[]{:S(2)}) copy-start(s32[1,2,4096]{2,1,0:T(2,128)} %param.5) | copy-start | bytes 98308
  2.7 3.8 %collective-permute-start = (f32[24,128]{1,0:T(8,128)S(1)}, f32[24,128]{1,0:T(8,128)S(1)}, u32[]{:S(2)}, u32[]{:S(2)}) collective-permute-start(f32[24,128]{1,0:T(8,128)S(1)} %get-tuple-element.27), channel_id=1, source_target_pairs={{0,1},{1,2},{2,3},{3,0},{4,5},{5,6},{6,7},{7,4},{8,9},{9,10},{10,1... | collective-permute-start | bytes 36872 | tf_op jit(solution)/shard_map/ppermute | solution.py:364
  3.2 3.4 %collective-permute-start.1 = (f32[24,128]{1,0:T(8,128)S(1)}, f32[24,128]{1,0:T(8,128)S(1)}, u32[]{:S(2)}, u32[]{:S(2)}) collective-permute-start(f32[24,128]{1,0:T(8,128)S(1)} %get-tuple-element.28), channel_id=1, source_target_pairs={{0,3},{1,0},{2,1},{3,2},{4,7},{5,4},{6,5},{7,6},{8,11},{9,8},{10,9... | collective-permute-start | bytes 36872 | tf_op jit(solution)/shard_map/ppermute | solution.py:365
  6.8 8.2 %collective-permute-start.2 = (f32[168,128]{1,0:T(8,128)S(1)}, f32[168,128]{1,0:T(8,128)S(1)}, u32[]{:S(2)}, u32[]{:S(2)}) collective-permute-start(f32[168,128]{1,0:T(8,128)S(1)} %get-tuple-element.30), channel_id=1, source_target_pairs={{0,4},{4,0},{8,12},{12,8},{16,20},{20,16},{24,28},{28,24},{1,5},{5... | collective-permute-start | bytes 258056 | tf_op jit(solution)/shard_map/ppermute | solution.py:359
  9.1 9.5 %collective-permute-start.3 = (f32[168,128]{1,0:T(8,128)S(1)}, f32[168,128]{1,0:T(8,128)S(1)}, u32[]{:S(2)}, u32[]{:S(2)}) collective-permute-start(f32[168,128]{1,0:T(8,128)S(1)} %get-tuple-element.31), channel_id=1, source_target_pairs={{0,8},{4,12},{8,0},{12,4},{16,24},{20,28},{24,16},{28,20},{1,9},{5... | collective-permute-start | bytes 258056 | tf_op jit(solution)/shard_map/ppermute | solution.py:359
  10.7 8.7 %collective-permute-start.4 = (f32[168,128]{1,0:T(8,128)S(1)}, f32[168,128]{1,0:T(8,128)S(1)}, u32[]{:S(2)}, u32[]{:S(2)}) collective-permute-start(f32[168,128]{1,0:T(8,128)S(1)} %get-tuple-element.32), channel_id=1, source_target_pairs={{0,12},{4,8},{8,4},{12,0},{16,28},{20,24},{24,20},{28,16},{1,13},{... | collective-permute-start | bytes 258056 | tf_op jit(solution)/shard_map/ppermute | solution.py:359
  10.7 8.7 %collective-permute-start.5 = (f32[168,128]{1,0:T(8,128)S(1)}, f32[168,128]{1,0:T(8,128)S(1)}, u32[]{:S(2)}, u32[]{:S(2)}) collective-permute-start(f32[168,128]{1,0:T(8,128)S(1)} %get-tuple-element.33), channel_id=1, source_target_pairs={{0,16},{4,20},{8,24},{12,28},{16,0},{20,4},{24,8},{28,12},{1,17},{... | collective-permute-start | bytes 258056 | tf_op jit(solution)/shard_map/ppermute | solution.py:359
  13.6 14.5 %collective-permute-start.6 = (f32[168,128]{1,0:T(8,128)S(1)}, f32[168,128]{1,0:T(8,128)S(1)}, u32[]{:S(2)}, u32[]{:S(2)}) collective-permute-start(f32[168,128]{1,0:T(8,128)S(1)} %get-tuple-element.34), channel_id=1, source_target_pairs={{0,20},{4,16},{8,28},{12,24},{16,4},{20,0},{24,12},{28,8},{1,21},{... | collective-permute-start | bytes 258056 | tf_op jit(solution)/shard_map/ppermute | solution.py:359
  14.9 13.2 %collective-permute-start.7 = (f32[168,128]{1,0:T(8,128)S(1)}, f32[168,128]{1,0:T(8,128)S(1)}, u32[]{:S(2)}, u32[]{:S(2)}) collective-permute-start(f32[168,128]{1,0:T(8,128)S(1)} %get-tuple-element.35), channel_id=1, source_target_pairs={{0,24},{4,28},{8,16},{12,20},{16,8},{20,12},{24,0},{28,4},{1,25},{... | collective-permute-start | bytes 258056 | tf_op jit(solution)/shard_map/ppermute | solution.py:359
  18.5 9.6 %collective-permute-start.8 = (f32[168,128]{1,0:T(8,128)S(1)}, f32[168,128]{1,0:T(8,128)S(1)}, u32[]{:S(2)}, u32[]{:S(2)}) collective-permute-start(f32[168,128]{1,0:T(8,128)S(1)} %get-tuple-element.36), channel_id=1, source_target_pairs={{0,28},{4,24},{8,20},{12,16},{16,12},{20,8},{24,4},{28,0},{1,29},{... | collective-permute-start | bytes 258056 | tf_op jit(solution)/shard_map/ppermute | solution.py:359
  31.5 9.1 %collective-permute-start.9 = (f32[152,128]{1,0:T(8,128)S(1)}, f32[152,128]{1,0:T(8,128)S(1)}, u32[]{:S(2)}, u32[]{:S(2)}) collective-permute-start(f32[152,128]{1,0:T(8,128)S(1)} %get-tuple-element.38), channel_id=1, source_target_pairs={{0,4},{4,0},{8,12},{12,8},{16,20},{20,16},{24,28},{28,24},{1,5},{5... | collective-permute-start | bytes 233480 | tf_op jit(solution)/shard_map/ppermute | solution.py:359
  32.7 10.4 %collective-permute-start.10 = (f32[152,128]{1,0:T(8,128)S(1)}, f32[152,128]{1,0:T(8,128)S(1)}, u32[]{:S(2)}, u32[]{:S(2)}) collective-permute-start(f32[152,128]{1,0:T(8,128)S(1)} %get-tuple-element.39), channel_id=1, source_target_pairs={{0,8},{4,12},{8,0},{12,4},{16,24},{20,28},{24,16},{28,20},{1,9},{5... | collective-permute-start | bytes 233480 | tf_op jit(solution)/shard_map/ppermute | solution.py:359
  36.8 8.6 %collective-permute-start.11 = (f32[152,128]{1,0:T(8,128)S(1)}, f32[152,128]{1,0:T(8,128)S(1)}, u32[]{:S(2)}, u32[]{:S(2)}) collective-permute-start(f32[152,128]{1,0:T(8,128)S(1)} %get-tuple-element.40), channel_id=1, source_target_pairs={{0,12},{4,8},{8,4},{12,0},{16,28},{20,24},{24,20},{28,16},{1,13},{... | collective-permute-start | bytes 233480 | tf_op jit(solution)/shard_map/ppermute | solution.py:359
  37.0 12.2 %collective-permute-start.12 = (f32[152,128]{1,0:T(8,128)S(1)}, f32[152,128]{1,0:T(8,128)S(1)}, u32[]{:S(2)}, u32[]{:S(2)}) collective-permute-start(f32[152,128]{1,0:T(8,128)S(1)} %get-tuple-element.41), channel_id=1, source_target_pairs={{0,16},{4,20},{8,24},{12,28},{16,0},{20,4},{24,8},{28,12},{1,17},{... | collective-permute-start | bytes 233480 | tf_op jit(solution)/shard_map/ppermute | solution.py:359
  40.6 11.7 %collective-permute-start.13 = (f32[152,128]{1,0:T(8,128)S(1)}, f32[152,128]{1,0:T(8,128)S(1)}, u32[]{:S(2)}, u32[]{:S(2)}) collective-permute-start(f32[152,128]{1,0:T(8,128)S(1)} %get-tuple-element.42), channel_id=1, source_target_pairs={{0,20},{4,16},{8,28},{12,24},{16,4},{20,0},{24,12},{28,8},{1,21},{... | collective-permute-start | bytes 233480 | tf_op jit(solution)/shard_map/ppermute | solution.py:359
  40.7 11.6 %collective-permute-start.14 = (f32[152,128]{1,0:T(8,128)S(1)}, f32[152,128]{1,0:T(8,128)S(1)}, u32[]{:S(2)}, u32[]{:S(2)}) collective-permute-start(f32[152,128]{1,0:T(8,128)S(1)} %get-tuple-element.43), channel_id=1, source_target_pairs={{0,24},{4,28},{8,16},{12,20},{16,8},{20,12},{24,0},{28,4},{1,25},{... | collective-permute-start | bytes 233480 | tf_op jit(solution)/shard_map/ppermute | solution.py:359
  43.0 9.2 %collective-permute-start.15 = (f32[152,128]{1,0:T(8,128)S(1)}, f32[152,128]{1,0:T(8,128)S(1)}, u32[]{:S(2)}, u32[]{:S(2)}) collective-permute-start(f32[152,128]{1,0:T(8,128)S(1)} %get-tuple-element.44), channel_id=1, source_target_pairs={{0,28},{4,24},{8,20},{12,16},{16,12},{20,8},{24,4},{28,0},{1,29},{... | collective-permute-start | bytes 233480 | tf_op jit(solution)/shard_map/ppermute | solution.py:359
  52.4 3.2 %collective-permute-start.16 = (f32[24,128]{1,0:T(8,128)S(1)}, f32[24,128]{1,0:T(8,128)S(1)}, u32[]{:S(2)}, u32[]{:S(2)}) collective-permute-start(f32[24,128]{1,0:T(8,128)S(1)} %get-tuple-element.45), channel_id=1, source_target_pairs={{0,1},{1,2},{2,3},{3,0},{4,5},{5,6},{6,7},{7,4},{8,9},{9,10},{10,1... | collective-permute-start | bytes 36872 | tf_op jit(solution)/shard_map/ppermute | solution.py:364
  52.5 3.1 %collective-permute-start.17 = (f32[24,128]{1,0:T(8,128)S(1)}, f32[24,128]{1,0:T(8,128)S(1)}, u32[]{:S(2)}, u32[]{:S(2)}) collective-permute-start(f32[24,128]{1,0:T(8,128)S(1)} %get-tuple-element.46), channel_id=1, source_target_pairs={{0,3},{1,0},{2,1},{3,2},{4,7},{5,4},{6,5},{7,6},{8,11},{9,8},{10,9... | collective-permute-start | bytes 36872 | tf_op jit(solution)/shard_map/ppermute | solution.py:365

commit v4 on v3

--- a/solution.py
+++ b/solution.py
@@ -39,7 +39,6 @@
 DOWNWARD = tuple(p for p in range(Q) if VELOCITIES[p][0] == -1)
 
 VMEM_SPEC = pl.BlockSpec(memory_space=pltpu.VMEM)
-PARAMS = pltpu.CompilerParams(vmem_limit_bytes=40 * 1024 * 1024)
 
 
 def dynamic_place(owner, odd_slab, owners):
@@ -136,11 +135,26 @@
     rows_hop = faces + 4
     f32 = jnp.float32
 
+    order = [0]
+    for bit in reversed(range(owners.bit_length() - 1)):
+        order += range(1 << bit, 2 << bit)
+    slot_of = [order.index(d) for d in range(owners)]
+
     def position():
         me = lax.axis_index("gx")
         return me, lax.axis_index("gy") % 2
 
-    def edge_kernel(pops, mask, slots, swaps, up, down, own, cells, solid, held, given, sem):
+    def sides(odd, near, far):
+        return (
+            jnp.where(odd == 1, near[...], far[...]),
+            jnp.where(odd == 1, far[...], near[...]),
+        )
+
+    def send_sides(odd, up, down, near, far):
+        near[...] = jnp.where(odd == 1, down[...], up[...])
+        far[...] = jnp.where(odd == 1, up[...], down[...])
+
+    def edge_kernel(pops, mask, slots, swaps, near, far, own, up, down, cells, solid, held, given, sem):
         ends = (WHOLE - 8, 0)
         copies = []
         for n, start in enumerate(ends):
@@ -163,16 +177,9 @@
             for m, p in enumerate(chosen):
                 out[pl.ds(m * PLANE, PLANE), :] = after[p][inside : inside + PLANE]
             out[pl.ds(faces, 4), :] = own[0:4]
-
-    def collide_kernel(pops, mask, post, cells, solid, sem):
-        copies = (
-            pltpu.make_async_copy(pops, cells, sem.at[0]),
-            pltpu.make_async_copy(mask, solid, sem.at[1]),
-        )
-        for copy in copies:
-            copy.start()
-        for copy in copies:
-            copy.wait()
+        send_sides(position()[1], up, down, near, far)
+
+    def collide_kernel(cells, solid, post):
         for start in range(0, WHOLE, 8):
             here = pl.ds(start, 8)
             after = collide([cells[p, here, :] for p in range(Q)], solid[here, :] > 0)
@@ -180,34 +187,36 @@
                 post[p, pl.ds(8 + start, 8), :] = after[p]
             post[Q, pl.ds(8 + start, 8), :] = solid[here, :].astype(f32)
 
-    def pack_kernel(post, own, below, above, *outs):
+    def pack_kernel(post, own, near, far, *outs):
         me, odd = position()
+        below, above = sides(odd, near, far)
         for d in range(owners):
-            out = outs[d]
+            out = outs[slot_of[d]]
             place = dynamic_place(me ^ d, odd, owners)
             here = pl.multiple_of(place * share, min(share, 8))
             for p in range(Q + 1):
                 cx = VELOCITIES[p][0] if p < Q else 0
                 out[pl.ds(p * share, share), :] = post[p, pl.ds(8 + here - cx * PLANE, share), :]
             out[pl.ds(head, 2), :] = own[0:2]
-            out[pl.ds(head + 2, 2), :] = below[pl.ds(faces, 2), :]
-            out[pl.ds(head + 4, 2), :] = above[pl.ds(faces, 2), :]
+            out[pl.ds(head + 2, 2), :] = below[faces : faces + 2]
+            out[pl.ds(head + 4, 2), :] = above[faces : faces + 2]
             out[pl.ds(head + 6, 2), :] = own[2:4]
 
             @pl.when(place == 0)
             def _():
                 for n, p in enumerate(UPWARD):
-                    out[pl.ds(p * share, PLANE), :] = below[pl.ds(n * PLANE, PLANE), :]
+                    out[pl.ds(p * share, PLANE), :] = below[n * PLANE : (n + 1) * PLANE]
 
             @pl.when(place == owners - 1)
             def _():
                 for n, p in enumerate(DOWNWARD):
                     out[pl.ds(p * share + share - PLANE, PLANE), :] = above[
-                        pl.ds(n * PLANE, PLANE), :
+                        n * PLANE : (n + 1) * PLANE
                     ]
 
     def middle_kernel(*refs):
-        got, outs = refs[:owners], refs[owners : 2 * owners]
+        got = [refs[slot_of[d]] for d in range(owners)]
+        outs = [refs[owners + slot_of[d]] for d in range(owners)]
         lattice, ready, table, sem = refs[2 * owners :]
         me, odd = position()
         place = dynamic_place(me, odd, owners)
@@ -297,7 +306,8 @@
                         ]
 
     def crossing_kernel(*refs):
-        got, up, down = refs[:owners], refs[owners], refs[owners + 1]
+        got = [refs[slot_of[d]] for d in range(owners)]
+        near, far, up, down = refs[owners:]
         me, odd = position()
         for d in range(owners):
             place = dynamic_place(me ^ d, odd, owners)
@@ -316,9 +326,10 @@
 
         for out in (up, down):
             out[pl.ds(faces, 4), :] = jnp.zeros((4, LANES), f32)
+        send_sides(odd, up, down, near, far)
 
     def unpack_kernel(*refs):
-        got, main = refs[:owners], refs[owners]
+        got, main = [refs[slot_of[d]] for d in range(owners)], refs[owners]
         me, odd = position()
         for d in range(owners):
             place = dynamic_place(me ^ d, odd, owners)
@@ -329,18 +340,19 @@
                     pl.ds(p * share, share), :
                 ]
 
-    def finish_kernel(main, below, above, out):
+    def finish_kernel(main, near, far, out):
+        below, above = sides(position()[1], near, far)
         for p in range(Q):
             out[pl.ds(p * WHOLE, WHOLE), :] = main[p, pl.ds(8, WHOLE), :]
         for n, p in enumerate(UPWARD):
-            out[pl.ds(p * WHOLE, PLANE), :] = below[pl.ds(n * PLANE, PLANE), :]
+            out[pl.ds(p * WHOLE, PLANE), :] = below[n * PLANE : (n + 1) * PLANE]
         for n, p in enumerate(DOWNWARD):
-            out[pl.ds(p * WHOLE + WHOLE - PLANE, PLANE), :] = above[pl.ds(n * PLANE, PLANE), :]
+            out[pl.ds(p * WHOLE + WHOLE - PLANE, PLANE), :] = above[n * PLANE : (n + 1) * PLANE]
 
     def shape(*dims):
         return jax.ShapeDtypeStruct(dims, f32)
 
-    def call(kernel, name, out_shape, inputs, cost, scratch=(), spec=VMEM_SPEC):
+    def call(kernel, name, out_shape, inputs, cost, scratch=(), spec=VMEM_SPEC, limit=40):
         outs = jax.tree.map(lambda _: VMEM_SPEC, out_shape)
         return pl.pallas_call(
             kernel,
@@ -348,21 +360,23 @@
             in_specs=[spec] * len(inputs),
             out_specs=outs,
             scratch_shapes=list(scratch),
-            compiler_params=PARAMS,
+            compiler_params=pltpu.CompilerParams(vmem_limit_bytes=limit * 1024 * 1024),
             cost_estimate=pl.CostEstimate(flops=cost, bytes_accessed=cost, transcendentals=0),
             name=name,
         )(*inputs)
 
     def exchange(parts):
-        here = list(parts)
-        for d in reversed(range(1, owners)):
-            here[d] = lax.ppermute(parts[d], "gx", [(g, g ^ d) for g in range(owners)])
-        return here
-
-    def hop(up, down):
+        return [parts[0]] + [
+            lax.ppermute(parts[n], "gx", [(g, g ^ order[n]) for g in range(owners)])
+            for n in range(1, owners)
+        ]
+
+    def hop(near, far):
+        ahead = [(s + 1) % slabs if s % 2 == 0 else (s - 1) % slabs for s in range(slabs)]
+        behind = [(s - 1) % slabs if s % 2 == 0 else (s + 1) % slabs for s in range(slabs)]
         return (
-            lax.ppermute(up, "gy", [(s, (s + 1) % slabs) for s in range(slabs)]),
-            lax.ppermute(down, "gy", [(s, (s - 1) % slabs) for s in range(slabs)]),
+            lax.ppermute(near, "gy", list(enumerate(ahead))),
+            lax.ppermute(far, "gy", list(enumerate(behind))),
         )
 
     def padded(count):
@@ -377,14 +391,16 @@
         pops = pops.transpose(0, 2, 1, 3).reshape(Q, WHOLE, LANES)
         mask = solid_mask[0].reshape(NB, tiles, LANES).transpose(1, 0, 2).reshape(WHOLE, LANES)
         swaps = swap_slots[0, 0].T
-        in_place = pl.BlockSpec(memory_space=pl.ANY)
-        up, down, own = call(
+        in_place = pl.BlockSpec(memory_space=pltpu.HBM)
+        near, far, own = call(
             edge_kernel,
             "edge_planes",
             (shape(rows_hop, LANES), shape(rows_hop, LANES), shape(8, LANES)),
             (pops, mask, slot_blocks, swaps),
             small,
             (
+                pltpu.VMEM((rows_hop, LANES), f32),
+                pltpu.VMEM((rows_hop, LANES), f32),
                 pltpu.VMEM((2, Q, 8, LANES), f32),
                 pltpu.VMEM((2, 8, LANES), jnp.int32),
                 pltpu.VMEM(slot_blocks.shape, jnp.int32),
@@ -392,26 +408,21 @@
                 pltpu.SemaphoreType.DMA((6,)),
             ),
             in_place,
-        )
-        below, above = hop(up, down)
+            62,
+        )
+        near, far = hop(near, far)
         post = call(
             collide_kernel,
             "first_collision",
             padded(Q + 1),
             (pops, mask),
             large,
-            (
-                pltpu.VMEM(pops.shape, f32),
-                pltpu.VMEM(mask.shape, jnp.int32),
-                pltpu.SemaphoreType.DMA((2,)),
-            ),
-            in_place,
         )
         parts = call(
             pack_kernel,
             "pack_planes",
             (shape(rows_in, LANES),) * owners,
-            (post, own, below, above),
+            (post, own, near, far),
             large,
         )
         got = exchange(parts)
@@ -429,11 +440,18 @@
             ),
         )
         home = exchange(parts)
-        up, down = call(crossing_kernel, "crossing_planes", (shape(rows_hop, LANES),) * 2, home, small)
-        below, above = hop(up, down)
+        near, far = call(
+            crossing_kernel,
+            "crossing_planes",
+            (shape(rows_hop, LANES),) * 2,
+            home,
+            small,
+            (pltpu.VMEM((rows_hop, LANES), f32),) * 2,
+        )
+        near, far = hop(near, far)
         main = call(unpack_kernel, "unpack_planes", padded(Q), home, large)
         out = call(
-            finish_kernel, "finish", shape(Q * WHOLE, LANES), (main, below, above), small
+            finish_kernel, "finish", shape(Q * WHOLE, LANES), (main, near, far), small
         )
         out = out.reshape(Q, tiles, NB, LANES).transpose(0, 2, 1, 3)
         return out.reshape(Q, NB, B * B * B).transpose(1, 0, 2)[None]

time: 57.5 us -> 55.1 us (0.958); the launches traced: 56.5 us -> 54.9 us
  local copies, waits for them, and re-layouts: 2.51 us -> 0.01 us
  Pallas kernels: 5.35 us -> 6.56 us
  waiting for transfers between devices: 18.7 us -> 18 us
    unnamed x8 -> x6, local copies, waits for them, and re-layouts: 2.51 us -> 0.01 us
    pallas_call x7, Pallas kernels: 5.35 us -> 6.56 us  [call(): pl.pallas_call(kernel, out_shape=out_shape, in_specs=[spec] * len(inputs)...]
    ppermute x18, waiting for transfers between devices: 18.7 us -> 18 us  [the longest x14 15.2 us: exchange(): lax.ppermute(parts[n], 'gx', [(g, g ^ order[n]) for g in range(owners)])]
  transfers between devices with their start and end apart: 18 -> 18, of which waited for: 7 -> 10; matrix products, arithmetic and copies ran while one was open for 0% -> 0% of each run, Pallas kernels for 1% -> 1%
where the time goes in v4:
time: 55.1 us; the launch traced here: 54.9 us
  starting transfers between devices  30.3 us (55%)
  waiting for transfers between devices  18 us (33%)
  Pallas kernels  6.56 us (12%)
    ppermute x14, starting transfers between devices, exchange(): lax.ppermute(parts[n], 'gx', [(g, g ^ order[n]) for g in range(owners)])  25.5 us
    ppermute x14, waiting for transfers between devices, exchange(): lax.ppermute(parts[n], 'gx', [(g, g ^ order[n]) for g in range(owners)])  15.2 us
    pallas_call x7, Pallas kernels, call(): pl.pallas_call(kernel, out_shape=out_shape, in_specs=[spec] * len(inputs)...  6.56 us
    ppermute x2, starting transfers between devices, hop(): lax.ppermute(far, 'gy', list(enumerate(behind)))  4.22 us
    ppermute x2, waiting for transfers between devices, hop(): lax.ppermute(far, 'gy', list(enumerate(behind)))  2.8 us
  transfers between devices with their start and end apart: 18, of which 10 were waited for; matrix products, arithmetic and copies ran while one was open for 0% of the time, Pallas kernels for 1%

profile of v4, /device:TPU:0, one launch (start us, length us, event | category | flops | bytes accessed | tf_op | source)
XLA Modules:
  0.0 54.9 jit_solution(13779638000940587012)
XLA Ops:
  0.0 0.0 copy-start
  0.0 0.0 copy-start.1
  0.0 1.7 %edge_planes.1 = (f32[24,128]{1,0:T(8,128)}, f32[24,128]{1,0:T(8,128)}, f32[8,128]{1,0:T(8,128)}) custom-call(f32[19,64,128]{2,1,0:T(8,128)} %bitcast.26, s32[64,128]{1,0:T(8,128)} %bitcast.28, s32[1,2]{1,0:T(1,128)} %slots.1, s32[2,3]{1,0:T(2,128)} %bitcast.30), custom_call_target="tpu_custom_call" | custom-call | flops 100000 | bytes 100000 | tf_op jit(solution)/shard_map/edge_planes/pallas_call | solution.py:357
  1.7 0.5 collective-permute-start
  2.2 2.6 %collective-permute-start.1 = (f32[24,128]{1,0:T(8,128)}, f32[24,128]{1,0:T(8,128)S(1)}, u32[]{:S(2)}, u32[]{:S(2)}) collective-permute-start(f32[24,128]{1,0:T(8,128)} %get-tuple-element.28), channel_id=1, source_target_pairs={{0,3},{1,2},{2,1},{3,0},{4,7},{5,6},{6,5},{7,4},{8,11},{9,10},{10,... | collective-permute-start | bytes 36872 | tf_op jit(solution)/shard_map/ppermute | solution.py:379
  4.9 0.0 copy-done
  4.9 0.0 copy-done.1
  4.9 0.0 copy-start.2
  4.9 0.2 first_collision.1.post
  5.1 0.0 collective-permute-done.near
  5.1 1.4 %collective-permute-done.1.far = f32[24,128]{1,0:T(8,128)S(1)} collective-permute-done((f32[24,128]{1,0:T(8,128)}, f32[24,128]{1,0:T(8,128)S(1)}, u32[]{:S(2)}, u32[]{:S(2)}) %collective-permute-start.1) | collective-permute-done | bytes 12320 | tf_op jit(solution)/shard_map/ppermute | solution.py:379
  6.5 0.0 copy-done.2
  6.5 0.2 pack_planes.1
  6.7 2.8 %collective-permute-start.2 = (f32[168,128]{1,0:T(8,128)S(1)}, f32[168,128]{1,0:T(8,128)S(1)}, u32[]{:S(2)}, u32[]{:S(2)}) collective-permute-start(f32[168,128]{1,0:T(8,128)S(1)} %get-tuple-element.30), channel_id=1, source_target_pairs={{0,16},{4,20},{8,24},{12,28},{16,0},{20,4},{24,8},{28,12},{1,17},{... | collective-permute-start | bytes 258056 | tf_op jit(solution)/shard_map/ppermute | solution.py:370
  9.5 1.3 %collective-permute-start.3 = (f32[168,128]{1,0:T(8,128)S(1)}, f32[168,128]{1,0:T(8,128)S(1)}, u32[]{:S(2)}, u32[]{:S(2)}) collective-permute-start(f32[168,128]{1,0:T(8,128)S(1)} %get-tuple-element.31), channel_id=1, source_target_pairs={{0,20},{4,16},{8,28},{12,24},{16,4},{20,0},{24,12},{28,8},{1,21},{... | collective-permute-start | bytes 258056 | tf_op jit(solution)/shard_map/ppermute | solution.py:370
  10.8 3.6 %collective-permute-start.4 = (f32[168,128]{1,0:T(8,128)S(1)}, f32[168,128]{1,0:T(8,128)S(1)}, u32[]{:S(2)}, u32[]{:S(2)}) collective-permute-start(f32[168,128]{1,0:T(8,128)S(1)} %get-tuple-element.32), channel_id=1, source_target_pairs={{0,24},{4,28},{8,16},{12,20},{16,8},{20,12},{24,0},{28,4},{1,25},{... | collective-permute-start | bytes 258056 | tf_op jit(solution)/shard_map/ppermute | solution.py:370
  14.4 0.0 collective-permute-start.5
  14.4 0.0 collective-permute-start.6
  14.4 0.4 collective-permute-done.2.refs_1_
  14.8 7.0 %collective-permute-start.7 = (f32[168,128]{1,0:T(8,128)S(1)}, f32[168,128]{1,0:T(8,128)S(1)}, u32[]{:S(2)}, u32[]{:S(2)}) collective-permute-start(f32[168,128]{1,0:T(8,128)S(1)} %get-tuple-element.35), channel_id=1, source_target_pairs={{0,12},{4,8},{8,4},{12,0},{16,28},{20,24},{24,20},{28,16},{1,13},{... | collective-permute-start | bytes 258056 | tf_op jit(solution)/shard_map/ppermute | solution.py:370
  21.8 1.6 %collective-permute-done.3.refs_2_ = f32[168,128]{1,0:T(8,128)S(1)} collective-permute-done((f32[168,128]{1,0:T(8,128)S(1)}, f32[168,128]{1,0:T(8,128)S(1)}, u32[]{:S(2)}, u32[]{:S(2)}) %collective-permute-start.3) | collective-permute-done | bytes 86048 | tf_op jit(solution)/shard_map/ppermute | solution.py:370
  23.4 0.5 collective-permute-start.8
  23.9 0.0 collective-permute-done.4.refs_3_
  23.9 0.0 collective-permute-done.5.refs_4_
  23.9 0.0 collective-permute-done.6.refs_5_
  23.9 2.7 %collective-permute-done.7.refs_6_ = f32[168,128]{1,0:T(8,128)S(1)} collective-permute-done((f32[168,128]{1,0:T(8,128)S(1)}, f32[168,128]{1,0:T(8,128)S(1)}, u32[]{:S(2)}, u32[]{:S(2)}) %collective-permute-start.7) | collective-permute-done | bytes 86048 | tf_op jit(solution)/shard_map/ppermute | solution.py:370
  26.6 1.7 %collective-permute-done.8.refs_7_ = f32[168,128]{1,0:T(8,128)S(1)} collective-permute-done((f32[168,128]{1,0:T(8,128)S(1)}, f32[168,128]{1,0:T(8,128)S(1)}, u32[]{:S(2)}, u32[]{:S(2)}) %collective-permute-start.8) | collective-permute-done | bytes 86048 | tf_op jit(solution)/shard_map/ppermute | solution.py:370
  28.3 3.4 %second_step.1 = (f32[152,128]{1,0:T(8,128)S(1)}, f32[152,128]{1,0:T(8,128)S(1)}, f32[152,128]{1,0:T(8,128)S(1)}, f32[152,128]{1,0:T(8,128)S(1)}, f32[152,128]{1...) custom-call(f32[168,128]{1,0:T(8,128)S(1)} %get-tuple-element.29.refs_0_, ...), custom_call_target="tpu_custom_call" | custom-call | flops 4000000 | bytes 4000000 | tf_op jit(solution)/shard_map/second_step/pallas_call | solution.py:357
  31.7 3.4 %collective-permute-start.9 = (f32[152,128]{1,0:T(8,128)S(1)}, f32[152,128]{1,0:T(8,128)S(1)}, u32[]{:S(2)}, u32[]{:S(2)}) collective-permute-start(f32[152,128]{1,0:T(8,128)S(1)} %get-tuple-element.38), channel_id=1, source_target_pairs={{0,16},{4,20},{8,24},{12,28},{16,0},{20,4},{24,8},{28,12},{1,17},{... | collective-permute-start | bytes 233480 | tf_op jit(solution)/shard_map/ppermute | solution.py:370
  35.1 0.0 collective-permute-start.10
  35.1 3.2 %collective-permute-start.11 = (f32[152,128]{1,0:T(8,128)S(1)}, f32[152,128]{1,0:T(8,128)S(1)}, u32[]{:S(2)}, u32[]{:S(2)}) collective-permute-start(f32[152,128]{1,0:T(8,128)S(1)} %get-tuple-element.40), channel_id=1, source_target_pairs={{0,24},{4,28},{8,16},{12,20},{16,8},{20,12},{24,0},{28,4},{1,25},{... | collective-permute-start | bytes 233480 | tf_op jit(solution)/shard_map/ppermute | solution.py:370
  38.3 1.6 %collective-permute-start.12 = (f32[152,128]{1,0:T(8,128)S(1)}, f32[152,128]{1,0:T(8,128)S(1)}, u32[]{:S(2)}, u32[]{:S(2)}) collective-permute-start(f32[152,128]{1,0:T(8,128)S(1)} %get-tuple-element.41), channel_id=1, source_target_pairs={{0,28},{4,24},{8,20},{12,16},{16,12},{20,8},{24,4},{28,0},{1,29},{... | collective-permute-start | bytes 233480 | tf_op jit(solution)/shard_map/ppermute | solution.py:370
  39.9 0.0 collective-permute-start.13
  39.9 4.0 %collective-permute-done.9.refs_1_ = f32[152,128]{1,0:T(8,128)S(1)} collective-permute-done((f32[152,128]{1,0:T(8,128)S(1)}, f32[152,128]{1,0:T(8,128)S(1)}, u32[]{:S(2)}, u32[]{:S(2)}) %collective-permute-start.9) | collective-permute-done | bytes 77856 | tf_op jit(solution)/shard_map/ppermute | solution.py:370
  43.9 0.6 %collective-permute-start.14 = (f32[152,128]{1,0:T(8,128)S(1)}, f32[152,128]{1,0:T(8,128)S(1)}, u32[]{:S(2)}, u32[]{:S(2)}) collective-permute-start(f32[152,128]{1,0:T(8,128)S(1)} %get-tuple-element.43), channel_id=1, source_target_pairs={{0,12},{4,8},{8,4},{12,0},{16,28},{20,24},{24,20},{28,16},{1,13},{... | collective-permute-start | bytes 233480 | tf_op jit(solution)/shard_map/ppermute | solution.py:370
  44.5 1.8 %collective-permute-done.10.refs_2_ = f32[152,128]{1,0:T(8,128)S(1)} collective-permute-done((f32[152,128]{1,0:T(8,128)S(1)}, f32[152,128]{1,0:T(8,128)S(1)}, u32[]{:S(2)}, u32[]{:S(2)}) %collective-permute-start.10) | collective-permute-done | bytes 77856 | tf_op jit(solution)/shard_map/ppermute | solution.py:370
  46.4 1.5 %collective-permute-start.15 = (f32[152,128]{1,0:T(8,128)S(1)}, f32[152,128]{1,0:T(8,128)S(1)}, u32[]{:S(2)}, u32[]{:S(2)}) collective-permute-start(f32[152,128]{1,0:T(8,128)S(1)} %get-tuple-element.44), channel_id=1, source_target_pairs={{0,4},{4,0},{8,12},{12,8},{16,20},{20,16},{24,28},{28,24},{1,5},{5... | collective-permute-start | bytes 233480 | tf_op jit(solution)/shard_map/ppermute | solution.py:370
  47.8 0.0 collective-permute-done.11.refs_3_
  47.8 0.0 collective-permute-done.12.refs_4_
  47.8 0.0 collective-permute-done.13.refs_5_
  47.8 1.5 %collective-permute-done.14.refs_6_ = f32[152,128]{1,0:T(8,128)S(1)} collective-permute-done((f32[152,128]{1,0:T(8,128)S(1)}, f32[152,128]{1,0:T(8,128)S(1)}, u32[]{:S(2)}, u32[]{:S(2)}) %collective-permute-start.14) | collective-permute-done | bytes 77856 | tf_op jit(solution)/shard_map/ppermute | solution.py:370
  49.3 1.5 %collective-permute-done.15.refs_7_ = f32[152,128]{1,0:T(8,128)S(1)} collective-permute-done((f32[152,128]{1,0:T(8,128)S(1)}, f32[152,128]{1,0:T(8,128)S(1)}, u32[]{:S(2)}, u32[]{:S(2)}) %collective-permute-start.15) | collective-permute-done | bytes 77856 | tf_op jit(solution)/shard_map/ppermute | solution.py:370
  50.8 0.1 collective-permute-start.16
  50.9 1.6 %collective-permute-start.17 = (f32[24,128]{1,0:T(8,128)S(1)}, f32[24,128]{1,0:T(8,128)S(1)}, u32[]{:S(2)}, u32[]{:S(2)}) collective-permute-start(f32[24,128]{1,0:T(8,128)S(1)} %get-tuple-element.46), channel_id=1, source_target_pairs={{0,3},{1,2},{2,1},{3,0},{4,7},{5,6},{6,5},{7,4},{8,11},{9,10},{10,... | collective-permute-start | bytes 36872 | tf_op jit(solution)/shard_map/ppermute | solution.py:379
  52.5 0.1 unpack_planes.1.main
  52.6 0.0 collective-permute-done.16.near
  52.6 1.4 %collective-permute-done.17.far = f32[24,128]{1,0:T(8,128)S(1)} collective-permute-done((f32[24,128]{1,0:T(8,128)S(1)}, f32[24,128]{1,0:T(8,128)S(1)}, u32[]{:S(2)}, u32[]{:S(2)}) %collective-permute-start.17) | collective-permute-done | bytes 12320 | tf_op jit(solution)/shard_map/ppermute | solution.py:379
  54.0 0.9 %finish.1 = f32[1216,128]{1,0:T(8,128)} custom-call(f32[19,80,128]{2,1,0:T(8,128)S(1)} %unpack_planes.1.main, f32[24,128]{1,0:T(8,128)S(1)} %collective-permute-done.16.near, f32[24,128]{1,0:T(8,128)S(1)} %collective-permute-done.17.far), custom_call_target="tpu_custom_call" | custom-call | flops 100000 | bytes 100000 | tf_op jit(solution)/shard_map/finish/pallas_call | solution.py:357
  (1 shorter events, 0.0 us)
Async XLA Ops:
  0.0 4.9 %copy-start = (f32[1,2,19,4096]{3,1,2,0:T(2,128)S(1)}, f32[1,2,19,4096]{3,1,2,0:T(2,128)}, u32[]{:S(2)}) copy-start(f32[1,2,19,4096]{3,1,2,0:T(2,128)} %param.4) | copy-start | bytes 1867780
  0.0 4.9 %copy-start.1 = (s32[1,2,4096]{2,1,0:T(2,128)S(1)}, s32[1,2,4096]{2,1,0:T(2,128)}, u32[]{:S(2)}) copy-start(s32[1,2,4096]{2,1,0:T(2,128)} %param.5) | copy-start | bytes 98308
  1.7 3.4 %collective-permute-start = (f32[24,128]{1,0:T(8,128)}, f32[24,128]{1,0:T(8,128)S(1)}, u32[]{:S(2)}, u32[]{:S(2)}) collective-permute-start(f32[24,128]{1,0:T(8,128)} %get-tuple-element.27), channel_id=1, source_target_pairs={{0,1},{1,0},{2,3},{3,2},{4,5},{5,4},{6,7},{7,6},{8,9},{9,8},{10,11... | collective-permute-start | bytes 36872 | tf_op jit(solution)/shard_map/ppermute | solution.py:378
  2.2 4.2 %collective-permute-start.1 = (f32[24,128]{1,0:T(8,128)}, f32[24,128]{1,0:T(8,128)S(1)}, u32[]{:S(2)}, u32[]{:S(2)}) collective-permute-start(f32[24,128]{1,0:T(8,128)} %get-tuple-element.28), channel_id=1, source_target_pairs={{0,3},{1,2},{2,1},{3,0},{4,7},{5,6},{6,5},{7,4},{8,11},{9,10},{10,... | collective-permute-start | bytes 36872 | tf_op jit(solution)/shard_map/ppermute | solution.py:379
  4.9 1.6 %copy-start.2 = (f32[8,128]{1,0:T(8,128)S(1)}, f32[8,128]{1,0:T(8,128)}, u32[]{:S(2)}) copy-start(f32[8,128]{1,0:T(8,128)} %get-tuple-element.26.own) | copy-start | bytes 12292
  6.7 8.1 %collective-permute-start.2 = (f32[168,128]{1,0:T(8,128)S(1)}, f32[168,128]{1,0:T(8,128)S(1)}, u32[]{:S(2)}, u32[]{:S(2)}) collective-permute-start(f32[168,128]{1,0:T(8,128)S(1)} %get-tuple-element.30), channel_id=1, source_target_pairs={{0,16},{4,20},{8,24},{12,28},{16,0},{20,4},{24,8},{28,12},{1,17},{... | collective-permute-start | bytes 258056 | tf_op jit(solution)/shard_map/ppermute | solution.py:370
  9.5 13.9 %collective-permute-start.3 = (f32[168,128]{1,0:T(8,128)S(1)}, f32[168,128]{1,0:T(8,128)S(1)}, u32[]{:S(2)}, u32[]{:S(2)}) collective-permute-start(f32[168,128]{1,0:T(8,128)S(1)} %get-tuple-element.31), channel_id=1, source_target_pairs={{0,20},{4,16},{8,28},{12,24},{16,4},{20,0},{24,12},{28,8},{1,21},{... | collective-permute-start | bytes 258056 | tf_op jit(solution)/shard_map/ppermute | solution.py:370
  10.8 13.1 %collective-permute-start.4 = (f32[168,128]{1,0:T(8,128)S(1)}, f32[168,128]{1,0:T(8,128)S(1)}, u32[]{:S(2)}, u32[]{:S(2)}) collective-permute-start(f32[168,128]{1,0:T(8,128)S(1)} %get-tuple-element.32), channel_id=1, source_target_pairs={{0,24},{4,28},{8,16},{12,20},{16,8},{20,12},{24,0},{28,4},{1,25},{... | collective-permute-start | bytes 258056 | tf_op jit(solution)/shard_map/ppermute | solution.py:370
  14.4 9.5 %collective-permute-start.5 = (f32[168,128]{1,0:T(8,128)S(1)}, f32[168,128]{1,0:T(8,128)S(1)}, u32[]{:S(2)}, u32[]{:S(2)}) collective-permute-start(f32[168,128]{1,0:T(8,128)S(1)} %get-tuple-element.33), channel_id=1, source_target_pairs={{0,28},{4,24},{8,20},{12,16},{16,12},{20,8},{24,4},{28,0},{1,29},{... | collective-permute-start | bytes 258056 | tf_op jit(solution)/shard_map/ppermute | solution.py:370
  14.4 9.5 %collective-permute-start.6 = (f32[168,128]{1,0:T(8,128)S(1)}, f32[168,128]{1,0:T(8,128)S(1)}, u32[]{:S(2)}, u32[]{:S(2)}) collective-permute-start(f32[168,128]{1,0:T(8,128)S(1)} %get-tuple-element.34), channel_id=1, source_target_pairs={{0,8},{4,12},{8,0},{12,4},{16,24},{20,28},{24,16},{28,20},{1,9},{5... | collective-permute-start | bytes 258056 | tf_op jit(solution)/shard_map/ppermute | solution.py:370
  14.8 11.8 %collective-permute-start.7 = (f32[168,128]{1,0:T(8,128)S(1)}, f32[168,128]{1,0:T(8,128)S(1)}, u32[]{:S(2)}, u32[]{:S(2)}) collective-permute-start(f32[168,128]{1,0:T(8,128)S(1)} %get-tuple-element.35), channel_id=1, source_target_pairs={{0,12},{4,8},{8,4},{12,0},{16,28},{20,24},{24,20},{28,16},{1,13},{... | collective-permute-start | bytes 258056 | tf_op jit(solution)/shard_map/ppermute | solution.py:370
  23.4 4.9 %collective-permute-start.8 = (f32[168,128]{1,0:T(8,128)S(1)}, f32[168,128]{1,0:T(8,128)S(1)}, u32[]{:S(2)}, u32[]{:S(2)}) collective-permute-start(f32[168,128]{1,0:T(8,128)S(1)} %get-tuple-element.36), channel_id=1, source_target_pairs={{0,4},{4,0},{8,12},{12,8},{16,20},{20,16},{24,28},{28,24},{1,5},{5... | collective-permute-start | bytes 258056 | tf_op jit(solution)/shard_map/ppermute | solution.py:370
  31.7 12.2 %collective-permute-start.9 = (f32[152,128]{1,0:T(8,128)S(1)}, f32[152,128]{1,0:T(8,128)S(1)}, u32[]{:S(2)}, u32[]{:S(2)}) collective-permute-start(f32[152,128]{1,0:T(8,128)S(1)} %get-tuple-element.38), channel_id=1, source_target_pairs={{0,16},{4,20},{8,24},{12,28},{16,0},{20,4},{24,8},{28,12},{1,17},{... | collective-permute-start | bytes 233480 | tf_op jit(solution)/shard_map/ppermute | solution.py:370
  35.1 11.3 %collective-permute-start.10 = (f32[152,128]{1,0:T(8,128)S(1)}, f32[152,128]{1,0:T(8,128)S(1)}, u32[]{:S(2)}, u32[]{:S(2)}) collective-permute-start(f32[152,128]{1,0:T(8,128)S(1)} %get-tuple-element.39), channel_id=1, source_target_pairs={{0,20},{4,16},{8,28},{12,24},{16,4},{20,0},{24,12},{28,8},{1,21},{... | collective-permute-start | bytes 233480 | tf_op jit(solution)/shard_map/ppermute | solution.py:370
  35.1 12.7 %collective-permute-start.11 = (f32[152,128]{1,0:T(8,128)S(1)}, f32[152,128]{1,0:T(8,128)S(1)}, u32[]{:S(2)}, u32[]{:S(2)}) collective-permute-start(f32[152,128]{1,0:T(8,128)S(1)} %get-tuple-element.40), channel_id=1, source_target_pairs={{0,24},{4,28},{8,16},{12,20},{16,8},{20,12},{24,0},{28,4},{1,25},{... | collective-permute-start | bytes 233480 | tf_op jit(solution)/shard_map/ppermute | solution.py:370
  38.3 9.5 %collective-permute-start.12 = (f32[152,128]{1,0:T(8,128)S(1)}, f32[152,128]{1,0:T(8,128)S(1)}, u32[]{:S(2)}, u32[]{:S(2)}) collective-permute-start(f32[152,128]{1,0:T(8,128)S(1)} %get-tuple-element.41), channel_id=1, source_target_pairs={{0,28},{4,24},{8,20},{12,16},{16,12},{20,8},{24,4},{28,0},{1,29},{... | collective-permute-start | bytes 233480 | tf_op jit(solution)/shard_map/ppermute | solution.py:370
  39.9 7.9 %collective-permute-start.13 = (f32[152,128]{1,0:T(8,128)S(1)}, f32[152,128]{1,0:T(8,128)S(1)}, u32[]{:S(2)}, u32[]{:S(2)}) collective-permute-start(f32[152,128]{1,0:T(8,128)S(1)} %get-tuple-element.42), channel_id=1, source_target_pairs={{0,8},{4,12},{8,0},{12,4},{16,24},{20,28},{24,16},{28,20},{1,9},{5... | collective-permute-start | bytes 233480 | tf_op jit(solution)/shard_map/ppermute | solution.py:370
  43.9 5.4 %collective-permute-start.14 = (f32[152,128]{1,0:T(8,128)S(1)}, f32[152,128]{1,0:T(8,128)S(1)}, u32[]{:S(2)}, u32[]{:S(2)}) collective-permute-start(f32[152,128]{1,0:T(8,128)S(1)} %get-tuple-element.43), channel_id=1, source_target_pairs={{0,12},{4,8},{8,4},{12,0},{16,28},{20,24},{24,20},{28,16},{1,13},{... | collective-permute-start | bytes 233480 | tf_op jit(solution)/shard_map/ppermute | solution.py:370
  46.4 4.4 %collective-permute-start.15 = (f32[152,128]{1,0:T(8,128)S(1)}, f32[152,128]{1,0:T(8,128)S(1)}, u32[]{:S(2)}, u32[]{:S(2)}) collective-permute-start(f32[152,128]{1,0:T(8,128)S(1)} %get-tuple-element.44), channel_id=1, source_target_pairs={{0,4},{4,0},{8,12},{12,8},{16,20},{20,16},{24,28},{28,24},{1,5},{5... | collective-permute-start | bytes 233480 | tf_op jit(solution)/shard_map/ppermute | solution.py:370
  50.8 1.8 %collective-permute-start.16 = (f32[24,128]{1,0:T(8,128)S(1)}, f32[24,128]{1,0:T(8,128)S(1)}, u32[]{:S(2)}, u32[]{:S(2)}) collective-permute-start(f32[24,128]{1,0:T(8,128)S(1)} %get-tuple-element.45), channel_id=1, source_target_pairs={{0,1},{1,0},{2,3},{3,2},{4,5},{5,4},{6,7},{7,6},{8,9},{9,8},{10,11... | collective-permute-start | bytes 36872 | tf_op jit(solution)/shard_map/ppermute | solution.py:378
  50.9 3.2 %collective-permute-start.17 = (f32[24,128]{1,0:T(8,128)S(1)}, f32[24,128]{1,0:T(8,128)S(1)}, u32[]{:S(2)}, u32[]{:S(2)}) collective-permute-start(f32[24,128]{1,0:T(8,128)S(1)} %get-tuple-element.46), channel_id=1, source_target_pairs={{0,3},{1,2},{2,1},{3,0},{4,7},{5,6},{6,5},{7,4},{8,11},{9,10},{10,... | collective-permute-start | bytes 36872 | tf_op jit(solution)/shard_map/ppermute | solution.py:379

commit v5 on v4

--- a/solution.py
+++ b/solution.py
@@ -135,10 +135,24 @@
     rows_hop = faces + 4
     f32 = jnp.float32
 
-    order = [0]
-    for bit in reversed(range(owners.bit_length() - 1)):
-        order += range(1 << bit, 2 << bit)
-    slot_of = [order.index(d) for d in range(owners)]
+    half = owners // 2
+    near_group = range(2, half)
+
+    def sent(d, size):
+        if d < half:
+            return d, 0
+        e = d - half
+        return (half, (e - 2) * size) if e in near_group else (half + 1, e * size)
+
+    def arrived(d, size):
+        if d < half:
+            return d, 0
+        e = d - half
+        return (e, size) if e in near_group else (half + e, 0)
+
+    def pieces(refs, where, size):
+        found = [where(d, size) for d in range(owners)]
+        return [refs[which].at[pl.ds(base, size), :] for which, base in found]
 
     def position():
         me = lax.axis_index("gx")
@@ -190,8 +204,9 @@
     def pack_kernel(post, own, near, far, *outs):
         me, odd = position()
         below, above = sides(odd, near, far)
+        outs = pieces(outs, sent, rows_in)
         for d in range(owners):
-            out = outs[slot_of[d]]
+            out = outs[d]
             place = dynamic_place(me ^ d, odd, owners)
             here = pl.multiple_of(place * share, min(share, 8))
             for p in range(Q + 1):
@@ -214,10 +229,18 @@
                         n * PLANE : (n + 1) * PLANE
                     ]
 
+    def relay_kernel(*refs):
+        own, far, outs = refs[: half - 2], refs[half - 2], refs[half - 1 :]
+        size = own[0].shape[0]
+        for e in near_group:
+            outs[e - 2][pl.ds(0, size), :] = own[e - 2][...]
+            outs[e - 2][pl.ds(size, size), :] = far[pl.ds((e - 2) * size, size), :]
+
     def middle_kernel(*refs):
-        got = [refs[slot_of[d]] for d in range(owners)]
-        outs = [refs[owners + slot_of[d]] for d in range(owners)]
-        lattice, ready, table, sem = refs[2 * owners :]
+        inputs, outputs = half + 2, half + 2
+        got = pieces(refs[:inputs], arrived, rows_in)
+        outs = pieces(refs[inputs : inputs + outputs], sent, rows_out)
+        lattice, ready, table, sem = refs[inputs + outputs :]
         me, odd = position()
         place = dynamic_place(me, odd, owners)
         first, last = place == 0, place == owners - 1
@@ -306,8 +329,8 @@
                         ]
 
     def crossing_kernel(*refs):
-        got = [refs[slot_of[d]] for d in range(owners)]
-        near, far, up, down = refs[owners:]
+        got = pieces(refs[: half + 2], arrived, rows_out)
+        near, far, up, down = refs[half + 2 :]
         me, odd = position()
         for d in range(owners):
             place = dynamic_place(me ^ d, odd, owners)
@@ -329,7 +352,7 @@
         send_sides(odd, up, down, near, far)
 
     def unpack_kernel(*refs):
-        got, main = [refs[slot_of[d]] for d in range(owners)], refs[owners]
+        got, main = pieces(refs[: half + 2], arrived, rows_out), refs[half + 2]
         me, odd = position()
         for d in range(owners):
             place = dynamic_place(me ^ d, odd, owners)
@@ -365,11 +388,30 @@
             name=name,
         )(*inputs)
 
+    def part_shapes(size):
+        return (
+            (shape(size, LANES),) * half
+            + (shape((half - 2) * size, LANES), shape(2 * size, LANES))
+        )
+
+    def swapped(value, d):
+        return lax.ppermute(value, "gx", [(g, g ^ d) for g in range(owners)])
+
     def exchange(parts):
-        return [parts[0]] + [
-            lax.ppermute(parts[n], "gx", [(g, g ^ order[n]) for g in range(owners)])
-            for n in range(1, owners)
-        ]
+        size = parts[0].shape[0]
+        relayed = swapped(parts[half], half)
+        direct = swapped(parts[half + 1], half)
+        beside = swapped(parts[1], 1)
+        doubled = call(
+            relay_kernel,
+            "relay",
+            (shape(2 * size, LANES),) * (half - 2),
+            (*parts[2:half], relayed),
+            small,
+        )
+        doubled = [swapped(doubled[e - 2], e) for e in near_group]
+        last = swapped(direct[size:], 1)
+        return (parts[0], beside, *doubled, direct, last)
 
     def hop(near, far):
         ahead = [(s + 1) % slabs if s % 2 == 0 else (s - 1) % slabs for s in range(slabs)]
@@ -382,8 +424,8 @@
     def padded(count):
         return shape(count, 8 + WHOLE + 8, LANES)
 
+    small, large = 100_000, 4_000_000
     work = pltpu.VMEM((Q + 1, planes, NB, rows, LANES), f32)
-    small, large = 100_000, 4_000_000
 
     def shards(populations, solid_mask, slot_blocks, swap_slots):
         tiles = B * B * B // LANES
@@ -421,7 +463,7 @@
         parts = call(
             pack_kernel,
             "pack_planes",
-            (shape(rows_in, LANES),) * owners,
+            part_shapes(rows_in),
             (post, own, near, far),
             large,
         )
@@ -429,7 +471,7 @@
         parts = call(
             middle_kernel,
             "second_step",
-            (shape(rows_out, LANES),) * owners,
+            part_shapes(rows_out),
             got,
             large,
             (

time: 55.1 us -> 67 us (1.22)
  waiting for transfers between devices: 18 us -> 39.3 us
  starting transfers between devices: 30.3 us -> 20.7 us
    ppermute x14 -> x12, waiting for transfers between devices: 15.2 us -> 36.4 us  [swapped(): return lax.ppermute(value, 'gx', [(g, g ^ d) for g in range(owners)])]
    ppermute x14 -> x12, starting transfers between devices: 25.5 us -> 15.9 us  [swapped(): return lax.ppermute(value, 'gx', [(g, g ^ d) for g in range(owners)])]
    pallas_call x7 -> x9, Pallas kernels: 6.56 us -> 6.76 us  [call(): pl.pallas_call(kernel, out_shape=out_shape, in_specs=[spec] * len(inputs)...]
  transfers between devices with their start and end apart: 18 -> 16, of which waited for: 10 -> 8; matrix products, arithmetic and copies ran while one was open for 0% -> 0% of each run, Pallas kernels for 1% -> 1%
where the time goes in v5:
time: 67 us; the launch traced here: 66.9 us
  waiting for transfers between devices  39.3 us (59%)
  starting transfers between devices  20.7 us (31%)
  Pallas kernels  6.76 us (10%)
    ppermute x12, waiting for transfers between devices, swapped(): return lax.ppermute(value, 'gx', [(g, g ^ d) for g in range(owners)])  36.4 us
    ppermute x12, starting transfers between devices, swapped(): return lax.ppermute(value, 'gx', [(g, g ^ d) for g in range(owners)])  15.9 us
    pallas_call x9, Pallas kernels, call(): pl.pallas_call(kernel, out_shape=out_shape, in_specs=[spec] * len(inputs)...  6.76 us
    ppermute x2, starting transfers between devices, hop(): lax.ppermute(far, 'gy', list(enumerate(behind)))  4.15 us
    ppermute x2, waiting for transfers between devices, hop(): lax.ppermute(far, 'gy', list(enumerate(behind)))  2.87 us
  transfers between devices with their start and end apart: 16, of which 8 were waited for; matrix products, arithmetic and copies ran while one was open for 0% of the time, Pallas kernels for 1%

profile of v5, /device:TPU:0, one launch (start us, length us, event | category | flops | bytes accessed | tf_op | source)
XLA Modules:
  0.0 66.9 jit_solution(5014798783219071417)
XLA Ops:
  0.0 0.0 copy-start
  0.0 0.0 copy-start.1
  0.0 1.7 %edge_planes.1 = (f32[24,128]{1,0:T(8,128)}, f32[24,128]{1,0:T(8,128)}, f32[8,128]{1,0:T(8,128)}) custom-call(f32[19,64,128]{2,1,0:T(8,128)} %bitcast.26, s32[64,128]{1,0:T(8,128)} %bitcast.28, s32[1,2]{1,0:T(1,128)} %slots.1, s32[2,3]{1,0:T(2,128)} %bitcast.30), custom_call_target="tpu_custom_call" | custom-call | flops 100000 | bytes 100000 | tf_op jit(solution)/shard_map/edge_planes/pallas_call | solution.py:380
  1.7 0.5 collective-permute-start
  2.2 2.6 %collective-permute-start.1 = (f32[24,128]{1,0:T(8,128)}, f32[24,128]{1,0:T(8,128)S(1)}, u32[]{:S(2)}, u32[]{:S(2)}) collective-permute-start(f32[24,128]{1,0:T(8,128)} %get-tuple-element.28), channel_id=1, source_target_pairs={{0,3},{1,2},{2,1},{3,0},{4,7},{5,6},{6,5},{7,4},{8,11},{9,10},{10,... | collective-permute-start | bytes 36872 | tf_op jit(solution)/shard_map/ppermute | solution.py:421
  4.9 0.0 copy-done
  4.9 0.0 copy-done.1
  4.9 0.0 copy-start.2
  4.9 0.2 first_collision.1.post
  5.1 0.0 collective-permute-done.near
  5.1 1.4 %collective-permute-done.1.far = f32[24,128]{1,0:T(8,128)S(1)} collective-permute-done((f32[24,128]{1,0:T(8,128)}, f32[24,128]{1,0:T(8,128)S(1)}, u32[]{:S(2)}, u32[]{:S(2)}) %collective-permute-start.1) | collective-permute-done | bytes 12320 | tf_op jit(solution)/shard_map/ppermute | solution.py:421
  6.5 0.0 copy-done.2
  6.5 0.2 pack_planes.1
  6.7 2.8 %collective-permute-start.3 = (f32[336,128]{1,0:T(8,128)S(1)}, f32[336,128]{1,0:T(8,128)S(1)}, u32[]{:S(2)}, u32[]{:S(2)}) collective-permute-start(f32[336,128]{1,0:T(8,128)S(1)} %get-tuple-element.33), channel_id=1, source_target_pairs={{0,16},{4,20},{8,24},{12,28},{16,0},{20,4},{24,8},{28,12},{1,17},{... | collective-permute-start | bytes 516104 | tf_op jit(solution)/shard_map/ppermute | solution.py:398
  9.5 0.2 collective-permute-start.6
  9.7 12.5 %collective-permute-done.3.refs_2_ = f32[336,128]{1,0:T(8,128)S(1)} collective-permute-done((f32[336,128]{1,0:T(8,128)S(1)}, f32[336,128]{1,0:T(8,128)S(1)}, u32[]{:S(2)}, u32[]{:S(2)}) %collective-permute-start.3) | collective-permute-done | bytes 172064 | tf_op jit(solution)/shard_map/ppermute | solution.py:398
  22.2 0.5 collective-permute-start.4
  22.7 2.7 %collective-permute-start.5 = (f32[336,128]{1,0:T(8,128)S(1)}, f32[336,128]{1,0:T(8,128)S(1)}, u32[]{:S(2)}, u32[]{:S(2)}) collective-permute-start(f32[336,128]{1,0:T(8,128)S(1)} %get-tuple-element.35), channel_id=1, source_target_pairs={{0,12},{4,8},{8,4},{12,0},{16,28},{20,24},{24,20},{28,16},{1,13},{... | collective-permute-start | bytes 516104 | tf_op jit(solution)/shard_map/ppermute | solution.py:398
  25.4 0.3 collective-permute-start.2
  25.8 0.0 collective-permute-done.6.refs_4_
  25.8 1.8 %collective-permute-start.7 = (f32[168,128]{1,0:T(8,128)S(1)}, f32[168,128]{1,0:T(8,128)S(1)}, u32[]{:S(2)}, u32[]{:S(2)}) collective-permute-start(f32[168,128]{1,0:T(8,128)S(1)} %slice.8), channel_id=1, source_target_pairs={{0,4},{4,0},{8,12},{12,8},{16,20},{20,16},{24,28},{28,24},{1,5},{5... | collective-permute-start | bytes 258056 | tf_op jit(solution)/shard_map/ppermute | solution.py:398
  27.5 2.5 %collective-permute-done.2.refs_1_ = f32[168,128]{1,0:T(8,128)S(1)} collective-permute-done((f32[168,128]{1,0:T(8,128)S(1)}, f32[168,128]{1,0:T(8,128)S(1)}, u32[]{:S(2)}, u32[]{:S(2)}) %collective-permute-start.2) | collective-permute-done | bytes 86048 | tf_op jit(solution)/shard_map/ppermute | solution.py:398
  30.1 4.4 %collective-permute-done.7.refs_5_ = f32[168,128]{1,0:T(8,128)S(1)} collective-permute-done((f32[168,128]{1,0:T(8,128)S(1)}, f32[168,128]{1,0:T(8,128)S(1)}, u32[]{:S(2)}, u32[]{:S(2)}) %collective-permute-start.7) | collective-permute-done | bytes 86048 | tf_op jit(solution)/shard_map/ppermute | solution.py:398
  34.5 0.0 collective-permute-done.4.refs_2_
  34.5 0.0 collective-permute-done.5.refs_3_
  34.5 3.4 %second_step.1 = (f32[152,128]{1,0:T(8,128)S(1)}, f32[152,128]{1,0:T(8,128)S(1)}, f32[152,128]{1,0:T(8,128)S(1)}, f32[152,128]{1,0:T(8,128)S(1)}, f32[304,128]{1,0:T(8,128)S(1)}, /*index=5*/f32[304,128]{1,0:T(8,128)S(1)}) custom-call(f32[168,128]{1,0:T(8,128)S(1)} %get-tuple-element.29.refs_0_, f32[168,128]{1,0:T(8,128)S(1)} %collective-permute-done.2.refs_1_, ...), custom_call_target="tpu_custom_call" | custom-call | flops 4000000 | bytes 4000000 | tf_op jit(solution)/shard_map/second_step/pallas_call | solution.py:380
  38.0 2.4 %collective-permute-start.9 = (f32[304,128]{1,0:T(8,128)S(1)}, f32[304,128]{1,0:T(8,128)S(1)}, u32[]{:S(2)}, u32[]{:S(2)}) collective-permute-start(f32[304,128]{1,0:T(8,128)S(1)} %get-tuple-element.41), channel_id=1, source_target_pairs={{0,16},{4,20},{8,24},{12,28},{16,0},{20,4},{24,8},{28,12},{1,17},{... | collective-permute-start | bytes 466952 | tf_op jit(solution)/shard_map/ppermute | solution.py:398
  40.4 0.6 collective-permute-start.12
  41.0 11.0 %collective-permute-done.9.refs_2_ = f32[304,128]{1,0:T(8,128)S(1)} collective-permute-done((f32[304,128]{1,0:T(8,128)S(1)}, f32[304,128]{1,0:T(8,128)S(1)}, u32[]{:S(2)}, u32[]{:S(2)}) %collective-permute-start.9) | collective-permute-done | bytes 155680 | tf_op jit(solution)/shard_map/ppermute | solution.py:398
  52.0 0.1 collective-permute-start.10
  52.1 2.4 %collective-permute-start.11 = (f32[304,128]{1,0:T(8,128)S(1)}, f32[304,128]{1,0:T(8,128)S(1)}, u32[]{:S(2)}, u32[]{:S(2)}) collective-permute-start(f32[304,128]{1,0:T(8,128)S(1)} %get-tuple-element.43), channel_id=1, source_target_pairs={{0,12},{4,8},{8,4},{12,0},{16,28},{20,24},{24,20},{28,16},{1,13},{... | collective-permute-start | bytes 466952 | tf_op jit(solution)/shard_map/ppermute | solution.py:398
  54.5 1.0 %collective-permute-start.8 = (f32[152,128]{1,0:T(8,128)S(1)}, f32[152,128]{1,0:T(8,128)S(1)}, u32[]{:S(2)}, u32[]{:S(2)}) collective-permute-start(f32[152,128]{1,0:T(8,128)S(1)} %get-tuple-element.38), channel_id=1, source_target_pairs={{0,4},{4,0},{8,12},{12,8},{16,20},{20,16},{24,28},{28,24},{1,5},{5... | collective-permute-start | bytes 233480 | tf_op jit(solution)/shard_map/ppermute | solution.py:398
  55.6 0.0 collective-permute-done.12.refs_4_
  55.6 1.0 %collective-permute-start.13 = (f32[152,128]{1,0:T(8,128)S(1)}, f32[152,128]{1,0:T(8,128)S(1)}, u32[]{:S(2)}, u32[]{:S(2)}) collective-permute-start(f32[152,128]{1,0:T(8,128)S(1)} %slice.9), channel_id=1, source_target_pairs={{0,4},{4,0},{8,12},{12,8},{16,20},{20,16},{24,28},{28,24},{1,5},{5... | collective-permute-start | bytes 233480 | tf_op jit(solution)/shard_map/ppermute | solution.py:398
  56.6 5.1 %collective-permute-done.8.refs_1_ = f32[152,128]{1,0:T(8,128)S(1)} collective-permute-done((f32[152,128]{1,0:T(8,128)S(1)}, f32[152,128]{1,0:T(8,128)S(1)}, u32[]{:S(2)}, u32[]{:S(2)}) %collective-permute-start.8) | collective-permute-done | bytes 77856 | tf_op jit(solution)/shard_map/ppermute | solution.py:398
  61.7 0.8 %collective-permute-done.13.refs_5_ = f32[152,128]{1,0:T(8,128)S(1)} collective-permute-done((f32[152,128]{1,0:T(8,128)S(1)}, f32[152,128]{1,0:T(8,128)S(1)}, u32[]{:S(2)}, u32[]{:S(2)}) %collective-permute-start.13) | collective-permute-done | bytes 77856 | tf_op jit(solution)/shard_map/ppermute | solution.py:398
  62.5 0.0 collective-permute-done.10.refs_2_
  62.5 0.0 collective-permute-done.11.refs_3_
  62.5 0.2 crossing_planes.1
  62.7 0.1 collective-permute-start.14
  62.8 1.5 %collective-permute-start.15 = (f32[24,128]{1,0:T(8,128)S(1)}, f32[24,128]{1,0:T(8,128)S(1)}, u32[]{:S(2)}, u32[]{:S(2)}) collective-permute-start(f32[24,128]{1,0:T(8,128)S(1)} %get-tuple-element.46), channel_id=1, source_target_pairs={{0,3},{1,2},{2,1},{3,0},{4,7},{5,6},{6,5},{7,4},{8,11},{9,10},{10,... | collective-permute-start | bytes 36872 | tf_op jit(solution)/shard_map/ppermute | solution.py:421
  64.3 0.1 unpack_planes.1.main
  64.5 0.0 collective-permute-done.14.near
  64.5 1.5 %collective-permute-done.15.far = f32[24,128]{1,0:T(8,128)S(1)} collective-permute-done((f32[24,128]{1,0:T(8,128)S(1)}, f32[24,128]{1,0:T(8,128)S(1)}, u32[]{:S(2)}, u32[]{:S(2)}) %collective-permute-start.15) | collective-permute-done | bytes 12320 | tf_op jit(solution)/shard_map/ppermute | solution.py:421
  66.0 0.9 %finish.1 = f32[1216,128]{1,0:T(8,128)} custom-call(f32[19,80,128]{2,1,0:T(8,128)S(1)} %unpack_planes.1.main, f32[24,128]{1,0:T(8,128)S(1)} %collective-permute-done.14.near, f32[24,128]{1,0:T(8,128)S(1)} %collective-permute-done.15.far), custom_call_target="tpu_custom_call" | custom-call | flops 100000 | bytes 100000 | tf_op jit(solution)/shard_map/finish/pallas_call | solution.py:380
  (4 shorter events, 0.1 us)
Async XLA Ops:
  0.0 4.9 %copy-start = (f32[1,2,19,4096]{3,1,2,0:T(2,128)S(1)}, f32[1,2,19,4096]{3,1,2,0:T(2,128)}, u32[]{:S(2)}) copy-start(f32[1,2,19,4096]{3,1,2,0:T(2,128)} %param.4) | copy-start | bytes 1867780
  0.0 4.9 %copy-start.1 = (s32[1,2,4096]{2,1,0:T(2,128)S(1)}, s32[1,2,4096]{2,1,0:T(2,128)}, u32[]{:S(2)}) copy-start(s32[1,2,4096]{2,1,0:T(2,128)} %param.5) | copy-start | bytes 98308
  1.7 3.4 %collective-permute-start = (f32[24,128]{1,0:T(8,128)}, f32[24,128]{1,0:T(8,128)S(1)}, u32[]{:S(2)}, u32[]{:S(2)}) collective-permute-start(f32[24,128]{1,0:T(8,128)} %get-tuple-element.27), channel_id=1, source_target_pairs={{0,1},{1,0},{2,3},{3,2},{4,5},{5,4},{6,7},{7,6},{8,9},{9,8},{10,11... | collective-permute-start | bytes 36872 | tf_op jit(solution)/shard_map/ppermute | solution.py:420
  2.2 4.2 %collective-permute-start.1 = (f32[24,128]{1,0:T(8,128)}, f32[24,128]{1,0:T(8,128)S(1)}, u32[]{:S(2)}, u32[]{:S(2)}) collective-permute-start(f32[24,128]{1,0:T(8,128)} %get-tuple-element.28), channel_id=1, source_target_pairs={{0,3},{1,2},{2,1},{3,0},{4,7},{5,6},{6,5},{7,4},{8,11},{9,10},{10,... | collective-permute-start | bytes 36872 | tf_op jit(solution)/shard_map/ppermute | solution.py:421
  4.9 1.6 %copy-start.2 = (f32[8,128]{1,0:T(8,128)S(1)}, f32[8,128]{1,0:T(8,128)}, u32[]{:S(2)}) copy-start(f32[8,128]{1,0:T(8,128)} %get-tuple-element.26.own) | copy-start | bytes 12292
  6.7 15.5 %collective-permute-start.3 = (f32[336,128]{1,0:T(8,128)S(1)}, f32[336,128]{1,0:T(8,128)S(1)}, u32[]{:S(2)}, u32[]{:S(2)}) collective-permute-start(f32[336,128]{1,0:T(8,128)S(1)} %get-tuple-element.33), channel_id=1, source_target_pairs={{0,16},{4,20},{8,24},{12,28},{16,0},{20,4},{24,8},{28,12},{1,17},{... | collective-permute-start | bytes 516104 | tf_op jit(solution)/shard_map/ppermute | solution.py:398
  9.5 16.3 %collective-permute-start.6 = (f32[336,128]{1,0:T(8,128)S(1)}, f32[336,128]{1,0:T(8,128)S(1)}, u32[]{:S(2)}, u32[]{:S(2)}) collective-permute-start(f32[336,128]{1,0:T(8,128)S(1)} %get-tuple-element.36), channel_id=1, source_target_pairs={{0,16},{4,20},{8,24},{12,28},{16,0},{20,4},{24,8},{28,12},{1,17},{... | collective-permute-start | bytes 516104 | tf_op jit(solution)/shard_map/ppermute | solution.py:398
  22.2 12.3 %collective-permute-start.4 = (f32[336,128]{1,0:T(8,128)S(1)}, f32[336,128]{1,0:T(8,128)S(1)}, u32[]{:S(2)}, u32[]{:S(2)}) collective-permute-start(f32[336,128]{1,0:T(8,128)S(1)} %get-tuple-element.34), channel_id=1, source_target_pairs={{0,8},{4,12},{8,0},{12,4},{16,24},{20,28},{24,16},{28,20},{1,9},{5... | collective-permute-start | bytes 516104 | tf_op jit(solution)/shard_map/ppermute | solution.py:398
  22.7 11.8 %collective-permute-start.5 = (f32[336,128]{1,0:T(8,128)S(1)}, f32[336,128]{1,0:T(8,128)S(1)}, u32[]{:S(2)}, u32[]{:S(2)}) collective-permute-start(f32[336,128]{1,0:T(8,128)S(1)} %get-tuple-element.35), channel_id=1, source_target_pairs={{0,12},{4,8},{8,4},{12,0},{16,28},{20,24},{24,20},{28,16},{1,13},{... | collective-permute-start | bytes 516104 | tf_op jit(solution)/shard_map/ppermute | solution.py:398
  25.4 4.6 %collective-permute-start.2 = (f32[168,128]{1,0:T(8,128)S(1)}, f32[168,128]{1,0:T(8,128)S(1)}, u32[]{:S(2)}, u32[]{:S(2)}) collective-permute-start(f32[168,128]{1,0:T(8,128)S(1)} %get-tuple-element.30), channel_id=1, source_target_pairs={{0,4},{4,0},{8,12},{12,8},{16,20},{20,16},{24,28},{28,24},{1,5},{5... | collective-permute-start | bytes 258056 | tf_op jit(solution)/shard_map/ppermute | solution.py:398
  25.8 8.8 %collective-permute-start.7 = (f32[168,128]{1,0:T(8,128)S(1)}, f32[168,128]{1,0:T(8,128)S(1)}, u32[]{:S(2)}, u32[]{:S(2)}) collective-permute-start(f32[168,128]{1,0:T(8,128)S(1)} %slice.8), channel_id=1, source_target_pairs={{0,4},{4,0},{8,12},{12,8},{16,20},{20,16},{24,28},{28,24},{1,5},{5... | collective-permute-start | bytes 258056 | tf_op jit(solution)/shard_map/ppermute | solution.py:398
  38.0 14.0 %collective-permute-start.9 = (f32[304,128]{1,0:T(8,128)S(1)}, f32[304,128]{1,0:T(8,128)S(1)}, u32[]{:S(2)}, u32[]{:S(2)}) collective-permute-start(f32[304,128]{1,0:T(8,128)S(1)} %get-tuple-element.41), channel_id=1, source_target_pairs={{0,16},{4,20},{8,24},{12,28},{16,0},{20,4},{24,8},{28,12},{1,17},{... | collective-permute-start | bytes 466952 | tf_op jit(solution)/shard_map/ppermute | solution.py:398
  40.4 15.2 %collective-permute-start.12 = (f32[304,128]{1,0:T(8,128)S(1)}, f32[304,128]{1,0:T(8,128)S(1)}, u32[]{:S(2)}, u32[]{:S(2)}) collective-permute-start(f32[304,128]{1,0:T(8,128)S(1)} %get-tuple-element.44), channel_id=1, source_target_pairs={{0,16},{4,20},{8,24},{12,28},{16,0},{20,4},{24,8},{28,12},{1,17},{... | collective-permute-start | bytes 466952 | tf_op jit(solution)/shard_map/ppermute | solution.py:398
  52.0 10.5 %collective-permute-start.10 = (f32[304,128]{1,0:T(8,128)S(1)}, f32[304,128]{1,0:T(8,128)S(1)}, u32[]{:S(2)}, u32[]{:S(2)}) collective-permute-start(f32[304,128]{1,0:T(8,128)S(1)} %get-tuple-element.42), channel_id=1, source_target_pairs={{0,8},{4,12},{8,0},{12,4},{16,24},{20,28},{24,16},{28,20},{1,9},{5... | collective-permute-start | bytes 466952 | tf_op jit(solution)/shard_map/ppermute | solution.py:398
  52.1 10.4 %collective-permute-start.11 = (f32[304,128]{1,0:T(8,128)S(1)}, f32[304,128]{1,0:T(8,128)S(1)}, u32[]{:S(2)}, u32[]{:S(2)}) collective-permute-start(f32[304,128]{1,0:T(8,128)S(1)} %get-tuple-element.43), channel_id=1, source_target_pairs={{0,12},{4,8},{8,4},{12,0},{16,28},{20,24},{24,20},{28,16},{1,13},{... | collective-permute-start | bytes 466952 | tf_op jit(solution)/shard_map/ppermute | solution.py:398
  54.5 7.2 %collective-permute-start.8 = (f32[152,128]{1,0:T(8,128)S(1)}, f32[152,128]{1,0:T(8,128)S(1)}, u32[]{:S(2)}, u32[]{:S(2)}) collective-permute-start(f32[152,128]{1,0:T(8,128)S(1)} %get-tuple-element.38), channel_id=1, source_target_pairs={{0,4},{4,0},{8,12},{12,8},{16,20},{20,16},{24,28},{28,24},{1,5},{5... | collective-permute-start | bytes 233480 | tf_op jit(solution)/shard_map/ppermute | solution.py:398
  55.6 6.9 %collective-permute-start.13 = (f32[152,128]{1,0:T(8,128)S(1)}, f32[152,128]{1,0:T(8,128)S(1)}, u32[]{:S(2)}, u32[]{:S(2)}) collective-permute-start(f32[152,128]{1,0:T(8,128)S(1)} %slice.9), channel_id=1, source_target_pairs={{0,4},{4,0},{8,12},{12,8},{16,20},{20,16},{24,28},{28,24},{1,5},{5... | collective-permute-start | bytes 233480 | tf_op jit(solution)/shard_map/ppermute | solution.py:398
  62.7 1.7 %collective-permute-start.14 = (f32[24,128]{1,0:T(8,128)S(1)}, f32[24,128]{1,0:T(8,128)S(1)}, u32[]{:S(2)}, u32[]{:S(2)}) collective-permute-start(f32[24,128]{1,0:T(8,128)S(1)} %get-tuple-element.45), channel_id=1, source_target_pairs={{0,1},{1,0},{2,3},{3,2},{4,5},{5,4},{6,7},{7,6},{8,9},{9,8},{10,11... | collective-permute-start | bytes 36872 | tf_op jit(solution)/shard_map/ppermute | solution.py:420
  62.8 3.2 %collective-permute-start.15 = (f32[24,128]{1,0:T(8,128)S(1)}, f32[24,128]{1,0:T(8,128)S(1)}, u32[]{:S(2)}, u32[]{:S(2)}) collective-permute-start(f32[24,128]{1,0:T(8,128)S(1)} %get-tuple-element.46), channel_id=1, source_target_pairs={{0,3},{1,2},{2,1},{3,0},{4,7},{5,6},{6,5},{7,4},{8,11},{9,10},{10,... | collective-permute-start | bytes 36872 | tf_op jit(solution)/shard_map/ppermute | solution.py:421

commit v6 on v5

--- a/solution.py
+++ b/solution.py
@@ -136,19 +136,15 @@
     f32 = jnp.float32
 
     half = owners // 2
-    near_group = range(2, half)
+    near_group = range(1, half)
 
     def sent(d, size):
-        if d < half:
-            return d, 0
-        e = d - half
-        return (half, (e - 2) * size) if e in near_group else (half + 1, e * size)
+        return (d, 0) if d < half else (half, (d - half) * size)
 
     def arrived(d, size):
         if d < half:
             return d, 0
-        e = d - half
-        return (e, size) if e in near_group else (half + e, 0)
+        return (half, 0) if d == half else (d - half, size)
 
     def pieces(refs, where, size):
         found = [where(d, size) for d in range(owners)]
@@ -230,14 +226,14 @@
                     ]
 
     def relay_kernel(*refs):
-        own, far, outs = refs[: half - 2], refs[half - 2], refs[half - 1 :]
+        own, far, outs = refs[: half - 1], refs[half - 1], refs[half:]
         size = own[0].shape[0]
         for e in near_group:
-            outs[e - 2][pl.ds(0, size), :] = own[e - 2][...]
-            outs[e - 2][pl.ds(size, size), :] = far[pl.ds((e - 2) * size, size), :]
+            outs[e - 1][pl.ds(0, size), :] = own[e - 1][...]
+            outs[e - 1][pl.ds(size, size), :] = far[pl.ds(e * size, size), :]
 
     def middle_kernel(*refs):
-        inputs, outputs = half + 2, half + 2
+        inputs, outputs = half + 1, half + 1
         got = pieces(refs[:inputs], arrived, rows_in)
         outs = pieces(refs[inputs : inputs + outputs], sent, rows_out)
         lattice, ready, table, sem = refs[inputs + outputs :]
@@ -329,8 +325,8 @@
                         ]
 
     def crossing_kernel(*refs):
-        got = pieces(refs[: half + 2], arrived, rows_out)
-        near, far, up, down = refs[half + 2 :]
+        got = pieces(refs[: half + 1], arrived, rows_out)
+        near, far, up, down = refs[half + 1 :]
         me, odd = position()
         for d in range(owners):
             place = dynamic_place(me ^ d, odd, owners)
@@ -352,7 +348,7 @@
         send_sides(odd, up, down, near, far)
 
     def unpack_kernel(*refs):
-        got, main = pieces(refs[: half + 2], arrived, rows_out), refs[half + 2]
+        got, main = pieces(refs[: half + 1], arrived, rows_out), refs[half + 1]
         me, odd = position()
         for d in range(owners):
             place = dynamic_place(me ^ d, odd, owners)
@@ -389,29 +385,22 @@
         )(*inputs)
 
     def part_shapes(size):
-        return (
-            (shape(size, LANES),) * half
-            + (shape((half - 2) * size, LANES), shape(2 * size, LANES))
-        )
+        return (shape(size, LANES),) * half + (shape(half * size, LANES),)
 
     def swapped(value, d):
         return lax.ppermute(value, "gx", [(g, g ^ d) for g in range(owners)])
 
     def exchange(parts):
         size = parts[0].shape[0]
-        relayed = swapped(parts[half], half)
-        direct = swapped(parts[half + 1], half)
-        beside = swapped(parts[1], 1)
+        across = swapped(parts[half], half)
         doubled = call(
             relay_kernel,
             "relay",
-            (shape(2 * size, LANES),) * (half - 2),
-            (*parts[2:half], relayed),
+            (shape(2 * size, LANES),) * (half - 1),
+            (*parts[1:half], across),
             small,
         )
-        doubled = [swapped(doubled[e - 2], e) for e in near_group]
-        last = swapped(direct[size:], 1)
-        return (parts[0], beside, *doubled, direct, last)
+        return (parts[0], *(swapped(doubled[e - 1], e) for e in near_group), across)
 
     def hop(near, far):
         ahead = [(s + 1) % slabs if s % 2 == 0 else (s - 1) % slabs for s in range(slabs)]

time: 67 us -> 70.6 us (1.054)
  waiting for transfers between devices: 39.3 us -> 46.3 us
  starting transfers between devices: 20.7 us -> 17.5 us
    ppermute x12 -> x8, waiting for transfers between devices: 36.4 us -> 43.5 us  [swapped(): return lax.ppermute(value, 'gx', [(g, g ^ d) for g in range(owners)])]
    ppermute x12 -> x8, starting transfers between devices: 15.9 us -> 12.7 us  [swapped(): return lax.ppermute(value, 'gx', [(g, g ^ d) for g in range(owners)])]
  transfers between devices with their start and end apart: 16 -> 12, of which waited for: 8 -> 10; matrix products, arithmetic and copies ran while one was open for 0% -> 0% of each run, Pallas kernels for 1% -> 1%
where the time goes in v6:
time: 70.6 us; the launch traced here: 70.5 us
  waiting for transfers between devices  46.3 us (66%)
  starting transfers between devices  17.5 us (25%)
  Pallas kernels  6.63 us (9%)
    ppermute x8, waiting for transfers between devices, swapped(): return lax.ppermute(value, 'gx', [(g, g ^ d) for g in range(owners)])  43.5 us
    ppermute x8, starting transfers between devices, swapped(): return lax.ppermute(value, 'gx', [(g, g ^ d) for g in range(owners)])  12.7 us
    pallas_call x9, Pallas kernels, call(): pl.pallas_call(kernel, out_shape=out_shape, in_specs=[spec] * len(inputs)...  6.63 us
    ppermute x2, starting transfers between devices, hop(): lax.ppermute(far, 'gy', list(enumerate(behind)))  4.22 us
    ppermute x2, waiting for transfers between devices, hop(): lax.ppermute(far, 'gy', list(enumerate(behind)))  2.8 us
  transfers between devices with their start and end apart: 12, of which 10 were waited for; matrix products, arithmetic and copies ran while one was open for 0% of the time, Pallas kernels for 1%

profile of v6, /device:TPU:0, one launch (start us, length us, event | category | flops | bytes accessed | tf_op | source)
XLA Modules:
  0.0 70.5 jit_solution(15709882990677445647)
XLA Ops:
  0.0 0.0 copy-start
  0.0 0.0 copy-start.1
  0.0 1.7 %edge_planes.1 = (f32[24,128]{1,0:T(8,128)}, f32[24,128]{1,0:T(8,128)}, f32[8,128]{1,0:T(8,128)}) custom-call(f32[19,64,128]{2,1,0:T(8,128)} %bitcast.26, s32[64,128]{1,0:T(8,128)} %bitcast.28, s32[1,2]{1,0:T(1,128)} %slots.1, s32[2,3]{1,0:T(2,128)} %bitcast.30), custom_call_target="tpu_custom_call" | custom-call | flops 100000 | bytes 100000 | tf_op jit(solution)/shard_map/edge_planes/pallas_call | solution.py:376
  1.7 0.5 collective-permute-start
  2.2 2.6 %collective-permute-start.1 = (f32[24,128]{1,0:T(8,128)}, f32[24,128]{1,0:T(8,128)S(1)}, u32[]{:S(2)}, u32[]{:S(2)}) collective-permute-start(f32[24,128]{1,0:T(8,128)} %get-tuple-element.28), channel_id=1, source_target_pairs={{0,3},{1,2},{2,1},{3,0},{4,7},{5,6},{6,5},{7,4},{8,11},{9,10},{10,... | collective-permute-start | bytes 36872 | tf_op jit(solution)/shard_map/ppermute | solution.py:410
  4.9 0.0 copy-done
  4.9 0.0 copy-done.1
  4.9 0.0 copy-start.2
  4.9 0.2 first_collision.1.post
  5.1 0.0 collective-permute-done.near
  5.1 1.4 %collective-permute-done.1.far = f32[24,128]{1,0:T(8,128)S(1)} collective-permute-done((f32[24,128]{1,0:T(8,128)}, f32[24,128]{1,0:T(8,128)S(1)}, u32[]{:S(2)}, u32[]{:S(2)}) %collective-permute-start.1) | collective-permute-done | bytes 12320 | tf_op jit(solution)/shard_map/ppermute | solution.py:410
  6.5 0.0 copy-done.2
  6.5 0.2 pack_planes.1
  6.7 2.8 %collective-permute-start.2 = (f32[672,128]{1,0:T(8,128)S(1)}, f32[672,128]{1,0:T(8,128)S(1)}, u32[]{:S(2)}, u32[]{:S(2)}) collective-permute-start(f32[672,128]{1,0:T(8,128)S(1)} %get-tuple-element.33), channel_id=1, source_target_pairs={{0,16},{4,20},{8,24},{12,28},{16,0},{20,4},{24,8},{28,12},{1,17},{... | collective-permute-start | bytes 1032200 | tf_op jit(solution)/shard_map/ppermute | solution.py:391
  9.5 16.0 %collective-permute-done.2.refs_3_.refs_4_ = f32[672,128]{1,0:T(8,128)S(1)} collective-permute-done((f32[672,128]{1,0:T(8,128)S(1)}, f32[672,128]{1,0:T(8,128)S(1)}, u32[]{:S(2)}, u32[]{:S(2)}) %collective-permute-start.2) | collective-permute-done | bytes 344096 | tf_op jit(solution)/shard_map/ppermute | solution.py:391
  25.6 1.6 %collective-permute-start.3 = (f32[336,128]{1,0:T(8,128)S(1)}, f32[336,128]{1,0:T(8,128)S(1)}, u32[]{:S(2)}, u32[]{:S(2)}) collective-permute-start(f32[336,128]{1,0:T(8,128)S(1)} %get-tuple-element.34), channel_id=1, source_target_pairs={{0,4},{4,0},{8,12},{12,8},{16,20},{20,16},{24,28},{28,24},{1,5},{5... | collective-permute-start | bytes 516104 | tf_op jit(solution)/shard_map/ppermute | solution.py:391
  27.2 0.7 collective-permute-start.4
  27.9 1.2 %collective-permute-start.5 = (f32[336,128]{1,0:T(8,128)S(1)}, f32[336,128]{1,0:T(8,128)S(1)}, u32[]{:S(2)}, u32[]{:S(2)}) collective-permute-start(f32[336,128]{1,0:T(8,128)S(1)} %get-tuple-element.36), channel_id=1, source_target_pairs={{0,12},{4,8},{8,4},{12,0},{16,28},{20,24},{24,20},{28,16},{1,13},{... | collective-permute-start | bytes 516104 | tf_op jit(solution)/shard_map/ppermute | solution.py:391
  29.1 2.9 %collective-permute-done.3.refs_1_ = f32[336,128]{1,0:T(8,128)S(1)} collective-permute-done((f32[336,128]{1,0:T(8,128)S(1)}, f32[336,128]{1,0:T(8,128)S(1)}, u32[]{:S(2)}, u32[]{:S(2)}) %collective-permute-start.3) | collective-permute-done | bytes 172064 | tf_op jit(solution)/shard_map/ppermute | solution.py:391
  32.1 2.5 %collective-permute-done.4.refs_2_ = f32[336,128]{1,0:T(8,128)S(1)} collective-permute-done((f32[336,128]{1,0:T(8,128)S(1)}, f32[336,128]{1,0:T(8,128)S(1)}, u32[]{:S(2)}, u32[]{:S(2)}) %collective-permute-start.4) | collective-permute-done | bytes 172064 | tf_op jit(solution)/shard_map/ppermute | solution.py:391
  34.5 2.1 %collective-permute-done.5.refs_3_ = f32[336,128]{1,0:T(8,128)S(1)} collective-permute-done((f32[336,128]{1,0:T(8,128)S(1)}, f32[336,128]{1,0:T(8,128)S(1)}, u32[]{:S(2)}, u32[]{:S(2)}) %collective-permute-start.5) | collective-permute-done | bytes 172064 | tf_op jit(solution)/shard_map/ppermute | solution.py:391
  36.6 3.4 %second_step.1 = (f32[152,128]{1,0:T(8,128)S(1)}, f32[152,128]{1,0:T(8,128)S(1)}, f32[152,128]{1,0:T(8,128)S(1)}, f32[152,128]{1,0:T(8,128)S(1)}, f32[608,128]{1,0:T(8,128)S(1)}) custom-call(f32[168,128]{1,0:T(8,128)S(1)} %get-tuple-element.29.refs_0_, f32[336,128]{1,0:T(8,128)S(1)} %collective-permute-done.3.refs_1_, ...), custom_call_target="tpu_custom_call" | custom-call | flops 4000000 | bytes 4000000 | tf_op jit(solution)/shard_map/second_step/pallas_call | solution.py:376
  40.0 2.7 %collective-permute-start.6 = (f32[608,128]{1,0:T(8,128)S(1)}, f32[608,128]{1,0:T(8,128)S(1)}, u32[]{:S(2)}, u32[]{:S(2)}) collective-permute-start(f32[608,128]{1,0:T(8,128)S(1)} %get-tuple-element.41), channel_id=1, source_target_pairs={{0,16},{4,20},{8,24},{12,28},{16,0},{20,4},{24,8},{28,12},{1,17},{... | collective-permute-start | bytes 933896 | tf_op jit(solution)/shard_map/ppermute | solution.py:391
  42.8 13.4 %collective-permute-done.6.refs_3_.refs_4_ = f32[608,128]{1,0:T(8,128)S(1)} collective-permute-done((f32[608,128]{1,0:T(8,128)S(1)}, f32[608,128]{1,0:T(8,128)S(1)}, u32[]{:S(2)}, u32[]{:S(2)}) %collective-permute-start.6) | collective-permute-done | bytes 311328 | tf_op jit(solution)/shard_map/ppermute | solution.py:391
  56.2 1.6 %collective-permute-start.7 = (f32[304,128]{1,0:T(8,128)S(1)}, f32[304,128]{1,0:T(8,128)S(1)}, u32[]{:S(2)}, u32[]{:S(2)}) collective-permute-start(f32[304,128]{1,0:T(8,128)S(1)} %get-tuple-element.42), channel_id=1, source_target_pairs={{0,4},{4,0},{8,12},{12,8},{16,20},{20,16},{24,28},{28,24},{1,5},{5... | collective-permute-start | bytes 466952 | tf_op jit(solution)/shard_map/ppermute | solution.py:391
  57.8 0.7 collective-permute-start.8
  58.5 1.3 %collective-permute-start.9 = (f32[304,128]{1,0:T(8,128)S(1)}, f32[304,128]{1,0:T(8,128)S(1)}, u32[]{:S(2)}, u32[]{:S(2)}) collective-permute-start(f32[304,128]{1,0:T(8,128)S(1)} %get-tuple-element.44), channel_id=1, source_target_pairs={{0,12},{4,8},{8,4},{12,0},{16,28},{20,24},{24,20},{28,16},{1,13},{... | collective-permute-start | bytes 466952 | tf_op jit(solution)/shard_map/ppermute | solution.py:391
  59.8 1.9 %collective-permute-done.7.refs_1_ = f32[304,128]{1,0:T(8,128)S(1)} collective-permute-done((f32[304,128]{1,0:T(8,128)S(1)}, f32[304,128]{1,0:T(8,128)S(1)}, u32[]{:S(2)}, u32[]{:S(2)}) %collective-permute-start.7) | collective-permute-done | bytes 155680 | tf_op jit(solution)/shard_map/ppermute | solution.py:391
  61.7 2.5 %collective-permute-done.8.refs_2_ = f32[304,128]{1,0:T(8,128)S(1)} collective-permute-done((f32[304,128]{1,0:T(8,128)S(1)}, f32[304,128]{1,0:T(8,128)S(1)}, u32[]{:S(2)}, u32[]{:S(2)}) %collective-permute-start.8) | collective-permute-done | bytes 155680 | tf_op jit(solution)/shard_map/ppermute | solution.py:391
  64.2 2.1 %collective-permute-done.9.refs_3_ = f32[304,128]{1,0:T(8,128)S(1)} collective-permute-done((f32[304,128]{1,0:T(8,128)S(1)}, f32[304,128]{1,0:T(8,128)S(1)}, u32[]{:S(2)}, u32[]{:S(2)}) %collective-permute-start.9) | collective-permute-done | bytes 155680 | tf_op jit(solution)/shard_map/ppermute | solution.py:391
  66.3 0.1 collective-permute-start.10
  66.4 1.6 %collective-permute-start.11 = (f32[24,128]{1,0:T(8,128)S(1)}, f32[24,128]{1,0:T(8,128)S(1)}, u32[]{:S(2)}, u32[]{:S(2)}) collective-permute-start(f32[24,128]{1,0:T(8,128)S(1)} %get-tuple-element.46), channel_id=1, source_target_pairs={{0,3},{1,2},{2,1},{3,0},{4,7},{5,6},{6,5},{7,4},{8,11},{9,10},{10,... | collective-permute-start | bytes 36872 | tf_op jit(solution)/shard_map/ppermute | solution.py:410
  68.0 0.1 unpack_planes.1.main
  68.1 0.0 collective-permute-done.10.near
  68.1 1.4 %collective-permute-done.11.far = f32[24,128]{1,0:T(8,128)S(1)} collective-permute-done((f32[24,128]{1,0:T(8,128)S(1)}, f32[24,128]{1,0:T(8,128)S(1)}, u32[]{:S(2)}, u32[]{:S(2)}) %collective-permute-start.11) | collective-permute-done | bytes 12320 | tf_op jit(solution)/shard_map/ppermute | solution.py:410
  69.6 0.9 %finish.1 = f32[1216,128]{1,0:T(8,128)} custom-call(f32[19,80,128]{2,1,0:T(8,128)S(1)} %unpack_planes.1.main, f32[24,128]{1,0:T(8,128)S(1)} %collective-permute-done.10.near, f32[24,128]{1,0:T(8,128)S(1)} %collective-permute-done.11.far), custom_call_target="tpu_custom_call" | custom-call | flops 100000 | bytes 100000 | tf_op jit(solution)/shard_map/finish/pallas_call | solution.py:376
  (3 shorter events, 0.1 us)
Async XLA Ops:
  0.0 4.9 %copy-start = (f32[1,2,19,4096]{3,1,2,0:T(2,128)S(1)}, f32[1,2,19,4096]{3,1,2,0:T(2,128)}, u32[]{:S(2)}) copy-start(f32[1,2,19,4096]{3,1,2,0:T(2,128)} %param.4) | copy-start | bytes 1867780
  0.0 4.9 %copy-start.1 = (s32[1,2,4096]{2,1,0:T(2,128)S(1)}, s32[1,2,4096]{2,1,0:T(2,128)}, u32[]{:S(2)}) copy-start(s32[1,2,4096]{2,1,0:T(2,128)} %param.5) | copy-start | bytes 98308
  1.7 3.4 %collective-permute-start = (f32[24,128]{1,0:T(8,128)}, f32[24,128]{1,0:T(8,128)S(1)}, u32[]{:S(2)}, u32[]{:S(2)}) collective-permute-start(f32[24,128]{1,0:T(8,128)} %get-tuple-element.27), channel_id=1, source_target_pairs={{0,1},{1,0},{2,3},{3,2},{4,5},{5,4},{6,7},{7,6},{8,9},{9,8},{10,11... | collective-permute-start | bytes 36872 | tf_op jit(solution)/shard_map/ppermute | solution.py:409
  2.2 4.2 %collective-permute-start.1 = (f32[24,128]{1,0:T(8,128)}, f32[24,128]{1,0:T(8,128)S(1)}, u32[]{:S(2)}, u32[]{:S(2)}) collective-permute-start(f32[24,128]{1,0:T(8,128)} %get-tuple-element.28), channel_id=1, source_target_pairs={{0,3},{1,2},{2,1},{3,0},{4,7},{5,6},{6,5},{7,4},{8,11},{9,10},{10,... | collective-permute-start | bytes 36872 | tf_op jit(solution)/shard_map/ppermute | solution.py:410
  4.9 1.6 %copy-start.2 = (f32[8,128]{1,0:T(8,128)S(1)}, f32[8,128]{1,0:T(8,128)}, u32[]{:S(2)}) copy-start(f32[8,128]{1,0:T(8,128)} %get-tuple-element.26.own) | copy-start | bytes 12292
  6.7 18.9 %collective-permute-start.2 = (f32[672,128]{1,0:T(8,128)S(1)}, f32[672,128]{1,0:T(8,128)S(1)}, u32[]{:S(2)}, u32[]{:S(2)}) collective-permute-start(f32[672,128]{1,0:T(8,128)S(1)} %get-tuple-element.33), channel_id=1, source_target_pairs={{0,16},{4,20},{8,24},{12,28},{16,0},{20,4},{24,8},{28,12},{1,17},{... | collective-permute-start | bytes 1032200 | tf_op jit(solution)/shard_map/ppermute | solution.py:391
  25.6 6.5 %collective-permute-start.3 = (f32[336,128]{1,0:T(8,128)S(1)}, f32[336,128]{1,0:T(8,128)S(1)}, u32[]{:S(2)}, u32[]{:S(2)}) collective-permute-start(f32[336,128]{1,0:T(8,128)S(1)} %get-tuple-element.34), channel_id=1, source_target_pairs={{0,4},{4,0},{8,12},{12,8},{16,20},{20,16},{24,28},{28,24},{1,5},{5... | collective-permute-start | bytes 516104 | tf_op jit(solution)/shard_map/ppermute | solution.py:391
  27.2 7.3 %collective-permute-start.4 = (f32[336,128]{1,0:T(8,128)S(1)}, f32[336,128]{1,0:T(8,128)S(1)}, u32[]{:S(2)}, u32[]{:S(2)}) collective-permute-start(f32[336,128]{1,0:T(8,128)S(1)} %get-tuple-element.35), channel_id=1, source_target_pairs={{0,8},{4,12},{8,0},{12,4},{16,24},{20,28},{24,16},{28,20},{1,9},{5... | collective-permute-start | bytes 516104 | tf_op jit(solution)/shard_map/ppermute | solution.py:391
  27.9 8.7 %collective-permute-start.5 = (f32[336,128]{1,0:T(8,128)S(1)}, f32[336,128]{1,0:T(8,128)S(1)}, u32[]{:S(2)}, u32[]{:S(2)}) collective-permute-start(f32[336,128]{1,0:T(8,128)S(1)} %get-tuple-element.36), channel_id=1, source_target_pairs={{0,12},{4,8},{8,4},{12,0},{16,28},{20,24},{24,20},{28,16},{1,13},{... | collective-permute-start | bytes 516104 | tf_op jit(solution)/shard_map/ppermute | solution.py:391
  40.0 16.2 %collective-permute-start.6 = (f32[608,128]{1,0:T(8,128)S(1)}, f32[608,128]{1,0:T(8,128)S(1)}, u32[]{:S(2)}, u32[]{:S(2)}) collective-permute-start(f32[608,128]{1,0:T(8,128)S(1)} %get-tuple-element.41), channel_id=1, source_target_pairs={{0,16},{4,20},{8,24},{12,28},{16,0},{20,4},{24,8},{28,12},{1,17},{... | collective-permute-start | bytes 933896 | tf_op jit(solution)/shard_map/ppermute | solution.py:391
  56.2 5.5 %collective-permute-start.7 = (f32[304,128]{1,0:T(8,128)S(1)}, f32[304,128]{1,0:T(8,128)S(1)}, u32[]{:S(2)}, u32[]{:S(2)}) collective-permute-start(f32[304,128]{1,0:T(8,128)S(1)} %get-tuple-element.42), channel_id=1, source_target_pairs={{0,4},{4,0},{8,12},{12,8},{16,20},{20,16},{24,28},{28,24},{1,5},{5... | collective-permute-start | bytes 466952 | tf_op jit(solution)/shard_map/ppermute | solution.py:391
  57.8 6.4 %collective-permute-start.8 = (f32[304,128]{1,0:T(8,128)S(1)}, f32[304,128]{1,0:T(8,128)S(1)}, u32[]{:S(2)}, u32[]{:S(2)}) collective-permute-start(f32[304,128]{1,0:T(8,128)S(1)} %get-tuple-element.43), channel_id=1, source_target_pairs={{0,8},{4,12},{8,0},{12,4},{16,24},{20,28},{24,16},{28,20},{1,9},{5... | collective-permute-start | bytes 466952 | tf_op jit(solution)/shard_map/ppermute | solution.py:391
  58.5 7.8 %collective-permute-start.9 = (f32[304,128]{1,0:T(8,128)S(1)}, f32[304,128]{1,0:T(8,128)S(1)}, u32[]{:S(2)}, u32[]{:S(2)}) collective-permute-start(f32[304,128]{1,0:T(8,128)S(1)} %get-tuple-element.44), channel_id=1, source_target_pairs={{0,12},{4,8},{8,4},{12,0},{16,28},{20,24},{24,20},{28,16},{1,13},{... | collective-permute-start | bytes 466952 | tf_op jit(solution)/shard_map/ppermute | solution.py:391
  66.3 1.8 %collective-permute-start.10 = (f32[24,128]{1,0:T(8,128)S(1)}, f32[24,128]{1,0:T(8,128)S(1)}, u32[]{:S(2)}, u32[]{:S(2)}) collective-permute-start(f32[24,128]{1,0:T(8,128)S(1)} %get-tuple-element.45), channel_id=1, source_target_pairs={{0,1},{1,0},{2,3},{3,2},{4,5},{5,4},{6,7},{7,6},{8,9},{9,8},{10,11... | collective-permute-start | bytes 36872 | tf_op jit(solution)/shard_map/ppermute | solution.py:409
  66.4 3.2 %collective-permute-start.11 = (f32[24,128]{1,0:T(8,128)S(1)}, f32[24,128]{1,0:T(8,128)S(1)}, u32[]{:S(2)}, u32[]{:S(2)}) collective-permute-start(f32[24,128]{1,0:T(8,128)S(1)} %get-tuple-element.46), channel_id=1, source_target_pairs={{0,3},{1,2},{2,1},{3,0},{4,7},{5,6},{6,5},{7,4},{8,11},{9,10},{10,... | collective-permute-start | bytes 36872 | tf_op jit(solution)/shard_map/ppermute | solution.py:410

commit v7 on v4

--- a/solution.py
+++ b/solution.py
@@ -10,6 +10,7 @@
 LANES = 128
 PLANE_ROWS = B * B // LANES
 PLANE = PLANE_ROWS * NB
+FLIGHT = 5
 WHOLE = B * PLANE
 
 VELOCITIES = (
@@ -37,6 +38,9 @@
 Q = len(VELOCITIES)
 UPWARD = tuple(p for p in range(Q) if VELOCITIES[p][0] == 1)
 DOWNWARD = tuple(p for p in range(Q) if VELOCITIES[p][0] == -1)
+
+LEVEL = tuple(p for p in range(Q) if VELOCITIES[p][0] == 0)
+SLOPED = UPWARD + DOWNWARD
 
 VMEM_SPEC = pl.BlockSpec(memory_space=pltpu.VMEM)
 
@@ -128,17 +132,32 @@
     planes = B // owners
     share = planes * PLANE
     rows = owners * PLANE_ROWS
-    head = (Q + 1) * share
-    rows_in = head + 8
-    rows_out = Q * share
+    level_in = LEVEL + (Q,)
+    head = len(SLOPED) * share
+    sizes_in = (len(level_in) * share, head + 8)
+    sizes_out = (len(LEVEL) * share, head)
+    half = owners // 2
     faces = len(UPWARD) * PLANE
     rows_hop = faces + 4
     f32 = jnp.float32
 
-    order = [0]
-    for bit in reversed(range(owners.bit_length() - 1)):
-        order += range(1 << bit, 2 << bit)
-    slot_of = [order.index(d) for d in range(owners)]
+    def spot(p):
+        if p in SLOPED:
+            return 1, SLOPED.index(p) * share
+        return 0, level_in.index(p) * share
+
+    def pieces(whole, level, sloped, sizes):
+        pairs = [
+            (ref.at[pl.ds(0, sizes[0]), :], ref.at[pl.ds(sizes[0], sizes[1]), :]) for ref in whole
+        ]
+        return pairs + list(zip(level, sloped))
+
+    def cut(refs, lengths):
+        groups, start = [], 0
+        for length in lengths:
+            groups.append(refs[start : start + length])
+            start += length
+        return groups + [refs[start:]]
 
     def position():
         me = lax.axis_index("gx")
@@ -190,13 +209,17 @@
     def pack_kernel(post, own, near, far, *outs):
         me, odd = position()
         below, above = sides(odd, near, far)
+        outs = pieces(outs, (), (), sizes_in)
         for d in range(owners):
-            out = outs[slot_of[d]]
             place = dynamic_place(me ^ d, odd, owners)
             here = pl.multiple_of(place * share, min(share, 8))
             for p in range(Q + 1):
                 cx = VELOCITIES[p][0] if p < Q else 0
-                out[pl.ds(p * share, share), :] = post[p, pl.ds(8 + here - cx * PLANE, share), :]
+                part, row = spot(p)
+                outs[d][part][pl.ds(row, share), :] = post[
+                    p, pl.ds(8 + here - cx * PLANE, share), :
+                ]
+            out = outs[d][1]
             out[pl.ds(head, 2), :] = own[0:2]
             out[pl.ds(head + 2, 2), :] = below[faces : faces + 2]
             out[pl.ds(head + 4, 2), :] = above[faces : faces + 2]
@@ -205,24 +228,25 @@
             @pl.when(place == 0)
             def _():
                 for n, p in enumerate(UPWARD):
-                    out[pl.ds(p * share, PLANE), :] = below[n * PLANE : (n + 1) * PLANE]
+                    out[pl.ds(spot(p)[1], PLANE), :] = below[n * PLANE : (n + 1) * PLANE]
 
             @pl.when(place == owners - 1)
             def _():
                 for n, p in enumerate(DOWNWARD):
-                    out[pl.ds(p * share + share - PLANE, PLANE), :] = above[
+                    out[pl.ds(spot(p)[1] + share - PLANE, PLANE), :] = above[
                         n * PLANE : (n + 1) * PLANE
                     ]
 
     def middle_kernel(*refs):
-        got = [refs[slot_of[d]] for d in range(owners)]
-        outs = [refs[owners + slot_of[d]] for d in range(owners)]
-        lattice, ready, table, sem = refs[2 * owners :]
+        got, *groups, rest = cut(refs, (owners, half, half, half))
+        got = pieces(got, (), (), sizes_in)
+        outs = pieces(*groups, sizes_out)
+        lattice, ready, table, sem = rest
         me, odd = position()
         place = dynamic_place(me, odd, owners)
         first, last = place == 0, place == owners - 1
         copies = [
-            pltpu.make_async_copy(got[d].at[pl.ds(head, 8), :], table.at[d], sem.at[d])
+            pltpu.make_async_copy(got[d][1].at[pl.ds(head, 8), :], table.at[d], sem.at[d])
             for d in range(owners)
         ]
         for copy in copies:
@@ -261,8 +285,9 @@
                             kz, y = at_below
                         if cx == -1 and i == planes - 1:
                             kz, y = at_above
-                        lattice[p, i, kz, pl.ds(y, PLANE_ROWS), :] = got[d][
-                            pl.ds(p * share + i * PLANE + t, PLANE_ROWS, stride=NB), :
+                        part, row = spot(p)
+                        lattice[p, i, kz, pl.ds(y, PLANE_ROWS), :] = got[d][part][
+                            pl.ds(row + i * PLANE + t, PLANE_ROWS, stride=NB), :
                         ]
         lane = lax.broadcasted_iota(jnp.int32, (rows, LANES), 1)
 
@@ -301,13 +326,15 @@
                             kz, y = at_above
                         if cx == -1 and i == 0:
                             kz, y = at_below
-                        outs[d][pl.ds(p * share + i * PLANE + t, PLANE_ROWS, stride=NB), :] = ready[
+                        part, row = spot(p)
+                        outs[d][part][pl.ds(row + i * PLANE + t, PLANE_ROWS, stride=NB), :] = ready[
                             p, i, kz, pl.ds(y, PLANE_ROWS), :
                         ]
 
     def crossing_kernel(*refs):
-        got = [refs[slot_of[d]] for d in range(owners)]
-        near, far, up, down = refs[owners:]
+        whole, sloped, rest = cut(refs, (half, half))
+        got = pieces(whole, (None,) * half, sloped, sizes_out)
+        near, far, up, down = rest
         me, odd = position()
         for d in range(owners):
             place = dynamic_place(me ^ d, odd, owners)
@@ -315,29 +342,33 @@
             @pl.when(place == owners - 1)
             def _():
                 for n, p in enumerate(UPWARD):
-                    up[pl.ds(n * PLANE, PLANE), :] = got[d][
-                        pl.ds(p * share + share - PLANE, PLANE), :
+                    up[pl.ds(n * PLANE, PLANE), :] = got[d][1][
+                        pl.ds(spot(p)[1] + share - PLANE, PLANE), :
                     ]
 
             @pl.when(place == 0)
             def _():
                 for n, p in enumerate(DOWNWARD):
-                    down[pl.ds(n * PLANE, PLANE), :] = got[d][pl.ds(p * share, PLANE), :]
+                    down[pl.ds(n * PLANE, PLANE), :] = got[d][1][
+                        pl.ds(spot(p)[1], PLANE), :
+                    ]
 
         for out in (up, down):
             out[pl.ds(faces, 4), :] = jnp.zeros((4, LANES), f32)
         send_sides(odd, up, down, near, far)
 
     def unpack_kernel(*refs):
-        got, main = [refs[slot_of[d]] for d in range(owners)], refs[owners]
+        *groups, (main,) = cut(refs, (half,) * 3)
+        got = pieces(*groups, sizes_out)
         me, odd = position()
         for d in range(owners):
             place = dynamic_place(me ^ d, odd, owners)
             here = pl.multiple_of(place * share, min(share, 8))
             for p in range(Q):
                 cx = VELOCITIES[p][0]
-                main[p, pl.ds(8 + here + cx * PLANE, share), :] = got[d][
-                    pl.ds(p * share, share), :
+                part, row = spot(p)
+                main[p, pl.ds(8 + here + cx * PLANE, share), :] = got[d][part][
+                    pl.ds(row, share), :
                 ]
 
     def finish_kernel(main, near, far, out):
@@ -366,10 +397,15 @@
         )(*inputs)
 
     def exchange(parts):
-        return [parts[0]] + [
-            lax.ppermute(parts[n], "gx", [(g, g ^ order[n]) for g in range(owners)])
-            for n in range(1, owners)
-        ]
+        done = []
+        for n, (part, d) in enumerate(parts):
+            if n >= FLIGHT:
+                done[n - FLIGHT], part = lax.optimization_barrier((done[n - FLIGHT], part))
+            done.append(lax.ppermute(part, "gx", [(g, g ^ d) for g in range(owners)]))
+        return done
+
+    def several(size, count=half):
+        return (shape(size, LANES),) * count
 
     def hop(near, far):
         ahead = [(s + 1) % slabs if s % 2 == 0 else (s - 1) % slabs for s in range(slabs)]
@@ -421,15 +457,17 @@
         parts = call(
             pack_kernel,
             "pack_planes",
-            (shape(rows_in, LANES),) * owners,
+            several(sum(sizes_in), owners),
             (post, own, near, far),
             large,
         )
-        got = exchange(parts)
+        lines = [*range(1, 3), half, half + 1, *range(3, half), *range(half + 2, owners)]
+        got = exchange([(parts[d], d) for d in lines])
+        got = [parts[0]] + [got[lines.index(d)] for d in range(1, owners)]
         parts = call(
             middle_kernel,
             "second_step",
-            (shape(rows_out, LANES),) * owners,
+            several(sum(sizes_out)) + several(sizes_out[0]) + several(sizes_out[1]),
             got,
             large,
             (
@@ -439,17 +477,25 @@
                 pltpu.SemaphoreType.DMA((owners,)),
             ),
         )
-        home = exchange(parts)
+        whole, level, sloped, _ = cut(parts, (half,) * 3)
+        lines = [(whole[d], d) for d in range(1, half)]
+        lines += [(part, d) for d, part in enumerate(sloped, half)]
+        lines += [(part, d) for d, part in enumerate(level, half)]
+        home = exchange(lines)
+        own, sloped, level = whole[0], home[half - 1 :], home[half - 1 + half :]
+        whole, sloped = [own] + home[: half - 1], sloped[:half]
         near, far = call(
             crossing_kernel,
             "crossing_planes",
-            (shape(rows_hop, LANES),) * 2,
-            home,
+            several(rows_hop, 2),
+            (*whole, *sloped),
             small,
             (pltpu.VMEM((rows_hop, LANES), f32),) * 2,
         )
         near, far = hop(near, far)
-        main = call(unpack_kernel, "unpack_planes", padded(Q), home, large)
+        main = call(
+            unpack_kernel, "unpack_planes", padded(Q), (*whole, *level, *sloped), large
+        )
         out = call(
             finish_kernel, "finish", shape(Q * WHOLE, LANES), (main, near, far), small
         )

time: 55.1 us -> 55.9 us (1.015)
  starting transfers between devices: 30.3 us -> 34.5 us
  waiting for transfers between devices: 18 us -> 14.5 us
    ppermute x14 -> x18, starting transfers between devices: 25.5 us -> 29.9 us  [exchange(): done.append(lax.ppermute(part, 'gx', [(g, g ^ d) for g in range(owners)]))]
    ppermute x14 -> x18, waiting for transfers between devices: 15.2 us -> 13.1 us  [exchange(): done.append(lax.ppermute(part, 'gx', [(g, g ^ d) for g in range(owners)]))]
    ppermute x2, waiting for transfers between devices: 2.8 us -> 1.36 us  [hop(): lax.ppermute(far, 'gy', list(enumerate(behind)))]
  transfers between devices with their start and end apart: 18 -> 22, of which waited for: 10 -> 7; matrix products, arithmetic and copies ran while one was open for 0% -> 0% of each run, Pallas kernels for 1% -> 1%
where the time goes in v7:
time: 55.9 us; the launch traced here: 55.7 us
  starting transfers between devices  34.5 us (62%)
  waiting for transfers between devices  14.5 us (26%)
  Pallas kernels  6.57 us (12%)
    ppermute x18, starting transfers between devices, exchange(): done.append(lax.ppermute(part, 'gx', [(g, g ^ d) for g in range(owners)]))  29.9 us
    ppermute x18, waiting for transfers between devices, exchange(): done.append(lax.ppermute(part, 'gx', [(g, g ^ d) for g in range(owners)]))  13.1 us
    pallas_call x7, Pallas kernels, call(): pl.pallas_call(kernel, out_shape=out_shape, in_specs=[spec] * len(inputs)...  6.57 us
    ppermute x2, starting transfers between devices, hop(): lax.ppermute(far, 'gy', list(enumerate(behind)))  4.07 us
    ppermute x2, waiting for transfers between devices, hop(): lax.ppermute(far, 'gy', list(enumerate(behind)))  1.36 us
  transfers between devices with their start and end apart: 22, of which 7 were waited for; matrix products, arithmetic and copies ran while one was open for 0% of the time, Pallas kernels for 1%

profile of v7, /device:TPU:0, one launch (start us, length us, event | category | flops | bytes accessed | tf_op | source)
XLA Modules:
  0.0 55.7 jit_solution(17506654282157339353)
XLA Ops:
  0.0 1.7 %edge_planes.1 = (f32[24,128]{1,0:T(8,128)}, f32[24,128]{1,0:T(8,128)}, f32[8,128]{1,0:T(8,128)}) custom-call(f32[19,64,128]{2,1,0:T(8,128)} %bitcast.26, s32[64,128]{1,0:T(8,128)} %bitcast.28, s32[1,2]{1,0:T(1,128)} %slots.1, s32[2,3]{1,0:T(2,128)} %bitcast.30), custom_call_target="tpu_custom_call" | custom-call | flops 100000 | bytes 100000 | tf_op jit(solution)/shard_map/edge_planes/pallas_call | solution.py:388
  1.7 0.5 collective-permute-start
  2.2 2.6 %collective-permute-start.1 = (f32[24,128]{1,0:T(8,128)}, f32[24,128]{1,0:T(8,128)S(1)}, u32[]{:S(2)}, u32[]{:S(2)}) collective-permute-start(f32[24,128]{1,0:T(8,128)} %get-tuple-element.48), channel_id=1, source_target_pairs={{0,3},{1,2},{2,1},{3,0},{4,7},{5,6},{6,5},{7,4},{8,11},{9,10},{10,... | collective-permute-start | bytes 36872 | tf_op jit(solution)/shard_map/ppermute | solution.py:415
  4.9 0.2 first_collision.1.post
  5.1 0.0 collective-permute-done.near
  5.1 1.4 %collective-permute-done.1.far = f32[24,128]{1,0:T(8,128)S(1)} collective-permute-done((f32[24,128]{1,0:T(8,128)}, f32[24,128]{1,0:T(8,128)S(1)}, u32[]{:S(2)}, u32[]{:S(2)}) %collective-permute-start.1) | collective-permute-done | bytes 12320 | tf_op jit(solution)/shard_map/ppermute | solution.py:415
  6.5 0.2 pack_planes.1
  6.7 1.8 %collective-permute-start.2 = (f32[168,128]{1,0:T(8,128)S(1)}, f32[168,128]{1,0:T(8,128)S(1)}, u32[]{:S(2)}, u32[]{:S(2)}) collective-permute-start(f32[168,128]{1,0:T(8,128)S(1)} %get-tuple-element.50), channel_id=1, source_target_pairs={{0,4},{4,0},{8,12},{12,8},{16,20},{20,16},{24,28},{28,24},{1,5},{5... | collective-permute-start | bytes 258056 | tf_op jit(solution)/shard_map/ppermute | solution.py:404
  8.4 1.6 %collective-permute-start.3 = (f32[168,128]{1,0:T(8,128)S(1)}, f32[168,128]{1,0:T(8,128)S(1)}, u32[]{:S(2)}, u32[]{:S(2)}) collective-permute-start(f32[168,128]{1,0:T(8,128)S(1)} %get-tuple-element.53), channel_id=1, source_target_pairs={{0,8},{4,12},{8,0},{12,4},{16,24},{20,28},{24,16},{28,20},{1,9},{5... | collective-permute-start | bytes 258056 | tf_op jit(solution)/shard_map/ppermute | solution.py:404
  10.0 0.2 collective-permute-start.4
  10.2 2.8 %collective-permute-start.5 = (f32[168,128]{1,0:T(8,128)S(1)}, f32[168,128]{1,0:T(8,128)S(1)}, u32[]{:S(2)}, u32[]{:S(2)}) collective-permute-start(f32[168,128]{1,0:T(8,128)S(1)} %get-tuple-element.57), channel_id=1, source_target_pairs={{0,16},{4,20},{8,24},{12,28},{16,0},{20,4},{24,8},{28,12},{1,17},{... | collective-permute-start | bytes 258056 | tf_op jit(solution)/shard_map/ppermute | solution.py:404
  13.0 1.3 %collective-permute-start.6 = (f32[168,128]{1,0:T(8,128)S(1)}, f32[168,128]{1,0:T(8,128)S(1)}, u32[]{:S(2)}, u32[]{:S(2)}) collective-permute-start(f32[168,128]{1,0:T(8,128)S(1)} %get-tuple-element.58), channel_id=1, source_target_pairs={{0,20},{4,16},{8,28},{12,24},{16,4},{20,0},{24,12},{28,8},{1,21},{... | collective-permute-start | bytes 258056 | tf_op jit(solution)/shard_map/ppermute | solution.py:404
  14.3 0.0 collective-permute-done.2.refs_1_
  14.3 3.6 %collective-permute-start.7 = (f32[168,128]{1,0:T(8,128)S(1)}, f32[168,128]{1,0:T(8,128)S(1)}, u32[]{:S(2)}, u32[]{:S(2)}) collective-permute-start(f32[168,128]{1,0:T(8,128)S(1)} %get-tuple-element.59), channel_id=1, source_target_pairs={{0,24},{4,28},{8,16},{12,20},{16,8},{20,12},{24,0},{28,4},{1,25},{... | collective-permute-start | bytes 258056 | tf_op jit(solution)/shard_map/ppermute | solution.py:404
  17.9 0.0 collective-permute-done.3.refs_2_
  17.9 0.0 collective-permute-start.8
  17.9 0.0 collective-permute-done.4.refs_3_
  17.9 0.0 collective-permute-done.5.refs_4_
  17.9 8.6 %collective-permute-done.6.refs_5_ = f32[168,128]{1,0:T(8,128)S(1)} collective-permute-done((f32[168,128]{1,0:T(8,128)S(1)}, f32[168,128]{1,0:T(8,128)S(1)}, u32[]{:S(2)}, u32[]{:S(2)}) %collective-permute-start.6) | collective-permute-done | bytes 86048 | tf_op jit(solution)/shard_map/ppermute | solution.py:404
  26.5 0.0 collective-permute-done.7.refs_6_
  26.5 0.0 collective-permute-done.8.refs_7_
  26.5 3.4 %second_step.1 = (f32[152,128]{1,0:T(8,128)S(1)}, f32[152,128]{1,0:T(8,128)S(1)}, f32[152,128]{1,0:T(8,128)S(1)}, f32[152,128]{1,0:T(8,128)S(1)}, f32[72,128]{1,...) custom-call(f32[168,128]{1,0:T(8,128)S(1)} %get-tuple-element.49.ref, ...), custom_call_target="tpu_custom_call" | custom-call | flops 4000000 | bytes 4000000 | tf_op jit(solution)/shard_map/second_step/pallas_call | solution.py:388
  30.0 1.3 %collective-permute-start.9 = (f32[152,128]{1,0:T(8,128)S(1)}, f32[152,128]{1,0:T(8,128)S(1)}, u32[]{:S(2)}, u32[]{:S(2)}) collective-permute-start(f32[152,128]{1,0:T(8,128)S(1)} %get-tuple-element.62), channel_id=1, source_target_pairs={{0,4},{4,0},{8,12},{12,8},{16,20},{20,16},{24,28},{28,24},{1,5},{5... | collective-permute-start | bytes 233480 | tf_op jit(solution)/shard_map/ppermute | solution.py:404
  31.3 3.7 %collective-permute-start.10 = (f32[152,128]{1,0:T(8,128)S(1)}, f32[152,128]{1,0:T(8,128)S(1)}, u32[]{:S(2)}, u32[]{:S(2)}) collective-permute-start(f32[152,128]{1,0:T(8,128)S(1)} %get-tuple-element.65), channel_id=1, source_target_pairs={{0,8},{4,12},{8,0},{12,4},{16,24},{20,28},{24,16},{28,20},{1,9},{5... | collective-permute-start | bytes 233480 | tf_op jit(solution)/shard_map/ppermute | solution.py:404
  35.0 0.2 collective-permute-start.11
  35.2 3.7 %collective-permute-start.13 = (f32[80,128]{1,0:T(8,128)S(1)}, f32[80,128]{1,0:T(8,128)S(1)}, u32[]{:S(2)}, u32[]{:S(2)}) collective-permute-start(f32[80,128]{1,0:T(8,128)S(1)} %get-tuple-element.72), channel_id=1, source_target_pairs={{0,16},{4,20},{8,24},{12,28},{16,0},{20,4},{24,8},{28,12},{1,17},{... | collective-permute-start | bytes 122888 | tf_op jit(solution)/shard_map/ppermute | solution.py:404
  38.9 0.0 collective-permute-start.15
  38.9 0.0 collective-permute-done.9.refs_1_
  38.9 2.4 %collective-permute-start.17 = (f32[80,128]{1,0:T(8,128)S(1)}, f32[80,128]{1,0:T(8,128)S(1)}, u32[]{:S(2)}, u32[]{:S(2)}) collective-permute-start(f32[80,128]{1,0:T(8,128)S(1)} %get-tuple-element.78), channel_id=1, source_target_pairs={{0,24},{4,28},{8,16},{12,20},{16,8},{20,12},{24,0},{28,4},{1,25},{... | collective-permute-start | bytes 122888 | tf_op jit(solution)/shard_map/ppermute | solution.py:404
  41.3 0.0 collective-permute-done.10.refs_2_
  41.3 2.4 %collective-permute-start.19 = (f32[80,128]{1,0:T(8,128)S(1)}, f32[80,128]{1,0:T(8,128)S(1)}, u32[]{:S(2)}, u32[]{:S(2)}) collective-permute-start(f32[80,128]{1,0:T(8,128)S(1)} %get-tuple-element.84), channel_id=1, source_target_pairs={{0,28},{4,24},{8,20},{12,16},{16,12},{20,8},{24,4},{28,0},{1,29},{... | collective-permute-start | bytes 122888 | tf_op jit(solution)/shard_map/ppermute | solution.py:404
  43.6 0.0 collective-permute-done.13.refs_8_.refs_4_
  43.6 1.1 %collective-permute-start.14 = (f32[72,128]{1,0:T(8,128)S(1)}, f32[72,128]{1,0:T(8,128)S(1)}, u32[]{:S(2)}, u32[]{:S(2)}) collective-permute-start(f32[72,128]{1,0:T(8,128)S(1)} %get-tuple-element.74), channel_id=1, source_target_pairs={{0,20},{4,16},{8,28},{12,24},{16,4},{20,0},{24,12},{28,8},{1,21},{... | collective-permute-start | bytes 110600 | tf_op jit(solution)/shard_map/ppermute | solution.py:404
  44.7 1.7 %collective-permute-done.15.refs_9_.refs_5_ = f32[80,128]{1,0:T(8,128)S(1)} collective-permute-done((f32[80,128]{1,0:T(8,128)S(1)}, f32[80,128]{1,0:T(8,128)S(1)}, u32[]{:S(2)}, u32[]{:S(2)}) %collective-permute-start.15) | collective-permute-done | bytes 40992 | tf_op jit(solution)/shard_map/ppermute | solution.py:404
  46.5 0.7 %collective-permute-start.16 = (f32[72,128]{1,0:T(8,128)S(1)}, f32[72,128]{1,0:T(8,128)S(1)}, u32[]{:S(2)}, u32[]{:S(2)}) collective-permute-start(f32[72,128]{1,0:T(8,128)S(1)} %get-tuple-element.77), channel_id=1, source_target_pairs={{0,24},{4,28},{8,16},{12,20},{16,8},{20,12},{24,0},{28,4},{1,25},{... | collective-permute-start | bytes 110600 | tf_op jit(solution)/shard_map/ppermute | solution.py:404
  47.1 0.0 collective-permute-done.11.refs_3_
  47.1 0.9 %collective-permute-start.12 = (f32[72,128]{1,0:T(8,128)S(1)}, f32[72,128]{1,0:T(8,128)S(1)}, u32[]{:S(2)}, u32[]{:S(2)}) collective-permute-start(f32[72,128]{1,0:T(8,128)S(1)} %get-tuple-element.71), channel_id=1, source_target_pairs={{0,16},{4,20},{8,24},{12,28},{16,0},{20,4},{24,8},{28,12},{1,17},{... | collective-permute-start | bytes 110600 | tf_op jit(solution)/shard_map/ppermute | solution.py:404
  48.0 0.0 collective-permute-done.17.refs_10_.refs_6_
  48.0 2.4 %collective-permute-start.18 = (f32[72,128]{1,0:T(8,128)S(1)}, f32[72,128]{1,0:T(8,128)S(1)}, u32[]{:S(2)}, u32[]{:S(2)}) collective-permute-start(f32[72,128]{1,0:T(8,128)S(1)} %get-tuple-element.80), channel_id=1, source_target_pairs={{0,28},{4,24},{8,20},{12,16},{16,12},{20,8},{24,4},{28,0},{1,29},{... | collective-permute-start | bytes 110600 | tf_op jit(solution)/shard_map/ppermute | solution.py:404
  50.4 0.1 collective-permute-start.20
  50.5 0.1 collective-permute-done.14.refs_5_
  50.6 1.5 %collective-permute-start.21 = (f32[24,128]{1,0:T(8,128)S(1)}, f32[24,128]{1,0:T(8,128)S(1)}, u32[]{:S(2)}, u32[]{:S(2)}) collective-permute-start(f32[24,128]{1,0:T(8,128)S(1)} %get-tuple-element.86), channel_id=1, source_target_pairs={{0,3},{1,2},{2,1},{3,0},{4,7},{5,6},{6,5},{7,4},{8,11},{9,10},{10,... | collective-permute-start | bytes 36872 | tf_op jit(solution)/shard_map/ppermute | solution.py:415
  52.1 0.2 collective-permute-done.16.refs_6_
  52.3 0.5 collective-permute-done.12.refs_4_
  52.8 1.9 %collective-permute-done.18.refs_7_ = f32[72,128]{1,0:T(8,128)S(1)} collective-permute-done((f32[72,128]{1,0:T(8,128)S(1)}, f32[72,128]{1,0:T(8,128)S(1)}, u32[]{:S(2)}, u32[]{:S(2)}) %collective-permute-start.18) | collective-permute-done | bytes 36896 | tf_op jit(solution)/shard_map/ppermute | solution.py:404
  54.7 0.1 unpack_planes.1.main
  54.8 0.0 collective-permute-done.20.near
  54.8 0.9 %finish.1 = f32[1216,128]{1,0:T(8,128)} custom-call(f32[19,80,128]{2,1,0:T(8,128)S(1)} %unpack_planes.1.main, f32[24,128]{1,0:T(8,128)S(1)} %collective-permute-done.20.near, f32[24,128]{1,0:T(8,128)S(1)} %collective-permute-done.21.far), custom_call_target="tpu_custom_call" | custom-call | flops 100000 | bytes 100000 | tf_op jit(solution)/shard_map/finish/pallas_call | solution.py:388
  (9 shorter events, 0.0 us)
Async XLA Ops:
  0.0 4.9 %copy-start = (f32[1,2,19,4096]{3,1,2,0:T(2,128)S(1)}, f32[1,2,19,4096]{3,1,2,0:T(2,128)}, u32[]{:S(2)}) copy-start(f32[1,2,19,4096]{3,1,2,0:T(2,128)} %param.4) | copy-start | bytes 1867780
  0.0 4.9 %copy-start.1 = (s32[1,2,4096]{2,1,0:T(2,128)S(1)}, s32[1,2,4096]{2,1,0:T(2,128)}, u32[]{:S(2)}) copy-start(s32[1,2,4096]{2,1,0:T(2,128)} %param.5) | copy-start | bytes 98308
  1.7 3.4 %collective-permute-start = (f32[24,128]{1,0:T(8,128)}, f32[24,128]{1,0:T(8,128)S(1)}, u32[]{:S(2)}, u32[]{:S(2)}) collective-permute-start(f32[24,128]{1,0:T(8,128)} %get-tuple-element.47), channel_id=1, source_target_pairs={{0,1},{1,0},{2,3},{3,2},{4,5},{5,4},{6,7},{7,6},{8,9},{9,8},{10,11... | collective-permute-start | bytes 36872 | tf_op jit(solution)/shard_map/ppermute | solution.py:414
  2.2 4.2 %collective-permute-start.1 = (f32[24,128]{1,0:T(8,128)}, f32[24,128]{1,0:T(8,128)S(1)}, u32[]{:S(2)}, u32[]{:S(2)}) collective-permute-start(f32[24,128]{1,0:T(8,128)} %get-tuple-element.48), channel_id=1, source_target_pairs={{0,3},{1,2},{2,1},{3,0},{4,7},{5,6},{6,5},{7,4},{8,11},{9,10},{10,... | collective-permute-start | bytes 36872 | tf_op jit(solution)/shard_map/ppermute | solution.py:415
  4.9 1.6 %copy-start.2 = (f32[8,128]{1,0:T(8,128)S(1)}, f32[8,128]{1,0:T(8,128)}, u32[]{:S(2)}) copy-start(f32[8,128]{1,0:T(8,128)} %get-tuple-element.46.own) | copy-start | bytes 12292
  6.7 7.6 %collective-permute-start.2 = (f32[168,128]{1,0:T(8,128)S(1)}, f32[168,128]{1,0:T(8,128)S(1)}, u32[]{:S(2)}, u32[]{:S(2)}) collective-permute-start(f32[168,128]{1,0:T(8,128)S(1)} %get-tuple-element.50), channel_id=1, source_target_pairs={{0,4},{4,0},{8,12},{12,8},{16,20},{20,16},{24,28},{28,24},{1,5},{5... | collective-permute-start | bytes 258056 | tf_op jit(solution)/shard_map/ppermute | solution.py:404
  8.4 9.5 %collective-permute-start.3 = (f32[168,128]{1,0:T(8,128)S(1)}, f32[168,128]{1,0:T(8,128)S(1)}, u32[]{:S(2)}, u32[]{:S(2)}) collective-permute-start(f32[168,128]{1,0:T(8,128)S(1)} %get-tuple-element.53), channel_id=1, source_target_pairs={{0,8},{4,12},{8,0},{12,4},{16,24},{20,28},{24,16},{28,20},{1,9},{5... | collective-permute-start | bytes 258056 | tf_op jit(solution)/shard_map/ppermute | solution.py:404
  10.0 7.9 %collective-permute-start.4 = (f32[168,128]{1,0:T(8,128)S(1)}, f32[168,128]{1,0:T(8,128)S(1)}, u32[]{:S(2)}, u32[]{:S(2)}) collective-permute-start(f32[168,128]{1,0:T(8,128)S(1)} %get-tuple-element.56), channel_id=1, source_target_pairs={{0,12},{4,8},{8,4},{12,0},{16,28},{20,24},{24,20},{28,16},{1,13},{... | collective-permute-start | bytes 258056 | tf_op jit(solution)/shard_map/ppermute | solution.py:404
  10.2 7.7 %collective-permute-start.5 = (f32[168,128]{1,0:T(8,128)S(1)}, f32[168,128]{1,0:T(8,128)S(1)}, u32[]{:S(2)}, u32[]{:S(2)}) collective-permute-start(f32[168,128]{1,0:T(8,128)S(1)} %get-tuple-element.57), channel_id=1, source_target_pairs={{0,16},{4,20},{8,24},{12,28},{16,0},{20,4},{24,8},{28,12},{1,17},{... | collective-permute-start | bytes 258056 | tf_op jit(solution)/shard_map/ppermute | solution.py:404
  13.0 13.5 %collective-permute-start.6 = (f32[168,128]{1,0:T(8,128)S(1)}, f32[168,128]{1,0:T(8,128)S(1)}, u32[]{:S(2)}, u32[]{:S(2)}) collective-permute-start(f32[168,128]{1,0:T(8,128)S(1)} %get-tuple-element.58), channel_id=1, source_target_pairs={{0,20},{4,16},{8,28},{12,24},{16,4},{20,0},{24,12},{28,8},{1,21},{... | collective-permute-start | bytes 258056 | tf_op jit(solution)/shard_map/ppermute | solution.py:404
  14.3 12.3 %collective-permute-start.7 = (f32[168,128]{1,0:T(8,128)S(1)}, f32[168,128]{1,0:T(8,128)S(1)}, u32[]{:S(2)}, u32[]{:S(2)}) collective-permute-start(f32[168,128]{1,0:T(8,128)S(1)} %get-tuple-element.59), channel_id=1, source_target_pairs={{0,24},{4,28},{8,16},{12,20},{16,8},{20,12},{24,0},{28,4},{1,25},{... | collective-permute-start | bytes 258056 | tf_op jit(solution)/shard_map/ppermute | solution.py:404
  17.9 8.7 %collective-permute-start.8 = (f32[168,128]{1,0:T(8,128)S(1)}, f32[168,128]{1,0:T(8,128)S(1)}, u32[]{:S(2)}, u32[]{:S(2)}) collective-permute-start(f32[168,128]{1,0:T(8,128)S(1)} %get-tuple-element.60), channel_id=1, source_target_pairs={{0,28},{4,24},{8,20},{12,16},{16,12},{20,8},{24,4},{28,0},{1,29},{... | collective-permute-start | bytes 258056 | tf_op jit(solution)/shard_map/ppermute | solution.py:404
  30.0 8.9 %collective-permute-start.9 = (f32[152,128]{1,0:T(8,128)S(1)}, f32[152,128]{1,0:T(8,128)S(1)}, u32[]{:S(2)}, u32[]{:S(2)}) collective-permute-start(f32[152,128]{1,0:T(8,128)S(1)} %get-tuple-element.62), channel_id=1, source_target_pairs={{0,4},{4,0},{8,12},{12,8},{16,20},{20,16},{24,28},{28,24},{1,5},{5... | collective-permute-start | bytes 233480 | tf_op jit(solution)/shard_map/ppermute | solution.py:404
  31.3 10.0 %collective-permute-start.10 = (f32[152,128]{1,0:T(8,128)S(1)}, f32[152,128]{1,0:T(8,128)S(1)}, u32[]{:S(2)}, u32[]{:S(2)}) collective-permute-start(f32[152,128]{1,0:T(8,128)S(1)} %get-tuple-element.65), channel_id=1, source_target_pairs={{0,8},{4,12},{8,0},{12,4},{16,24},{20,28},{24,16},{28,20},{1,9},{5... | collective-permute-start | bytes 233480 | tf_op jit(solution)/shard_map/ppermute | solution.py:404
  35.0 12.2 %collective-permute-start.11 = (f32[152,128]{1,0:T(8,128)S(1)}, f32[152,128]{1,0:T(8,128)S(1)}, u32[]{:S(2)}, u32[]{:S(2)}) collective-permute-start(f32[152,128]{1,0:T(8,128)S(1)} %get-tuple-element.68), channel_id=1, source_target_pairs={{0,12},{4,8},{8,4},{12,0},{16,28},{20,24},{24,20},{28,16},{1,13},{... | collective-permute-start | bytes 233480 | tf_op jit(solution)/shard_map/ppermute | solution.py:404
  35.2 8.4 %collective-permute-start.13 = (f32[80,128]{1,0:T(8,128)S(1)}, f32[80,128]{1,0:T(8,128)S(1)}, u32[]{:S(2)}, u32[]{:S(2)}) collective-permute-start(f32[80,128]{1,0:T(8,128)S(1)} %get-tuple-element.72), channel_id=1, source_target_pairs={{0,16},{4,20},{8,24},{12,28},{16,0},{20,4},{24,8},{28,12},{1,17},{... | collective-permute-start | bytes 122888 | tf_op jit(solution)/shard_map/ppermute | solution.py:404
  38.9 7.6 %collective-permute-start.15 = (f32[80,128]{1,0:T(8,128)S(1)}, f32[80,128]{1,0:T(8,128)S(1)}, u32[]{:S(2)}, u32[]{:S(2)}) collective-permute-start(f32[80,128]{1,0:T(8,128)S(1)} %get-tuple-element.75), channel_id=1, source_target_pairs={{0,20},{4,16},{8,28},{12,24},{16,4},{20,0},{24,12},{28,8},{1,21},{... | collective-permute-start | bytes 122888 | tf_op jit(solution)/shard_map/ppermute | solution.py:404
  38.9 9.1 %collective-permute-start.17 = (f32[80,128]{1,0:T(8,128)S(1)}, f32[80,128]{1,0:T(8,128)S(1)}, u32[]{:S(2)}, u32[]{:S(2)}) collective-permute-start(f32[80,128]{1,0:T(8,128)S(1)} %get-tuple-element.78), channel_id=1, source_target_pairs={{0,24},{4,28},{8,16},{12,20},{16,8},{20,12},{24,0},{28,4},{1,25},{... | collective-permute-start | bytes 122888 | tf_op jit(solution)/shard_map/ppermute | solution.py:404
  41.3 9.1 %collective-permute-start.19 = (f32[80,128]{1,0:T(8,128)S(1)}, f32[80,128]{1,0:T(8,128)S(1)}, u32[]{:S(2)}, u32[]{:S(2)}) collective-permute-start(f32[80,128]{1,0:T(8,128)S(1)} %get-tuple-element.84), channel_id=1, source_target_pairs={{0,28},{4,24},{8,20},{12,16},{16,12},{20,8},{24,4},{28,0},{1,29},{... | collective-permute-start | bytes 122888 | tf_op jit(solution)/shard_map/ppermute | solution.py:404
  43.6 7.0 %collective-permute-start.14 = (f32[72,128]{1,0:T(8,128)S(1)}, f32[72,128]{1,0:T(8,128)S(1)}, u32[]{:S(2)}, u32[]{:S(2)}) collective-permute-start(f32[72,128]{1,0:T(8,128)S(1)} %get-tuple-element.74), channel_id=1, source_target_pairs={{0,20},{4,16},{8,28},{12,24},{16,4},{20,0},{24,12},{28,8},{1,21},{... | collective-permute-start | bytes 110600 | tf_op jit(solution)/shard_map/ppermute | solution.py:404
  46.5 5.9 %collective-permute-start.16 = (f32[72,128]{1,0:T(8,128)S(1)}, f32[72,128]{1,0:T(8,128)S(1)}, u32[]{:S(2)}, u32[]{:S(2)}) collective-permute-start(f32[72,128]{1,0:T(8,128)S(1)} %get-tuple-element.77), channel_id=1, source_target_pairs={{0,24},{4,28},{8,16},{12,20},{16,8},{20,12},{24,0},{28,4},{1,25},{... | collective-permute-start | bytes 110600 | tf_op jit(solution)/shard_map/ppermute | solution.py:404
  47.1 5.6 %collective-permute-start.12 = (f32[72,128]{1,0:T(8,128)S(1)}, f32[72,128]{1,0:T(8,128)S(1)}, u32[]{:S(2)}, u32[]{:S(2)}) collective-permute-start(f32[72,128]{1,0:T(8,128)S(1)} %get-tuple-element.71), channel_id=1, source_target_pairs={{0,16},{4,20},{8,24},{12,28},{16,0},{20,4},{24,8},{28,12},{1,17},{... | collective-permute-start | bytes 110600 | tf_op jit(solution)/shard_map/ppermute | solution.py:404
  48.0 6.7 %collective-permute-start.18 = (f32[72,128]{1,0:T(8,128)S(1)}, f32[72,128]{1,0:T(8,128)S(1)}, u32[]{:S(2)}, u32[]{:S(2)}) collective-permute-start(f32[72,128]{1,0:T(8,128)S(1)} %get-tuple-element.80), channel_id=1, source_target_pairs={{0,28},{4,24},{8,20},{12,16},{16,12},{20,8},{24,4},{28,0},{1,29},{... | collective-permute-start | bytes 110600 | tf_op jit(solution)/shard_map/ppermute | solution.py:404
  50.4 4.4 %collective-permute-start.20 = (f32[24,128]{1,0:T(8,128)S(1)}, f32[24,128]{1,0:T(8,128)S(1)}, u32[]{:S(2)}, u32[]{:S(2)}) collective-permute-start(f32[24,128]{1,0:T(8,128)S(1)} %get-tuple-element.85), channel_id=1, source_target_pairs={{0,1},{1,0},{2,3},{3,2},{4,5},{5,4},{6,7},{7,6},{8,9},{9,8},{10,11... | collective-permute-start | bytes 36872 | tf_op jit(solution)/shard_map/ppermute | solution.py:414
  50.6 4.2 %collective-permute-start.21 = (f32[24,128]{1,0:T(8,128)S(1)}, f32[24,128]{1,0:T(8,128)S(1)}, u32[]{:S(2)}, u32[]{:S(2)}) collective-permute-start(f32[24,128]{1,0:T(8,128)S(1)} %get-tuple-element.86), channel_id=1, source_target_pairs={{0,3},{1,2},{2,1},{3,0},{4,7},{5,6},{6,5},{7,4},{8,11},{9,10},{10,... | collective-permute-start | bytes 36872 | tf_op jit(solution)/shard_map/ppermute | solution.py:415

commit v8 on v4

--- a/solution.py
+++ b/solution.py
@@ -135,9 +135,8 @@
     rows_hop = faces + 4
     f32 = jnp.float32
 
-    order = [0]
-    for bit in reversed(range(owners.bit_length() - 1)):
-        order += range(1 << bit, 2 << bit)
+    half = owners // 2
+    order = [0, 1, half, 2, *range(half + 1, owners), *range(3, half)]
     slot_of = [order.index(d) for d in range(owners)]
 
     def position():

time: 55.1 us -> 51.2 us (0.929)
  starting transfers between devices: 30.3 us -> 26.6 us
    ppermute x14, starting transfers between devices: 25.5 us -> 21.8 us  [exchange(): lax.ppermute(parts[n], 'gx', [(g, g ^ order[n]) for g in range(owners)])]
  transfers between devices with their start and end apart: 18 -> 18, of which waited for: 10 -> 6; matrix products, arithmetic and copies ran while one was open for 0% -> 0% of each run, Pallas kernels for 1% -> 1%
where the time goes in v8:
time: 51.2 us; the launch traced here: 51 us
  starting transfers between devices  26.6 us (52%)
  waiting for transfers between devices  17.8 us (35%)
  Pallas kernels  6.56 us (13%)
    ppermute x14, starting transfers between devices, exchange(): lax.ppermute(parts[n], 'gx', [(g, g ^ order[n]) for g in range(owners)])  21.8 us
    ppermute x14, waiting for transfers between devices, exchange(): lax.ppermute(parts[n], 'gx', [(g, g ^ order[n]) for g in range(owners)])  15 us
    pallas_call x7, Pallas kernels, call(): pl.pallas_call(kernel, out_shape=out_shape, in_specs=[spec] * len(inputs)...  6.56 us
    ppermute x2, starting transfers between devices, hop(): lax.ppermute(far, 'gy', list(enumerate(behind)))  4.22 us
    ppermute x2, waiting for transfers between devices, hop(): lax.ppermute(far, 'gy', list(enumerate(behind)))  2.8 us
  transfers between devices with their start and end apart: 18, of which 6 were waited for; matrix products, arithmetic and copies ran while one was open for 0% of the time, Pallas kernels for 1%

profile of v8, /device:TPU:0, one launch (start us, length us, event | category | flops | bytes accessed | tf_op | source)
XLA Modules:
  0.0 51.0 jit_solution(11461221244328497277)
XLA Ops:
  0.0 0.0 copy-start
  0.0 0.0 copy-start.1
  0.0 1.7 %edge_planes.1 = (f32[24,128]{1,0:T(8,128)}, f32[24,128]{1,0:T(8,128)}, f32[8,128]{1,0:T(8,128)}) custom-call(f32[19,64,128]{2,1,0:T(8,128)} %bitcast.26, s32[64,128]{1,0:T(8,128)} %bitcast.28, s32[1,2]{1,0:T(1,128)} %slots.1, s32[2,3]{1,0:T(2,128)} %bitcast.30), custom_call_target="tpu_custom_call" | custom-call | flops 100000 | bytes 100000 | tf_op jit(solution)/shard_map/edge_planes/pallas_call | solution.py:356
  1.7 0.5 %collective-permute-start = (f32[24,128]{1,0:T(8,128)}, f32[24,128]{1,0:T(8,128)S(1)}, u32[]{:S(2)}, u32[]{:S(2)}) collective-permute-start(f32[24,128]{1,0:T(8,128)} %get-tuple-element.27), channel_id=1, source_target_pairs={{0,1},{1,0},{2,3},{3,2},{4,5},{5,4},{6,7},{7,6},{8,9},{9,8},{10,11... | collective-permute-start | bytes 36872 | tf_op jit(solution)/shard_map/ppermute | solution.py:377
  2.2 2.6 %collective-permute-start.1 = (f32[24,128]{1,0:T(8,128)}, f32[24,128]{1,0:T(8,128)S(1)}, u32[]{:S(2)}, u32[]{:S(2)}) collective-permute-start(f32[24,128]{1,0:T(8,128)} %get-tuple-element.28), channel_id=1, source_target_pairs={{0,3},{1,2},{2,1},{3,0},{4,7},{5,6},{6,5},{7,4},{8,11},{9,10},{10,... | collective-permute-start | bytes 36872 | tf_op jit(solution)/shard_map/ppermute | solution.py:378
  4.9 0.0 copy-done
  4.9 0.0 copy-done.1
  4.9 0.0 copy-start.2
  4.9 0.2 first_collision.1.post
  5.1 0.0 collective-permute-done.near
  5.1 1.4 %collective-permute-done.1.far = f32[24,128]{1,0:T(8,128)S(1)} collective-permute-done((f32[24,128]{1,0:T(8,128)}, f32[24,128]{1,0:T(8,128)S(1)}, u32[]{:S(2)}, u32[]{:S(2)}) %collective-permute-start.1) | collective-permute-done | bytes 12320 | tf_op jit(solution)/shard_map/ppermute | solution.py:378
  6.5 0.0 copy-done.2
  6.5 0.2 pack_planes.1
  6.7 1.8 %collective-permute-start.2 = (f32[168,128]{1,0:T(8,128)S(1)}, f32[168,128]{1,0:T(8,128)S(1)}, u32[]{:S(2)}, u32[]{:S(2)}) collective-permute-start(f32[168,128]{1,0:T(8,128)S(1)} %get-tuple-element.30), channel_id=1, source_target_pairs={{0,4},{4,0},{8,12},{12,8},{16,20},{20,16},{24,28},{28,24},{1,5},{5... | collective-permute-start | bytes 258056 | tf_op jit(solution)/shard_map/ppermute | solution.py:369
  8.4 2.6 %collective-permute-start.3 = (f32[168,128]{1,0:T(8,128)S(1)}, f32[168,128]{1,0:T(8,128)S(1)}, u32[]{:S(2)}, u32[]{:S(2)}) collective-permute-start(f32[168,128]{1,0:T(8,128)S(1)} %get-tuple-element.31), channel_id=1, source_target_pairs={{0,16},{4,20},{8,24},{12,28},{16,0},{20,4},{24,8},{28,12},{1,17},{... | collective-permute-start | bytes 258056 | tf_op jit(solution)/shard_map/ppermute | solution.py:369
  11.0 1.6 %collective-permute-start.4 = (f32[168,128]{1,0:T(8,128)S(1)}, f32[168,128]{1,0:T(8,128)S(1)}, u32[]{:S(2)}, u32[]{:S(2)}) collective-permute-start(f32[168,128]{1,0:T(8,128)S(1)} %get-tuple-element.32), channel_id=1, source_target_pairs={{0,8},{4,12},{8,0},{12,4},{16,24},{20,28},{24,16},{28,20},{1,9},{5... | collective-permute-start | bytes 258056 | tf_op jit(solution)/shard_map/ppermute | solution.py:369
  12.6 0.3 collective-permute-start.5
  12.9 2.5 %collective-permute-start.6 = (f32[168,128]{1,0:T(8,128)S(1)}, f32[168,128]{1,0:T(8,128)S(1)}, u32[]{:S(2)}, u32[]{:S(2)}) collective-permute-start(f32[168,128]{1,0:T(8,128)S(1)} %get-tuple-element.34), channel_id=1, source_target_pairs={{0,24},{4,28},{8,16},{12,20},{16,8},{20,12},{24,0},{28,4},{1,25},{... | collective-permute-start | bytes 258056 | tf_op jit(solution)/shard_map/ppermute | solution.py:369
  15.4 0.0 collective-permute-done.2.refs_1_
  15.4 2.3 %collective-permute-start.7 = (f32[168,128]{1,0:T(8,128)S(1)}, f32[168,128]{1,0:T(8,128)S(1)}, u32[]{:S(2)}, u32[]{:S(2)}) collective-permute-start(f32[168,128]{1,0:T(8,128)S(1)} %get-tuple-element.35), channel_id=1, source_target_pairs={{0,28},{4,24},{8,20},{12,16},{16,12},{20,8},{24,4},{28,0},{1,29},{... | collective-permute-start | bytes 258056 | tf_op jit(solution)/shard_map/ppermute | solution.py:369
  17.7 0.0 collective-permute-done.3.refs_2_
  17.7 0.0 collective-permute-start.8
  17.7 0.0 collective-permute-done.4.refs_3_
  17.7 6.6 %collective-permute-done.5.refs_4_ = f32[168,128]{1,0:T(8,128)S(1)} collective-permute-done((f32[168,128]{1,0:T(8,128)S(1)}, f32[168,128]{1,0:T(8,128)S(1)}, u32[]{:S(2)}, u32[]{:S(2)}) %collective-permute-start.5) | collective-permute-done | bytes 86048 | tf_op jit(solution)/shard_map/ppermute | solution.py:369
  24.3 0.0 collective-permute-done.6.refs_5_
  24.3 0.0 collective-permute-done.7.refs_6_
  24.3 1.5 %collective-permute-done.8.refs_7_ = f32[168,128]{1,0:T(8,128)S(1)} collective-permute-done((f32[168,128]{1,0:T(8,128)S(1)}, f32[168,128]{1,0:T(8,128)S(1)}, u32[]{:S(2)}, u32[]{:S(2)}) %collective-permute-start.8) | collective-permute-done | bytes 86048 | tf_op jit(solution)/shard_map/ppermute | solution.py:369
  25.8 3.4 %second_step.1 = (f32[152,128]{1,0:T(8,128)S(1)}, f32[152,128]{1,0:T(8,128)S(1)}, f32[152,128]{1,0:T(8,128)S(1)}, f32[152,128]{1,0:T(8,128)S(1)}, f32[152,128]{1...) custom-call(f32[168,128]{1,0:T(8,128)S(1)} %get-tuple-element.29.refs_0_, ...), custom_call_target="tpu_custom_call" | custom-call | flops 4000000 | bytes 4000000 | tf_op jit(solution)/shard_map/second_step/pallas_call | solution.py:356
  29.2 0.5 %collective-permute-start.9 = (f32[152,128]{1,0:T(8,128)S(1)}, f32[152,128]{1,0:T(8,128)S(1)}, u32[]{:S(2)}, u32[]{:S(2)}) collective-permute-start(f32[152,128]{1,0:T(8,128)S(1)} %get-tuple-element.38), channel_id=1, source_target_pairs={{0,4},{4,0},{8,12},{12,8},{16,20},{20,16},{24,28},{28,24},{1,5},{5... | collective-permute-start | bytes 233480 | tf_op jit(solution)/shard_map/ppermute | solution.py:369
  29.8 4.7 %collective-permute-start.10 = (f32[152,128]{1,0:T(8,128)S(1)}, f32[152,128]{1,0:T(8,128)S(1)}, u32[]{:S(2)}, u32[]{:S(2)}) collective-permute-start(f32[152,128]{1,0:T(8,128)S(1)} %get-tuple-element.39), channel_id=1, source_target_pairs={{0,16},{4,20},{8,24},{12,28},{16,0},{20,4},{24,8},{28,12},{1,17},{... | collective-permute-start | bytes 233480 | tf_op jit(solution)/shard_map/ppermute | solution.py:369
  34.5 0.0 collective-permute-start.11
  34.5 1.7 %collective-permute-start.12 = (f32[152,128]{1,0:T(8,128)S(1)}, f32[152,128]{1,0:T(8,128)S(1)}, u32[]{:S(2)}, u32[]{:S(2)}) collective-permute-start(f32[152,128]{1,0:T(8,128)S(1)} %get-tuple-element.41), channel_id=1, source_target_pairs={{0,20},{4,16},{8,28},{12,24},{16,4},{20,0},{24,12},{28,8},{1,21},{... | collective-permute-start | bytes 233480 | tf_op jit(solution)/shard_map/ppermute | solution.py:369
  36.2 2.6 %collective-permute-start.13 = (f32[152,128]{1,0:T(8,128)S(1)}, f32[152,128]{1,0:T(8,128)S(1)}, u32[]{:S(2)}, u32[]{:S(2)}) collective-permute-start(f32[152,128]{1,0:T(8,128)S(1)} %get-tuple-element.42), channel_id=1, source_target_pairs={{0,24},{4,28},{8,16},{12,20},{16,8},{20,12},{24,0},{28,4},{1,25},{... | collective-permute-start | bytes 233480 | tf_op jit(solution)/shard_map/ppermute | solution.py:369
  38.8 0.0 collective-permute-done.9.refs_1_
  38.8 1.2 %collective-permute-start.14 = (f32[152,128]{1,0:T(8,128)S(1)}, f32[152,128]{1,0:T(8,128)S(1)}, u32[]{:S(2)}, u32[]{:S(2)}) collective-permute-start(f32[152,128]{1,0:T(8,128)S(1)} %get-tuple-element.43), channel_id=1, source_target_pairs={{0,28},{4,24},{8,20},{12,16},{16,12},{20,8},{24,4},{28,0},{1,29},{... | collective-permute-start | bytes 233480 | tf_op jit(solution)/shard_map/ppermute | solution.py:369
  40.0 0.0 collective-permute-done.10.refs_2_
  40.0 0.0 collective-permute-start.15
  40.1 0.0 collective-permute-done.11.refs_3_
  40.1 6.3 %collective-permute-done.12.refs_4_ = f32[152,128]{1,0:T(8,128)S(1)} collective-permute-done((f32[152,128]{1,0:T(8,128)S(1)}, f32[152,128]{1,0:T(8,128)S(1)}, u32[]{:S(2)}, u32[]{:S(2)}) %collective-permute-start.12) | collective-permute-done | bytes 77856 | tf_op jit(solution)/shard_map/ppermute | solution.py:369
  46.4 0.0 collective-permute-done.13.refs_5_
  46.4 0.0 collective-permute-done.14.refs_6_
  46.4 0.5 %collective-permute-done.15.refs_7_ = f32[152,128]{1,0:T(8,128)S(1)} collective-permute-done((f32[152,128]{1,0:T(8,128)S(1)}, f32[152,128]{1,0:T(8,128)S(1)}, u32[]{:S(2)}, u32[]{:S(2)}) %collective-permute-start.15) | collective-permute-done | bytes 77856 | tf_op jit(solution)/shard_map/ppermute | solution.py:369
  46.9 0.1 collective-permute-start.16
  47.0 1.6 %collective-permute-start.17 = (f32[24,128]{1,0:T(8,128)S(1)}, f32[24,128]{1,0:T(8,128)S(1)}, u32[]{:S(2)}, u32[]{:S(2)}) collective-permute-start(f32[24,128]{1,0:T(8,128)S(1)} %get-tuple-element.46), channel_id=1, source_target_pairs={{0,3},{1,2},{2,1},{3,0},{4,7},{5,6},{6,5},{7,4},{8,11},{9,10},{10,... | collective-permute-start | bytes 36872 | tf_op jit(solution)/shard_map/ppermute | solution.py:378
  48.6 0.1 unpack_planes.1.main
  48.7 0.0 collective-permute-done.16.near
  48.7 1.4 %collective-permute-done.17.far = f32[24,128]{1,0:T(8,128)S(1)} collective-permute-done((f32[24,128]{1,0:T(8,128)S(1)}, f32[24,128]{1,0:T(8,128)S(1)}, u32[]{:S(2)}, u32[]{:S(2)}) %collective-permute-start.17) | collective-permute-done | bytes 12320 | tf_op jit(solution)/shard_map/ppermute | solution.py:378
  50.2 0.9 %finish.1 = f32[1216,128]{1,0:T(8,128)} custom-call(f32[19,80,128]{2,1,0:T(8,128)S(1)} %unpack_planes.1.main, f32[24,128]{1,0:T(8,128)S(1)} %collective-permute-done.16.near, f32[24,128]{1,0:T(8,128)S(1)} %collective-permute-done.17.far), custom_call_target="tpu_custom_call" | custom-call | flops 100000 | bytes 100000 | tf_op jit(solution)/shard_map/finish/pallas_call | solution.py:356
  (1 shorter events, 0.0 us)
Async XLA Ops:
  0.0 4.9 %copy-start = (f32[1,2,19,4096]{3,1,2,0:T(2,128)S(1)}, f32[1,2,19,4096]{3,1,2,0:T(2,128)}, u32[]{:S(2)}) copy-start(f32[1,2,19,4096]{3,1,2,0:T(2,128)} %param.4) | copy-start | bytes 1867780
  0.0 4.9 %copy-start.1 = (s32[1,2,4096]{2,1,0:T(2,128)S(1)}, s32[1,2,4096]{2,1,0:T(2,128)}, u32[]{:S(2)}) copy-start(s32[1,2,4096]{2,1,0:T(2,128)} %param.5) | copy-start | bytes 98308
  1.7 3.4 %collective-permute-start = (f32[24,128]{1,0:T(8,128)}, f32[24,128]{1,0:T(8,128)S(1)}, u32[]{:S(2)}, u32[]{:S(2)}) collective-permute-start(f32[24,128]{1,0:T(8,128)} %get-tuple-element.27), channel_id=1, source_target_pairs={{0,1},{1,0},{2,3},{3,2},{4,5},{5,4},{6,7},{7,6},{8,9},{9,8},{10,11... | collective-permute-start | bytes 36872 | tf_op jit(solution)/shard_map/ppermute | solution.py:377
  2.2 4.2 %collective-permute-start.1 = (f32[24,128]{1,0:T(8,128)}, f32[24,128]{1,0:T(8,128)S(1)}, u32[]{:S(2)}, u32[]{:S(2)}) collective-permute-start(f32[24,128]{1,0:T(8,128)} %get-tuple-element.28), channel_id=1, source_target_pairs={{0,3},{1,2},{2,1},{3,0},{4,7},{5,6},{6,5},{7,4},{8,11},{9,10},{10,... | collective-permute-start | bytes 36872 | tf_op jit(solution)/shard_map/ppermute | solution.py:378
  4.9 1.6 %copy-start.2 = (f32[8,128]{1,0:T(8,128)S(1)}, f32[8,128]{1,0:T(8,128)}, u32[]{:S(2)}) copy-start(f32[8,128]{1,0:T(8,128)} %get-tuple-element.26.own) | copy-start | bytes 12292
  6.7 8.7 %collective-permute-start.2 = (f32[168,128]{1,0:T(8,128)S(1)}, f32[168,128]{1,0:T(8,128)S(1)}, u32[]{:S(2)}, u32[]{:S(2)}) collective-permute-start(f32[168,128]{1,0:T(8,128)S(1)} %get-tuple-element.30), channel_id=1, source_target_pairs={{0,4},{4,0},{8,12},{12,8},{16,20},{20,16},{24,28},{28,24},{1,5},{5... | collective-permute-start | bytes 258056 | tf_op jit(solution)/shard_map/ppermute | solution.py:369
  8.4 9.2 %collective-permute-start.3 = (f32[168,128]{1,0:T(8,128)S(1)}, f32[168,128]{1,0:T(8,128)S(1)}, u32[]{:S(2)}, u32[]{:S(2)}) collective-permute-start(f32[168,128]{1,0:T(8,128)S(1)} %get-tuple-element.31), channel_id=1, source_target_pairs={{0,16},{4,20},{8,24},{12,28},{16,0},{20,4},{24,8},{28,12},{1,17},{... | collective-permute-start | bytes 258056 | tf_op jit(solution)/shard_map/ppermute | solution.py:369
  11.0 6.6 %collective-permute-start.4 = (f32[168,128]{1,0:T(8,128)S(1)}, f32[168,128]{1,0:T(8,128)S(1)}, u32[]{:S(2)}, u32[]{:S(2)}) collective-permute-start(f32[168,128]{1,0:T(8,128)S(1)} %get-tuple-element.32), channel_id=1, source_target_pairs={{0,8},{4,12},{8,0},{12,4},{16,24},{20,28},{24,16},{28,20},{1,9},{5... | collective-permute-start | bytes 258056 | tf_op jit(solution)/shard_map/ppermute | solution.py:369
  12.6 11.7 %collective-permute-start.5 = (f32[168,128]{1,0:T(8,128)S(1)}, f32[168,128]{1,0:T(8,128)S(1)}, u32[]{:S(2)}, u32[]{:S(2)}) collective-permute-start(f32[168,128]{1,0:T(8,128)S(1)} %get-tuple-element.33), channel_id=1, source_target_pairs={{0,20},{4,16},{8,28},{12,24},{16,4},{20,0},{24,12},{28,8},{1,21},{... | collective-permute-start | bytes 258056 | tf_op jit(solution)/shard_map/ppermute | solution.py:369
  12.9 11.4 %collective-permute-start.6 = (f32[168,128]{1,0:T(8,128)S(1)}, f32[168,128]{1,0:T(8,128)S(1)}, u32[]{:S(2)}, u32[]{:S(2)}) collective-permute-start(f32[168,128]{1,0:T(8,128)S(1)} %get-tuple-element.34), channel_id=1, source_target_pairs={{0,24},{4,28},{8,16},{12,20},{16,8},{20,12},{24,0},{28,4},{1,25},{... | collective-permute-start | bytes 258056 | tf_op jit(solution)/shard_map/ppermute | solution.py:369
  15.4 8.9 %collective-permute-start.7 = (f32[168,128]{1,0:T(8,128)S(1)}, f32[168,128]{1,0:T(8,128)S(1)}, u32[]{:S(2)}, u32[]{:S(2)}) collective-permute-start(f32[168,128]{1,0:T(8,128)S(1)} %get-tuple-element.35), channel_id=1, source_target_pairs={{0,28},{4,24},{8,20},{12,16},{16,12},{20,8},{24,4},{28,0},{1,29},{... | collective-permute-start | bytes 258056 | tf_op jit(solution)/shard_map/ppermute | solution.py:369
  17.7 8.1 %collective-permute-start.8 = (f32[168,128]{1,0:T(8,128)S(1)}, f32[168,128]{1,0:T(8,128)S(1)}, u32[]{:S(2)}, u32[]{:S(2)}) collective-permute-start(f32[168,128]{1,0:T(8,128)S(1)} %get-tuple-element.36), channel_id=1, source_target_pairs={{0,12},{4,8},{8,4},{12,0},{16,28},{20,24},{24,20},{28,16},{1,13},{... | collective-permute-start | bytes 258056 | tf_op jit(solution)/shard_map/ppermute | solution.py:369
  29.2 9.6 %collective-permute-start.9 = (f32[152,128]{1,0:T(8,128)S(1)}, f32[152,128]{1,0:T(8,128)S(1)}, u32[]{:S(2)}, u32[]{:S(2)}) collective-permute-start(f32[152,128]{1,0:T(8,128)S(1)} %get-tuple-element.38), channel_id=1, source_target_pairs={{0,4},{4,0},{8,12},{12,8},{16,20},{20,16},{24,28},{28,24},{1,5},{5... | collective-permute-start | bytes 233480 | tf_op jit(solution)/shard_map/ppermute | solution.py:369
  29.8 10.3 %collective-permute-start.10 = (f32[152,128]{1,0:T(8,128)S(1)}, f32[152,128]{1,0:T(8,128)S(1)}, u32[]{:S(2)}, u32[]{:S(2)}) collective-permute-start(f32[152,128]{1,0:T(8,128)S(1)} %get-tuple-element.39), channel_id=1, source_target_pairs={{0,16},{4,20},{8,24},{12,28},{16,0},{20,4},{24,8},{28,12},{1,17},{... | collective-permute-start | bytes 233480 | tf_op jit(solution)/shard_map/ppermute | solution.py:369
  34.5 5.6 %collective-permute-start.11 = (f32[152,128]{1,0:T(8,128)S(1)}, f32[152,128]{1,0:T(8,128)S(1)}, u32[]{:S(2)}, u32[]{:S(2)}) collective-permute-start(f32[152,128]{1,0:T(8,128)S(1)} %get-tuple-element.40), channel_id=1, source_target_pairs={{0,8},{4,12},{8,0},{12,4},{16,24},{20,28},{24,16},{28,20},{1,9},{5... | collective-permute-start | bytes 233480 | tf_op jit(solution)/shard_map/ppermute | solution.py:369
  34.5 11.9 %collective-permute-start.12 = (f32[152,128]{1,0:T(8,128)S(1)}, f32[152,128]{1,0:T(8,128)S(1)}, u32[]{:S(2)}, u32[]{:S(2)}) collective-permute-start(f32[152,128]{1,0:T(8,128)S(1)} %get-tuple-element.41), channel_id=1, source_target_pairs={{0,20},{4,16},{8,28},{12,24},{16,4},{20,0},{24,12},{28,8},{1,21},{... | collective-permute-start | bytes 233480 | tf_op jit(solution)/shard_map/ppermute | solution.py:369
  36.2 10.2 %collective-permute-start.13 = (f32[152,128]{1,0:T(8,128)S(1)}, f32[152,128]{1,0:T(8,128)S(1)}, u32[]{:S(2)}, u32[]{:S(2)}) collective-permute-start(f32[152,128]{1,0:T(8,128)S(1)} %get-tuple-element.42), channel_id=1, source_target_pairs={{0,24},{4,28},{8,16},{12,20},{16,8},{20,12},{24,0},{28,4},{1,25},{... | collective-permute-start | bytes 233480 | tf_op jit(solution)/shard_map/ppermute | solution.py:369
  38.8 7.6 %collective-permute-start.14 = (f32[152,128]{1,0:T(8,128)S(1)}, f32[152,128]{1,0:T(8,128)S(1)}, u32[]{:S(2)}, u32[]{:S(2)}) collective-permute-start(f32[152,128]{1,0:T(8,128)S(1)} %get-tuple-element.43), channel_id=1, source_target_pairs={{0,28},{4,24},{8,20},{12,16},{16,12},{20,8},{24,4},{28,0},{1,29},{... | collective-permute-start | bytes 233480 | tf_op jit(solution)/shard_map/ppermute | solution.py:369
  40.0 6.8 %collective-permute-start.15 = (f32[152,128]{1,0:T(8,128)S(1)}, f32[152,128]{1,0:T(8,128)S(1)}, u32[]{:S(2)}, u32[]{:S(2)}) collective-permute-start(f32[152,128]{1,0:T(8,128)S(1)} %get-tuple-element.44), channel_id=1, source_target_pairs={{0,12},{4,8},{8,4},{12,0},{16,28},{20,24},{24,20},{28,16},{1,13},{... | collective-permute-start | bytes 233480 | tf_op jit(solution)/shard_map/ppermute | solution.py:369
  46.9 1.8 %collective-permute-start.16 = (f32[24,128]{1,0:T(8,128)S(1)}, f32[24,128]{1,0:T(8,128)S(1)}, u32[]{:S(2)}, u32[]{:S(2)}) collective-permute-start(f32[24,128]{1,0:T(8,128)S(1)} %get-tuple-element.45), channel_id=1, source_target_pairs={{0,1},{1,0},{2,3},{3,2},{4,5},{5,4},{6,7},{7,6},{8,9},{9,8},{10,11... | collective-permute-start | bytes 36872 | tf_op jit(solution)/shard_map/ppermute | solution.py:377
  47.0 3.2 %collective-permute-start.17 = (f32[24,128]{1,0:T(8,128)S(1)}, f32[24,128]{1,0:T(8,128)S(1)}, u32[]{:S(2)}, u32[]{:S(2)}) collective-permute-start(f32[24,128]{1,0:T(8,128)S(1)} %get-tuple-element.46), channel_id=1, source_target_pairs={{0,3},{1,2},{2,1},{3,0},{4,7},{5,6},{6,5},{7,4},{8,11},{9,10},{10,... | collective-permute-start | bytes 36872 | tf_op jit(solution)/shard_map/ppermute | solution.py:378

commit v9 on v8

--- a/solution.py
+++ b/solution.py
@@ -104,13 +104,16 @@
     return [jnp.where(fluid, relaxed[p], f[OPPOSITE[p]]) for p in range(Q)]
 
 
-def shift_y(value, step, lane):
+def shift_y(value, step, lane, row, block):
     rows = value.shape[0]
+    turned = pltpu.roll(value, B if step == 1 else LANES - B, 1)
     if step == 1:
-        turned = pltpu.roll(value, B, 1)
-        return jnp.where(lane < B, pltpu.roll(turned, 1, 0), turned)
-    turned = pltpu.roll(value, LANES - B, 1)
-    return jnp.where(lane >= LANES - B, pltpu.roll(turned, rows - 1, 0), turned)
+        edge, start = lane < B, row % PLANE_ROWS == 0
+        near, far = pltpu.roll(turned, 1, 0), pltpu.roll(turned, block - 1, 0)
+    else:
+        edge, start = lane >= LANES - B, row % PLANE_ROWS == PLANE_ROWS - 1
+        near, far = pltpu.roll(turned, rows - 1, 0), pltpu.roll(turned, rows - block + 1, 0)
+    return jnp.where(edge, jnp.where(start, far, near), turned)
 
 
 def shift_z(value, other, step, lane):
@@ -127,7 +130,8 @@
     owners, slabs = mesh.shape["gx"], mesh.shape["gy"]
     planes = B // owners
     share = planes * PLANE
-    rows = owners * PLANE_ROWS
+    block = planes * PLANE_ROWS
+    rows = owners * block
     head = (Q + 1) * share
     rows_in = head + 8
     rows_out = Q * share
@@ -136,7 +140,7 @@
     f32 = jnp.float32
 
     half = owners // 2
-    order = [0, 1, half, 2, *range(half + 1, owners), *range(3, half)]
+    order = [0, half, 1, half + 1, 2, *range(half + 2, owners), *range(3, half)]
     slot_of = [order.index(d) for d in range(owners)]
 
     def position():
@@ -232,77 +236,95 @@
         def number(d, row, column):
             return table[d, row, column].astype(jnp.int32)
 
-        def held(d, t, which):
-            return number(d, 2 * which, t)
-
-        def final(d, t, which):
+        other = jnp.where(first, 1, jnp.where(last, 2, 0))
+
+        def seats(blocks):
+            return [(b % NB, pl.multiple_of((b // NB) * block, block)) for b in blocks]
+
+        def held(d, which):
+            return [number(d, 2 * which, t) for t in range(NB)]
+
+        def final(d, which):
             def lead(e, r):
                 return number(d ^ e, 2 * which + 1, r)
 
             flip = lead(0, 2) + lead(4, 2) + lead(4, 1) + lead(6, 1) + lead(6, 0) + lead(7, 0)
-            one, two = held(d ^ 7, t, which), held(d ^ 7, 1 - t, which)
-            return jnp.where(flip % 2 == 1, two, one)
-
-        def seat(b):
-            return b % NB, pl.multiple_of((b // NB) * PLANE_ROWS, PLANE_ROWS)
+            one, two = held(d ^ 7, which)
+            crossed = flip % 2 == 1
+            return [jnp.where(crossed, two, one), jnp.where(crossed, one, two)]
 
         for d in range(owners):
-            for t in range(NB):
-                usual = held(d, t, 0)
-                at_usual = seat(usual)
-                at_below = seat(jnp.where(first, held(d, t, 1), usual))
-                at_above = seat(jnp.where(last, held(d, t, 2), usual))
+            for t, (kz, y) in enumerate(seats(held(d, 0))):
                 for p in range(Q + 1):
-                    cx = VELOCITIES[p][0] if p < Q else 0
-                    for i in range(planes):
-                        kz, y = at_usual
-                        if cx == 1 and i == 0:
-                            kz, y = at_below
-                        if cx == -1 and i == planes - 1:
-                            kz, y = at_above
-                        lattice[p, i, kz, pl.ds(y, PLANE_ROWS), :] = got[d][
+                    lattice[p, kz, pl.ds(y, block), :] = got[d][
+                        pl.ds(p * share + t, block, stride=NB), :
+                    ]
+
+        def bring(chosen, i):
+            for d in range(owners):
+                for t, (kz, y) in enumerate(seats(held(d, other))):
+                    for p in chosen:
+                        lattice[p, kz, pl.ds(y + i * PLANE_ROWS, PLANE_ROWS), :] = got[d][
                             pl.ds(p * share + i * PLANE + t, PLANE_ROWS, stride=NB), :
                         ]
+
+        @pl.when(first)
+        def _():
+            bring(UPWARD, 0)
+
+        @pl.when(last)
+        def _():
+            bring(DOWNWARD, planes - 1)
+
         lane = lax.broadcasted_iota(jnp.int32, (rows, LANES), 1)
+        row = lax.broadcasted_iota(jnp.int32, (rows, LANES), 0)
 
         def passed(pair, p):
             cx, cy, cz = VELOCITIES[p]
             if cy:
-                pair = [shift_y(value, cy, lane) for value in pair]
+                pair = [shift_y(value, cy, lane, row, block) for value in pair]
             if cz:
                 pair = [shift_z(pair[kz], pair[1 - kz], cz, lane) for kz in range(NB)]
             return pair
 
-        for i in range(planes):
-            for p in range(Q):
-                pair = passed([lattice[p, i, kz] for kz in range(NB)], p)
-                for kz in range(NB):
-                    ready[p, i, kz] = pair[kz]
+        for p in range(Q):
+            pair = passed([lattice[p, kz] for kz in range(NB)], p)
             for kz in range(NB):
-                after = collide([ready[p, i, kz] for p in range(Q)], lattice[Q, i, kz] > 0.5)
+                ready[p, kz] = pair[kz]
+        for kz in range(NB):
+            for start in range(0, rows, 16):
+                here = pl.ds(start, 16)
+                after = collide(
+                    [ready[p, kz, here, :] for p in range(Q)], lattice[Q, kz, here, :] > 0.5
+                )
                 for p in range(Q):
-                    lattice[p, i, kz] = after[p]
-            for p in range(Q):
-                pair = passed([lattice[p, i, kz] for kz in range(NB)], p)
-                for kz in range(NB):
-                    ready[p, i, kz] = pair[kz]
+                    lattice[p, kz, here, :] = after[p]
+        for p in range(Q):
+            pair = passed([lattice[p, kz] for kz in range(NB)], p)
+            for kz in range(NB):
+                ready[p, kz] = pair[kz]
         for d in range(owners):
-            for t in range(NB):
-                usual = final(d, t, 0)
-                at_usual = seat(usual)
-                at_below = seat(jnp.where(first, final(d, t, 1), usual))
-                at_above = seat(jnp.where(last, final(d, t, 2), usual))
+            for t, (kz, y) in enumerate(seats(final(d, 0))):
                 for p in range(Q):
-                    cx = VELOCITIES[p][0]
-                    for i in range(planes):
-                        kz, y = at_usual
-                        if cx == 1 and i == planes - 1:
-                            kz, y = at_above
-                        if cx == -1 and i == 0:
-                            kz, y = at_below
-                        outs[d][pl.ds(p * share + i * PLANE + t, PLANE_ROWS, stride=NB), :] = ready[
-                            p, i, kz, pl.ds(y, PLANE_ROWS), :
-                        ]
+                    outs[d][pl.ds(p * share + t, block, stride=NB), :] = ready[
+                        p, kz, pl.ds(y, block), :
+                    ]
+
+        def bring_back(chosen, i):
+            for d in range(owners):
+                for t, (kz, y) in enumerate(seats(final(d, other))):
+                    for p in chosen:
+                        outs[d][
+                            pl.ds(p * share + i * PLANE + t, PLANE_ROWS, stride=NB), :
+                        ] = ready[p, kz, pl.ds(y + i * PLANE_ROWS, PLANE_ROWS), :]
+
+        @pl.when(last)
+        def _():
+            bring_back(UPWARD, planes - 1)
+
+        @pl.when(first)
+        def _():
+            bring_back(DOWNWARD, 0)
 
     def crossing_kernel(*refs):
         got = [refs[slot_of[d]] for d in range(owners)]
@@ -381,7 +403,7 @@
     def padded(count):
         return shape(count, 8 + WHOLE + 8, LANES)
 
-    work = pltpu.VMEM((Q + 1, planes, NB, rows, LANES), f32)
+    work = pltpu.VMEM((Q + 1, NB, rows, LANES), f32)
     small, large = 100_000, 4_000_000
 
     def shards(populations, solid_mask, slot_blocks, swap_slots):

time: 51.2 us -> 50.5 us (0.986)
  waiting for transfers between devices: 17.8 us -> 13.9 us
  starting transfers between devices: 26.6 us -> 30 us
    ppermute x14, waiting for transfers between devices: 15 us -> 11.1 us  [exchange(): lax.ppermute(parts[n], 'gx', [(g, g ^ order[n]) for g in range(owners)])]
    ppermute x14, starting transfers between devices: 21.8 us -> 25.2 us  [exchange(): lax.ppermute(parts[n], 'gx', [(g, g ^ order[n]) for g in range(owners)])]
  transfers between devices with their start and end apart: 18 -> 18, of which waited for: 6 -> 9; matrix products, arithmetic and copies ran while one was open for 0% -> 0% of each run, Pallas kernels for 1% -> 1%
where the time goes in v9:
time: 50.5 us; the launch traced here: 50.3 us
  starting transfers between devices  30 us (59%)
  waiting for transfers between devices  13.9 us (28%)
  Pallas kernels  6.3 us (12%)
    ppermute x14, starting transfers between devices, exchange(): lax.ppermute(parts[n], 'gx', [(g, g ^ order[n]) for g in range(owners)])  25.2 us
    ppermute x14, waiting for transfers between devices, exchange(): lax.ppermute(parts[n], 'gx', [(g, g ^ order[n]) for g in range(owners)])  11.1 us
    pallas_call x7, Pallas kernels, call(): pl.pallas_call(kernel, out_shape=out_shape, in_specs=[spec] * len(inputs)...  6.3 us
    ppermute x2, starting transfers between devices, hop(): lax.ppermute(far, 'gy', list(enumerate(behind)))  4.22 us
    ppermute x2, waiting for transfers between devices, hop(): lax.ppermute(far, 'gy', list(enumerate(behind)))  2.8 us
  transfers between devices with their start and end apart: 18, of which 9 were waited for; matrix products, arithmetic and copies ran while one was open for 0% of the time, Pallas kernels for 1%

profile of v9, /device:TPU:0, one launch (start us, length us, event | category | flops | bytes accessed | tf_op | source)
XLA Modules:
  0.0 50.3 jit_solution(6777850113598803892)
XLA Ops:
  0.0 0.0 copy-start
  0.0 0.0 copy-start.1
  0.0 1.7 %edge_planes.1 = (f32[24,128]{1,0:T(8,128)}, f32[24,128]{1,0:T(8,128)}, f32[8,128]{1,0:T(8,128)}) custom-call(f32[19,64,128]{2,1,0:T(8,128)} %bitcast.26, s32[64,128]{1,0:T(8,128)} %bitcast.28, s32[1,2]{1,0:T(1,128)} %slots.1, s32[2,3]{1,0:T(2,128)} %bitcast.30), custom_call_target="tpu_custom_call" | custom-call | flops 100000 | bytes 100000 | tf_op jit(solution)/shard_map/edge_planes/pallas_call | solution.py:378
  1.7 0.5 %collective-permute-start = (f32[24,128]{1,0:T(8,128)}, f32[24,128]{1,0:T(8,128)S(1)}, u32[]{:S(2)}, u32[]{:S(2)}) collective-permute-start(f32[24,128]{1,0:T(8,128)} %get-tuple-element.27), channel_id=1, source_target_pairs={{0,1},{1,0},{2,3},{3,2},{4,5},{5,4},{6,7},{7,6},{8,9},{9,8},{10,11... | collective-permute-start | bytes 36872 | tf_op jit(solution)/shard_map/ppermute | solution.py:399
  2.2 2.6 %collective-permute-start.1 = (f32[24,128]{1,0:T(8,128)}, f32[24,128]{1,0:T(8,128)S(1)}, u32[]{:S(2)}, u32[]{:S(2)}) collective-permute-start(f32[24,128]{1,0:T(8,128)} %get-tuple-element.28), channel_id=1, source_target_pairs={{0,3},{1,2},{2,1},{3,0},{4,7},{5,6},{6,5},{7,4},{8,11},{9,10},{10,... | collective-permute-start | bytes 36872 | tf_op jit(solution)/shard_map/ppermute | solution.py:400
  4.9 0.0 copy-done
  4.9 0.0 copy-done.1
  4.9 0.0 copy-start.2
  4.9 0.2 first_collision.1.post
  5.1 0.0 collective-permute-done.near
  5.1 1.4 %collective-permute-done.1.far = f32[24,128]{1,0:T(8,128)S(1)} collective-permute-done((f32[24,128]{1,0:T(8,128)}, f32[24,128]{1,0:T(8,128)S(1)}, u32[]{:S(2)}, u32[]{:S(2)}) %collective-permute-start.1) | collective-permute-done | bytes 12320 | tf_op jit(solution)/shard_map/ppermute | solution.py:400
  6.5 0.0 copy-done.2
  6.5 0.2 pack_planes.1
  6.7 2.8 %collective-permute-start.2 = (f32[168,128]{1,0:T(8,128)S(1)}, f32[168,128]{1,0:T(8,128)S(1)}, u32[]{:S(2)}, u32[]{:S(2)}) collective-permute-start(f32[168,128]{1,0:T(8,128)S(1)} %get-tuple-element.30), channel_id=1, source_target_pairs={{0,16},{4,20},{8,24},{12,28},{16,0},{20,4},{24,8},{28,12},{1,17},{... | collective-permute-start | bytes 258056 | tf_op jit(solution)/shard_map/ppermute | solution.py:391
  9.5 1.5 %collective-permute-start.3 = (f32[168,128]{1,0:T(8,128)S(1)}, f32[168,128]{1,0:T(8,128)S(1)}, u32[]{:S(2)}, u32[]{:S(2)}) collective-permute-start(f32[168,128]{1,0:T(8,128)S(1)} %get-tuple-element.31), channel_id=1, source_target_pairs={{0,4},{4,0},{8,12},{12,8},{16,20},{20,16},{24,28},{28,24},{1,5},{5... | collective-permute-start | bytes 258056 | tf_op jit(solution)/shard_map/ppermute | solution.py:391
  11.0 0.1 collective-permute-start.4
  11.1 1.7 %collective-permute-start.5 = (f32[168,128]{1,0:T(8,128)S(1)}, f32[168,128]{1,0:T(8,128)S(1)}, u32[]{:S(2)}, u32[]{:S(2)}) collective-permute-start(f32[168,128]{1,0:T(8,128)S(1)} %get-tuple-element.33), channel_id=1, source_target_pairs={{0,8},{4,12},{8,0},{12,4},{16,24},{20,28},{24,16},{28,20},{1,9},{5... | collective-permute-start | bytes 258056 | tf_op jit(solution)/shard_map/ppermute | solution.py:391
  12.9 2.5 %collective-permute-start.6 = (f32[168,128]{1,0:T(8,128)S(1)}, f32[168,128]{1,0:T(8,128)S(1)}, u32[]{:S(2)}, u32[]{:S(2)}) collective-permute-start(f32[168,128]{1,0:T(8,128)S(1)} %get-tuple-element.34), channel_id=1, source_target_pairs={{0,24},{4,28},{8,16},{12,20},{16,8},{20,12},{24,0},{28,4},{1,25},{... | collective-permute-start | bytes 258056 | tf_op jit(solution)/shard_map/ppermute | solution.py:391
  15.4 0.0 collective-permute-done.2.refs_1_
  15.4 7.5 %collective-permute-start.7 = (f32[168,128]{1,0:T(8,128)S(1)}, f32[168,128]{1,0:T(8,128)S(1)}, u32[]{:S(2)}, u32[]{:S(2)}) collective-permute-start(f32[168,128]{1,0:T(8,128)S(1)} %get-tuple-element.35), channel_id=1, source_target_pairs={{0,28},{4,24},{8,20},{12,16},{16,12},{20,8},{24,4},{28,0},{1,29},{... | collective-permute-start | bytes 258056 | tf_op jit(solution)/shard_map/ppermute | solution.py:391
  22.8 0.0 collective-permute-done.3.refs_2_
  22.8 0.0 collective-permute-start.8
  22.8 0.0 collective-permute-done.4.refs_3_
  22.8 0.0 collective-permute-done.5.refs_4_
  22.8 0.0 collective-permute-done.6.refs_5_
  22.8 2.6 %collective-permute-done.7.refs_6_ = f32[168,128]{1,0:T(8,128)S(1)} collective-permute-done((f32[168,128]{1,0:T(8,128)S(1)}, f32[168,128]{1,0:T(8,128)S(1)}, u32[]{:S(2)}, u32[]{:S(2)}) %collective-permute-start.7) | collective-permute-done | bytes 86048 | tf_op jit(solution)/shard_map/ppermute | solution.py:391
  25.5 2.7 %collective-permute-done.8.refs_7_ = f32[168,128]{1,0:T(8,128)S(1)} collective-permute-done((f32[168,128]{1,0:T(8,128)S(1)}, f32[168,128]{1,0:T(8,128)S(1)}, u32[]{:S(2)}, u32[]{:S(2)}) %collective-permute-start.8) | collective-permute-done | bytes 86048 | tf_op jit(solution)/shard_map/ppermute | solution.py:391
  28.2 3.2 %second_step.1 = (f32[152,128]{1,0:T(8,128)S(1)}, f32[152,128]{1,0:T(8,128)S(1)}, f32[152,128]{1,0:T(8,128)S(1)}, f32[152,128]{1,0:T(8,128)S(1)}, f32[152,128]{1...) custom-call(f32[168,128]{1,0:T(8,128)S(1)} %get-tuple-element.29.refs_0_, ...), custom_call_target="tpu_custom_call" | custom-call | flops 4000000 | bytes 4000000 | tf_op jit(solution)/shard_map/second_step/pallas_call | solution.py:378
  31.4 0.6 %collective-permute-start.9 = (f32[152,128]{1,0:T(8,128)S(1)}, f32[152,128]{1,0:T(8,128)S(1)}, u32[]{:S(2)}, u32[]{:S(2)}) collective-permute-start(f32[152,128]{1,0:T(8,128)S(1)} %get-tuple-element.38), channel_id=1, source_target_pairs={{0,16},{4,20},{8,24},{12,28},{16,0},{20,4},{24,8},{28,12},{1,17},{... | collective-permute-start | bytes 233480 | tf_op jit(solution)/shard_map/ppermute | solution.py:391
  32.0 0.0 collective-permute-start.10
  32.0 3.8 %collective-permute-start.11 = (f32[152,128]{1,0:T(8,128)S(1)}, f32[152,128]{1,0:T(8,128)S(1)}, u32[]{:S(2)}, u32[]{:S(2)}) collective-permute-start(f32[152,128]{1,0:T(8,128)S(1)} %get-tuple-element.40), channel_id=1, source_target_pairs={{0,20},{4,16},{8,28},{12,24},{16,4},{20,0},{24,12},{28,8},{1,21},{... | collective-permute-start | bytes 233480 | tf_op jit(solution)/shard_map/ppermute | solution.py:391
  35.8 0.0 collective-permute-start.12
  35.8 2.0 %collective-permute-start.13 = (f32[152,128]{1,0:T(8,128)S(1)}, f32[152,128]{1,0:T(8,128)S(1)}, u32[]{:S(2)}, u32[]{:S(2)}) collective-permute-start(f32[152,128]{1,0:T(8,128)S(1)} %get-tuple-element.42), channel_id=1, source_target_pairs={{0,24},{4,28},{8,16},{12,20},{16,8},{20,12},{24,0},{28,4},{1,25},{... | collective-permute-start | bytes 233480 | tf_op jit(solution)/shard_map/ppermute | solution.py:391
  37.8 0.3 collective-permute-done.9.refs_1_
  38.1 2.0 %collective-permute-start.14 = (f32[152,128]{1,0:T(8,128)S(1)}, f32[152,128]{1,0:T(8,128)S(1)}, u32[]{:S(2)}, u32[]{:S(2)}) collective-permute-start(f32[152,128]{1,0:T(8,128)S(1)} %get-tuple-element.43), channel_id=1, source_target_pairs={{0,28},{4,24},{8,20},{12,16},{16,12},{20,8},{24,4},{28,0},{1,29},{... | collective-permute-start | bytes 233480 | tf_op jit(solution)/shard_map/ppermute | solution.py:391
  40.1 0.0 collective-permute-done.10.refs_2_
  40.1 0.6 %collective-permute-start.15 = (f32[152,128]{1,0:T(8,128)S(1)}, f32[152,128]{1,0:T(8,128)S(1)}, u32[]{:S(2)}, u32[]{:S(2)}) collective-permute-start(f32[152,128]{1,0:T(8,128)S(1)} %get-tuple-element.44), channel_id=1, source_target_pairs={{0,12},{4,8},{8,4},{12,0},{16,28},{20,24},{24,20},{28,16},{1,13},{... | collective-permute-start | bytes 233480 | tf_op jit(solution)/shard_map/ppermute | solution.py:391
  40.8 0.6 %collective-permute-done.11.refs_3_ = f32[152,128]{1,0:T(8,128)S(1)} collective-permute-done((f32[152,128]{1,0:T(8,128)S(1)}, f32[152,128]{1,0:T(8,128)S(1)}, u32[]{:S(2)}, u32[]{:S(2)}) %collective-permute-start.11) | collective-permute-done | bytes 77856 | tf_op jit(solution)/shard_map/ppermute | solution.py:391
  41.3 2.3 %collective-permute-done.12.refs_4_ = f32[152,128]{1,0:T(8,128)S(1)} collective-permute-done((f32[152,128]{1,0:T(8,128)S(1)}, f32[152,128]{1,0:T(8,128)S(1)}, u32[]{:S(2)}, u32[]{:S(2)}) %collective-permute-start.12) | collective-permute-done | bytes 77856 | tf_op jit(solution)/shard_map/ppermute | solution.py:391
  43.6 0.0 collective-permute-done.13.refs_5_
  43.6 1.8 %collective-permute-done.14.refs_6_ = f32[152,128]{1,0:T(8,128)S(1)} collective-permute-done((f32[152,128]{1,0:T(8,128)S(1)}, f32[152,128]{1,0:T(8,128)S(1)}, u32[]{:S(2)}, u32[]{:S(2)}) %collective-permute-start.14) | collective-permute-done | bytes 77856 | tf_op jit(solution)/shard_map/ppermute | solution.py:391
  45.4 0.8 %collective-permute-done.15.refs_7_ = f32[152,128]{1,0:T(8,128)S(1)} collective-permute-done((f32[152,128]{1,0:T(8,128)S(1)}, f32[152,128]{1,0:T(8,128)S(1)}, u32[]{:S(2)}, u32[]{:S(2)}) %collective-permute-start.15) | collective-permute-done | bytes 77856 | tf_op jit(solution)/shard_map/ppermute | solution.py:391
  46.2 0.1 collective-permute-start.16
  46.3 1.6 %collective-permute-start.17 = (f32[24,128]{1,0:T(8,128)S(1)}, f32[24,128]{1,0:T(8,128)S(1)}, u32[]{:S(2)}, u32[]{:S(2)}) collective-permute-start(f32[24,128]{1,0:T(8,128)S(1)} %get-tuple-element.46), channel_id=1, source_target_pairs={{0,3},{1,2},{2,1},{3,0},{4,7},{5,6},{6,5},{7,4},{8,11},{9,10},{10,... | collective-permute-start | bytes 36872 | tf_op jit(solution)/shard_map/ppermute | solution.py:400
  47.9 0.1 unpack_planes.1.main
  48.0 0.0 collective-permute-done.16.near
  48.0 1.4 %collective-permute-done.17.far = f32[24,128]{1,0:T(8,128)S(1)} collective-permute-done((f32[24,128]{1,0:T(8,128)S(1)}, f32[24,128]{1,0:T(8,128)S(1)}, u32[]{:S(2)}, u32[]{:S(2)}) %collective-permute-start.17) | collective-permute-done | bytes 12320 | tf_op jit(solution)/shard_map/ppermute | solution.py:400
  49.5 0.9 %finish.1 = f32[1216,128]{1,0:T(8,128)} custom-call(f32[19,80,128]{2,1,0:T(8,128)S(1)} %unpack_planes.1.main, f32[24,128]{1,0:T(8,128)S(1)} %collective-permute-done.16.near, f32[24,128]{1,0:T(8,128)S(1)} %collective-permute-done.17.far), custom_call_target="tpu_custom_call" | custom-call | flops 100000 | bytes 100000 | tf_op jit(solution)/shard_map/finish/pallas_call | solution.py:378
  (1 shorter events, 0.0 us)
Async XLA Ops:
  0.0 4.9 %copy-start = (f32[1,2,19,4096]{3,1,2,0:T(2,128)S(1)}, f32[1,2,19,4096]{3,1,2,0:T(2,128)}, u32[]{:S(2)}) copy-start(f32[1,2,19,4096]{3,1,2,0:T(2,128)} %param.4) | copy-start | bytes 1867780
  0.0 4.9 %copy-start.1 = (s32[1,2,4096]{2,1,0:T(2,128)S(1)}, s32[1,2,4096]{2,1,0:T(2,128)}, u32[]{:S(2)}) copy-start(s32[1,2,4096]{2,1,0:T(2,128)} %param.5) | copy-start | bytes 98308
  1.7 3.4 %collective-permute-start = (f32[24,128]{1,0:T(8,128)}, f32[24,128]{1,0:T(8,128)S(1)}, u32[]{:S(2)}, u32[]{:S(2)}) collective-permute-start(f32[24,128]{1,0:T(8,128)} %get-tuple-element.27), channel_id=1, source_target_pairs={{0,1},{1,0},{2,3},{3,2},{4,5},{5,4},{6,7},{7,6},{8,9},{9,8},{10,11... | collective-permute-start | bytes 36872 | tf_op jit(solution)/shard_map/ppermute | solution.py:399
  2.2 4.2 %collective-permute-start.1 = (f32[24,128]{1,0:T(8,128)}, f32[24,128]{1,0:T(8,128)S(1)}, u32[]{:S(2)}, u32[]{:S(2)}) collective-permute-start(f32[24,128]{1,0:T(8,128)} %get-tuple-element.28), channel_id=1, source_target_pairs={{0,3},{1,2},{2,1},{3,0},{4,7},{5,6},{6,5},{7,4},{8,11},{9,10},{10,... | collective-permute-start | bytes 36872 | tf_op jit(solution)/shard_map/ppermute | solution.py:400
  4.9 1.6 %copy-start.2 = (f32[8,128]{1,0:T(8,128)S(1)}, f32[8,128]{1,0:T(8,128)}, u32[]{:S(2)}) copy-start(f32[8,128]{1,0:T(8,128)} %get-tuple-element.26.own) | copy-start | bytes 12292
  6.7 8.7 %collective-permute-start.2 = (f32[168,128]{1,0:T(8,128)S(1)}, f32[168,128]{1,0:T(8,128)S(1)}, u32[]{:S(2)}, u32[]{:S(2)}) collective-permute-start(f32[168,128]{1,0:T(8,128)S(1)} %get-tuple-element.30), channel_id=1, source_target_pairs={{0,16},{4,20},{8,24},{12,28},{16,0},{20,4},{24,8},{28,12},{1,17},{... | collective-permute-start | bytes 258056 | tf_op jit(solution)/shard_map/ppermute | solution.py:391
  9.5 13.3 %collective-permute-start.3 = (f32[168,128]{1,0:T(8,128)S(1)}, f32[168,128]{1,0:T(8,128)S(1)}, u32[]{:S(2)}, u32[]{:S(2)}) collective-permute-start(f32[168,128]{1,0:T(8,128)S(1)} %get-tuple-element.31), channel_id=1, source_target_pairs={{0,4},{4,0},{8,12},{12,8},{16,20},{20,16},{24,28},{28,24},{1,5},{5... | collective-permute-start | bytes 258056 | tf_op jit(solution)/shard_map/ppermute | solution.py:391
  11.0 11.8 %collective-permute-start.4 = (f32[168,128]{1,0:T(8,128)S(1)}, f32[168,128]{1,0:T(8,128)S(1)}, u32[]{:S(2)}, u32[]{:S(2)}) collective-permute-start(f32[168,128]{1,0:T(8,128)S(1)} %get-tuple-element.32), channel_id=1, source_target_pairs={{0,20},{4,16},{8,28},{12,24},{16,4},{20,0},{24,12},{28,8},{1,21},{... | collective-permute-start | bytes 258056 | tf_op jit(solution)/shard_map/ppermute | solution.py:391
  11.1 11.7 %collective-permute-start.5 = (f32[168,128]{1,0:T(8,128)S(1)}, f32[168,128]{1,0:T(8,128)S(1)}, u32[]{:S(2)}, u32[]{:S(2)}) collective-permute-start(f32[168,128]{1,0:T(8,128)S(1)} %get-tuple-element.33), channel_id=1, source_target_pairs={{0,8},{4,12},{8,0},{12,4},{16,24},{20,28},{24,16},{28,20},{1,9},{5... | collective-permute-start | bytes 258056 | tf_op jit(solution)/shard_map/ppermute | solution.py:391
  12.9 10.0 %collective-permute-start.6 = (f32[168,128]{1,0:T(8,128)S(1)}, f32[168,128]{1,0:T(8,128)S(1)}, u32[]{:S(2)}, u32[]{:S(2)}) collective-permute-start(f32[168,128]{1,0:T(8,128)S(1)} %get-tuple-element.34), channel_id=1, source_target_pairs={{0,24},{4,28},{8,16},{12,20},{16,8},{20,12},{24,0},{28,4},{1,25},{... | collective-permute-start | bytes 258056 | tf_op jit(solution)/shard_map/ppermute | solution.py:391
  15.4 10.1 %collective-permute-start.7 = (f32[168,128]{1,0:T(8,128)S(1)}, f32[168,128]{1,0:T(8,128)S(1)}, u32[]{:S(2)}, u32[]{:S(2)}) collective-permute-start(f32[168,128]{1,0:T(8,128)S(1)} %get-tuple-element.35), channel_id=1, source_target_pairs={{0,28},{4,24},{8,20},{12,16},{16,12},{20,8},{24,4},{28,0},{1,29},{... | collective-permute-start | bytes 258056 | tf_op jit(solution)/shard_map/ppermute | solution.py:391
  22.8 5.4 %collective-permute-start.8 = (f32[168,128]{1,0:T(8,128)S(1)}, f32[168,128]{1,0:T(8,128)S(1)}, u32[]{:S(2)}, u32[]{:S(2)}) collective-permute-start(f32[168,128]{1,0:T(8,128)S(1)} %get-tuple-element.36), channel_id=1, source_target_pairs={{0,12},{4,8},{8,4},{12,0},{16,28},{20,24},{24,20},{28,16},{1,13},{... | collective-permute-start | bytes 258056 | tf_op jit(solution)/shard_map/ppermute | solution.py:391
  31.4 6.8 %collective-permute-start.9 = (f32[152,128]{1,0:T(8,128)S(1)}, f32[152,128]{1,0:T(8,128)S(1)}, u32[]{:S(2)}, u32[]{:S(2)}) collective-permute-start(f32[152,128]{1,0:T(8,128)S(1)} %get-tuple-element.38), channel_id=1, source_target_pairs={{0,16},{4,20},{8,24},{12,28},{16,0},{20,4},{24,8},{28,12},{1,17},{... | collective-permute-start | bytes 233480 | tf_op jit(solution)/shard_map/ppermute | solution.py:391
  32.0 8.1 %collective-permute-start.10 = (f32[152,128]{1,0:T(8,128)S(1)}, f32[152,128]{1,0:T(8,128)S(1)}, u32[]{:S(2)}, u32[]{:S(2)}) collective-permute-start(f32[152,128]{1,0:T(8,128)S(1)} %get-tuple-element.39), channel_id=1, source_target_pairs={{0,4},{4,0},{8,12},{12,8},{16,20},{20,16},{24,28},{28,24},{1,5},{5... | collective-permute-start | bytes 233480 | tf_op jit(solution)/shard_map/ppermute | solution.py:391
  32.0 9.3 %collective-permute-start.11 = (f32[152,128]{1,0:T(8,128)S(1)}, f32[152,128]{1,0:T(8,128)S(1)}, u32[]{:S(2)}, u32[]{:S(2)}) collective-permute-start(f32[152,128]{1,0:T(8,128)S(1)} %get-tuple-element.40), channel_id=1, source_target_pairs={{0,20},{4,16},{8,28},{12,24},{16,4},{20,0},{24,12},{28,8},{1,21},{... | collective-permute-start | bytes 233480 | tf_op jit(solution)/shard_map/ppermute | solution.py:391
  35.8 7.8 %collective-permute-start.12 = (f32[152,128]{1,0:T(8,128)S(1)}, f32[152,128]{1,0:T(8,128)S(1)}, u32[]{:S(2)}, u32[]{:S(2)}) collective-permute-start(f32[152,128]{1,0:T(8,128)S(1)} %get-tuple-element.41), channel_id=1, source_target_pairs={{0,8},{4,12},{8,0},{12,4},{16,24},{20,28},{24,16},{28,20},{1,9},{5... | collective-permute-start | bytes 233480 | tf_op jit(solution)/shard_map/ppermute | solution.py:391
  35.8 7.8 %collective-permute-start.13 = (f32[152,128]{1,0:T(8,128)S(1)}, f32[152,128]{1,0:T(8,128)S(1)}, u32[]{:S(2)}, u32[]{:S(2)}) collective-permute-start(f32[152,128]{1,0:T(8,128)S(1)} %get-tuple-element.42), channel_id=1, source_target_pairs={{0,24},{4,28},{8,16},{12,20},{16,8},{20,12},{24,0},{28,4},{1,25},{... | collective-permute-start | bytes 233480 | tf_op jit(solution)/shard_map/ppermute | solution.py:391
  38.1 7.3 %collective-permute-start.14 = (f32[152,128]{1,0:T(8,128)S(1)}, f32[152,128]{1,0:T(8,128)S(1)}, u32[]{:S(2)}, u32[]{:S(2)}) collective-permute-start(f32[152,128]{1,0:T(8,128)S(1)} %get-tuple-element.43), channel_id=1, source_target_pairs={{0,28},{4,24},{8,20},{12,16},{16,12},{20,8},{24,4},{28,0},{1,29},{... | collective-permute-start | bytes 233480 | tf_op jit(solution)/shard_map/ppermute | solution.py:391
  40.1 6.0 %collective-permute-start.15 = (f32[152,128]{1,0:T(8,128)S(1)}, f32[152,128]{1,0:T(8,128)S(1)}, u32[]{:S(2)}, u32[]{:S(2)}) collective-permute-start(f32[152,128]{1,0:T(8,128)S(1)} %get-tuple-element.44), channel_id=1, source_target_pairs={{0,12},{4,8},{8,4},{12,0},{16,28},{20,24},{24,20},{28,16},{1,13},{... | collective-permute-start | bytes 233480 | tf_op jit(solution)/shard_map/ppermute | solution.py:391
  46.2 1.8 %collective-permute-start.16 = (f32[24,128]{1,0:T(8,128)S(1)}, f32[24,128]{1,0:T(8,128)S(1)}, u32[]{:S(2)}, u32[]{:S(2)}) collective-permute-start(f32[24,128]{1,0:T(8,128)S(1)} %get-tuple-element.45), channel_id=1, source_target_pairs={{0,1},{1,0},{2,3},{3,2},{4,5},{5,4},{6,7},{7,6},{8,9},{9,8},{10,11... | collective-permute-start | bytes 36872 | tf_op jit(solution)/shard_map/ppermute | solution.py:399
  46.3 3.2 %collective-permute-start.17 = (f32[24,128]{1,0:T(8,128)S(1)}, f32[24,128]{1,0:T(8,128)S(1)}, u32[]{:S(2)}, u32[]{:S(2)}) collective-permute-start(f32[24,128]{1,0:T(8,128)S(1)} %get-tuple-element.46), channel_id=1, source_target_pairs={{0,3},{1,2},{2,1},{3,0},{4,7},{5,6},{6,5},{7,4},{8,11},{9,10},{10,... | collective-permute-start | bytes 36872 | tf_op jit(solution)/shard_map/ppermute | solution.py:400

commit v10 on v9

--- a/solution.py
+++ b/solution.py
@@ -140,8 +140,12 @@
     f32 = jnp.float32
 
     half = owners // 2
-    order = [0, half, 1, half + 1, 2, *range(half + 2, owners), *range(3, half)]
-    slot_of = [order.index(d) for d in range(owners)]
+    spare = [*range(half + 2, owners), *range(4, half), 1]
+    order_in = [0, 2, half, 3, half + 1, *spare]
+    order_out = [0, half, 2, half + 1, 3, *spare]
+
+    def by_owner(refs, order):
+        return [refs[order.index(d)] for d in range(owners)]
 
     def position():
         me = lax.axis_index("gx")
@@ -193,8 +197,9 @@
     def pack_kernel(post, own, near, far, *outs):
         me, odd = position()
         below, above = sides(odd, near, far)
+        outs = by_owner(outs, order_in)
         for d in range(owners):
-            out = outs[slot_of[d]]
+            out = outs[d]
             place = dynamic_place(me ^ d, odd, owners)
             here = pl.multiple_of(place * share, min(share, 8))
             for p in range(Q + 1):
@@ -218,8 +223,8 @@
                     ]
 
     def middle_kernel(*refs):
-        got = [refs[slot_of[d]] for d in range(owners)]
-        outs = [refs[owners + slot_of[d]] for d in range(owners)]
+        got = by_owner(refs[:owners], order_in)
+        outs = by_owner(refs[owners : 2 * owners], order_out)
         lattice, ready, table, sem = refs[2 * owners :]
         me, odd = position()
         place = dynamic_place(me, odd, owners)
@@ -327,7 +332,7 @@
             bring_back(DOWNWARD, 0)
 
     def crossing_kernel(*refs):
-        got = [refs[slot_of[d]] for d in range(owners)]
+        got = by_owner(refs[:owners], order_out)
         near, far, up, down = refs[owners:]
         me, odd = position()
         for d in range(owners):
@@ -350,7 +355,7 @@
         send_sides(odd, up, down, near, far)
 
     def unpack_kernel(*refs):
-        got, main = [refs[slot_of[d]] for d in range(owners)], refs[owners]
+        got, main = by_owner(refs[:owners], order_out), refs[owners]
         me, odd = position()
         for d in range(owners):
             place = dynamic_place(me ^ d, odd, owners)
@@ -386,7 +391,7 @@
             name=name,
         )(*inputs)
 
-    def exchange(parts):
+    def exchange(parts, order):
         return [parts[0]] + [
             lax.ppermute(parts[n], "gx", [(g, g ^ order[n]) for g in range(owners)])
             for n in range(1, owners)
@@ -446,7 +451,7 @@
             (post, own, near, far),
             large,
         )
-        got = exchange(parts)
+        got = exchange(parts, order_in)
         parts = call(
             middle_kernel,
             "second_step",
@@ -460,7 +465,7 @@
                 pltpu.SemaphoreType.DMA((owners,)),
             ),
         )
-        home = exchange(parts)
+        home = exchange(parts, order_out)
         near, far = call(
             crossing_kernel,
             "crossing_planes",

time: 50.5 us -> 49.1 us (0.972)
  starting transfers between devices: 30 us -> 28.7 us
    ppermute x14, starting transfers between devices: 25.2 us -> 23.9 us  [exchange(): lax.ppermute(parts[n], 'gx', [(g, g ^ order[n]) for g in range(owners)])]
  transfers between devices with their start and end apart: 18 -> 18, of which waited for: 9 -> 6; matrix products, arithmetic and copies ran while one was open for 0% -> 0% of each run, Pallas kernels for 1% -> 1%
where the time goes in v10:
time: 49.1 us; the launch traced here: 49 us
  starting transfers between devices  28.7 us (58%)
  waiting for transfers between devices  13.9 us (28%)
  Pallas kernels  6.33 us (13%)
    ppermute x14, starting transfers between devices, exchange(): lax.ppermute(parts[n], 'gx', [(g, g ^ order[n]) for g in range(owners)])  23.9 us
    ppermute x14, waiting for transfers between devices, exchange(): lax.ppermute(parts[n], 'gx', [(g, g ^ order[n]) for g in range(owners)])  11.1 us
    pallas_call x7, Pallas kernels, call(): pl.pallas_call(kernel, out_shape=out_shape, in_specs=[spec] * len(inputs)...  6.33 us
    ppermute x2, starting transfers between devices, hop(): lax.ppermute(far, 'gy', list(enumerate(behind)))  4.22 us
    ppermute x2, waiting for transfers between devices, hop(): lax.ppermute(far, 'gy', list(enumerate(behind)))  2.8 us
  transfers between devices with their start and end apart: 18, of which 6 were waited for; matrix products, arithmetic and copies ran while one was open for 0% of the time, Pallas kernels for 1%

profile of v10, /device:TPU:0, one launch (start us, length us, event | category | flops | bytes accessed | tf_op | source)
XLA Modules:
  0.0 49.0 jit_solution(4607482275294475354)
XLA Ops:
  0.0 0.0 copy-start
  0.0 0.0 copy-start.1
  0.0 1.7 %edge_planes.1 = (f32[24,128]{1,0:T(8,128)}, f32[24,128]{1,0:T(8,128)}, f32[8,128]{1,0:T(8,128)}) custom-call(f32[19,64,128]{2,1,0:T(8,128)} %bitcast.26, s32[64,128]{1,0:T(8,128)} %bitcast.28, s32[1,2]{1,0:T(1,128)} %slots.1, s32[2,3]{1,0:T(2,128)} %bitcast.30), custom_call_target="tpu_custom_call" | custom-call | flops 100000 | bytes 100000 | tf_op jit(solution)/shard_map/edge_planes/pallas_call | solution.py:383
  1.7 0.5 %collective-permute-start = (f32[24,128]{1,0:T(8,128)}, f32[24,128]{1,0:T(8,128)S(1)}, u32[]{:S(2)}, u32[]{:S(2)}) collective-permute-start(f32[24,128]{1,0:T(8,128)} %get-tuple-element.27), channel_id=1, source_target_pairs={{0,1},{1,0},{2,3},{3,2},{4,5},{5,4},{6,7},{7,6},{8,9},{9,8},{10,11... | collective-permute-start | bytes 36872 | tf_op jit(solution)/shard_map/ppermute | solution.py:404
  2.2 2.6 %collective-permute-start.1 = (f32[24,128]{1,0:T(8,128)}, f32[24,128]{1,0:T(8,128)S(1)}, u32[]{:S(2)}, u32[]{:S(2)}) collective-permute-start(f32[24,128]{1,0:T(8,128)} %get-tuple-element.28), channel_id=1, source_target_pairs={{0,3},{1,2},{2,1},{3,0},{4,7},{5,6},{6,5},{7,4},{8,11},{9,10},{10,... | collective-permute-start | bytes 36872 | tf_op jit(solution)/shard_map/ppermute | solution.py:405
  4.9 0.0 copy-done
  4.9 0.0 copy-done.1
  4.9 0.0 copy-start.2
  4.9 0.2 first_collision.1.post
  5.1 0.0 collective-permute-done.near
  5.1 1.4 %collective-permute-done.1.far = f32[24,128]{1,0:T(8,128)S(1)} collective-permute-done((f32[24,128]{1,0:T(8,128)}, f32[24,128]{1,0:T(8,128)S(1)}, u32[]{:S(2)}, u32[]{:S(2)}) %collective-permute-start.1) | collective-permute-done | bytes 12320 | tf_op jit(solution)/shard_map/ppermute | solution.py:405
  6.5 0.0 copy-done.2
  6.5 0.2 pack_planes.1
  6.7 1.8 %collective-permute-start.2 = (f32[168,128]{1,0:T(8,128)S(1)}, f32[168,128]{1,0:T(8,128)S(1)}, u32[]{:S(2)}, u32[]{:S(2)}) collective-permute-start(f32[168,128]{1,0:T(8,128)S(1)} %get-tuple-element.30), channel_id=1, source_target_pairs={{0,8},{4,12},{8,0},{12,4},{16,24},{20,28},{24,16},{28,20},{1,9},{5... | collective-permute-start | bytes 258056 | tf_op jit(solution)/shard_map/ppermute | solution.py:396
  8.5 2.6 %collective-permute-start.3 = (f32[168,128]{1,0:T(8,128)S(1)}, f32[168,128]{1,0:T(8,128)S(1)}, u32[]{:S(2)}, u32[]{:S(2)}) collective-permute-start(f32[168,128]{1,0:T(8,128)S(1)} %get-tuple-element.31), channel_id=1, source_target_pairs={{0,16},{4,20},{8,24},{12,28},{16,0},{20,4},{24,8},{28,12},{1,17},{... | collective-permute-start | bytes 258056 | tf_op jit(solution)/shard_map/ppermute | solution.py:396
  11.1 1.4 %collective-permute-start.4 = (f32[168,128]{1,0:T(8,128)S(1)}, f32[168,128]{1,0:T(8,128)S(1)}, u32[]{:S(2)}, u32[]{:S(2)}) collective-permute-start(f32[168,128]{1,0:T(8,128)S(1)} %get-tuple-element.32), channel_id=1, source_target_pairs={{0,12},{4,8},{8,4},{12,0},{16,28},{20,24},{24,20},{28,16},{1,13},{... | collective-permute-start | bytes 258056 | tf_op jit(solution)/shard_map/ppermute | solution.py:396
  12.5 0.1 collective-permute-start.5
  12.6 3.8 %collective-permute-start.6 = (f32[168,128]{1,0:T(8,128)S(1)}, f32[168,128]{1,0:T(8,128)S(1)}, u32[]{:S(2)}, u32[]{:S(2)}) collective-permute-start(f32[168,128]{1,0:T(8,128)S(1)} %get-tuple-element.34), channel_id=1, source_target_pairs={{0,24},{4,28},{8,16},{12,20},{16,8},{20,12},{24,0},{28,4},{1,25},{... | collective-permute-start | bytes 258056 | tf_op jit(solution)/shard_map/ppermute | solution.py:396
  16.4 0.0 collective-permute-done.2.refs_1_
  16.4 1.6 %collective-permute-start.7 = (f32[168,128]{1,0:T(8,128)S(1)}, f32[168,128]{1,0:T(8,128)S(1)}, u32[]{:S(2)}, u32[]{:S(2)}) collective-permute-start(f32[168,128]{1,0:T(8,128)S(1)} %get-tuple-element.35), channel_id=1, source_target_pairs={{0,28},{4,24},{8,20},{12,16},{16,12},{20,8},{24,4},{28,0},{1,29},{... | collective-permute-start | bytes 258056 | tf_op jit(solution)/shard_map/ppermute | solution.py:396
  17.9 0.0 collective-permute-done.3.refs_2_
  17.9 0.5 %collective-permute-start.8 = (f32[168,128]{1,0:T(8,128)S(1)}, f32[168,128]{1,0:T(8,128)S(1)}, u32[]{:S(2)}, u32[]{:S(2)}) collective-permute-start(f32[168,128]{1,0:T(8,128)S(1)} %get-tuple-element.36), channel_id=1, source_target_pairs={{0,4},{4,0},{8,12},{12,8},{16,20},{20,16},{24,28},{28,24},{1,5},{5... | collective-permute-start | bytes 258056 | tf_op jit(solution)/shard_map/ppermute | solution.py:396
  18.4 0.0 collective-permute-done.4.refs_3_
  18.4 6.8 %collective-permute-done.5.refs_4_ = f32[168,128]{1,0:T(8,128)S(1)} collective-permute-done((f32[168,128]{1,0:T(8,128)S(1)}, f32[168,128]{1,0:T(8,128)S(1)}, u32[]{:S(2)}, u32[]{:S(2)}) %collective-permute-start.5) | collective-permute-done | bytes 86048 | tf_op jit(solution)/shard_map/ppermute | solution.py:396
  25.3 0.0 collective-permute-done.6.refs_5_
  25.3 0.0 collective-permute-done.7.refs_6_
  25.3 0.0 collective-permute-done.8.refs_7_
  25.3 3.2 %second_step.1 = (f32[152,128]{1,0:T(8,128)S(1)}, f32[152,128]{1,0:T(8,128)S(1)}, f32[152,128]{1,0:T(8,128)S(1)}, f32[152,128]{1,0:T(8,128)S(1)}, f32[152,128]{1...) custom-call(f32[168,128]{1,0:T(8,128)S(1)} %get-tuple-element.29.refs_0_, ...), custom_call_target="tpu_custom_call" | custom-call | flops 4000000 | bytes 4000000 | tf_op jit(solution)/shard_map/second_step/pallas_call | solution.py:383
  28.5 3.8 %collective-permute-start.9 = (f32[152,128]{1,0:T(8,128)S(1)}, f32[152,128]{1,0:T(8,128)S(1)}, u32[]{:S(2)}, u32[]{:S(2)}) collective-permute-start(f32[152,128]{1,0:T(8,128)S(1)} %get-tuple-element.38), channel_id=1, source_target_pairs={{0,16},{4,20},{8,24},{12,28},{16,0},{20,4},{24,8},{28,12},{1,17},{... | collective-permute-start | bytes 233480 | tf_op jit(solution)/shard_map/ppermute | solution.py:396
  32.3 0.0 collective-permute-start.10
  32.3 1.8 %collective-permute-start.11 = (f32[152,128]{1,0:T(8,128)S(1)}, f32[152,128]{1,0:T(8,128)S(1)}, u32[]{:S(2)}, u32[]{:S(2)}) collective-permute-start(f32[152,128]{1,0:T(8,128)S(1)} %get-tuple-element.40), channel_id=1, source_target_pairs={{0,20},{4,16},{8,28},{12,24},{16,4},{20,0},{24,12},{28,8},{1,21},{... | collective-permute-start | bytes 233480 | tf_op jit(solution)/shard_map/ppermute | solution.py:396
  34.1 1.2 %collective-permute-start.12 = (f32[152,128]{1,0:T(8,128)S(1)}, f32[152,128]{1,0:T(8,128)S(1)}, u32[]{:S(2)}, u32[]{:S(2)}) collective-permute-start(f32[152,128]{1,0:T(8,128)S(1)} %get-tuple-element.41), channel_id=1, source_target_pairs={{0,12},{4,8},{8,4},{12,0},{16,28},{20,24},{24,20},{28,16},{1,13},{... | collective-permute-start | bytes 233480 | tf_op jit(solution)/shard_map/ppermute | solution.py:396
  35.3 2.3 %collective-permute-start.13 = (f32[152,128]{1,0:T(8,128)S(1)}, f32[152,128]{1,0:T(8,128)S(1)}, u32[]{:S(2)}, u32[]{:S(2)}) collective-permute-start(f32[152,128]{1,0:T(8,128)S(1)} %get-tuple-element.42), channel_id=1, source_target_pairs={{0,24},{4,28},{8,16},{12,20},{16,8},{20,12},{24,0},{28,4},{1,25},{... | collective-permute-start | bytes 233480 | tf_op jit(solution)/shard_map/ppermute | solution.py:396
  37.6 0.0 collective-permute-done.9.refs_1_
  37.6 1.5 %collective-permute-start.14 = (f32[152,128]{1,0:T(8,128)S(1)}, f32[152,128]{1,0:T(8,128)S(1)}, u32[]{:S(2)}, u32[]{:S(2)}) collective-permute-start(f32[152,128]{1,0:T(8,128)S(1)} %get-tuple-element.43), channel_id=1, source_target_pairs={{0,28},{4,24},{8,20},{12,16},{16,12},{20,8},{24,4},{28,0},{1,29},{... | collective-permute-start | bytes 233480 | tf_op jit(solution)/shard_map/ppermute | solution.py:396
  39.1 0.0 collective-permute-done.10.refs_2_
  39.1 1.5 %collective-permute-start.15 = (f32[152,128]{1,0:T(8,128)S(1)}, f32[152,128]{1,0:T(8,128)S(1)}, u32[]{:S(2)}, u32[]{:S(2)}) collective-permute-start(f32[152,128]{1,0:T(8,128)S(1)} %get-tuple-element.44), channel_id=1, source_target_pairs={{0,4},{4,0},{8,12},{12,8},{16,20},{20,16},{24,28},{28,24},{1,5},{5... | collective-permute-start | bytes 233480 | tf_op jit(solution)/shard_map/ppermute | solution.py:396
  40.6 0.6 %collective-permute-done.11.refs_3_ = f32[152,128]{1,0:T(8,128)S(1)} collective-permute-done((f32[152,128]{1,0:T(8,128)S(1)}, f32[152,128]{1,0:T(8,128)S(1)}, u32[]{:S(2)}, u32[]{:S(2)}) %collective-permute-start.11) | collective-permute-done | bytes 77856 | tf_op jit(solution)/shard_map/ppermute | solution.py:396
  41.1 0.0 collective-permute-done.12.refs_4_
  41.1 1.6 %collective-permute-done.13.refs_5_ = f32[152,128]{1,0:T(8,128)S(1)} collective-permute-done((f32[152,128]{1,0:T(8,128)S(1)}, f32[152,128]{1,0:T(8,128)S(1)}, u32[]{:S(2)}, u32[]{:S(2)}) %collective-permute-start.13) | collective-permute-done | bytes 77856 | tf_op jit(solution)/shard_map/ppermute | solution.py:396
  42.7 2.0 %collective-permute-done.14.refs_6_ = f32[152,128]{1,0:T(8,128)S(1)} collective-permute-done((f32[152,128]{1,0:T(8,128)S(1)}, f32[152,128]{1,0:T(8,128)S(1)}, u32[]{:S(2)}, u32[]{:S(2)}) %collective-permute-start.14) | collective-permute-done | bytes 77856 | tf_op jit(solution)/shard_map/ppermute | solution.py:396
  44.8 0.0 collective-permute-done.15.refs_7_
  44.8 0.1 collective-permute-start.16
  44.9 1.6 %collective-permute-start.17 = (f32[24,128]{1,0:T(8,128)S(1)}, f32[24,128]{1,0:T(8,128)S(1)}, u32[]{:S(2)}, u32[]{:S(2)}) collective-permute-start(f32[24,128]{1,0:T(8,128)S(1)} %get-tuple-element.46), channel_id=1, source_target_pairs={{0,3},{1,2},{2,1},{3,0},{4,7},{5,6},{6,5},{7,4},{8,11},{9,10},{10,... | collective-permute-start | bytes 36872 | tf_op jit(solution)/shard_map/ppermute | solution.py:405
  46.5 0.1 unpack_planes.1.main
  46.6 0.0 collective-permute-done.16.near
  46.6 1.4 %collective-permute-done.17.far = f32[24,128]{1,0:T(8,128)S(1)} collective-permute-done((f32[24,128]{1,0:T(8,128)S(1)}, f32[24,128]{1,0:T(8,128)S(1)}, u32[]{:S(2)}, u32[]{:S(2)}) %collective-permute-start.17) | collective-permute-done | bytes 12320 | tf_op jit(solution)/shard_map/ppermute | solution.py:405
  48.1 0.9 %finish.1 = f32[1216,128]{1,0:T(8,128)} custom-call(f32[19,80,128]{2,1,0:T(8,128)S(1)} %unpack_planes.1.main, f32[24,128]{1,0:T(8,128)S(1)} %collective-permute-done.16.near, f32[24,128]{1,0:T(8,128)S(1)} %collective-permute-done.17.far), custom_call_target="tpu_custom_call" | custom-call | flops 100000 | bytes 100000 | tf_op jit(solution)/shard_map/finish/pallas_call | solution.py:383
  (1 shorter events, 0.0 us)
Async XLA Ops:
  0.0 4.9 %copy-start = (f32[1,2,19,4096]{3,1,2,0:T(2,128)S(1)}, f32[1,2,19,4096]{3,1,2,0:T(2,128)}, u32[]{:S(2)}) copy-start(f32[1,2,19,4096]{3,1,2,0:T(2,128)} %param.4) | copy-start | bytes 1867780
  0.0 4.9 %copy-start.1 = (s32[1,2,4096]{2,1,0:T(2,128)S(1)}, s32[1,2,4096]{2,1,0:T(2,128)}, u32[]{:S(2)}) copy-start(s32[1,2,4096]{2,1,0:T(2,128)} %param.5) | copy-start | bytes 98308
  1.7 3.4 %collective-permute-start = (f32[24,128]{1,0:T(8,128)}, f32[24,128]{1,0:T(8,128)S(1)}, u32[]{:S(2)}, u32[]{:S(2)}) collective-permute-start(f32[24,128]{1,0:T(8,128)} %get-tuple-element.27), channel_id=1, source_target_pairs={{0,1},{1,0},{2,3},{3,2},{4,5},{5,4},{6,7},{7,6},{8,9},{9,8},{10,11... | collective-permute-start | bytes 36872 | tf_op jit(solution)/shard_map/ppermute | solution.py:404
  2.2 4.2 %collective-permute-start.1 = (f32[24,128]{1,0:T(8,128)}, f32[24,128]{1,0:T(8,128)S(1)}, u32[]{:S(2)}, u32[]{:S(2)}) collective-permute-start(f32[24,128]{1,0:T(8,128)} %get-tuple-element.28), channel_id=1, source_target_pairs={{0,3},{1,2},{2,1},{3,0},{4,7},{5,6},{6,5},{7,4},{8,11},{9,10},{10,... | collective-permute-start | bytes 36872 | tf_op jit(solution)/shard_map/ppermute | solution.py:405
  4.9 1.6 %copy-start.2 = (f32[8,128]{1,0:T(8,128)S(1)}, f32[8,128]{1,0:T(8,128)}, u32[]{:S(2)}) copy-start(f32[8,128]{1,0:T(8,128)} %get-tuple-element.26.own) | copy-start | bytes 12292
  6.7 9.7 %collective-permute-start.2 = (f32[168,128]{1,0:T(8,128)S(1)}, f32[168,128]{1,0:T(8,128)S(1)}, u32[]{:S(2)}, u32[]{:S(2)}) collective-permute-start(f32[168,128]{1,0:T(8,128)S(1)} %get-tuple-element.30), channel_id=1, source_target_pairs={{0,8},{4,12},{8,0},{12,4},{16,24},{20,28},{24,16},{28,20},{1,9},{5... | collective-permute-start | bytes 258056 | tf_op jit(solution)/shard_map/ppermute | solution.py:396
  8.5 9.4 %collective-permute-start.3 = (f32[168,128]{1,0:T(8,128)S(1)}, f32[168,128]{1,0:T(8,128)S(1)}, u32[]{:S(2)}, u32[]{:S(2)}) collective-permute-start(f32[168,128]{1,0:T(8,128)S(1)} %get-tuple-element.31), channel_id=1, source_target_pairs={{0,16},{4,20},{8,24},{12,28},{16,0},{20,4},{24,8},{28,12},{1,17},{... | collective-permute-start | bytes 258056 | tf_op jit(solution)/shard_map/ppermute | solution.py:396
  11.1 7.3 %collective-permute-start.4 = (f32[168,128]{1,0:T(8,128)S(1)}, f32[168,128]{1,0:T(8,128)S(1)}, u32[]{:S(2)}, u32[]{:S(2)}) collective-permute-start(f32[168,128]{1,0:T(8,128)S(1)} %get-tuple-element.32), channel_id=1, source_target_pairs={{0,12},{4,8},{8,4},{12,0},{16,28},{20,24},{24,20},{28,16},{1,13},{... | collective-permute-start | bytes 258056 | tf_op jit(solution)/shard_map/ppermute | solution.py:396
  12.5 12.8 %collective-permute-start.5 = (f32[168,128]{1,0:T(8,128)S(1)}, f32[168,128]{1,0:T(8,128)S(1)}, u32[]{:S(2)}, u32[]{:S(2)}) collective-permute-start(f32[168,128]{1,0:T(8,128)S(1)} %get-tuple-element.33), channel_id=1, source_target_pairs={{0,20},{4,16},{8,28},{12,24},{16,4},{20,0},{24,12},{28,8},{1,21},{... | collective-permute-start | bytes 258056 | tf_op jit(solution)/shard_map/ppermute | solution.py:396
  12.6 12.7 %collective-permute-start.6 = (f32[168,128]{1,0:T(8,128)S(1)}, f32[168,128]{1,0:T(8,128)S(1)}, u32[]{:S(2)}, u32[]{:S(2)}) collective-permute-start(f32[168,128]{1,0:T(8,128)S(1)} %get-tuple-element.34), channel_id=1, source_target_pairs={{0,24},{4,28},{8,16},{12,20},{16,8},{20,12},{24,0},{28,4},{1,25},{... | collective-permute-start | bytes 258056 | tf_op jit(solution)/shard_map/ppermute | solution.py:396
  16.4 8.9 %collective-permute-start.7 = (f32[168,128]{1,0:T(8,128)S(1)}, f32[168,128]{1,0:T(8,128)S(1)}, u32[]{:S(2)}, u32[]{:S(2)}) collective-permute-start(f32[168,128]{1,0:T(8,128)S(1)} %get-tuple-element.35), channel_id=1, source_target_pairs={{0,28},{4,24},{8,20},{12,16},{16,12},{20,8},{24,4},{28,0},{1,29},{... | collective-permute-start | bytes 258056 | tf_op jit(solution)/shard_map/ppermute | solution.py:396
  17.9 7.4 %collective-permute-start.8 = (f32[168,128]{1,0:T(8,128)S(1)}, f32[168,128]{1,0:T(8,128)S(1)}, u32[]{:S(2)}, u32[]{:S(2)}) collective-permute-start(f32[168,128]{1,0:T(8,128)S(1)} %get-tuple-element.36), channel_id=1, source_target_pairs={{0,4},{4,0},{8,12},{12,8},{16,20},{20,16},{24,28},{28,24},{1,5},{5... | collective-permute-start | bytes 258056 | tf_op jit(solution)/shard_map/ppermute | solution.py:396
  28.5 9.1 %collective-permute-start.9 = (f32[152,128]{1,0:T(8,128)S(1)}, f32[152,128]{1,0:T(8,128)S(1)}, u32[]{:S(2)}, u32[]{:S(2)}) collective-permute-start(f32[152,128]{1,0:T(8,128)S(1)} %get-tuple-element.38), channel_id=1, source_target_pairs={{0,16},{4,20},{8,24},{12,28},{16,0},{20,4},{24,8},{28,12},{1,17},{... | collective-permute-start | bytes 233480 | tf_op jit(solution)/shard_map/ppermute | solution.py:396
  32.3 6.8 %collective-permute-start.10 = (f32[152,128]{1,0:T(8,128)S(1)}, f32[152,128]{1,0:T(8,128)S(1)}, u32[]{:S(2)}, u32[]{:S(2)}) collective-permute-start(f32[152,128]{1,0:T(8,128)S(1)} %get-tuple-element.39), channel_id=1, source_target_pairs={{0,8},{4,12},{8,0},{12,4},{16,24},{20,28},{24,16},{28,20},{1,9},{5... | collective-permute-start | bytes 233480 | tf_op jit(solution)/shard_map/ppermute | solution.py:396
  32.3 8.9 %collective-permute-start.11 = (f32[152,128]{1,0:T(8,128)S(1)}, f32[152,128]{1,0:T(8,128)S(1)}, u32[]{:S(2)}, u32[]{:S(2)}) collective-permute-start(f32[152,128]{1,0:T(8,128)S(1)} %get-tuple-element.40), channel_id=1, source_target_pairs={{0,20},{4,16},{8,28},{12,24},{16,4},{20,0},{24,12},{28,8},{1,21},{... | collective-permute-start | bytes 233480 | tf_op jit(solution)/shard_map/ppermute | solution.py:396
  34.1 7.1 %collective-permute-start.12 = (f32[152,128]{1,0:T(8,128)S(1)}, f32[152,128]{1,0:T(8,128)S(1)}, u32[]{:S(2)}, u32[]{:S(2)}) collective-permute-start(f32[152,128]{1,0:T(8,128)S(1)} %get-tuple-element.41), channel_id=1, source_target_pairs={{0,12},{4,8},{8,4},{12,0},{16,28},{20,24},{24,20},{28,16},{1,13},{... | collective-permute-start | bytes 233480 | tf_op jit(solution)/shard_map/ppermute | solution.py:396
  35.3 7.4 %collective-permute-start.13 = (f32[152,128]{1,0:T(8,128)S(1)}, f32[152,128]{1,0:T(8,128)S(1)}, u32[]{:S(2)}, u32[]{:S(2)}) collective-permute-start(f32[152,128]{1,0:T(8,128)S(1)} %get-tuple-element.42), channel_id=1, source_target_pairs={{0,24},{4,28},{8,16},{12,20},{16,8},{20,12},{24,0},{28,4},{1,25},{... | collective-permute-start | bytes 233480 | tf_op jit(solution)/shard_map/ppermute | solution.py:396
  37.6 7.2 %collective-permute-start.14 = (f32[152,128]{1,0:T(8,128)S(1)}, f32[152,128]{1,0:T(8,128)S(1)}, u32[]{:S(2)}, u32[]{:S(2)}) collective-permute-start(f32[152,128]{1,0:T(8,128)S(1)} %get-tuple-element.43), channel_id=1, source_target_pairs={{0,28},{4,24},{8,20},{12,16},{16,12},{20,8},{24,4},{28,0},{1,29},{... | collective-permute-start | bytes 233480 | tf_op jit(solution)/shard_map/ppermute | solution.py:396
  39.1 5.7 %collective-permute-start.15 = (f32[152,128]{1,0:T(8,128)S(1)}, f32[152,128]{1,0:T(8,128)S(1)}, u32[]{:S(2)}, u32[]{:S(2)}) collective-permute-start(f32[152,128]{1,0:T(8,128)S(1)} %get-tuple-element.44), channel_id=1, source_target_pairs={{0,4},{4,0},{8,12},{12,8},{16,20},{20,16},{24,28},{28,24},{1,5},{5... | collective-permute-start | bytes 233480 | tf_op jit(solution)/shard_map/ppermute | solution.py:396
  44.8 1.8 %collective-permute-start.16 = (f32[24,128]{1,0:T(8,128)S(1)}, f32[24,128]{1,0:T(8,128)S(1)}, u32[]{:S(2)}, u32[]{:S(2)}) collective-permute-start(f32[24,128]{1,0:T(8,128)S(1)} %get-tuple-element.45), channel_id=1, source_target_pairs={{0,1},{1,0},{2,3},{3,2},{4,5},{5,4},{6,7},{7,6},{8,9},{9,8},{10,11... | collective-permute-start | bytes 36872 | tf_op jit(solution)/shard_map/ppermute | solution.py:404
  44.9 3.2 %collective-permute-start.17 = (f32[24,128]{1,0:T(8,128)S(1)}, f32[24,128]{1,0:T(8,128)S(1)}, u32[]{:S(2)}, u32[]{:S(2)}) collective-permute-start(f32[24,128]{1,0:T(8,128)S(1)} %get-tuple-element.46), channel_id=1, source_target_pairs={{0,3},{1,2},{2,1},{3,0},{4,7},{5,6},{6,5},{7,4},{8,11},{9,10},{10,... | collective-permute-start | bytes 36872 | tf_op jit(solution)/shard_map/ppermute | solution.py:405

commit v11 on v10

--- a/solution.py
+++ b/solution.py
@@ -141,7 +141,7 @@
 
     half = owners // 2
     spare = [*range(half + 2, owners), *range(4, half), 1]
-    order_in = [0, 2, half, 3, half + 1, *spare]
+    order_in = [0, half, 2, half + 1, 3, *spare]
     order_out = [0, half, 2, half + 1, 3, *spare]
 
     def by_owner(refs, order):

time: 49.1 us -> 49 us (level)
  waiting for transfers between devices: 13.9 us -> 13 us
  starting transfers between devices: 28.7 us -> 29.4 us
    ppermute x14, waiting for transfers between devices: 11.1 us -> 10.2 us  [exchange(): lax.ppermute(parts[n], 'gx', [(g, g ^ order[n]) for g in range(owners)])]
    ppermute x14, starting transfers between devices: 23.9 us -> 24.6 us  [exchange(): lax.ppermute(parts[n], 'gx', [(g, g ^ order[n]) for g in range(owners)])]
  transfers between devices with their start and end apart: 18 -> 18, of which waited for: 6 -> 10; matrix products, arithmetic and copies ran while one was open for 0% -> 0% of each run, Pallas kernels for 1% -> 1%
where the time goes in v11:
time: 49 us; the launch traced here: 48.8 us
  starting transfers between devices  29.4 us (60%)
  waiting for transfers between devices  13 us (27%)
  Pallas kernels  6.3 us (13%)
    ppermute x14, starting transfers between devices, exchange(): lax.ppermute(parts[n], 'gx', [(g, g ^ order[n]) for g in range(owners)])  24.6 us
    ppermute x14, waiting for transfers between devices, exchange(): lax.ppermute(parts[n], 'gx', [(g, g ^ order[n]) for g in range(owners)])  10.2 us
    pallas_call x7, Pallas kernels, call(): pl.pallas_call(kernel, out_shape=out_shape, in_specs=[spec] * len(inputs)...  6.3 us
    ppermute x2, starting transfers between devices, hop(): lax.ppermute(far, 'gy', list(enumerate(behind)))  4.22 us
    ppermute x2, waiting for transfers between devices, hop(): lax.ppermute(far, 'gy', list(enumerate(behind)))  2.8 us
  transfers between devices with their start and end apart: 18, of which 10 were waited for; matrix products, arithmetic and copies ran while one was open for 0% of the time, Pallas kernels for 1%

profile of v11, /device:TPU:0, one launch (start us, length us, event | category | flops | bytes accessed | tf_op | source)
XLA Modules:
  0.0 48.8 jit_solution(3101634540349879472)
XLA Ops:
  0.0 0.0 copy-start
  0.0 0.0 copy-start.1
  0.0 1.7 %edge_planes.1 = (f32[24,128]{1,0:T(8,128)}, f32[24,128]{1,0:T(8,128)}, f32[8,128]{1,0:T(8,128)}) custom-call(f32[19,64,128]{2,1,0:T(8,128)} %bitcast.26, s32[64,128]{1,0:T(8,128)} %bitcast.28, s32[1,2]{1,0:T(1,128)} %slots.1, s32[2,3]{1,0:T(2,128)} %bitcast.30), custom_call_target="tpu_custom_call" | custom-call | flops 100000 | bytes 100000 | tf_op jit(solution)/shard_map/edge_planes/pallas_call | solution.py:383
  1.7 0.5 %collective-permute-start = (f32[24,128]{1,0:T(8,128)}, f32[24,128]{1,0:T(8,128)S(1)}, u32[]{:S(2)}, u32[]{:S(2)}) collective-permute-start(f32[24,128]{1,0:T(8,128)} %get-tuple-element.27), channel_id=1, source_target_pairs={{0,1},{1,0},{2,3},{3,2},{4,5},{5,4},{6,7},{7,6},{8,9},{9,8},{10,11... | collective-permute-start | bytes 36872 | tf_op jit(solution)/shard_map/ppermute | solution.py:404
  2.2 2.6 %collective-permute-start.1 = (f32[24,128]{1,0:T(8,128)}, f32[24,128]{1,0:T(8,128)S(1)}, u32[]{:S(2)}, u32[]{:S(2)}) collective-permute-start(f32[24,128]{1,0:T(8,128)} %get-tuple-element.28), channel_id=1, source_target_pairs={{0,3},{1,2},{2,1},{3,0},{4,7},{5,6},{6,5},{7,4},{8,11},{9,10},{10,... | collective-permute-start | bytes 36872 | tf_op jit(solution)/shard_map/ppermute | solution.py:405
  4.9 0.0 copy-done
  4.9 0.0 copy-done.1
  4.9 0.0 copy-start.2
  4.9 0.2 first_collision.1.post
  5.1 0.0 collective-permute-done.near
  5.1 1.4 %collective-permute-done.1.far = f32[24,128]{1,0:T(8,128)S(1)} collective-permute-done((f32[24,128]{1,0:T(8,128)}, f32[24,128]{1,0:T(8,128)S(1)}, u32[]{:S(2)}, u32[]{:S(2)}) %collective-permute-start.1) | collective-permute-done | bytes 12320 | tf_op jit(solution)/shard_map/ppermute | solution.py:405
  6.5 0.0 copy-done.2
  6.5 0.2 pack_planes.1
  6.7 2.8 %collective-permute-start.2 = (f32[168,128]{1,0:T(8,128)S(1)}, f32[168,128]{1,0:T(8,128)S(1)}, u32[]{:S(2)}, u32[]{:S(2)}) collective-permute-start(f32[168,128]{1,0:T(8,128)S(1)} %get-tuple-element.30), channel_id=1, source_target_pairs={{0,16},{4,20},{8,24},{12,28},{16,0},{20,4},{24,8},{28,12},{1,17},{... | collective-permute-start | bytes 258056 | tf_op jit(solution)/shard_map/ppermute | solution.py:396
  9.5 1.6 %collective-permute-start.3 = (f32[168,128]{1,0:T(8,128)S(1)}, f32[168,128]{1,0:T(8,128)S(1)}, u32[]{:S(2)}, u32[]{:S(2)}) collective-permute-start(f32[168,128]{1,0:T(8,128)S(1)} %get-tuple-element.31), channel_id=1, source_target_pairs={{0,8},{4,12},{8,0},{12,4},{16,24},{20,28},{24,16},{28,20},{1,9},{5... | collective-permute-start | bytes 258056 | tf_op jit(solution)/shard_map/ppermute | solution.py:396
  11.1 1.3 %collective-permute-start.4 = (f32[168,128]{1,0:T(8,128)S(1)}, f32[168,128]{1,0:T(8,128)S(1)}, u32[]{:S(2)}, u32[]{:S(2)}) collective-permute-start(f32[168,128]{1,0:T(8,128)S(1)} %get-tuple-element.32), channel_id=1, source_target_pairs={{0,20},{4,16},{8,28},{12,24},{16,4},{20,0},{24,12},{28,8},{1,21},{... | collective-permute-start | bytes 258056 | tf_op jit(solution)/shard_map/ppermute | solution.py:396
  12.4 0.2 collective-permute-start.5
  12.6 3.8 %collective-permute-start.6 = (f32[168,128]{1,0:T(8,128)S(1)}, f32[168,128]{1,0:T(8,128)S(1)}, u32[]{:S(2)}, u32[]{:S(2)}) collective-permute-start(f32[168,128]{1,0:T(8,128)S(1)} %get-tuple-element.34), channel_id=1, source_target_pairs={{0,24},{4,28},{8,16},{12,20},{16,8},{20,12},{24,0},{28,4},{1,25},{... | collective-permute-start | bytes 258056 | tf_op jit(solution)/shard_map/ppermute | solution.py:396
  16.4 0.0 collective-permute-done.2.refs_1_
  16.4 3.1 %collective-permute-start.7 = (f32[168,128]{1,0:T(8,128)S(1)}, f32[168,128]{1,0:T(8,128)S(1)}, u32[]{:S(2)}, u32[]{:S(2)}) collective-permute-start(f32[168,128]{1,0:T(8,128)S(1)} %get-tuple-element.35), channel_id=1, source_target_pairs={{0,28},{4,24},{8,20},{12,16},{16,12},{20,8},{24,4},{28,0},{1,29},{... | collective-permute-start | bytes 258056 | tf_op jit(solution)/shard_map/ppermute | solution.py:396
  19.5 0.0 collective-permute-done.3.refs_2_
  19.5 0.5 %collective-permute-start.8 = (f32[168,128]{1,0:T(8,128)S(1)}, f32[168,128]{1,0:T(8,128)S(1)}, u32[]{:S(2)}, u32[]{:S(2)}) collective-permute-start(f32[168,128]{1,0:T(8,128)S(1)} %get-tuple-element.36), channel_id=1, source_target_pairs={{0,4},{4,0},{8,12},{12,8},{16,20},{20,16},{24,28},{28,24},{1,5},{5... | collective-permute-start | bytes 258056 | tf_op jit(solution)/shard_map/ppermute | solution.py:396
  20.0 0.0 collective-permute-done.4.refs_3_
  20.0 0.0 collective-permute-done.5.refs_4_
  20.0 1.4 %collective-permute-done.6.refs_5_ = f32[168,128]{1,0:T(8,128)S(1)} collective-permute-done((f32[168,128]{1,0:T(8,128)S(1)}, f32[168,128]{1,0:T(8,128)S(1)}, u32[]{:S(2)}, u32[]{:S(2)}) %collective-permute-start.6) | collective-permute-done | bytes 86048 | tf_op jit(solution)/shard_map/ppermute | solution.py:396
  21.4 3.0 %collective-permute-done.7.refs_6_ = f32[168,128]{1,0:T(8,128)S(1)} collective-permute-done((f32[168,128]{1,0:T(8,128)S(1)}, f32[168,128]{1,0:T(8,128)S(1)}, u32[]{:S(2)}, u32[]{:S(2)}) %collective-permute-start.7) | collective-permute-done | bytes 86048 | tf_op jit(solution)/shard_map/ppermute | solution.py:396
  24.4 1.0 %collective-permute-done.8.refs_7_ = f32[168,128]{1,0:T(8,128)S(1)} collective-permute-done((f32[168,128]{1,0:T(8,128)S(1)}, f32[168,128]{1,0:T(8,128)S(1)}, u32[]{:S(2)}, u32[]{:S(2)}) %collective-permute-start.8) | collective-permute-done | bytes 86048 | tf_op jit(solution)/shard_map/ppermute | solution.py:396
  25.5 3.2 %second_step.1 = (f32[152,128]{1,0:T(8,128)S(1)}, f32[152,128]{1,0:T(8,128)S(1)}, f32[152,128]{1,0:T(8,128)S(1)}, f32[152,128]{1,0:T(8,128)S(1)}, f32[152,128]{1...) custom-call(f32[168,128]{1,0:T(8,128)S(1)} %get-tuple-element.29.refs_0_, ...), custom_call_target="tpu_custom_call" | custom-call | flops 4000000 | bytes 4000000 | tf_op jit(solution)/shard_map/second_step/pallas_call | solution.py:383
  28.6 3.3 %collective-permute-start.9 = (f32[152,128]{1,0:T(8,128)S(1)}, f32[152,128]{1,0:T(8,128)S(1)}, u32[]{:S(2)}, u32[]{:S(2)}) collective-permute-start(f32[152,128]{1,0:T(8,128)S(1)} %get-tuple-element.38), channel_id=1, source_target_pairs={{0,16},{4,20},{8,24},{12,28},{16,0},{20,4},{24,8},{28,12},{1,17},{... | collective-permute-start | bytes 233480 | tf_op jit(solution)/shard_map/ppermute | solution.py:396
  32.0 0.0 collective-permute-start.10
  32.0 1.7 %collective-permute-start.11 = (f32[152,128]{1,0:T(8,128)S(1)}, f32[152,128]{1,0:T(8,128)S(1)}, u32[]{:S(2)}, u32[]{:S(2)}) collective-permute-start(f32[152,128]{1,0:T(8,128)S(1)} %get-tuple-element.40), channel_id=1, source_target_pairs={{0,20},{4,16},{8,28},{12,24},{16,4},{20,0},{24,12},{28,8},{1,21},{... | collective-permute-start | bytes 233480 | tf_op jit(solution)/shard_map/ppermute | solution.py:396
  33.6 1.3 %collective-permute-start.12 = (f32[152,128]{1,0:T(8,128)S(1)}, f32[152,128]{1,0:T(8,128)S(1)}, u32[]{:S(2)}, u32[]{:S(2)}) collective-permute-start(f32[152,128]{1,0:T(8,128)S(1)} %get-tuple-element.41), channel_id=1, source_target_pairs={{0,12},{4,8},{8,4},{12,0},{16,28},{20,24},{24,20},{28,16},{1,13},{... | collective-permute-start | bytes 233480 | tf_op jit(solution)/shard_map/ppermute | solution.py:396
  35.0 2.3 %collective-permute-start.13 = (f32[152,128]{1,0:T(8,128)S(1)}, f32[152,128]{1,0:T(8,128)S(1)}, u32[]{:S(2)}, u32[]{:S(2)}) collective-permute-start(f32[152,128]{1,0:T(8,128)S(1)} %get-tuple-element.42), channel_id=1, source_target_pairs={{0,24},{4,28},{8,16},{12,20},{16,8},{20,12},{24,0},{28,4},{1,25},{... | collective-permute-start | bytes 233480 | tf_op jit(solution)/shard_map/ppermute | solution.py:396
  37.2 0.0 collective-permute-done.9.refs_1_
  37.2 1.5 %collective-permute-start.14 = (f32[152,128]{1,0:T(8,128)S(1)}, f32[152,128]{1,0:T(8,128)S(1)}, u32[]{:S(2)}, u32[]{:S(2)}) collective-permute-start(f32[152,128]{1,0:T(8,128)S(1)} %get-tuple-element.43), channel_id=1, source_target_pairs={{0,28},{4,24},{8,20},{12,16},{16,12},{20,8},{24,4},{28,0},{1,29},{... | collective-permute-start | bytes 233480 | tf_op jit(solution)/shard_map/ppermute | solution.py:396
  38.7 0.3 collective-permute-done.10.refs_2_
  39.1 1.2 %collective-permute-start.15 = (f32[152,128]{1,0:T(8,128)S(1)}, f32[152,128]{1,0:T(8,128)S(1)}, u32[]{:S(2)}, u32[]{:S(2)}) collective-permute-start(f32[152,128]{1,0:T(8,128)S(1)} %get-tuple-element.44), channel_id=1, source_target_pairs={{0,4},{4,0},{8,12},{12,8},{16,20},{20,16},{24,28},{28,24},{1,5},{5... | collective-permute-start | bytes 233480 | tf_op jit(solution)/shard_map/ppermute | solution.py:396
  40.3 1.2 %collective-permute-done.11.refs_3_ = f32[152,128]{1,0:T(8,128)S(1)} collective-permute-done((f32[152,128]{1,0:T(8,128)S(1)}, f32[152,128]{1,0:T(8,128)S(1)}, u32[]{:S(2)}, u32[]{:S(2)}) %collective-permute-start.11) | collective-permute-done | bytes 77856 | tf_op jit(solution)/shard_map/ppermute | solution.py:396
  41.5 0.0 collective-permute-done.12.refs_4_
  41.5 1.0 %collective-permute-done.13.refs_5_ = f32[152,128]{1,0:T(8,128)S(1)} collective-permute-done((f32[152,128]{1,0:T(8,128)S(1)}, f32[152,128]{1,0:T(8,128)S(1)}, u32[]{:S(2)}, u32[]{:S(2)}) %collective-permute-start.13) | collective-permute-done | bytes 77856 | tf_op jit(solution)/shard_map/ppermute | solution.py:396
  42.4 2.0 %collective-permute-done.14.refs_6_ = f32[152,128]{1,0:T(8,128)S(1)} collective-permute-done((f32[152,128]{1,0:T(8,128)S(1)}, f32[152,128]{1,0:T(8,128)S(1)}, u32[]{:S(2)}, u32[]{:S(2)}) %collective-permute-start.14) | collective-permute-done | bytes 77856 | tf_op jit(solution)/shard_map/ppermute | solution.py:396
  44.4 0.2 collective-permute-done.15.refs_7_
  44.7 0.1 collective-permute-start.16
  44.7 1.6 %collective-permute-start.17 = (f32[24,128]{1,0:T(8,128)S(1)}, f32[24,128]{1,0:T(8,128)S(1)}, u32[]{:S(2)}, u32[]{:S(2)}) collective-permute-start(f32[24,128]{1,0:T(8,128)S(1)} %get-tuple-element.46), channel_id=1, source_target_pairs={{0,3},{1,2},{2,1},{3,0},{4,7},{5,6},{6,5},{7,4},{8,11},{9,10},{10,... | collective-permute-start | bytes 36872 | tf_op jit(solution)/shard_map/ppermute | solution.py:405
  46.3 0.1 unpack_planes.1.main
  46.5 0.0 collective-permute-done.16.near
  46.5 1.4 %collective-permute-done.17.far = f32[24,128]{1,0:T(8,128)S(1)} collective-permute-done((f32[24,128]{1,0:T(8,128)S(1)}, f32[24,128]{1,0:T(8,128)S(1)}, u32[]{:S(2)}, u32[]{:S(2)}) %collective-permute-start.17) | collective-permute-done | bytes 12320 | tf_op jit(solution)/shard_map/ppermute | solution.py:405
  47.9 0.9 %finish.1 = f32[1216,128]{1,0:T(8,128)} custom-call(f32[19,80,128]{2,1,0:T(8,128)S(1)} %unpack_planes.1.main, f32[24,128]{1,0:T(8,128)S(1)} %collective-permute-done.16.near, f32[24,128]{1,0:T(8,128)S(1)} %collective-permute-done.17.far), custom_call_target="tpu_custom_call" | custom-call | flops 100000 | bytes 100000 | tf_op jit(solution)/shard_map/finish/pallas_call | solution.py:383
  (1 shorter events, 0.0 us)
Async XLA Ops:
  0.0 4.9 %copy-start = (f32[1,2,19,4096]{3,1,2,0:T(2,128)S(1)}, f32[1,2,19,4096]{3,1,2,0:T(2,128)}, u32[]{:S(2)}) copy-start(f32[1,2,19,4096]{3,1,2,0:T(2,128)} %param.4) | copy-start | bytes 1867780
  0.0 4.9 %copy-start.1 = (s32[1,2,4096]{2,1,0:T(2,128)S(1)}, s32[1,2,4096]{2,1,0:T(2,128)}, u32[]{:S(2)}) copy-start(s32[1,2,4096]{2,1,0:T(2,128)} %param.5) | copy-start | bytes 98308
  1.7 3.4 %collective-permute-start = (f32[24,128]{1,0:T(8,128)}, f32[24,128]{1,0:T(8,128)S(1)}, u32[]{:S(2)}, u32[]{:S(2)}) collective-permute-start(f32[24,128]{1,0:T(8,128)} %get-tuple-element.27), channel_id=1, source_target_pairs={{0,1},{1,0},{2,3},{3,2},{4,5},{5,4},{6,7},{7,6},{8,9},{9,8},{10,11... | collective-permute-start | bytes 36872 | tf_op jit(solution)/shard_map/ppermute | solution.py:404
  2.2 4.2 %collective-permute-start.1 = (f32[24,128]{1,0:T(8,128)}, f32[24,128]{1,0:T(8,128)S(1)}, u32[]{:S(2)}, u32[]{:S(2)}) collective-permute-start(f32[24,128]{1,0:T(8,128)} %get-tuple-element.28), channel_id=1, source_target_pairs={{0,3},{1,2},{2,1},{3,0},{4,7},{5,6},{6,5},{7,4},{8,11},{9,10},{10,... | collective-permute-start | bytes 36872 | tf_op jit(solution)/shard_map/ppermute | solution.py:405
  4.9 1.6 %copy-start.2 = (f32[8,128]{1,0:T(8,128)S(1)}, f32[8,128]{1,0:T(8,128)}, u32[]{:S(2)}) copy-start(f32[8,128]{1,0:T(8,128)} %get-tuple-element.26.own) | copy-start | bytes 12292
  6.7 9.7 %collective-permute-start.2 = (f32[168,128]{1,0:T(8,128)S(1)}, f32[168,128]{1,0:T(8,128)S(1)}, u32[]{:S(2)}, u32[]{:S(2)}) collective-permute-start(f32[168,128]{1,0:T(8,128)S(1)} %get-tuple-element.30), channel_id=1, source_target_pairs={{0,16},{4,20},{8,24},{12,28},{16,0},{20,4},{24,8},{28,12},{1,17},{... | collective-permute-start | bytes 258056 | tf_op jit(solution)/shard_map/ppermute | solution.py:396
  9.5 10.0 %collective-permute-start.3 = (f32[168,128]{1,0:T(8,128)S(1)}, f32[168,128]{1,0:T(8,128)S(1)}, u32[]{:S(2)}, u32[]{:S(2)}) collective-permute-start(f32[168,128]{1,0:T(8,128)S(1)} %get-tuple-element.31), channel_id=1, source_target_pairs={{0,8},{4,12},{8,0},{12,4},{16,24},{20,28},{24,16},{28,20},{1,9},{5... | collective-permute-start | bytes 258056 | tf_op jit(solution)/shard_map/ppermute | solution.py:396
  11.1 8.9 %collective-permute-start.4 = (f32[168,128]{1,0:T(8,128)S(1)}, f32[168,128]{1,0:T(8,128)S(1)}, u32[]{:S(2)}, u32[]{:S(2)}) collective-permute-start(f32[168,128]{1,0:T(8,128)S(1)} %get-tuple-element.32), channel_id=1, source_target_pairs={{0,20},{4,16},{8,28},{12,24},{16,4},{20,0},{24,12},{28,8},{1,21},{... | collective-permute-start | bytes 258056 | tf_op jit(solution)/shard_map/ppermute | solution.py:396
  12.4 7.6 %collective-permute-start.5 = (f32[168,128]{1,0:T(8,128)S(1)}, f32[168,128]{1,0:T(8,128)S(1)}, u32[]{:S(2)}, u32[]{:S(2)}) collective-permute-start(f32[168,128]{1,0:T(8,128)S(1)} %get-tuple-element.33), channel_id=1, source_target_pairs={{0,12},{4,8},{8,4},{12,0},{16,28},{20,24},{24,20},{28,16},{1,13},{... | collective-permute-start | bytes 258056 | tf_op jit(solution)/shard_map/ppermute | solution.py:396
  12.6 8.8 %collective-permute-start.6 = (f32[168,128]{1,0:T(8,128)S(1)}, f32[168,128]{1,0:T(8,128)S(1)}, u32[]{:S(2)}, u32[]{:S(2)}) collective-permute-start(f32[168,128]{1,0:T(8,128)S(1)} %get-tuple-element.34), channel_id=1, source_target_pairs={{0,24},{4,28},{8,16},{12,20},{16,8},{20,12},{24,0},{28,4},{1,25},{... | collective-permute-start | bytes 258056 | tf_op jit(solution)/shard_map/ppermute | solution.py:396
  16.4 8.1 %collective-permute-start.7 = (f32[168,128]{1,0:T(8,128)S(1)}, f32[168,128]{1,0:T(8,128)S(1)}, u32[]{:S(2)}, u32[]{:S(2)}) collective-permute-start(f32[168,128]{1,0:T(8,128)S(1)} %get-tuple-element.35), channel_id=1, source_target_pairs={{0,28},{4,24},{8,20},{12,16},{16,12},{20,8},{24,4},{28,0},{1,29},{... | collective-permute-start | bytes 258056 | tf_op jit(solution)/shard_map/ppermute | solution.py:396
  19.5 6.0 %collective-permute-start.8 = (f32[168,128]{1,0:T(8,128)S(1)}, f32[168,128]{1,0:T(8,128)S(1)}, u32[]{:S(2)}, u32[]{:S(2)}) collective-permute-start(f32[168,128]{1,0:T(8,128)S(1)} %get-tuple-element.36), channel_id=1, source_target_pairs={{0,4},{4,0},{8,12},{12,8},{16,20},{20,16},{24,28},{28,24},{1,5},{5... | collective-permute-start | bytes 258056 | tf_op jit(solution)/shard_map/ppermute | solution.py:396
  28.6 8.6 %collective-permute-start.9 = (f32[152,128]{1,0:T(8,128)S(1)}, f32[152,128]{1,0:T(8,128)S(1)}, u32[]{:S(2)}, u32[]{:S(2)}) collective-permute-start(f32[152,128]{1,0:T(8,128)S(1)} %get-tuple-element.38), channel_id=1, source_target_pairs={{0,16},{4,20},{8,24},{12,28},{16,0},{20,4},{24,8},{28,12},{1,17},{... | collective-permute-start | bytes 233480 | tf_op jit(solution)/shard_map/ppermute | solution.py:396
  32.0 7.1 %collective-permute-start.10 = (f32[152,128]{1,0:T(8,128)S(1)}, f32[152,128]{1,0:T(8,128)S(1)}, u32[]{:S(2)}, u32[]{:S(2)}) collective-permute-start(f32[152,128]{1,0:T(8,128)S(1)} %get-tuple-element.39), channel_id=1, source_target_pairs={{0,8},{4,12},{8,0},{12,4},{16,24},{20,28},{24,16},{28,20},{1,9},{5... | collective-permute-start | bytes 233480 | tf_op jit(solution)/shard_map/ppermute | solution.py:396
  32.0 9.5 %collective-permute-start.11 = (f32[152,128]{1,0:T(8,128)S(1)}, f32[152,128]{1,0:T(8,128)S(1)}, u32[]{:S(2)}, u32[]{:S(2)}) collective-permute-start(f32[152,128]{1,0:T(8,128)S(1)} %get-tuple-element.40), channel_id=1, source_target_pairs={{0,20},{4,16},{8,28},{12,24},{16,4},{20,0},{24,12},{28,8},{1,21},{... | collective-permute-start | bytes 233480 | tf_op jit(solution)/shard_map/ppermute | solution.py:396
  33.6 7.8 %collective-permute-start.12 = (f32[152,128]{1,0:T(8,128)S(1)}, f32[152,128]{1,0:T(8,128)S(1)}, u32[]{:S(2)}, u32[]{:S(2)}) collective-permute-start(f32[152,128]{1,0:T(8,128)S(1)} %get-tuple-element.41), channel_id=1, source_target_pairs={{0,12},{4,8},{8,4},{12,0},{16,28},{20,24},{24,20},{28,16},{1,13},{... | collective-permute-start | bytes 233480 | tf_op jit(solution)/shard_map/ppermute | solution.py:396
  35.0 7.5 %collective-permute-start.13 = (f32[152,128]{1,0:T(8,128)S(1)}, f32[152,128]{1,0:T(8,128)S(1)}, u32[]{:S(2)}, u32[]{:S(2)}) collective-permute-start(f32[152,128]{1,0:T(8,128)S(1)} %get-tuple-element.42), channel_id=1, source_target_pairs={{0,24},{4,28},{8,16},{12,20},{16,8},{20,12},{24,0},{28,4},{1,25},{... | collective-permute-start | bytes 233480 | tf_op jit(solution)/shard_map/ppermute | solution.py:396
  37.2 7.2 %collective-permute-start.14 = (f32[152,128]{1,0:T(8,128)S(1)}, f32[152,128]{1,0:T(8,128)S(1)}, u32[]{:S(2)}, u32[]{:S(2)}) collective-permute-start(f32[152,128]{1,0:T(8,128)S(1)} %get-tuple-element.43), channel_id=1, source_target_pairs={{0,28},{4,24},{8,20},{12,16},{16,12},{20,8},{24,4},{28,0},{1,29},{... | collective-permute-start | bytes 233480 | tf_op jit(solution)/shard_map/ppermute | solution.py:396
  39.1 5.6 %collective-permute-start.15 = (f32[152,128]{1,0:T(8,128)S(1)}, f32[152,128]{1,0:T(8,128)S(1)}, u32[]{:S(2)}, u32[]{:S(2)}) collective-permute-start(f32[152,128]{1,0:T(8,128)S(1)} %get-tuple-element.44), channel_id=1, source_target_pairs={{0,4},{4,0},{8,12},{12,8},{16,20},{20,16},{24,28},{28,24},{1,5},{5... | collective-permute-start | bytes 233480 | tf_op jit(solution)/shard_map/ppermute | solution.py:396
  44.7 1.8 %collective-permute-start.16 = (f32[24,128]{1,0:T(8,128)S(1)}, f32[24,128]{1,0:T(8,128)S(1)}, u32[]{:S(2)}, u32[]{:S(2)}) collective-permute-start(f32[24,128]{1,0:T(8,128)S(1)} %get-tuple-element.45), channel_id=1, source_target_pairs={{0,1},{1,0},{2,3},{3,2},{4,5},{5,4},{6,7},{7,6},{8,9},{9,8},{10,11... | collective-permute-start | bytes 36872 | tf_op jit(solution)/shard_map/ppermute | solution.py:404
  44.7 3.2 %collective-permute-start.17 = (f32[24,128]{1,0:T(8,128)S(1)}, f32[24,128]{1,0:T(8,128)S(1)}, u32[]{:S(2)}, u32[]{:S(2)}) collective-permute-start(f32[24,128]{1,0:T(8,128)S(1)} %get-tuple-element.46), channel_id=1, source_target_pairs={{0,3},{1,2},{2,1},{3,0},{4,7},{5,6},{6,5},{7,4},{8,11},{9,10},{10,... | collective-permute-start | bytes 36872 | tf_op jit(solution)/shard_map/ppermute | solution.py:405

commit v12 on v9

--- a/solution.py
+++ b/solution.py
@@ -37,6 +37,9 @@
 Q = len(VELOCITIES)
 UPWARD = tuple(p for p in range(Q) if VELOCITIES[p][0] == 1)
 DOWNWARD = tuple(p for p in range(Q) if VELOCITIES[p][0] == -1)
+
+LEVEL = tuple(p for p in range(Q) if VELOCITIES[p][0] == 0)
+SLOPED = UPWARD + DOWNWARD
 
 VMEM_SPEC = pl.BlockSpec(memory_space=pltpu.VMEM)
 
@@ -133,6 +136,7 @@
     block = planes * PLANE_ROWS
     rows = owners * block
     head = (Q + 1) * share
+    head_sloped = len(SLOPED) * share
     rows_in = head + 8
     rows_out = Q * share
     faces = len(UPWARD) * PLANE
@@ -140,8 +144,24 @@
     f32 = jnp.float32
 
     half = owners // 2
-    order = [0, half, 1, half + 1, 2, *range(half + 2, owners), *range(3, half)]
-    slot_of = [order.index(d) for d in range(owners)]
+    split = (half, half + 1)
+    middle = [(d, "whole") for d in range(half + 2, owners)]
+    beside = [(d, "whole") for d in range(1, half)]
+    level = [(d, "level") for d in split]
+    sloped = [(d, "sloped") for d in split]
+    own = [(0, "whole")]
+    rest = [*middle, *beside[3:], beside[0]]
+    lines_in = own + [(half, "whole"), beside[1], (half + 1, "whole"), beside[2], *rest]
+    lines_out = own + [sloped[0], beside[1], sloped[1], beside[2], *rest] + level
+    sizes_in = {"whole": rows_in}
+    sizes_out = {"whole": rows_out, "level": len(LEVEL) * share, "sloped": head_sloped}
+
+    def spot(refs, lines, d, p):
+        if (d, "whole") in lines:
+            return refs[lines.index((d, "whole"))], p * share
+        if p in SLOPED:
+            return refs[lines.index((d, "sloped"))], SLOPED.index(p) * share
+        return refs[lines.index((d, "level"))], LEVEL.index(p) * share
 
     def position():
         me = lax.axis_index("gx")
@@ -194,12 +214,12 @@
         me, odd = position()
         below, above = sides(odd, near, far)
         for d in range(owners):
-            out = outs[slot_of[d]]
             place = dynamic_place(me ^ d, odd, owners)
             here = pl.multiple_of(place * share, min(share, 8))
             for p in range(Q + 1):
                 cx = VELOCITIES[p][0] if p < Q else 0
-                out[pl.ds(p * share, share), :] = post[p, pl.ds(8 + here - cx * PLANE, share), :]
+                out, row = spot(outs, lines_in, d, p)
+                out[pl.ds(row, share), :] = post[p, pl.ds(8 + here - cx * PLANE, share), :]
             out[pl.ds(head, 2), :] = own[0:2]
             out[pl.ds(head + 2, 2), :] = below[faces : faces + 2]
             out[pl.ds(head + 4, 2), :] = above[faces : faces + 2]
@@ -208,25 +228,24 @@
             @pl.when(place == 0)
             def _():
                 for n, p in enumerate(UPWARD):
-                    out[pl.ds(p * share, PLANE), :] = below[n * PLANE : (n + 1) * PLANE]
+                    out, row = spot(outs, lines_in, d, p)
+                    out[pl.ds(row, PLANE), :] = below[n * PLANE : (n + 1) * PLANE]
 
             @pl.when(place == owners - 1)
             def _():
                 for n, p in enumerate(DOWNWARD):
-                    out[pl.ds(p * share + share - PLANE, PLANE), :] = above[
-                        n * PLANE : (n + 1) * PLANE
-                    ]
+                    out, row = spot(outs, lines_in, d, p)
+                    out[pl.ds(row + share - PLANE, PLANE), :] = above[n * PLANE : (n + 1) * PLANE]
 
     def middle_kernel(*refs):
-        got = [refs[slot_of[d]] for d in range(owners)]
-        outs = [refs[owners + slot_of[d]] for d in range(owners)]
-        lattice, ready, table, sem = refs[2 * owners :]
+        *messages, lattice, ready, table, sem = refs
+        got, outs = messages[:owners], messages[owners:]
         me, odd = position()
         place = dynamic_place(me, odd, owners)
         first, last = place == 0, place == owners - 1
         copies = [
-            pltpu.make_async_copy(got[d].at[pl.ds(head, 8), :], table.at[d], sem.at[d])
-            for d in range(owners)
+            pltpu.make_async_copy(ref.at[pl.ds(head, 8), :], table.at[d], sem.at[n])
+            for n, (ref, (d, _)) in enumerate(zip(got, lines_in))
         ]
         for copy in copies:
             copy.start()
@@ -256,16 +275,16 @@
         for d in range(owners):
             for t, (kz, y) in enumerate(seats(held(d, 0))):
                 for p in range(Q + 1):
-                    lattice[p, kz, pl.ds(y, block), :] = got[d][
-                        pl.ds(p * share + t, block, stride=NB), :
-                    ]
+                    ref, start = spot(got, lines_in, d, p)
+                    lattice[p, kz, pl.ds(y, block), :] = ref[pl.ds(start + t, block, stride=NB), :]
 
         def bring(chosen, i):
             for d in range(owners):
                 for t, (kz, y) in enumerate(seats(held(d, other))):
                     for p in chosen:
-                        lattice[p, kz, pl.ds(y + i * PLANE_ROWS, PLANE_ROWS), :] = got[d][
-                            pl.ds(p * share + i * PLANE + t, PLANE_ROWS, stride=NB), :
+                        ref, start = spot(got, lines_in, d, p)
+                        lattice[p, kz, pl.ds(y + i * PLANE_ROWS, PLANE_ROWS), :] = ref[
+                            pl.ds(start + i * PLANE + t, PLANE_ROWS, stride=NB), :
                         ]
 
         @pl.when(first)
@@ -306,17 +325,17 @@
         for d in range(owners):
             for t, (kz, y) in enumerate(seats(final(d, 0))):
                 for p in range(Q):
-                    outs[d][pl.ds(p * share + t, block, stride=NB), :] = ready[
-                        p, kz, pl.ds(y, block), :
-                    ]
+                    ref, start = spot(outs, lines_out, d, p)
+                    ref[pl.ds(start + t, block, stride=NB), :] = ready[p, kz, pl.ds(y, block), :]
 
         def bring_back(chosen, i):
             for d in range(owners):
                 for t, (kz, y) in enumerate(seats(final(d, other))):
                     for p in chosen:
-                        outs[d][
-                            pl.ds(p * share + i * PLANE + t, PLANE_ROWS, stride=NB), :
-                        ] = ready[p, kz, pl.ds(y + i * PLANE_ROWS, PLANE_ROWS), :]
+                        ref, start = spot(outs, lines_out, d, p)
+                        ref[pl.ds(start + i * PLANE + t, PLANE_ROWS, stride=NB), :] = ready[
+                            p, kz, pl.ds(y + i * PLANE_ROWS, PLANE_ROWS), :
+                        ]
 
         @pl.when(last)
         def _():
@@ -327,8 +346,7 @@
             bring_back(DOWNWARD, 0)
 
     def crossing_kernel(*refs):
-        got = [refs[slot_of[d]] for d in range(owners)]
-        near, far, up, down = refs[owners:]
+        got, (near, far, up, down) = refs[:owners], refs[owners:]
         me, odd = position()
         for d in range(owners):
             place = dynamic_place(me ^ d, odd, owners)
@@ -336,30 +354,29 @@
             @pl.when(place == owners - 1)
             def _():
                 for n, p in enumerate(UPWARD):
-                    up[pl.ds(n * PLANE, PLANE), :] = got[d][
-                        pl.ds(p * share + share - PLANE, PLANE), :
-                    ]
+                    ref, start = spot(got, lines_out, d, p)
+                    up[pl.ds(n * PLANE, PLANE), :] = ref[pl.ds(start + share - PLANE, PLANE), :]
 
             @pl.when(place == 0)
             def _():
                 for n, p in enumerate(DOWNWARD):
-                    down[pl.ds(n * PLANE, PLANE), :] = got[d][pl.ds(p * share, PLANE), :]
+                    ref, start = spot(got, lines_out, d, p)
+                    down[pl.ds(n * PLANE, PLANE), :] = ref[pl.ds(start, PLANE), :]
 
         for out in (up, down):
             out[pl.ds(faces, 4), :] = jnp.zeros((4, LANES), f32)
         send_sides(odd, up, down, near, far)
 
     def unpack_kernel(*refs):
-        got, main = [refs[slot_of[d]] for d in range(owners)], refs[owners]
+        *got, main = refs
         me, odd = position()
         for d in range(owners):
             place = dynamic_place(me ^ d, odd, owners)
             here = pl.multiple_of(place * share, min(share, 8))
             for p in range(Q):
                 cx = VELOCITIES[p][0]
-                main[p, pl.ds(8 + here + cx * PLANE, share), :] = got[d][
-                    pl.ds(p * share, share), :
-                ]
+                ref, start = spot(got, lines_out, d, p)
+                main[p, pl.ds(8 + here + cx * PLANE, share), :] = ref[pl.ds(start, share), :]
 
     def finish_kernel(main, near, far, out):
         below, above = sides(position()[1], near, far)
@@ -386,11 +403,14 @@
             name=name,
         )(*inputs)
 
-    def exchange(parts):
-        return [parts[0]] + [
-            lax.ppermute(parts[n], "gx", [(g, g ^ order[n]) for g in range(owners)])
-            for n in range(1, owners)
+    def exchange(parts, lines):
+        return [
+            part if d == 0 else lax.ppermute(part, "gx", [(g, g ^ d) for g in range(owners)])
+            for part, (d, kind) in zip(parts, lines)
         ]
+
+    def shapes(lines, sizes):
+        return tuple(shape(sizes[kind], LANES) for d, kind in lines)
 
     def hop(near, far):
         ahead = [(s + 1) % slabs if s % 2 == 0 else (s - 1) % slabs for s in range(slabs)]
@@ -440,18 +460,13 @@
             large,
         )
         parts = call(
-            pack_kernel,
-            "pack_planes",
-            (shape(rows_in, LANES),) * owners,
-            (post, own, near, far),
-            large,
-        )
-        got = exchange(parts)
+            pack_kernel, "pack_planes", shapes(lines_in, sizes_in), (post, own, near, far), large
+        )
         parts = call(
             middle_kernel,
             "second_step",
-            (shape(rows_out, LANES),) * owners,
-            got,
+            shapes(lines_out, sizes_out),
+            exchange(parts, lines_in),
             large,
             (
                 work,
@@ -460,12 +475,12 @@
                 pltpu.SemaphoreType.DMA((owners,)),
             ),
         )
-        home = exchange(parts)
+        home = exchange(parts, lines_out)
         near, far = call(
             crossing_kernel,
             "crossing_planes",
             (shape(rows_hop, LANES),) * 2,
-            home,
+            home[:owners],
             small,
             (pltpu.VMEM((rows_hop, LANES), f32),) * 2,
         )

time: 50.5 us -> 49.5 us (0.980)
  waiting for transfers between devices: 13.9 us -> 9.94 us
  starting transfers between devices: 30 us -> 32.6 us
    ppermute x14 -> x16, starting transfers between devices: 25.2 us -> 27.8 us  [exchange(): lax.ppermute(part, 'gx', [(g, g ^ d) for g in range(owners)])]
    ppermute x14 -> x16, waiting for transfers between devices: 11.1 us -> 8.57 us  [exchange(): lax.ppermute(part, 'gx', [(g, g ^ d) for g in range(owners)])]
    ppermute x2, waiting for transfers between devices: 2.8 us -> 1.36 us  [hop(): lax.ppermute(far, 'gy', list(enumerate(behind)))]
  transfers between devices with their start and end apart: 18 -> 20, of which waited for: 9 -> 7; matrix products, arithmetic and copies ran while one was open for 0% -> 0% of each run, Pallas kernels for 1% -> 1%
where the time goes in v12:
time: 49.5 us; the launch traced here: 49 us
  starting transfers between devices  32.6 us (66%)
  waiting for transfers between devices  9.94 us (20%)
  Pallas kernels  6.33 us (13%)
    ppermute x16, starting transfers between devices, exchange(): lax.ppermute(part, 'gx', [(g, g ^ d) for g in range(owners)])  27.8 us
    ppermute x16, waiting for transfers between devices, exchange(): lax.ppermute(part, 'gx', [(g, g ^ d) for g in range(owners)])  8.57 us
    pallas_call x7, Pallas kernels, call(): pl.pallas_call(kernel, out_shape=out_shape, in_specs=[spec] * len(inputs)...  6.33 us
    ppermute x2, starting transfers between devices, hop(): lax.ppermute(far, 'gy', list(enumerate(behind)))  4.22 us
    ppermute x2, waiting for transfers between devices, hop(): lax.ppermute(far, 'gy', list(enumerate(behind)))  1.36 us
  transfers between devices with their start and end apart: 20, of which 7 were waited for; matrix products, arithmetic and copies ran while one was open for 0% of the time, Pallas kernels for 1%

profile of v12, /device:TPU:0, one launch (start us, length us, event | category | flops | bytes accessed | tf_op | source)
XLA Modules:
  0.0 49.0 jit_solution(13623563152527811207)
XLA Ops:
  0.0 1.7 %edge_planes.1 = (f32[24,128]{1,0:T(8,128)}, f32[24,128]{1,0:T(8,128)}, f32[8,128]{1,0:T(8,128)}) custom-call(f32[19,64,128]{2,1,0:T(8,128)} %bitcast.26, s32[64,128]{1,0:T(8,128)} %bitcast.28, s32[1,2]{1,0:T(1,128)} %slots.1, s32[2,3]{1,0:T(2,128)} %bitcast.30), custom_call_target="tpu_custom_call" | custom-call | flops 100000 | bytes 100000 | tf_op jit(solution)/shard_map/edge_planes/pallas_call | solution.py:395
  1.7 0.5 %collective-permute-start = (f32[24,128]{1,0:T(8,128)}, f32[24,128]{1,0:T(8,128)S(1)}, u32[]{:S(2)}, u32[]{:S(2)}) collective-permute-start(f32[24,128]{1,0:T(8,128)} %get-tuple-element.29), channel_id=1, source_target_pairs={{0,1},{1,0},{2,3},{3,2},{4,5},{5,4},{6,7},{7,6},{8,9},{9,8},{10,11... | collective-permute-start | bytes 36872 | tf_op jit(solution)/shard_map/ppermute | solution.py:419
  2.2 2.6 %collective-permute-start.1 = (f32[24,128]{1,0:T(8,128)}, f32[24,128]{1,0:T(8,128)S(1)}, u32[]{:S(2)}, u32[]{:S(2)}) collective-permute-start(f32[24,128]{1,0:T(8,128)} %get-tuple-element.30), channel_id=1, source_target_pairs={{0,3},{1,2},{2,1},{3,0},{4,7},{5,6},{6,5},{7,4},{8,11},{9,10},{10,... | collective-permute-start | bytes 36872 | tf_op jit(solution)/shard_map/ppermute | solution.py:420
  4.9 0.0 copy-done
  4.9 0.2 first_collision.1.post
  5.1 0.0 collective-permute-done.near
  5.1 1.4 %collective-permute-done.1.far = f32[24,128]{1,0:T(8,128)S(1)} collective-permute-done((f32[24,128]{1,0:T(8,128)}, f32[24,128]{1,0:T(8,128)S(1)}, u32[]{:S(2)}, u32[]{:S(2)}) %collective-permute-start.1) | collective-permute-done | bytes 12320 | tf_op jit(solution)/shard_map/ppermute | solution.py:420
  6.5 0.0 copy-done.2
  6.5 0.2 pack_planes.1
  6.7 2.8 %collective-permute-start.2 = (f32[168,128]{1,0:T(8,128)S(1)}, f32[168,128]{1,0:T(8,128)S(1)}, u32[]{:S(2)}, u32[]{:S(2)}) collective-permute-start(f32[168,128]{1,0:T(8,128)S(1)} %get-tuple-element.32), channel_id=1, source_target_pairs={{0,16},{4,20},{8,24},{12,28},{16,0},{20,4},{24,8},{28,12},{1,17},{... | collective-permute-start | bytes 258056 | tf_op jit(solution)/shard_map/ppermute | solution.py:408
  9.5 1.6 %collective-permute-start.3 = (f32[168,128]{1,0:T(8,128)S(1)}, f32[168,128]{1,0:T(8,128)S(1)}, u32[]{:S(2)}, u32[]{:S(2)}) collective-permute-start(f32[168,128]{1,0:T(8,128)S(1)} %get-tuple-element.33), channel_id=1, source_target_pairs={{0,8},{4,12},{8,0},{12,4},{16,24},{20,28},{24,16},{28,20},{1,9},{5... | collective-permute-start | bytes 258056 | tf_op jit(solution)/shard_map/ppermute | solution.py:408
  11.1 1.3 %collective-permute-start.4 = (f32[168,128]{1,0:T(8,128)S(1)}, f32[168,128]{1,0:T(8,128)S(1)}, u32[]{:S(2)}, u32[]{:S(2)}) collective-permute-start(f32[168,128]{1,0:T(8,128)S(1)} %get-tuple-element.34), channel_id=1, source_target_pairs={{0,20},{4,16},{8,28},{12,24},{16,4},{20,0},{24,12},{28,8},{1,21},{... | collective-permute-start | bytes 258056 | tf_op jit(solution)/shard_map/ppermute | solution.py:408
  12.4 0.2 collective-permute-start.5
  12.6 3.8 %collective-permute-start.6 = (f32[168,128]{1,0:T(8,128)S(1)}, f32[168,128]{1,0:T(8,128)S(1)}, u32[]{:S(2)}, u32[]{:S(2)}) collective-permute-start(f32[168,128]{1,0:T(8,128)S(1)} %get-tuple-element.36), channel_id=1, source_target_pairs={{0,24},{4,28},{8,16},{12,20},{16,8},{20,12},{24,0},{28,4},{1,25},{... | collective-permute-start | bytes 258056 | tf_op jit(solution)/shard_map/ppermute | solution.py:408
  16.4 0.0 collective-permute-done.2.refs_1_
  16.4 3.1 %collective-permute-start.7 = (f32[168,128]{1,0:T(8,128)S(1)}, f32[168,128]{1,0:T(8,128)S(1)}, u32[]{:S(2)}, u32[]{:S(2)}) collective-permute-start(f32[168,128]{1,0:T(8,128)S(1)} %get-tuple-element.37), channel_id=1, source_target_pairs={{0,28},{4,24},{8,20},{12,16},{16,12},{20,8},{24,4},{28,0},{1,29},{... | collective-permute-start | bytes 258056 | tf_op jit(solution)/shard_map/ppermute | solution.py:408
  19.5 0.0 collective-permute-done.3.refs_2_
  19.5 0.5 %collective-permute-start.8 = (f32[168,128]{1,0:T(8,128)S(1)}, f32[168,128]{1,0:T(8,128)S(1)}, u32[]{:S(2)}, u32[]{:S(2)}) collective-permute-start(f32[168,128]{1,0:T(8,128)S(1)} %get-tuple-element.38), channel_id=1, source_target_pairs={{0,4},{4,0},{8,12},{12,8},{16,20},{20,16},{24,28},{28,24},{1,5},{5... | collective-permute-start | bytes 258056 | tf_op jit(solution)/shard_map/ppermute | solution.py:408
  20.0 0.0 collective-permute-done.4.refs_3_
  20.0 0.0 collective-permute-done.5.refs_4_
  20.0 1.4 %collective-permute-done.6.refs_5_ = f32[168,128]{1,0:T(8,128)S(1)} collective-permute-done((f32[168,128]{1,0:T(8,128)S(1)}, f32[168,128]{1,0:T(8,128)S(1)}, u32[]{:S(2)}, u32[]{:S(2)}) %collective-permute-start.6) | collective-permute-done | bytes 86048 | tf_op jit(solution)/shard_map/ppermute | solution.py:408
  21.4 3.0 %collective-permute-done.7.refs_6_ = f32[168,128]{1,0:T(8,128)S(1)} collective-permute-done((f32[168,128]{1,0:T(8,128)S(1)}, f32[168,128]{1,0:T(8,128)S(1)}, u32[]{:S(2)}, u32[]{:S(2)}) %collective-permute-start.7) | collective-permute-done | bytes 86048 | tf_op jit(solution)/shard_map/ppermute | solution.py:408
  24.4 1.0 %collective-permute-done.8.refs_7_ = f32[168,128]{1,0:T(8,128)S(1)} collective-permute-done((f32[168,128]{1,0:T(8,128)S(1)}, f32[168,128]{1,0:T(8,128)S(1)}, u32[]{:S(2)}, u32[]{:S(2)}) %collective-permute-start.8) | collective-permute-done | bytes 86048 | tf_op jit(solution)/shard_map/ppermute | solution.py:408
  25.5 3.2 %second_step.1 = (f32[152,128]{1,0:T(8,128)S(1)}, f32[80,128]{1,0:T(8,128)S(1)}, f32[152,128]{1,0:T(8,128)S(1)}, f32[80,128]{1,0:T(8,128)S(1)}, f32[152,128]{1,0...) custom-call(f32[168,128]{1,0:T(8,128)S(1)} %get-tuple-element.31.ref, ...), custom_call_target="tpu_custom_call" | custom-call | flops 4000000 | bytes 4000000 | tf_op jit(solution)/shard_map/second_step/pallas_call | solution.py:395
  28.6 3.3 %collective-permute-start.9 = (f32[80,128]{1,0:T(8,128)S(1)}, f32[80,128]{1,0:T(8,128)S(1)}, u32[]{:S(2)}, u32[]{:S(2)}) collective-permute-start(f32[80,128]{1,0:T(8,128)S(1)} %get-tuple-element.40), channel_id=1, source_target_pairs={{0,16},{4,20},{8,24},{12,28},{16,0},{20,4},{24,8},{28,12},{1,17},{... | collective-permute-start | bytes 122888 | tf_op jit(solution)/shard_map/ppermute | solution.py:408
  32.0 0.0 collective-permute-start.11
  32.0 1.7 %collective-permute-start.10 = (f32[152,128]{1,0:T(8,128)S(1)}, f32[152,128]{1,0:T(8,128)S(1)}, u32[]{:S(2)}, u32[]{:S(2)}) collective-permute-start(f32[152,128]{1,0:T(8,128)S(1)} %get-tuple-element.41), channel_id=1, source_target_pairs={{0,8},{4,12},{8,0},{12,4},{16,24},{20,28},{24,16},{28,20},{1,9},{5... | collective-permute-start | bytes 233480 | tf_op jit(solution)/shard_map/ppermute | solution.py:408
  33.6 1.3 %collective-permute-start.12 = (f32[152,128]{1,0:T(8,128)S(1)}, f32[152,128]{1,0:T(8,128)S(1)}, u32[]{:S(2)}, u32[]{:S(2)}) collective-permute-start(f32[152,128]{1,0:T(8,128)S(1)} %get-tuple-element.43), channel_id=1, source_target_pairs={{0,12},{4,8},{8,4},{12,0},{16,28},{20,24},{24,20},{28,16},{1,13},{... | collective-permute-start | bytes 233480 | tf_op jit(solution)/shard_map/ppermute | solution.py:408
  35.0 2.3 %collective-permute-start.13 = (f32[152,128]{1,0:T(8,128)S(1)}, f32[152,128]{1,0:T(8,128)S(1)}, u32[]{:S(2)}, u32[]{:S(2)}) collective-permute-start(f32[152,128]{1,0:T(8,128)S(1)} %get-tuple-element.44), channel_id=1, source_target_pairs={{0,24},{4,28},{8,16},{12,20},{16,8},{20,12},{24,0},{28,4},{1,25},{... | collective-permute-start | bytes 233480 | tf_op jit(solution)/shard_map/ppermute | solution.py:408
  37.2 0.0 collective-permute-done.9.refs_1_
  37.2 1.5 %collective-permute-start.14 = (f32[152,128]{1,0:T(8,128)S(1)}, f32[152,128]{1,0:T(8,128)S(1)}, u32[]{:S(2)}, u32[]{:S(2)}) collective-permute-start(f32[152,128]{1,0:T(8,128)S(1)} %get-tuple-element.45), channel_id=1, source_target_pairs={{0,28},{4,24},{8,20},{12,16},{16,12},{20,8},{24,4},{28,0},{1,29},{... | collective-permute-start | bytes 233480 | tf_op jit(solution)/shard_map/ppermute | solution.py:408
  38.7 0.0 collective-permute-done.11.refs_3_
  38.7 1.5 %collective-permute-start.15 = (f32[152,128]{1,0:T(8,128)S(1)}, f32[152,128]{1,0:T(8,128)S(1)}, u32[]{:S(2)}, u32[]{:S(2)}) collective-permute-start(f32[152,128]{1,0:T(8,128)S(1)} %get-tuple-element.46), channel_id=1, source_target_pairs={{0,4},{4,0},{8,12},{12,8},{16,20},{20,16},{24,28},{28,24},{1,5},{5... | collective-permute-start | bytes 233480 | tf_op jit(solution)/shard_map/ppermute | solution.py:408
  40.3 0.0 collective-permute-done.10.refs_2_
  40.3 1.0 %collective-permute-start.16 = (f32[72,128]{1,0:T(8,128)S(1)}, f32[72,128]{1,0:T(8,128)S(1)}, u32[]{:S(2)}, u32[]{:S(2)}) collective-permute-start(f32[72,128]{1,0:T(8,128)S(1)} %get-tuple-element.47), channel_id=1, source_target_pairs={{0,16},{4,20},{8,24},{12,28},{16,0},{20,4},{24,8},{28,12},{1,17},{... | collective-permute-start | bytes 110600 | tf_op jit(solution)/shard_map/ppermute | solution.py:408
  41.3 0.0 collective-permute-done.12.refs_4_
  41.3 1.8 %collective-permute-start.17 = (f32[72,128]{1,0:T(8,128)S(1)}, f32[72,128]{1,0:T(8,128)S(1)}, u32[]{:S(2)}, u32[]{:S(2)}) collective-permute-start(f32[72,128]{1,0:T(8,128)S(1)} %get-tuple-element.48), channel_id=1, source_target_pairs={{0,20},{4,16},{8,28},{12,24},{16,4},{20,0},{24,12},{28,8},{1,21},{... | collective-permute-start | bytes 110600 | tf_op jit(solution)/shard_map/ppermute | solution.py:408
  43.1 0.0 collective-permute-done.13.refs_5_
  43.1 1.3 %collective-permute-done.14.refs_6_ = f32[152,128]{1,0:T(8,128)S(1)} collective-permute-done((f32[152,128]{1,0:T(8,128)S(1)}, f32[152,128]{1,0:T(8,128)S(1)}, u32[]{:S(2)}, u32[]{:S(2)}) %collective-permute-start.14) | collective-permute-done | bytes 77856 | tf_op jit(solution)/shard_map/ppermute | solution.py:408
  44.5 0.0 collective-permute-done.15.refs_7_
  44.5 0.1 collective-permute-start.18
  44.6 1.6 %collective-permute-start.19 = (f32[24,128]{1,0:T(8,128)S(1)}, f32[24,128]{1,0:T(8,128)S(1)}, u32[]{:S(2)}, u32[]{:S(2)}) collective-permute-start(f32[24,128]{1,0:T(8,128)S(1)} %get-tuple-element.50), channel_id=1, source_target_pairs={{0,3},{1,2},{2,1},{3,0},{4,7},{5,6},{6,5},{7,4},{8,11},{9,10},{10,... | collective-permute-start | bytes 36872 | tf_op jit(solution)/shard_map/ppermute | solution.py:420
  46.2 0.8 %collective-permute-done.16.refs_8_ = f32[72,128]{1,0:T(8,128)S(1)} collective-permute-done((f32[72,128]{1,0:T(8,128)S(1)}, f32[72,128]{1,0:T(8,128)S(1)}, u32[]{:S(2)}, u32[]{:S(2)}) %collective-permute-start.16) | collective-permute-done | bytes 36896 | tf_op jit(solution)/shard_map/ppermute | solution.py:408
  47.0 1.0 %collective-permute-done.17.refs_9_ = f32[72,128]{1,0:T(8,128)S(1)} collective-permute-done((f32[72,128]{1,0:T(8,128)S(1)}, f32[72,128]{1,0:T(8,128)S(1)}, u32[]{:S(2)}, u32[]{:S(2)}) %collective-permute-start.17) | collective-permute-done | bytes 36896 | tf_op jit(solution)/shard_map/ppermute | solution.py:408
  48.0 0.1 unpack_planes.1.main
  48.1 0.0 collective-permute-done.18.near
  48.1 0.0 collective-permute-done.19.far
  48.1 0.9 %finish.1 = f32[1216,128]{1,0:T(8,128)} custom-call(f32[19,80,128]{2,1,0:T(8,128)S(1)} %unpack_planes.1.main, f32[24,128]{1,0:T(8,128)S(1)} %collective-permute-done.18.near, f32[24,128]{1,0:T(8,128)S(1)} %collective-permute-done.19.far), custom_call_target="tpu_custom_call" | custom-call | flops 100000 | bytes 100000 | tf_op jit(solution)/shard_map/finish/pallas_call | solution.py:395
  (5 shorter events, 0.0 us)
Async XLA Ops:
  0.0 4.9 %copy-start = (f32[1,2,19,4096]{3,1,2,0:T(2,128)S(1)}, f32[1,2,19,4096]{3,1,2,0:T(2,128)}, u32[]{:S(2)}) copy-start(f32[1,2,19,4096]{3,1,2,0:T(2,128)} %param.4) | copy-start | bytes 1867780
  0.0 4.9 %copy-start.1 = (s32[1,2,4096]{2,1,0:T(2,128)S(1)}, s32[1,2,4096]{2,1,0:T(2,128)}, u32[]{:S(2)}) copy-start(s32[1,2,4096]{2,1,0:T(2,128)} %param.5) | copy-start | bytes 98308
  1.7 3.4 %collective-permute-start = (f32[24,128]{1,0:T(8,128)}, f32[24,128]{1,0:T(8,128)S(1)}, u32[]{:S(2)}, u32[]{:S(2)}) collective-permute-start(f32[24,128]{1,0:T(8,128)} %get-tuple-element.29), channel_id=1, source_target_pairs={{0,1},{1,0},{2,3},{3,2},{4,5},{5,4},{6,7},{7,6},{8,9},{9,8},{10,11... | collective-permute-start | bytes 36872 | tf_op jit(solution)/shard_map/ppermute | solution.py:419
  2.2 4.2 %collective-permute-start.1 = (f32[24,128]{1,0:T(8,128)}, f32[24,128]{1,0:T(8,128)S(1)}, u32[]{:S(2)}, u32[]{:S(2)}) collective-permute-start(f32[24,128]{1,0:T(8,128)} %get-tuple-element.30), channel_id=1, source_target_pairs={{0,3},{1,2},{2,1},{3,0},{4,7},{5,6},{6,5},{7,4},{8,11},{9,10},{10,... | collective-permute-start | bytes 36872 | tf_op jit(solution)/shard_map/ppermute | solution.py:420
  4.9 1.6 %copy-start.2 = (f32[8,128]{1,0:T(8,128)S(1)}, f32[8,128]{1,0:T(8,128)}, u32[]{:S(2)}) copy-start(f32[8,128]{1,0:T(8,128)} %get-tuple-element.28.own) | copy-start | bytes 12292
  6.7 9.7 %collective-permute-start.2 = (f32[168,128]{1,0:T(8,128)S(1)}, f32[168,128]{1,0:T(8,128)S(1)}, u32[]{:S(2)}, u32[]{:S(2)}) collective-permute-start(f32[168,128]{1,0:T(8,128)S(1)} %get-tuple-element.32), channel_id=1, source_target_pairs={{0,16},{4,20},{8,24},{12,28},{16,0},{20,4},{24,8},{28,12},{1,17},{... | collective-permute-start | bytes 258056 | tf_op jit(solution)/shard_map/ppermute | solution.py:408
  9.5 10.0 %collective-permute-start.3 = (f32[168,128]{1,0:T(8,128)S(1)}, f32[168,128]{1,0:T(8,128)S(1)}, u32[]{:S(2)}, u32[]{:S(2)}) collective-permute-start(f32[168,128]{1,0:T(8,128)S(1)} %get-tuple-element.33), channel_id=1, source_target_pairs={{0,8},{4,12},{8,0},{12,4},{16,24},{20,28},{24,16},{28,20},{1,9},{5... | collective-permute-start | bytes 258056 | tf_op jit(solution)/shard_map/ppermute | solution.py:408
  11.1 8.9 %collective-permute-start.4 = (f32[168,128]{1,0:T(8,128)S(1)}, f32[168,128]{1,0:T(8,128)S(1)}, u32[]{:S(2)}, u32[]{:S(2)}) collective-permute-start(f32[168,128]{1,0:T(8,128)S(1)} %get-tuple-element.34), channel_id=1, source_target_pairs={{0,20},{4,16},{8,28},{12,24},{16,4},{20,0},{24,12},{28,8},{1,21},{... | collective-permute-start | bytes 258056 | tf_op jit(solution)/shard_map/ppermute | solution.py:408
  12.4 7.6 %collective-permute-start.5 = (f32[168,128]{1,0:T(8,128)S(1)}, f32[168,128]{1,0:T(8,128)S(1)}, u32[]{:S(2)}, u32[]{:S(2)}) collective-permute-start(f32[168,128]{1,0:T(8,128)S(1)} %get-tuple-element.35), channel_id=1, source_target_pairs={{0,12},{4,8},{8,4},{12,0},{16,28},{20,24},{24,20},{28,16},{1,13},{... | collective-permute-start | bytes 258056 | tf_op jit(solution)/shard_map/ppermute | solution.py:408
  12.6 8.8 %collective-permute-start.6 = (f32[168,128]{1,0:T(8,128)S(1)}, f32[168,128]{1,0:T(8,128)S(1)}, u32[]{:S(2)}, u32[]{:S(2)}) collective-permute-start(f32[168,128]{1,0:T(8,128)S(1)} %get-tuple-element.36), channel_id=1, source_target_pairs={{0,24},{4,28},{8,16},{12,20},{16,8},{20,12},{24,0},{28,4},{1,25},{... | collective-permute-start | bytes 258056 | tf_op jit(solution)/shard_map/ppermute | solution.py:408
  16.4 8.1 %collective-permute-start.7 = (f32[168,128]{1,0:T(8,128)S(1)}, f32[168,128]{1,0:T(8,128)S(1)}, u32[]{:S(2)}, u32[]{:S(2)}) collective-permute-start(f32[168,128]{1,0:T(8,128)S(1)} %get-tuple-element.37), channel_id=1, source_target_pairs={{0,28},{4,24},{8,20},{12,16},{16,12},{20,8},{24,4},{28,0},{1,29},{... | collective-permute-start | bytes 258056 | tf_op jit(solution)/shard_map/ppermute | solution.py:408
  19.5 6.0 %collective-permute-start.8 = (f32[168,128]{1,0:T(8,128)S(1)}, f32[168,128]{1,0:T(8,128)S(1)}, u32[]{:S(2)}, u32[]{:S(2)}) collective-permute-start(f32[168,128]{1,0:T(8,128)S(1)} %get-tuple-element.38), channel_id=1, source_target_pairs={{0,4},{4,0},{8,12},{12,8},{16,20},{20,16},{24,28},{28,24},{1,5},{5... | collective-permute-start | bytes 258056 | tf_op jit(solution)/shard_map/ppermute | solution.py:408
  28.6 8.6 %collective-permute-start.9 = (f32[80,128]{1,0:T(8,128)S(1)}, f32[80,128]{1,0:T(8,128)S(1)}, u32[]{:S(2)}, u32[]{:S(2)}) collective-permute-start(f32[80,128]{1,0:T(8,128)S(1)} %get-tuple-element.40), channel_id=1, source_target_pairs={{0,16},{4,20},{8,24},{12,28},{16,0},{20,4},{24,8},{28,12},{1,17},{... | collective-permute-start | bytes 122888 | tf_op jit(solution)/shard_map/ppermute | solution.py:408
  32.0 6.8 %collective-permute-start.11 = (f32[80,128]{1,0:T(8,128)S(1)}, f32[80,128]{1,0:T(8,128)S(1)}, u32[]{:S(2)}, u32[]{:S(2)}) collective-permute-start(f32[80,128]{1,0:T(8,128)S(1)} %get-tuple-element.42), channel_id=1, source_target_pairs={{0,20},{4,16},{8,28},{12,24},{16,4},{20,0},{24,12},{28,8},{1,21},{... | collective-permute-start | bytes 122888 | tf_op jit(solution)/shard_map/ppermute | solution.py:408
  32.0 8.3 %collective-permute-start.10 = (f32[152,128]{1,0:T(8,128)S(1)}, f32[152,128]{1,0:T(8,128)S(1)}, u32[]{:S(2)}, u32[]{:S(2)}) collective-permute-start(f32[152,128]{1,0:T(8,128)S(1)} %get-tuple-element.41), channel_id=1, source_target_pairs={{0,8},{4,12},{8,0},{12,4},{16,24},{20,28},{24,16},{28,20},{1,9},{5... | collective-permute-start | bytes 233480 | tf_op jit(solution)/shard_map/ppermute | solution.py:408
  33.6 7.7 %collective-permute-start.12 = (f32[152,128]{1,0:T(8,128)S(1)}, f32[152,128]{1,0:T(8,128)S(1)}, u32[]{:S(2)}, u32[]{:S(2)}) collective-permute-start(f32[152,128]{1,0:T(8,128)S(1)} %get-tuple-element.43), channel_id=1, source_target_pairs={{0,12},{4,8},{8,4},{12,0},{16,28},{20,24},{24,20},{28,16},{1,13},{... | collective-permute-start | bytes 233480 | tf_op jit(solution)/shard_map/ppermute | solution.py:408
  35.0 8.2 %collective-permute-start.13 = (f32[152,128]{1,0:T(8,128)S(1)}, f32[152,128]{1,0:T(8,128)S(1)}, u32[]{:S(2)}, u32[]{:S(2)}) collective-permute-start(f32[152,128]{1,0:T(8,128)S(1)} %get-tuple-element.44), channel_id=1, source_target_pairs={{0,24},{4,28},{8,16},{12,20},{16,8},{20,12},{24,0},{28,4},{1,25},{... | collective-permute-start | bytes 233480 | tf_op jit(solution)/shard_map/ppermute | solution.py:408
  37.2 7.2 %collective-permute-start.14 = (f32[152,128]{1,0:T(8,128)S(1)}, f32[152,128]{1,0:T(8,128)S(1)}, u32[]{:S(2)}, u32[]{:S(2)}) collective-permute-start(f32[152,128]{1,0:T(8,128)S(1)} %get-tuple-element.45), channel_id=1, source_target_pairs={{0,28},{4,24},{8,20},{12,16},{16,12},{20,8},{24,4},{28,0},{1,29},{... | collective-permute-start | bytes 233480 | tf_op jit(solution)/shard_map/ppermute | solution.py:408
  38.7 5.8 %collective-permute-start.15 = (f32[152,128]{1,0:T(8,128)S(1)}, f32[152,128]{1,0:T(8,128)S(1)}, u32[]{:S(2)}, u32[]{:S(2)}) collective-permute-start(f32[152,128]{1,0:T(8,128)S(1)} %get-tuple-element.46), channel_id=1, source_target_pairs={{0,4},{4,0},{8,12},{12,8},{16,20},{20,16},{24,28},{28,24},{1,5},{5... | collective-permute-start | bytes 233480 | tf_op jit(solution)/shard_map/ppermute | solution.py:408
  40.3 6.7 %collective-permute-start.16 = (f32[72,128]{1,0:T(8,128)S(1)}, f32[72,128]{1,0:T(8,128)S(1)}, u32[]{:S(2)}, u32[]{:S(2)}) collective-permute-start(f32[72,128]{1,0:T(8,128)S(1)} %get-tuple-element.47), channel_id=1, source_target_pairs={{0,16},{4,20},{8,24},{12,28},{16,0},{20,4},{24,8},{28,12},{1,17},{... | collective-permute-start | bytes 110600 | tf_op jit(solution)/shard_map/ppermute | solution.py:408
  41.3 6.7 %collective-permute-start.17 = (f32[72,128]{1,0:T(8,128)S(1)}, f32[72,128]{1,0:T(8,128)S(1)}, u32[]{:S(2)}, u32[]{:S(2)}) collective-permute-start(f32[72,128]{1,0:T(8,128)S(1)} %get-tuple-element.48), channel_id=1, source_target_pairs={{0,20},{4,16},{8,28},{12,24},{16,4},{20,0},{24,12},{28,8},{1,21},{... | collective-permute-start | bytes 110600 | tf_op jit(solution)/shard_map/ppermute | solution.py:408
  44.5 3.6 %collective-permute-start.18 = (f32[24,128]{1,0:T(8,128)S(1)}, f32[24,128]{1,0:T(8,128)S(1)}, u32[]{:S(2)}, u32[]{:S(2)}) collective-permute-start(f32[24,128]{1,0:T(8,128)S(1)} %get-tuple-element.49), channel_id=1, source_target_pairs={{0,1},{1,0},{2,3},{3,2},{4,5},{5,4},{6,7},{7,6},{8,9},{9,8},{10,11... | collective-permute-start | bytes 36872 | tf_op jit(solution)/shard_map/ppermute | solution.py:419
  44.6 3.5 %collective-permute-start.19 = (f32[24,128]{1,0:T(8,128)S(1)}, f32[24,128]{1,0:T(8,128)S(1)}, u32[]{:S(2)}, u32[]{:S(2)}) collective-permute-start(f32[24,128]{1,0:T(8,128)S(1)} %get-tuple-element.50), channel_id=1, source_target_pairs={{0,3},{1,2},{2,1},{3,0},{4,7},{5,6},{6,5},{7,4},{8,11},{9,10},{10,... | collective-permute-start | bytes 36872 | tf_op jit(solution)/shard_map/ppermute | solution.py:420

commit v13 on v11

--- a/solution.py
+++ b/solution.py
@@ -222,10 +222,38 @@
                         n * PLANE : (n + 1) * PLANE
                     ]
 
+    def seats(blocks):
+        return [(b % NB, pl.multiple_of((b // NB) * block, block)) for b in blocks]
+
+    def place_in(d, blocks, message, lattice):
+        for t, (kz, y) in enumerate(seats(blocks)):
+            for p in range(Q + 1):
+                lattice[p, kz, pl.ds(y, block), :] = message[
+                    pl.ds(p * share + t, block, stride=NB), :
+                ]
+
+    early = [0, half, 2, 3]
+    late = [d for d in order_in if d not in early]
+
+    def early_kernel(*refs):
+        *got, lattice, table, sem = refs
+        copies = [
+            pltpu.make_async_copy(ref.at[pl.ds(head, 8), :], table.at[n], sem.at[n])
+            for n, ref in enumerate(got)
+        ]
+        for copy in copies:
+            copy.start()
+        for copy in copies:
+            copy.wait()
+        for n, d in enumerate(early):
+            blocks = [table[n, 0, t].astype(jnp.int32) for t in range(NB)]
+            place_in(d, blocks, got[n], lattice)
+
     def middle_kernel(*refs):
         got = by_owner(refs[:owners], order_in)
-        outs = by_owner(refs[owners : 2 * owners], order_out)
-        lattice, ready, table, sem = refs[2 * owners :]
+        lattice = refs[owners]
+        outs = by_owner(refs[owners + 1 : 2 * owners + 1], order_out)
+        _, ready, table, sem = refs[2 * owners + 1 :]
         me, odd = position()
         place = dynamic_place(me, odd, owners)
         first, last = place == 0, place == owners - 1
@@ -243,9 +271,6 @@
 
         other = jnp.where(first, 1, jnp.where(last, 2, 0))
 
-        def seats(blocks):
-            return [(b % NB, pl.multiple_of((b // NB) * block, block)) for b in blocks]
-
         def held(d, which):
             return [number(d, 2 * which, t) for t in range(NB)]
 
@@ -258,12 +283,8 @@
             crossed = flip % 2 == 1
             return [jnp.where(crossed, two, one), jnp.where(crossed, one, two)]
 
-        for d in range(owners):
-            for t, (kz, y) in enumerate(seats(held(d, 0))):
-                for p in range(Q + 1):
-                    lattice[p, kz, pl.ds(y, block), :] = got[d][
-                        pl.ds(p * share + t, block, stride=NB), :
-                    ]
+        for d in late:
+            place_in(d, held(d, 0), got[d], lattice)
 
         def bring(chosen, i):
             for d in range(owners):
@@ -354,8 +375,10 @@
             out[pl.ds(faces, 4), :] = jnp.zeros((4, LANES), f32)
         send_sides(odd, up, down, near, far)
 
+    ends = [(p, 0) for p in UPWARD] + [(p, WHOLE - 8) for p in DOWNWARD]
+
     def unpack_kernel(*refs):
-        got, main = by_owner(refs[:owners], order_out), refs[owners]
+        got, (out, edge, main, sem) = by_owner(refs[:owners], order_out), refs[owners:]
         me, odd = position()
         for d in range(owners):
             place = dynamic_place(me ^ d, odd, owners)
@@ -365,27 +388,52 @@
                 main[p, pl.ds(8 + here + cx * PLANE, share), :] = got[d][
                     pl.ds(p * share, share), :
                 ]
-
-    def finish_kernel(main, near, far, out):
+        copy = pltpu.make_async_copy(main.at[:, pl.ds(8, WHOLE), :], out, sem.at[0])
+        copy.start()
+        for n, (p, start) in enumerate(ends):
+            edge[n] = main[p, pl.ds(8 + start, 8), :]
+        copy.wait()
+
+    def finish_kernel(_, edge, near, far, out, patch, sem):
         below, above = sides(position()[1], near, far)
-        for p in range(Q):
-            out[pl.ds(p * WHOLE, WHOLE), :] = main[p, pl.ds(8, WHOLE), :]
-        for n, p in enumerate(UPWARD):
-            out[pl.ds(p * WHOLE, PLANE), :] = below[n * PLANE : (n + 1) * PLANE]
-        for n, p in enumerate(DOWNWARD):
-            out[pl.ds(p * WHOLE + WHOLE - PLANE, PLANE), :] = above[n * PLANE : (n + 1) * PLANE]
+        for n in range(len(ends)):
+            patch[n] = edge[n]
+        for n in range(len(UPWARD)):
+            patch[n, pl.ds(0, PLANE), :] = below[n * PLANE : (n + 1) * PLANE]
+            patch[len(UPWARD) + n, pl.ds(8 - PLANE, PLANE), :] = above[n * PLANE : (n + 1) * PLANE]
+        copies = [
+            pltpu.make_async_copy(patch.at[n], out.at[p, pl.ds(start, 8), :], sem.at[n])
+            for n, (p, start) in enumerate(ends)
+        ]
+        for copy in copies:
+            copy.start()
+        for copy in copies:
+            copy.wait()
 
     def shape(*dims):
         return jax.ShapeDtypeStruct(dims, f32)
 
-    def call(kernel, name, out_shape, inputs, cost, scratch=(), spec=VMEM_SPEC, limit=40):
-        outs = jax.tree.map(lambda _: VMEM_SPEC, out_shape)
+    def call(
+        kernel,
+        name,
+        out_shape,
+        inputs,
+        cost,
+        scratch=(),
+        spec=VMEM_SPEC,
+        limit=40,
+        aliases=None,
+        out_specs=None,
+    ):
+        outs = out_specs or jax.tree.map(lambda _: VMEM_SPEC, out_shape)
+        specs = spec if isinstance(spec, tuple) else (spec,) * len(inputs)
         return pl.pallas_call(
             kernel,
             out_shape=out_shape,
-            in_specs=[spec] * len(inputs),
+            in_specs=specs,
             out_specs=outs,
             scratch_shapes=list(scratch),
+            input_output_aliases=aliases or {},
             compiler_params=pltpu.CompilerParams(vmem_limit_bytes=limit * 1024 * 1024),
             cost_estimate=pl.CostEstimate(flops=cost, bytes_accessed=cost, transcendentals=0),
             name=name,
@@ -408,7 +456,7 @@
     def padded(count):
         return shape(count, 8 + WHOLE + 8, LANES)
 
-    work = pltpu.VMEM((Q + 1, NB, rows, LANES), f32)
+    whole_lattice = (Q + 1, NB, rows, LANES)
     small, large = 100_000, 4_000_000
 
     def shards(populations, solid_mask, slot_blocks, swap_slots):
@@ -452,18 +500,26 @@
             large,
         )
         got = exchange(parts, order_in)
-        parts = call(
+        lattice = call(
+            early_kernel,
+            "place_early",
+            shape(*whole_lattice),
+            [got[order_in.index(d)] for d in early],
+            large,
+            (pltpu.SMEM((len(early), 8, LANES), f32), pltpu.SemaphoreType.DMA((len(early),))),
+        )
+        *parts, _ = call(
             middle_kernel,
             "second_step",
-            (shape(rows_out, LANES),) * owners,
-            got,
+            (shape(rows_out, LANES),) * owners + (shape(*whole_lattice),),
+            (*got, lattice),
             large,
             (
-                work,
-                work,
+                pltpu.VMEM(whole_lattice, f32),
                 pltpu.SMEM((owners, 8, LANES), f32),
                 pltpu.SemaphoreType.DMA((owners,)),
             ),
+            aliases={owners: owners},
         )
         home = exchange(parts, order_out)
         near, far = call(
@@ -475,9 +531,25 @@
             (pltpu.VMEM((rows_hop, LANES), f32),) * 2,
         )
         near, far = hop(near, far)
-        main = call(unpack_kernel, "unpack_planes", padded(Q), home, large)
+        out, edge = call(
+            unpack_kernel,
+            "unpack_planes",
+            (shape(Q, WHOLE, LANES), shape(len(ends), 8, LANES)),
+            home,
+            large,
+            (pltpu.VMEM((Q, 8 + WHOLE + 8, LANES), f32), pltpu.SemaphoreType.DMA((1,))),
+            out_specs=(in_place, VMEM_SPEC),
+        )
         out = call(
-            finish_kernel, "finish", shape(Q * WHOLE, LANES), (main, near, far), small
+            finish_kernel,
+            "finish",
+            shape(Q, WHOLE, LANES),
+            (out, edge, near, far),
+            small,
+            (pltpu.VMEM((len(ends), 8, LANES), f32), pltpu.SemaphoreType.DMA((len(ends),))),
+            spec=(in_place, VMEM_SPEC, VMEM_SPEC, VMEM_SPEC),
+            aliases={0: 0},
+            out_specs=in_place,
         )
         out = out.reshape(Q, tiles, NB, LANES).transpose(0, 2, 1, 3)
         return out.reshape(Q, NB, B * B * B).transpose(1, 0, 2)[None]

time: 49 us -> 48.6 us (level)
  waiting for transfers between devices: 13 us -> 11.3 us
  Pallas kernels: 6.3 us -> 7.81 us
    pallas_call x7 -> x8, Pallas kernels: 6.3 us -> 7.81 us  [call(): pl.pallas_call(kernel, out_shape=out_shape, in_specs=specs, out_specs=out...]
    ppermute x14, waiting for transfers between devices: 10.2 us -> 9.26 us  [exchange(): lax.ppermute(parts[n], 'gx', [(g, g ^ order[n]) for g in range(owners)])]
    ppermute x2, waiting for transfers between devices: 2.8 us -> 1.99 us  [hop(): lax.ppermute(far, 'gy', list(enumerate(behind)))]
  transfers between devices with their start and end apart: 18 -> 18, of which waited for: 10 -> 7; matrix products, arithmetic and copies ran while one was open for 0% -> 0% of each run, Pallas kernels for 1% -> 4%
where the time goes in v13:
time: 48.6 us; the launch traced here: 48.3 us
  starting transfers between devices  29.2 us (60%)
  waiting for transfers between devices  11.3 us (23%)
  Pallas kernels  7.81 us (16%)
    ppermute x14, starting transfers between devices, exchange(): lax.ppermute(parts[n], 'gx', [(g, g ^ order[n]) for g in range(owners)])  24.4 us
    ppermute x14, waiting for transfers between devices, exchange(): lax.ppermute(parts[n], 'gx', [(g, g ^ order[n]) for g in range(owners)])  9.26 us
    pallas_call x8, Pallas kernels, call(): pl.pallas_call(kernel, out_shape=out_shape, in_specs=specs, out_specs=out...  7.81 us
    ppermute x2, starting transfers between devices, hop(): lax.ppermute(far, 'gy', list(enumerate(behind)))  4.22 us
    ppermute x2, waiting for transfers between devices, hop(): lax.ppermute(far, 'gy', list(enumerate(behind)))  1.99 us
  transfers between devices with their start and end apart: 18, of which 7 were waited for; matrix products, arithmetic and copies ran while one was open for 0% of the time, Pallas kernels for 4%

profile of v13, /device:TPU:0, one launch (start us, length us, event | category | flops | bytes accessed | tf_op | source)
XLA Modules:
  0.0 48.3 jit_solution(16585630570746801613)
XLA Ops:
  0.0 0.0 copy-start
  0.0 0.0 copy-start.1
  0.0 1.7 %edge_planes.1 = (f32[24,128]{1,0:T(8,128)}, f32[24,128]{1,0:T(8,128)}, f32[8,128]{1,0:T(8,128)}) custom-call(f32[19,64,128]{2,1,0:T(8,128)} %bitcast.26, s32[64,128]{1,0:T(8,128)} %bitcast.28, s32[1,2]{1,0:T(1,128)} %slots.1, s32[2,3]{1,0:T(2,128)} %bitcast.30), custom_call_target="tpu_custom_call" | custom-call | flops 100000 | bytes 100000 | tf_op jit(solution)/shard_map/edge_planes/pallas_call | solution.py:430
  1.7 0.5 %collective-permute-start = (f32[24,128]{1,0:T(8,128)}, f32[24,128]{1,0:T(8,128)S(1)}, u32[]{:S(2)}, u32[]{:S(2)}) collective-permute-start(f32[24,128]{1,0:T(8,128)} %get-tuple-element.29), channel_id=1, source_target_pairs={{0,1},{1,0},{2,3},{3,2},{4,5},{5,4},{6,7},{7,6},{8,9},{9,8},{10,11... | collective-permute-start | bytes 36872 | tf_op jit(solution)/shard_map/ppermute | solution.py:452
  2.2 2.6 %collective-permute-start.1 = (f32[24,128]{1,0:T(8,128)}, f32[24,128]{1,0:T(8,128)S(1)}, u32[]{:S(2)}, u32[]{:S(2)}) collective-permute-start(f32[24,128]{1,0:T(8,128)} %get-tuple-element.30), channel_id=1, source_target_pairs={{0,3},{1,2},{2,1},{3,0},{4,7},{5,6},{6,5},{7,4},{8,11},{9,10},{10,... | collective-permute-start | bytes 36872 | tf_op jit(solution)/shard_map/ppermute | solution.py:453
  4.9 0.0 copy-done
  4.9 0.0 copy-done.1
  4.9 0.2 first_collision.1.post
  5.1 0.0 collective-permute-done.near
  5.1 1.4 %collective-permute-done.1.far = f32[24,128]{1,0:T(8,128)S(1)} collective-permute-done((f32[24,128]{1,0:T(8,128)}, f32[24,128]{1,0:T(8,128)S(1)}, u32[]{:S(2)}, u32[]{:S(2)}) %collective-permute-start.1) | collective-permute-done | bytes 12320 | tf_op jit(solution)/shard_map/ppermute | solution.py:453
  6.5 0.0 copy-done.2
  6.5 0.2 pack_planes.1
  6.7 2.8 %collective-permute-start.2 = (f32[168,128]{1,0:T(8,128)S(1)}, f32[168,128]{1,0:T(8,128)S(1)}, u32[]{:S(2)}, u32[]{:S(2)}) collective-permute-start(f32[168,128]{1,0:T(8,128)S(1)} %get-tuple-element.32), channel_id=1, source_target_pairs={{0,16},{4,20},{8,24},{12,28},{16,0},{20,4},{24,8},{28,12},{1,17},{... | collective-permute-start | bytes 258056 | tf_op jit(solution)/shard_map/ppermute | solution.py:444
  9.5 1.6 %collective-permute-start.3 = (f32[168,128]{1,0:T(8,128)S(1)}, f32[168,128]{1,0:T(8,128)S(1)}, u32[]{:S(2)}, u32[]{:S(2)}) collective-permute-start(f32[168,128]{1,0:T(8,128)S(1)} %get-tuple-element.33), channel_id=1, source_target_pairs={{0,8},{4,12},{8,0},{12,4},{16,24},{20,28},{24,16},{28,20},{1,9},{5... | collective-permute-start | bytes 258056 | tf_op jit(solution)/shard_map/ppermute | solution.py:444
  11.1 1.4 %collective-permute-start.5 = (f32[168,128]{1,0:T(8,128)S(1)}, f32[168,128]{1,0:T(8,128)S(1)}, u32[]{:S(2)}, u32[]{:S(2)}) collective-permute-start(f32[168,128]{1,0:T(8,128)S(1)} %get-tuple-element.35), channel_id=1, source_target_pairs={{0,12},{4,8},{8,4},{12,0},{16,28},{20,24},{24,20},{28,16},{1,13},{... | collective-permute-start | bytes 258056 | tf_op jit(solution)/shard_map/ppermute | solution.py:444
  12.5 0.1 collective-permute-start.4
  12.6 3.8 %collective-permute-start.6 = (f32[168,128]{1,0:T(8,128)S(1)}, f32[168,128]{1,0:T(8,128)S(1)}, u32[]{:S(2)}, u32[]{:S(2)}) collective-permute-start(f32[168,128]{1,0:T(8,128)S(1)} %get-tuple-element.36), channel_id=1, source_target_pairs={{0,24},{4,28},{8,16},{12,20},{16,8},{20,12},{24,0},{28,4},{1,25},{... | collective-permute-start | bytes 258056 | tf_op jit(solution)/shard_map/ppermute | solution.py:444
  16.4 0.0 collective-permute-done.2.refs_1_
  16.4 2.8 %collective-permute-start.7 = (f32[168,128]{1,0:T(8,128)S(1)}, f32[168,128]{1,0:T(8,128)S(1)}, u32[]{:S(2)}, u32[]{:S(2)}) collective-permute-start(f32[168,128]{1,0:T(8,128)S(1)} %get-tuple-element.37), channel_id=1, source_target_pairs={{0,28},{4,24},{8,20},{12,16},{16,12},{20,8},{24,4},{28,0},{1,29},{... | collective-permute-start | bytes 258056 | tf_op jit(solution)/shard_map/ppermute | solution.py:444
  19.1 0.0 collective-permute-done.3.refs_2_
  19.1 0.5 %collective-permute-start.8 = (f32[168,128]{1,0:T(8,128)S(1)}, f32[168,128]{1,0:T(8,128)S(1)}, u32[]{:S(2)}, u32[]{:S(2)}) collective-permute-start(f32[168,128]{1,0:T(8,128)S(1)} %get-tuple-element.38), channel_id=1, source_target_pairs={{0,4},{4,0},{8,12},{12,8},{16,20},{20,16},{24,28},{28,24},{1,5},{5... | collective-permute-start | bytes 258056 | tf_op jit(solution)/shard_map/ppermute | solution.py:444
  19.6 0.0 collective-permute-done.5.refs_3_.refs_4_
  19.6 0.9 %place_early.1.refs_8_ = f32[20,2,32,128]{3,2,1,0:T(8,128)S(1)} custom-call(f32[168,128]{1,0:T(8,128)S(1)} %get-tuple-element.31.refs_0_, f32[168,128]{1,0:T(8,128)S(1)} %collective-permute-done.2.refs_1_, f32[168,128]{1,0:T(8,128)S(1)} %collective-permute-done.3.refs_2_, f32[168,128]{1,0:T(8,128)S(1)} %collective-permute-done.5.refs_3_.refs_4_), custom_call_target="tpu_custom_call" | custom-call | flops 4000000 | bytes 4000000 | tf_op jit(solution)/shard_map/place_early/pallas_call | solution.py:430
  20.6 4.7 %collective-permute-done.4.refs_3_ = f32[168,128]{1,0:T(8,128)S(1)} collective-permute-done((f32[168,128]{1,0:T(8,128)S(1)}, f32[168,128]{1,0:T(8,128)S(1)}, u32[]{:S(2)}, u32[]{:S(2)}) %collective-permute-start.4) | collective-permute-done | bytes 86048 | tf_op jit(solution)/shard_map/ppermute | solution.py:444
  25.3 0.0 collective-permute-done.6.refs_5_
  25.3 0.0 collective-permute-done.7.refs_6_
  25.3 0.4 collective-permute-done.8.refs_7_
  25.7 3.0 %second_step.1 = (f32[152,128]{1,0:T(8,128)S(1)}, f32[152,128]{1,0:T(8,128)S(1)}, f32[152,128]{1,0:T(8,128)S(1)}, f32[152,128]{1,0:T(8,128)S(1)}, f32[152,128]{1...) custom-call(f32[168,128]{1,0:T(8,128)S(1)} %get-tuple-element.31.ref, ...), custom_call_target="tpu_custom_call", output_to_operand_aliasing={{8}: (8, {})} | custom-call | flops 4000000 | bytes 4000000 | tf_op jit(solution)/shard_map/second_step/pallas_call | solution.py:430
  28.8 3.1 %collective-permute-start.9 = (f32[152,128]{1,0:T(8,128)S(1)}, f32[152,128]{1,0:T(8,128)S(1)}, u32[]{:S(2)}, u32[]{:S(2)}) collective-permute-start(f32[152,128]{1,0:T(8,128)S(1)} %get-tuple-element.40), channel_id=1, source_target_pairs={{0,16},{4,20},{8,24},{12,28},{16,0},{20,4},{24,8},{28,12},{1,17},{... | collective-permute-start | bytes 233480 | tf_op jit(solution)/shard_map/ppermute | solution.py:444
  31.9 0.0 collective-permute-start.10
  31.9 1.8 %collective-permute-start.11 = (f32[152,128]{1,0:T(8,128)S(1)}, f32[152,128]{1,0:T(8,128)S(1)}, u32[]{:S(2)}, u32[]{:S(2)}) collective-permute-start(f32[152,128]{1,0:T(8,128)S(1)} %get-tuple-element.42), channel_id=1, source_target_pairs={{0,20},{4,16},{8,28},{12,24},{16,4},{20,0},{24,12},{28,8},{1,21},{... | collective-permute-start | bytes 233480 | tf_op jit(solution)/shard_map/ppermute | solution.py:444
  33.7 1.2 %collective-permute-start.12 = (f32[152,128]{1,0:T(8,128)S(1)}, f32[152,128]{1,0:T(8,128)S(1)}, u32[]{:S(2)}, u32[]{:S(2)}) collective-permute-start(f32[152,128]{1,0:T(8,128)S(1)} %get-tuple-element.43), channel_id=1, source_target_pairs={{0,12},{4,8},{8,4},{12,0},{16,28},{20,24},{24,20},{28,16},{1,13},{... | collective-permute-start | bytes 233480 | tf_op jit(solution)/shard_map/ppermute | solution.py:444
  34.9 2.3 %collective-permute-start.13 = (f32[152,128]{1,0:T(8,128)S(1)}, f32[152,128]{1,0:T(8,128)S(1)}, u32[]{:S(2)}, u32[]{:S(2)}) collective-permute-start(f32[152,128]{1,0:T(8,128)S(1)} %get-tuple-element.44), channel_id=1, source_target_pairs={{0,24},{4,28},{8,16},{12,20},{16,8},{20,12},{24,0},{28,4},{1,25},{... | collective-permute-start | bytes 233480 | tf_op jit(solution)/shard_map/ppermute | solution.py:444
  37.2 0.0 collective-permute-done.9.refs_1_
  37.2 1.5 %collective-permute-start.14 = (f32[152,128]{1,0:T(8,128)S(1)}, f32[152,128]{1,0:T(8,128)S(1)}, u32[]{:S(2)}, u32[]{:S(2)}) collective-permute-start(f32[152,128]{1,0:T(8,128)S(1)} %get-tuple-element.45), channel_id=1, source_target_pairs={{0,28},{4,24},{8,20},{12,16},{16,12},{20,8},{24,4},{28,0},{1,29},{... | collective-permute-start | bytes 233480 | tf_op jit(solution)/shard_map/ppermute | solution.py:444
  38.7 0.0 collective-permute-done.10.refs_2_
  38.7 1.5 %collective-permute-start.15 = (f32[152,128]{1,0:T(8,128)S(1)}, f32[152,128]{1,0:T(8,128)S(1)}, u32[]{:S(2)}, u32[]{:S(2)}) collective-permute-start(f32[152,128]{1,0:T(8,128)S(1)} %get-tuple-element.46), channel_id=1, source_target_pairs={{0,4},{4,0},{8,12},{12,8},{16,20},{20,16},{24,28},{28,24},{1,5},{5... | collective-permute-start | bytes 233480 | tf_op jit(solution)/shard_map/ppermute | solution.py:444
  40.2 1.0 %collective-permute-done.11.refs_3_ = f32[152,128]{1,0:T(8,128)S(1)} collective-permute-done((f32[152,128]{1,0:T(8,128)S(1)}, f32[152,128]{1,0:T(8,128)S(1)}, u32[]{:S(2)}, u32[]{:S(2)}) %collective-permute-start.11) | collective-permute-done | bytes 77856 | tf_op jit(solution)/shard_map/ppermute | solution.py:444
  41.2 0.0 collective-permute-done.12.refs_4_
  41.2 1.1 %collective-permute-done.13.refs_5_ = f32[152,128]{1,0:T(8,128)S(1)} collective-permute-done((f32[152,128]{1,0:T(8,128)S(1)}, f32[152,128]{1,0:T(8,128)S(1)}, u32[]{:S(2)}, u32[]{:S(2)}) %collective-permute-start.13) | collective-permute-done | bytes 77856 | tf_op jit(solution)/shard_map/ppermute | solution.py:444
  42.3 2.0 %collective-permute-done.14.refs_6_ = f32[152,128]{1,0:T(8,128)S(1)} collective-permute-done((f32[152,128]{1,0:T(8,128)S(1)}, f32[152,128]{1,0:T(8,128)S(1)}, u32[]{:S(2)}, u32[]{:S(2)}) %collective-permute-start.14) | collective-permute-done | bytes 77856 | tf_op jit(solution)/shard_map/ppermute | solution.py:444
  44.3 0.0 collective-permute-done.15.refs_7_
  44.4 0.1 collective-permute-start.16
  44.4 1.6 %collective-permute-start.17 = (f32[24,128]{1,0:T(8,128)S(1)}, f32[24,128]{1,0:T(8,128)S(1)}, u32[]{:S(2)}, u32[]{:S(2)}) collective-permute-start(f32[24,128]{1,0:T(8,128)S(1)} %get-tuple-element.50), channel_id=1, source_target_pairs={{0,3},{1,2},{2,1},{3,0},{4,7},{5,6},{6,5},{7,4},{8,11},{9,10},{10,... | collective-permute-start | bytes 36872 | tf_op jit(solution)/shard_map/ppermute | solution.py:453
  46.0 0.9 %unpack_planes.1 = (f32[19,64,128]{2,1,0:T(8,128)}, f32[10,8,128]{2,1,0:T(8,128)S(1)}) custom-call(f32[152,128]{1,0:T(8,128)S(1)} %get-tuple-element.39.refs_0_, f32[152,128]{1,0:T(8,128)S(1)} %collective-permute-done.9.refs_1_, f32[152,128]{1,0:T(8,128)S(1)} %collective-permute-done.10.refs_2_, f32[152,128]{1,0:T(8,128)S(1)} %collective-permute-done.11.refs_3_, ...), custom_call_target="tpu_custom_call" | custom-call | flops 4000000 | bytes 4000000 | tf_op jit(solution)/shard_map/unpack_planes/pallas_call | solution.py:430
  47.0 0.0 collective-permute-done.16.near
  47.0 0.6 %collective-permute-done.17.far = f32[24,128]{1,0:T(8,128)S(1)} collective-permute-done((f32[24,128]{1,0:T(8,128)S(1)}, f32[24,128]{1,0:T(8,128)S(1)}, u32[]{:S(2)}, u32[]{:S(2)}) %collective-permute-start.17) | collective-permute-done | bytes 12320 | tf_op jit(solution)/shard_map/ppermute | solution.py:453
  47.6 0.7 %finish.1 = f32[19,64,128]{2,1,0:T(8,128)} custom-call(f32[19,64,128]{2,1,0:T(8,128)} %get-tuple-element.47._, f32[10,8,128]{2,1,0:T(8,128)S(1)} %get-tuple-element.48.edge, f32[24,128]{1,0:T(8,128)S(1)} %collective-permute-done.16.near, f32[24,128]{1,0:T(8,128)S(1)} %collective-permute-done.17.far), custom_call_target="tpu_custom_call", output_to_operand_aliasing={{}: (0, {})} | custom-call | flops 100000 | bytes 100000 | tf_op jit(solution)/shard_map/finish/pallas_call | solution.py:430
  (2 shorter events, 0.0 us)
Async XLA Ops:
  0.0 4.9 %copy-start = (f32[1,2,19,4096]{3,1,2,0:T(2,128)S(1)}, f32[1,2,19,4096]{3,1,2,0:T(2,128)}, u32[]{:S(2)}) copy-start(f32[1,2,19,4096]{3,1,2,0:T(2,128)} %param.4) | copy-start | bytes 1867780
  0.0 4.9 %copy-start.1 = (s32[1,2,4096]{2,1,0:T(2,128)S(1)}, s32[1,2,4096]{2,1,0:T(2,128)}, u32[]{:S(2)}) copy-start(s32[1,2,4096]{2,1,0:T(2,128)} %param.5) | copy-start | bytes 98308
  1.7 3.4 %collective-permute-start = (f32[24,128]{1,0:T(8,128)}, f32[24,128]{1,0:T(8,128)S(1)}, u32[]{:S(2)}, u32[]{:S(2)}) collective-permute-start(f32[24,128]{1,0:T(8,128)} %get-tuple-element.29), channel_id=1, source_target_pairs={{0,1},{1,0},{2,3},{3,2},{4,5},{5,4},{6,7},{7,6},{8,9},{9,8},{10,11... | collective-permute-start | bytes 36872 | tf_op jit(solution)/shard_map/ppermute | solution.py:452
  2.2 4.2 %collective-permute-start.1 = (f32[24,128]{1,0:T(8,128)}, f32[24,128]{1,0:T(8,128)S(1)}, u32[]{:S(2)}, u32[]{:S(2)}) collective-permute-start(f32[24,128]{1,0:T(8,128)} %get-tuple-element.30), channel_id=1, source_target_pairs={{0,3},{1,2},{2,1},{3,0},{4,7},{5,6},{6,5},{7,4},{8,11},{9,10},{10,... | collective-permute-start | bytes 36872 | tf_op jit(solution)/shard_map/ppermute | solution.py:453
  4.9 1.6 %copy-start.2 = (f32[8,128]{1,0:T(8,128)S(1)}, f32[8,128]{1,0:T(8,128)}, u32[]{:S(2)}) copy-start(f32[8,128]{1,0:T(8,128)} %get-tuple-element.28.own) | copy-start | bytes 12292
  6.7 9.7 %collective-permute-start.2 = (f32[168,128]{1,0:T(8,128)S(1)}, f32[168,128]{1,0:T(8,128)S(1)}, u32[]{:S(2)}, u32[]{:S(2)}) collective-permute-start(f32[168,128]{1,0:T(8,128)S(1)} %get-tuple-element.32), channel_id=1, source_target_pairs={{0,16},{4,20},{8,24},{12,28},{16,0},{20,4},{24,8},{28,12},{1,17},{... | collective-permute-start | bytes 258056 | tf_op jit(solution)/shard_map/ppermute | solution.py:444
  9.5 9.6 %collective-permute-start.3 = (f32[168,128]{1,0:T(8,128)S(1)}, f32[168,128]{1,0:T(8,128)S(1)}, u32[]{:S(2)}, u32[]{:S(2)}) collective-permute-start(f32[168,128]{1,0:T(8,128)S(1)} %get-tuple-element.33), channel_id=1, source_target_pairs={{0,8},{4,12},{8,0},{12,4},{16,24},{20,28},{24,16},{28,20},{1,9},{5... | collective-permute-start | bytes 258056 | tf_op jit(solution)/shard_map/ppermute | solution.py:444
  11.1 8.6 %collective-permute-start.5 = (f32[168,128]{1,0:T(8,128)S(1)}, f32[168,128]{1,0:T(8,128)S(1)}, u32[]{:S(2)}, u32[]{:S(2)}) collective-permute-start(f32[168,128]{1,0:T(8,128)S(1)} %get-tuple-element.35), channel_id=1, source_target_pairs={{0,12},{4,8},{8,4},{12,0},{16,28},{20,24},{24,20},{28,16},{1,13},{... | collective-permute-start | bytes 258056 | tf_op jit(solution)/shard_map/ppermute | solution.py:444
  12.5 12.8 %collective-permute-start.4 = (f32[168,128]{1,0:T(8,128)S(1)}, f32[168,128]{1,0:T(8,128)S(1)}, u32[]{:S(2)}, u32[]{:S(2)}) collective-permute-start(f32[168,128]{1,0:T(8,128)S(1)} %get-tuple-element.34), channel_id=1, source_target_pairs={{0,20},{4,16},{8,28},{12,24},{16,4},{20,0},{24,12},{28,8},{1,21},{... | collective-permute-start | bytes 258056 | tf_op jit(solution)/shard_map/ppermute | solution.py:444
  12.6 12.7 %collective-permute-start.6 = (f32[168,128]{1,0:T(8,128)S(1)}, f32[168,128]{1,0:T(8,128)S(1)}, u32[]{:S(2)}, u32[]{:S(2)}) collective-permute-start(f32[168,128]{1,0:T(8,128)S(1)} %get-tuple-element.36), channel_id=1, source_target_pairs={{0,24},{4,28},{8,16},{12,20},{16,8},{20,12},{24,0},{28,4},{1,25},{... | collective-permute-start | bytes 258056 | tf_op jit(solution)/shard_map/ppermute | solution.py:444
  16.4 8.9 %collective-permute-start.7 = (f32[168,128]{1,0:T(8,128)S(1)}, f32[168,128]{1,0:T(8,128)S(1)}, u32[]{:S(2)}, u32[]{:S(2)}) collective-permute-start(f32[168,128]{1,0:T(8,128)S(1)} %get-tuple-element.37), channel_id=1, source_target_pairs={{0,28},{4,24},{8,20},{12,16},{16,12},{20,8},{24,4},{28,0},{1,29},{... | collective-permute-start | bytes 258056 | tf_op jit(solution)/shard_map/ppermute | solution.py:444
  19.1 6.6 %collective-permute-start.8 = (f32[168,128]{1,0:T(8,128)S(1)}, f32[168,128]{1,0:T(8,128)S(1)}, u32[]{:S(2)}, u32[]{:S(2)}) collective-permute-start(f32[168,128]{1,0:T(8,128)S(1)} %get-tuple-element.38), channel_id=1, source_target_pairs={{0,4},{4,0},{8,12},{12,8},{16,20},{20,16},{24,28},{28,24},{1,5},{5... | collective-permute-start | bytes 258056 | tf_op jit(solution)/shard_map/ppermute | solution.py:444
  28.8 8.4 %collective-permute-start.9 = (f32[152,128]{1,0:T(8,128)S(1)}, f32[152,128]{1,0:T(8,128)S(1)}, u32[]{:S(2)}, u32[]{:S(2)}) collective-permute-start(f32[152,128]{1,0:T(8,128)S(1)} %get-tuple-element.40), channel_id=1, source_target_pairs={{0,16},{4,20},{8,24},{12,28},{16,0},{20,4},{24,8},{28,12},{1,17},{... | collective-permute-start | bytes 233480 | tf_op jit(solution)/shard_map/ppermute | solution.py:444
  31.9 6.8 %collective-permute-start.10 = (f32[152,128]{1,0:T(8,128)S(1)}, f32[152,128]{1,0:T(8,128)S(1)}, u32[]{:S(2)}, u32[]{:S(2)}) collective-permute-start(f32[152,128]{1,0:T(8,128)S(1)} %get-tuple-element.41), channel_id=1, source_target_pairs={{0,8},{4,12},{8,0},{12,4},{16,24},{20,28},{24,16},{28,20},{1,9},{5... | collective-permute-start | bytes 233480 | tf_op jit(solution)/shard_map/ppermute | solution.py:444
  31.9 9.3 %collective-permute-start.11 = (f32[152,128]{1,0:T(8,128)S(1)}, f32[152,128]{1,0:T(8,128)S(1)}, u32[]{:S(2)}, u32[]{:S(2)}) collective-permute-start(f32[152,128]{1,0:T(8,128)S(1)} %get-tuple-element.42), channel_id=1, source_target_pairs={{0,20},{4,16},{8,28},{12,24},{16,4},{20,0},{24,12},{28,8},{1,21},{... | collective-permute-start | bytes 233480 | tf_op jit(solution)/shard_map/ppermute | solution.py:444
  33.7 7.6 %collective-permute-start.12 = (f32[152,128]{1,0:T(8,128)S(1)}, f32[152,128]{1,0:T(8,128)S(1)}, u32[]{:S(2)}, u32[]{:S(2)}) collective-permute-start(f32[152,128]{1,0:T(8,128)S(1)} %get-tuple-element.43), channel_id=1, source_target_pairs={{0,12},{4,8},{8,4},{12,0},{16,28},{20,24},{24,20},{28,16},{1,13},{... | collective-permute-start | bytes 233480 | tf_op jit(solution)/shard_map/ppermute | solution.py:444
  34.9 7.4 %collective-permute-start.13 = (f32[152,128]{1,0:T(8,128)S(1)}, f32[152,128]{1,0:T(8,128)S(1)}, u32[]{:S(2)}, u32[]{:S(2)}) collective-permute-start(f32[152,128]{1,0:T(8,128)S(1)} %get-tuple-element.44), channel_id=1, source_target_pairs={{0,24},{4,28},{8,16},{12,20},{16,8},{20,12},{24,0},{28,4},{1,25},{... | collective-permute-start | bytes 233480 | tf_op jit(solution)/shard_map/ppermute | solution.py:444
  37.2 7.1 %collective-permute-start.14 = (f32[152,128]{1,0:T(8,128)S(1)}, f32[152,128]{1,0:T(8,128)S(1)}, u32[]{:S(2)}, u32[]{:S(2)}) collective-permute-start(f32[152,128]{1,0:T(8,128)S(1)} %get-tuple-element.45), channel_id=1, source_target_pairs={{0,28},{4,24},{8,20},{12,16},{16,12},{20,8},{24,4},{28,0},{1,29},{... | collective-permute-start | bytes 233480 | tf_op jit(solution)/shard_map/ppermute | solution.py:444
  38.7 5.7 %collective-permute-start.15 = (f32[152,128]{1,0:T(8,128)S(1)}, f32[152,128]{1,0:T(8,128)S(1)}, u32[]{:S(2)}, u32[]{:S(2)}) collective-permute-start(f32[152,128]{1,0:T(8,128)S(1)} %get-tuple-element.46), channel_id=1, source_target_pairs={{0,4},{4,0},{8,12},{12,8},{16,20},{20,16},{24,28},{28,24},{1,5},{5... | collective-permute-start | bytes 233480 | tf_op jit(solution)/shard_map/ppermute | solution.py:444
  44.4 2.6 %collective-permute-start.16 = (f32[24,128]{1,0:T(8,128)S(1)}, f32[24,128]{1,0:T(8,128)S(1)}, u32[]{:S(2)}, u32[]{:S(2)}) collective-permute-start(f32[24,128]{1,0:T(8,128)S(1)} %get-tuple-element.49), channel_id=1, source_target_pairs={{0,1},{1,0},{2,3},{3,2},{4,5},{5,4},{6,7},{7,6},{8,9},{9,8},{10,11... | collective-permute-start | bytes 36872 | tf_op jit(solution)/shard_map/ppermute | solution.py:452
  44.4 3.2 %collective-permute-start.17 = (f32[24,128]{1,0:T(8,128)S(1)}, f32[24,128]{1,0:T(8,128)S(1)}, u32[]{:S(2)}, u32[]{:S(2)}) collective-permute-start(f32[24,128]{1,0:T(8,128)S(1)} %get-tuple-element.50), channel_id=1, source_target_pairs={{0,3},{1,2},{2,1},{3,0},{4,7},{5,6},{6,5},{7,4},{8,11},{9,10},{10,... | collective-permute-start | bytes 36872 | tf_op jit(solution)/shard_map/ppermute | solution.py:453

commit v14 on v13

--- a/solution.py
+++ b/solution.py
@@ -10,6 +10,7 @@
 LANES = 128
 PLANE_ROWS = B * B // LANES
 PLANE = PLANE_ROWS * NB
+FIELDS = NB + 3
 WHOLE = B * PLANE
 
 VELOCITIES = (
@@ -177,13 +178,16 @@
         for copy in copies:
             copy.wait()
         own[...] = jnp.zeros((8, LANES), f32)
-        own[0:1, 0:NB] = held[...].astype(f32)
-        own[1:2, 0:3] = given[0:1].astype(f32)
+        own[4:5, 0:NB] = held[...].astype(f32)
+        own[5:6, 0:3] = given[0:1].astype(f32)
+        lane = lax.broadcasted_iota(jnp.int32, (8, LANES), 1)
+        swaps_beside = pltpu.roll(pltpu.roll(own[...], NB, 1), 7, 0)
+        own[...] = jnp.where(lane < NB, own[...], swaps_beside)
         for n, (out, chosen, inside) in enumerate(((up, UPWARD, 8 - PLANE), (down, DOWNWARD, 0))):
             after = collide([cells[n, p] for p in range(Q)], solid[n] > 0)
             for m, p in enumerate(chosen):
                 out[pl.ds(m * PLANE, PLANE), :] = after[p][inside : inside + PLANE]
-            out[pl.ds(faces, 4), :] = own[0:4]
+            out[pl.ds(faces, 4), :] = own[4:8]
         send_sides(position()[1], up, down, near, far)
 
     def collide_kernel(cells, solid, post):
@@ -198,6 +202,11 @@
         me, odd = position()
         below, above = sides(odd, near, far)
         outs = by_owner(outs, order_in)
+        lane = lax.broadcasted_iota(jnp.int32, (8, LANES), 1)
+        tail_below = pltpu.roll(below[faces - 4 : faces + 4], FIELDS, 1)
+        tail_above = pltpu.roll(above[faces - 4 : faces + 4], 2 * FIELDS, 1)
+        header = jnp.where(lane < 2 * FIELDS, tail_below, tail_above)
+        header = jnp.where(lane < FIELDS, own[...], header)
         for d in range(owners):
             out = outs[d]
             place = dynamic_place(me ^ d, odd, owners)
@@ -205,10 +214,7 @@
             for p in range(Q + 1):
                 cx = VELOCITIES[p][0] if p < Q else 0
                 out[pl.ds(p * share, share), :] = post[p, pl.ds(8 + here - cx * PLANE, share), :]
-            out[pl.ds(head, 2), :] = own[0:2]
-            out[pl.ds(head + 2, 2), :] = below[faces : faces + 2]
-            out[pl.ds(head + 4, 2), :] = above[faces : faces + 2]
-            out[pl.ds(head + 6, 2), :] = own[2:4]
+            out[pl.ds(head, 8), :] = header
 
             @pl.when(place == 0)
             def _():
@@ -238,7 +244,7 @@
     def early_kernel(*refs):
         *got, lattice, table, sem = refs
         copies = [
-            pltpu.make_async_copy(ref.at[pl.ds(head, 8), :], table.at[n], sem.at[n])
+            pltpu.make_async_copy(ref.at[pl.ds(head + 4, 1), :], table.at[pl.ds(n, 1), :], sem.at[n])
             for n, ref in enumerate(got)
         ]
         for copy in copies:
@@ -246,7 +252,7 @@
         for copy in copies:
             copy.wait()
         for n, d in enumerate(early):
-            blocks = [table[n, 0, t].astype(jnp.int32) for t in range(NB)]
+            blocks = [table[n, t].astype(jnp.int32) for t in range(NB)]
             place_in(d, blocks, got[n], lattice)
 
     def middle_kernel(*refs):
@@ -258,7 +264,9 @@
         place = dynamic_place(me, odd, owners)
         first, last = place == 0, place == owners - 1
         copies = [
-            pltpu.make_async_copy(got[d].at[pl.ds(head, 8), :], table.at[d], sem.at[d])
+            pltpu.make_async_copy(
+                got[d].at[pl.ds(head + 4, 1), :], table.at[pl.ds(d, 1), :], sem.at[d]
+            )
             for d in range(owners)
         ]
         for copy in copies:
@@ -266,17 +274,17 @@
         for copy in copies:
             copy.wait()
 
-        def number(d, row, column):
-            return table[d, row, column].astype(jnp.int32)
+        def number(d, which, field):
+            return table[d, which * FIELDS + field].astype(jnp.int32)
 
         other = jnp.where(first, 1, jnp.where(last, 2, 0))
 
         def held(d, which):
-            return [number(d, 2 * which, t) for t in range(NB)]
+            return [number(d, which, t) for t in range(NB)]
 
         def final(d, which):
             def lead(e, r):
-                return number(d ^ e, 2 * which + 1, r)
+                return number(d ^ e, which, NB + r)
 
             flip = lead(0, 2) + lead(4, 2) + lead(4, 1) + lead(6, 1) + lead(6, 0) + lead(7, 0)
             one, two = held(d ^ 7, which)
@@ -506,7 +514,7 @@
             shape(*whole_lattice),
             [got[order_in.index(d)] for d in early],
             large,
-            (pltpu.SMEM((len(early), 8, LANES), f32), pltpu.SemaphoreType.DMA((len(early),))),
+            (pltpu.SMEM((len(early), LANES), f32), pltpu.SemaphoreType.DMA((len(early),))),
         )
         *parts, _ = call(
             middle_kernel,
@@ -516,7 +524,7 @@
             large,
             (
                 pltpu.VMEM(whole_lattice, f32),
-                pltpu.SMEM((owners, 8, LANES), f32),
+                pltpu.SMEM((owners, LANES), f32),
                 pltpu.SemaphoreType.DMA((owners,)),
             ),
             aliases={owners: owners},

time: 48.6 us -> 48.2 us (level)
  Pallas kernels: 7.81 us -> 7.22 us
    pallas_call x8, Pallas kernels: 7.81 us -> 7.22 us  [call(): pl.pallas_call(kernel, out_shape=out_shape, in_specs=specs, out_specs=out...]
where the time goes in v14:
time: 48.2 us; the launch traced here: 47.9 us
  starting transfers between devices  29.1 us (60%)
  waiting for transfers between devices  11.5 us (24%)
  Pallas kernels  7.22 us (15%)
    ppermute x14, starting transfers between devices, exchange(): lax.ppermute(parts[n], 'gx', [(g, g ^ order[n]) for g in range(owners)])  24.3 us
    ppermute x14, waiting for transfers between devices, exchange(): lax.ppermute(parts[n], 'gx', [(g, g ^ order[n]) for g in range(owners)])  9.49 us
    pallas_call x8, Pallas kernels, call(): pl.pallas_call(kernel, out_shape=out_shape, in_specs=specs, out_specs=out...  7.22 us
    ppermute x2, starting transfers between devices, hop(): lax.ppermute(far, 'gy', list(enumerate(behind)))  4.22 us
    ppermute x2, waiting for transfers between devices, hop(): lax.ppermute(far, 'gy', list(enumerate(behind)))  1.99 us
  transfers between devices with their start and end apart: 18, of which 7 were waited for; matrix products, arithmetic and copies ran while one was open for 0% of the time, Pallas kernels for 4%

profile of v14, /device:TPU:0, one launch (start us, length us, event | category | flops | bytes accessed | tf_op | source)
XLA Modules:
  0.0 47.9 jit_solution(5681237790070454763)
XLA Ops:
  0.0 0.0 copy-start
  0.0 0.0 copy-start.1
  0.0 1.8 %edge_planes.1 = (f32[24,128]{1,0:T(8,128)}, f32[24,128]{1,0:T(8,128)}, f32[8,128]{1,0:T(8,128)}) custom-call(f32[19,64,128]{2,1,0:T(8,128)} %bitcast.26, s32[64,128]{1,0:T(8,128)} %bitcast.28, s32[1,2]{1,0:T(1,128)} %slots.1, s32[2,3]{1,0:T(2,128)} %bitcast.30), custom_call_target="tpu_custom_call" | custom-call | flops 100000 | bytes 100000 | tf_op jit(solution)/shard_map/edge_planes/pallas_call | solution.py:438
  1.8 0.5 %collective-permute-start = (f32[24,128]{1,0:T(8,128)}, f32[24,128]{1,0:T(8,128)S(1)}, u32[]{:S(2)}, u32[]{:S(2)}) collective-permute-start(f32[24,128]{1,0:T(8,128)} %get-tuple-element.29), channel_id=1, source_target_pairs={{0,1},{1,0},{2,3},{3,2},{4,5},{5,4},{6,7},{7,6},{8,9},{9,8},{10,11... | collective-permute-start | bytes 36872 | tf_op jit(solution)/shard_map/ppermute | solution.py:460
  2.3 2.6 %collective-permute-start.1 = (f32[24,128]{1,0:T(8,128)}, f32[24,128]{1,0:T(8,128)S(1)}, u32[]{:S(2)}, u32[]{:S(2)}) collective-permute-start(f32[24,128]{1,0:T(8,128)} %get-tuple-element.30), channel_id=1, source_target_pairs={{0,3},{1,2},{2,1},{3,0},{4,7},{5,6},{6,5},{7,4},{8,11},{9,10},{10,... | collective-permute-start | bytes 36872 | tf_op jit(solution)/shard_map/ppermute | solution.py:461
  4.9 0.0 copy-done
  4.9 0.0 copy-done.1
  4.9 0.2 first_collision.1.post
  5.1 0.0 collective-permute-done.near
  5.2 1.4 %collective-permute-done.1.far = f32[24,128]{1,0:T(8,128)S(1)} collective-permute-done((f32[24,128]{1,0:T(8,128)}, f32[24,128]{1,0:T(8,128)S(1)}, u32[]{:S(2)}, u32[]{:S(2)}) %collective-permute-start.1) | collective-permute-done | bytes 12320 | tf_op jit(solution)/shard_map/ppermute | solution.py:461
  6.5 0.0 copy-done.2
  6.5 0.2 pack_planes.1
  6.7 2.8 %collective-permute-start.2 = (f32[168,128]{1,0:T(8,128)S(1)}, f32[168,128]{1,0:T(8,128)S(1)}, u32[]{:S(2)}, u32[]{:S(2)}) collective-permute-start(f32[168,128]{1,0:T(8,128)S(1)} %get-tuple-element.32), channel_id=1, source_target_pairs={{0,16},{4,20},{8,24},{12,28},{16,0},{20,4},{24,8},{28,12},{1,17},{... | collective-permute-start | bytes 258056 | tf_op jit(solution)/shard_map/ppermute | solution.py:452
  9.6 1.6 %collective-permute-start.3 = (f32[168,128]{1,0:T(8,128)S(1)}, f32[168,128]{1,0:T(8,128)S(1)}, u32[]{:S(2)}, u32[]{:S(2)}) collective-permute-start(f32[168,128]{1,0:T(8,128)S(1)} %get-tuple-element.33), channel_id=1, source_target_pairs={{0,8},{4,12},{8,0},{12,4},{16,24},{20,28},{24,16},{28,20},{1,9},{5... | collective-permute-start | bytes 258056 | tf_op jit(solution)/shard_map/ppermute | solution.py:452
  11.2 1.4 %collective-permute-start.5 = (f32[168,128]{1,0:T(8,128)S(1)}, f32[168,128]{1,0:T(8,128)S(1)}, u32[]{:S(2)}, u32[]{:S(2)}) collective-permute-start(f32[168,128]{1,0:T(8,128)S(1)} %get-tuple-element.35), channel_id=1, source_target_pairs={{0,12},{4,8},{8,4},{12,0},{16,28},{20,24},{24,20},{28,16},{1,13},{... | collective-permute-start | bytes 258056 | tf_op jit(solution)/shard_map/ppermute | solution.py:452
  12.6 0.1 collective-permute-start.4
  12.7 3.8 %collective-permute-start.6 = (f32[168,128]{1,0:T(8,128)S(1)}, f32[168,128]{1,0:T(8,128)S(1)}, u32[]{:S(2)}, u32[]{:S(2)}) collective-permute-start(f32[168,128]{1,0:T(8,128)S(1)} %get-tuple-element.36), channel_id=1, source_target_pairs={{0,24},{4,28},{8,16},{12,20},{16,8},{20,12},{24,0},{28,4},{1,25},{... | collective-permute-start | bytes 258056 | tf_op jit(solution)/shard_map/ppermute | solution.py:452
  16.5 0.0 collective-permute-done.2.refs_1_
  16.5 2.7 %collective-permute-start.7 = (f32[168,128]{1,0:T(8,128)S(1)}, f32[168,128]{1,0:T(8,128)S(1)}, u32[]{:S(2)}, u32[]{:S(2)}) collective-permute-start(f32[168,128]{1,0:T(8,128)S(1)} %get-tuple-element.37), channel_id=1, source_target_pairs={{0,28},{4,24},{8,20},{12,16},{16,12},{20,8},{24,4},{28,0},{1,29},{... | collective-permute-start | bytes 258056 | tf_op jit(solution)/shard_map/ppermute | solution.py:452
  19.2 0.0 collective-permute-done.3.refs_2_
  19.2 0.5 %collective-permute-start.8 = (f32[168,128]{1,0:T(8,128)S(1)}, f32[168,128]{1,0:T(8,128)S(1)}, u32[]{:S(2)}, u32[]{:S(2)}) collective-permute-start(f32[168,128]{1,0:T(8,128)S(1)} %get-tuple-element.38), channel_id=1, source_target_pairs={{0,4},{4,0},{8,12},{12,8},{16,20},{20,16},{24,28},{28,24},{1,5},{5... | collective-permute-start | bytes 258056 | tf_op jit(solution)/shard_map/ppermute | solution.py:452
  19.7 0.0 collective-permute-done.5.refs_3_.refs_4_
  19.7 0.7 %place_early.1.refs_8_ = f32[20,2,32,128]{3,2,1,0:T(8,128)S(1)} custom-call(f32[168,128]{1,0:T(8,128)S(1)} %get-tuple-element.31.refs_0_, f32[168,128]{1,0:T(8,128)S(1)} %collective-permute-done.2.refs_1_, f32[168,128]{1,0:T(8,128)S(1)} %collective-permute-done.3.refs_2_, f32[168,128]{1,0:T(8,128)S(1)} %collective-permute-done.5.refs_3_.refs_4_), custom_call_target="tpu_custom_call" | custom-call | flops 4000000 | bytes 4000000 | tf_op jit(solution)/shard_map/place_early/pallas_call | solution.py:438
  20.4 4.9 %collective-permute-done.4.refs_3_ = f32[168,128]{1,0:T(8,128)S(1)} collective-permute-done((f32[168,128]{1,0:T(8,128)S(1)}, f32[168,128]{1,0:T(8,128)S(1)}, u32[]{:S(2)}, u32[]{:S(2)}) %collective-permute-start.4) | collective-permute-done | bytes 86048 | tf_op jit(solution)/shard_map/ppermute | solution.py:452
  25.3 0.0 collective-permute-done.6.refs_5_
  25.3 0.0 collective-permute-done.7.refs_6_
  25.3 0.4 collective-permute-done.8.refs_7_
  25.8 2.6 %second_step.1 = (f32[152,128]{1,0:T(8,128)S(1)}, f32[152,128]{1,0:T(8,128)S(1)}, f32[152,128]{1,0:T(8,128)S(1)}, f32[152,128]{1,0:T(8,128)S(1)}, f32[152,128]{1...) custom-call(f32[168,128]{1,0:T(8,128)S(1)} %get-tuple-element.31.ref, ...), custom_call_target="tpu_custom_call", output_to_operand_aliasing={{8}: (8, {})} | custom-call | flops 4000000 | bytes 4000000 | tf_op jit(solution)/shard_map/second_step/pallas_call | solution.py:438
  28.4 3.1 %collective-permute-start.9 = (f32[152,128]{1,0:T(8,128)S(1)}, f32[152,128]{1,0:T(8,128)S(1)}, u32[]{:S(2)}, u32[]{:S(2)}) collective-permute-start(f32[152,128]{1,0:T(8,128)S(1)} %get-tuple-element.40), channel_id=1, source_target_pairs={{0,16},{4,20},{8,24},{12,28},{16,0},{20,4},{24,8},{28,12},{1,17},{... | collective-permute-start | bytes 233480 | tf_op jit(solution)/shard_map/ppermute | solution.py:452
  31.5 0.0 collective-permute-start.10
  31.5 1.8 %collective-permute-start.11 = (f32[152,128]{1,0:T(8,128)S(1)}, f32[152,128]{1,0:T(8,128)S(1)}, u32[]{:S(2)}, u32[]{:S(2)}) collective-permute-start(f32[152,128]{1,0:T(8,128)S(1)} %get-tuple-element.42), channel_id=1, source_target_pairs={{0,20},{4,16},{8,28},{12,24},{16,4},{20,0},{24,12},{28,8},{1,21},{... | collective-permute-start | bytes 233480 | tf_op jit(solution)/shard_map/ppermute | solution.py:452
  33.3 1.2 %collective-permute-start.12 = (f32[152,128]{1,0:T(8,128)S(1)}, f32[152,128]{1,0:T(8,128)S(1)}, u32[]{:S(2)}, u32[]{:S(2)}) collective-permute-start(f32[152,128]{1,0:T(8,128)S(1)} %get-tuple-element.43), channel_id=1, source_target_pairs={{0,12},{4,8},{8,4},{12,0},{16,28},{20,24},{24,20},{28,16},{1,13},{... | collective-permute-start | bytes 233480 | tf_op jit(solution)/shard_map/ppermute | solution.py:452
  34.5 2.3 %collective-permute-start.13 = (f32[152,128]{1,0:T(8,128)S(1)}, f32[152,128]{1,0:T(8,128)S(1)}, u32[]{:S(2)}, u32[]{:S(2)}) collective-permute-start(f32[152,128]{1,0:T(8,128)S(1)} %get-tuple-element.44), channel_id=1, source_target_pairs={{0,24},{4,28},{8,16},{12,20},{16,8},{20,12},{24,0},{28,4},{1,25},{... | collective-permute-start | bytes 233480 | tf_op jit(solution)/shard_map/ppermute | solution.py:452
  36.8 0.0 collective-permute-done.9.refs_1_
  36.8 1.5 %collective-permute-start.14 = (f32[152,128]{1,0:T(8,128)S(1)}, f32[152,128]{1,0:T(8,128)S(1)}, u32[]{:S(2)}, u32[]{:S(2)}) collective-permute-start(f32[152,128]{1,0:T(8,128)S(1)} %get-tuple-element.45), channel_id=1, source_target_pairs={{0,28},{4,24},{8,20},{12,16},{16,12},{20,8},{24,4},{28,0},{1,29},{... | collective-permute-start | bytes 233480 | tf_op jit(solution)/shard_map/ppermute | solution.py:452
  38.3 0.0 collective-permute-done.10.refs_2_
  38.3 1.5 %collective-permute-start.15 = (f32[152,128]{1,0:T(8,128)S(1)}, f32[152,128]{1,0:T(8,128)S(1)}, u32[]{:S(2)}, u32[]{:S(2)}) collective-permute-start(f32[152,128]{1,0:T(8,128)S(1)} %get-tuple-element.46), channel_id=1, source_target_pairs={{0,4},{4,0},{8,12},{12,8},{16,20},{20,16},{24,28},{28,24},{1,5},{5... | collective-permute-start | bytes 233480 | tf_op jit(solution)/shard_map/ppermute | solution.py:452
  39.8 1.0 %collective-permute-done.11.refs_3_ = f32[152,128]{1,0:T(8,128)S(1)} collective-permute-done((f32[152,128]{1,0:T(8,128)S(1)}, f32[152,128]{1,0:T(8,128)S(1)}, u32[]{:S(2)}, u32[]{:S(2)}) %collective-permute-start.11) | collective-permute-done | bytes 77856 | tf_op jit(solution)/shard_map/ppermute | solution.py:452
  40.8 0.0 collective-permute-done.12.refs_4_
  40.8 1.1 %collective-permute-done.13.refs_5_ = f32[152,128]{1,0:T(8,128)S(1)} collective-permute-done((f32[152,128]{1,0:T(8,128)S(1)}, f32[152,128]{1,0:T(8,128)S(1)}, u32[]{:S(2)}, u32[]{:S(2)}) %collective-permute-start.13) | collective-permute-done | bytes 77856 | tf_op jit(solution)/shard_map/ppermute | solution.py:452
  41.9 2.0 %collective-permute-done.14.refs_6_ = f32[152,128]{1,0:T(8,128)S(1)} collective-permute-done((f32[152,128]{1,0:T(8,128)S(1)}, f32[152,128]{1,0:T(8,128)S(1)}, u32[]{:S(2)}, u32[]{:S(2)}) %collective-permute-start.14) | collective-permute-done | bytes 77856 | tf_op jit(solution)/shard_map/ppermute | solution.py:452
  43.9 0.0 collective-permute-done.15.refs_7_
  44.0 0.1 collective-permute-start.16
  44.0 1.6 %collective-permute-start.17 = (f32[24,128]{1,0:T(8,128)S(1)}, f32[24,128]{1,0:T(8,128)S(1)}, u32[]{:S(2)}, u32[]{:S(2)}) collective-permute-start(f32[24,128]{1,0:T(8,128)S(1)} %get-tuple-element.50), channel_id=1, source_target_pairs={{0,3},{1,2},{2,1},{3,0},{4,7},{5,6},{6,5},{7,4},{8,11},{9,10},{10,... | collective-permute-start | bytes 36872 | tf_op jit(solution)/shard_map/ppermute | solution.py:461
  45.6 0.9 %unpack_planes.1 = (f32[19,64,128]{2,1,0:T(8,128)}, f32[10,8,128]{2,1,0:T(8,128)S(1)}) custom-call(f32[152,128]{1,0:T(8,128)S(1)} %get-tuple-element.39.refs_0_, f32[152,128]{1,0:T(8,128)S(1)} %collective-permute-done.9.refs_1_, f32[152,128]{1,0:T(8,128)S(1)} %collective-permute-done.10.refs_2_, f32[152,128]{1,0:T(8,128)S(1)} %collective-permute-done.11.refs_3_, ...), custom_call_target="tpu_custom_call" | custom-call | flops 4000000 | bytes 4000000 | tf_op jit(solution)/shard_map/unpack_planes/pallas_call | solution.py:438
  46.6 0.0 collective-permute-done.16.near
  46.6 0.6 %collective-permute-done.17.far = f32[24,128]{1,0:T(8,128)S(1)} collective-permute-done((f32[24,128]{1,0:T(8,128)S(1)}, f32[24,128]{1,0:T(8,128)S(1)}, u32[]{:S(2)}, u32[]{:S(2)}) %collective-permute-start.17) | collective-permute-done | bytes 12320 | tf_op jit(solution)/shard_map/ppermute | solution.py:461
  47.2 0.7 %finish.1 = f32[19,64,128]{2,1,0:T(8,128)} custom-call(f32[19,64,128]{2,1,0:T(8,128)} %get-tuple-element.47._, f32[10,8,128]{2,1,0:T(8,128)S(1)} %get-tuple-element.48.edge, f32[24,128]{1,0:T(8,128)S(1)} %collective-permute-done.16.near, f32[24,128]{1,0:T(8,128)S(1)} %collective-permute-done.17.far), custom_call_target="tpu_custom_call", output_to_operand_aliasing={{}: (0, {})} | custom-call | flops 100000 | bytes 100000 | tf_op jit(solution)/shard_map/finish/pallas_call | solution.py:438
  (2 shorter events, 0.0 us)
Async XLA Ops:
  0.0 4.9 %copy-start = (f32[1,2,19,4096]{3,1,2,0:T(2,128)S(1)}, f32[1,2,19,4096]{3,1,2,0:T(2,128)}, u32[]{:S(2)}) copy-start(f32[1,2,19,4096]{3,1,2,0:T(2,128)} %param.4) | copy-start | bytes 1867780
  0.0 4.9 %copy-start.1 = (s32[1,2,4096]{2,1,0:T(2,128)S(1)}, s32[1,2,4096]{2,1,0:T(2,128)}, u32[]{:S(2)}) copy-start(s32[1,2,4096]{2,1,0:T(2,128)} %param.5) | copy-start | bytes 98308
  1.8 3.4 %collective-permute-start = (f32[24,128]{1,0:T(8,128)}, f32[24,128]{1,0:T(8,128)S(1)}, u32[]{:S(2)}, u32[]{:S(2)}) collective-permute-start(f32[24,128]{1,0:T(8,128)} %get-tuple-element.29), channel_id=1, source_target_pairs={{0,1},{1,0},{2,3},{3,2},{4,5},{5,4},{6,7},{7,6},{8,9},{9,8},{10,11... | collective-permute-start | bytes 36872 | tf_op jit(solution)/shard_map/ppermute | solution.py:460
  2.3 4.2 %collective-permute-start.1 = (f32[24,128]{1,0:T(8,128)}, f32[24,128]{1,0:T(8,128)S(1)}, u32[]{:S(2)}, u32[]{:S(2)}) collective-permute-start(f32[24,128]{1,0:T(8,128)} %get-tuple-element.30), channel_id=1, source_target_pairs={{0,3},{1,2},{2,1},{3,0},{4,7},{5,6},{6,5},{7,4},{8,11},{9,10},{10,... | collective-permute-start | bytes 36872 | tf_op jit(solution)/shard_map/ppermute | solution.py:461
  4.9 1.6 %copy-start.2 = (f32[8,128]{1,0:T(8,128)S(1)}, f32[8,128]{1,0:T(8,128)}, u32[]{:S(2)}) copy-start(f32[8,128]{1,0:T(8,128)} %get-tuple-element.28.own) | copy-start | bytes 12292
  6.7 9.7 %collective-permute-start.2 = (f32[168,128]{1,0:T(8,128)S(1)}, f32[168,128]{1,0:T(8,128)S(1)}, u32[]{:S(2)}, u32[]{:S(2)}) collective-permute-start(f32[168,128]{1,0:T(8,128)S(1)} %get-tuple-element.32), channel_id=1, source_target_pairs={{0,16},{4,20},{8,24},{12,28},{16,0},{20,4},{24,8},{28,12},{1,17},{... | collective-permute-start | bytes 258056 | tf_op jit(solution)/shard_map/ppermute | solution.py:452
  9.6 9.6 %collective-permute-start.3 = (f32[168,128]{1,0:T(8,128)S(1)}, f32[168,128]{1,0:T(8,128)S(1)}, u32[]{:S(2)}, u32[]{:S(2)}) collective-permute-start(f32[168,128]{1,0:T(8,128)S(1)} %get-tuple-element.33), channel_id=1, source_target_pairs={{0,8},{4,12},{8,0},{12,4},{16,24},{20,28},{24,16},{28,20},{1,9},{5... | collective-permute-start | bytes 258056 | tf_op jit(solution)/shard_map/ppermute | solution.py:452
  11.2 8.5 %collective-permute-start.5 = (f32[168,128]{1,0:T(8,128)S(1)}, f32[168,128]{1,0:T(8,128)S(1)}, u32[]{:S(2)}, u32[]{:S(2)}) collective-permute-start(f32[168,128]{1,0:T(8,128)S(1)} %get-tuple-element.35), channel_id=1, source_target_pairs={{0,12},{4,8},{8,4},{12,0},{16,28},{20,24},{24,20},{28,16},{1,13},{... | collective-permute-start | bytes 258056 | tf_op jit(solution)/shard_map/ppermute | solution.py:452
  12.6 12.8 %collective-permute-start.4 = (f32[168,128]{1,0:T(8,128)S(1)}, f32[168,128]{1,0:T(8,128)S(1)}, u32[]{:S(2)}, u32[]{:S(2)}) collective-permute-start(f32[168,128]{1,0:T(8,128)S(1)} %get-tuple-element.34), channel_id=1, source_target_pairs={{0,20},{4,16},{8,28},{12,24},{16,4},{20,0},{24,12},{28,8},{1,21},{... | collective-permute-start | bytes 258056 | tf_op jit(solution)/shard_map/ppermute | solution.py:452
  12.7 12.7 %collective-permute-start.6 = (f32[168,128]{1,0:T(8,128)S(1)}, f32[168,128]{1,0:T(8,128)S(1)}, u32[]{:S(2)}, u32[]{:S(2)}) collective-permute-start(f32[168,128]{1,0:T(8,128)S(1)} %get-tuple-element.36), channel_id=1, source_target_pairs={{0,24},{4,28},{8,16},{12,20},{16,8},{20,12},{24,0},{28,4},{1,25},{... | collective-permute-start | bytes 258056 | tf_op jit(solution)/shard_map/ppermute | solution.py:452
  16.5 8.9 %collective-permute-start.7 = (f32[168,128]{1,0:T(8,128)S(1)}, f32[168,128]{1,0:T(8,128)S(1)}, u32[]{:S(2)}, u32[]{:S(2)}) collective-permute-start(f32[168,128]{1,0:T(8,128)S(1)} %get-tuple-element.37), channel_id=1, source_target_pairs={{0,28},{4,24},{8,20},{12,16},{16,12},{20,8},{24,4},{28,0},{1,29},{... | collective-permute-start | bytes 258056 | tf_op jit(solution)/shard_map/ppermute | solution.py:452
  19.2 6.6 %collective-permute-start.8 = (f32[168,128]{1,0:T(8,128)S(1)}, f32[168,128]{1,0:T(8,128)S(1)}, u32[]{:S(2)}, u32[]{:S(2)}) collective-permute-start(f32[168,128]{1,0:T(8,128)S(1)} %get-tuple-element.38), channel_id=1, source_target_pairs={{0,4},{4,0},{8,12},{12,8},{16,20},{20,16},{24,28},{28,24},{1,5},{5... | collective-permute-start | bytes 258056 | tf_op jit(solution)/shard_map/ppermute | solution.py:452
  28.4 8.4 %collective-permute-start.9 = (f32[152,128]{1,0:T(8,128)S(1)}, f32[152,128]{1,0:T(8,128)S(1)}, u32[]{:S(2)}, u32[]{:S(2)}) collective-permute-start(f32[152,128]{1,0:T(8,128)S(1)} %get-tuple-element.40), channel_id=1, source_target_pairs={{0,16},{4,20},{8,24},{12,28},{16,0},{20,4},{24,8},{28,12},{1,17},{... | collective-permute-start | bytes 233480 | tf_op jit(solution)/shard_map/ppermute | solution.py:452
  31.5 6.8 %collective-permute-start.10 = (f32[152,128]{1,0:T(8,128)S(1)}, f32[152,128]{1,0:T(8,128)S(1)}, u32[]{:S(2)}, u32[]{:S(2)}) collective-permute-start(f32[152,128]{1,0:T(8,128)S(1)} %get-tuple-element.41), channel_id=1, source_target_pairs={{0,8},{4,12},{8,0},{12,4},{16,24},{20,28},{24,16},{28,20},{1,9},{5... | collective-permute-start | bytes 233480 | tf_op jit(solution)/shard_map/ppermute | solution.py:452
  31.5 9.3 %collective-permute-start.11 = (f32[152,128]{1,0:T(8,128)S(1)}, f32[152,128]{1,0:T(8,128)S(1)}, u32[]{:S(2)}, u32[]{:S(2)}) collective-permute-start(f32[152,128]{1,0:T(8,128)S(1)} %get-tuple-element.42), channel_id=1, source_target_pairs={{0,20},{4,16},{8,28},{12,24},{16,4},{20,0},{24,12},{28,8},{1,21},{... | collective-permute-start | bytes 233480 | tf_op jit(solution)/shard_map/ppermute | solution.py:452
  33.3 7.6 %collective-permute-start.12 = (f32[152,128]{1,0:T(8,128)S(1)}, f32[152,128]{1,0:T(8,128)S(1)}, u32[]{:S(2)}, u32[]{:S(2)}) collective-permute-start(f32[152,128]{1,0:T(8,128)S(1)} %get-tuple-element.43), channel_id=1, source_target_pairs={{0,12},{4,8},{8,4},{12,0},{16,28},{20,24},{24,20},{28,16},{1,13},{... | collective-permute-start | bytes 233480 | tf_op jit(solution)/shard_map/ppermute | solution.py:452
  34.5 7.4 %collective-permute-start.13 = (f32[152,128]{1,0:T(8,128)S(1)}, f32[152,128]{1,0:T(8,128)S(1)}, u32[]{:S(2)}, u32[]{:S(2)}) collective-permute-start(f32[152,128]{1,0:T(8,128)S(1)} %get-tuple-element.44), channel_id=1, source_target_pairs={{0,24},{4,28},{8,16},{12,20},{16,8},{20,12},{24,0},{28,4},{1,25},{... | collective-permute-start | bytes 233480 | tf_op jit(solution)/shard_map/ppermute | solution.py:452
  36.8 7.1 %collective-permute-start.14 = (f32[152,128]{1,0:T(8,128)S(1)}, f32[152,128]{1,0:T(8,128)S(1)}, u32[]{:S(2)}, u32[]{:S(2)}) collective-permute-start(f32[152,128]{1,0:T(8,128)S(1)} %get-tuple-element.45), channel_id=1, source_target_pairs={{0,28},{4,24},{8,20},{12,16},{16,12},{20,8},{24,4},{28,0},{1,29},{... | collective-permute-start | bytes 233480 | tf_op jit(solution)/shard_map/ppermute | solution.py:452
  38.3 5.7 %collective-permute-start.15 = (f32[152,128]{1,0:T(8,128)S(1)}, f32[152,128]{1,0:T(8,128)S(1)}, u32[]{:S(2)}, u32[]{:S(2)}) collective-permute-start(f32[152,128]{1,0:T(8,128)S(1)} %get-tuple-element.46), channel_id=1, source_target_pairs={{0,4},{4,0},{8,12},{12,8},{16,20},{20,16},{24,28},{28,24},{1,5},{5... | collective-permute-start | bytes 233480 | tf_op jit(solution)/shard_map/ppermute | solution.py:452
  44.0 2.6 %collective-permute-start.16 = (f32[24,128]{1,0:T(8,128)S(1)}, f32[24,128]{1,0:T(8,128)S(1)}, u32[]{:S(2)}, u32[]{:S(2)}) collective-permute-start(f32[24,128]{1,0:T(8,128)S(1)} %get-tuple-element.49), channel_id=1, source_target_pairs={{0,1},{1,0},{2,3},{3,2},{4,5},{5,4},{6,7},{7,6},{8,9},{9,8},{10,11... | collective-permute-start | bytes 36872 | tf_op jit(solution)/shard_map/ppermute | solution.py:460
  44.0 3.2 %collective-permute-start.17 = (f32[24,128]{1,0:T(8,128)S(1)}, f32[24,128]{1,0:T(8,128)S(1)}, u32[]{:S(2)}, u32[]{:S(2)}) collective-permute-start(f32[24,128]{1,0:T(8,128)S(1)} %get-tuple-element.50), channel_id=1, source_target_pairs={{0,3},{1,2},{2,1},{3,0},{4,7},{5,6},{6,5},{7,4},{8,11},{9,10},{10,... | collective-permute-start | bytes 36872 | tf_op jit(solution)/shard_map/ppermute | solution.py:461

commit v15 on v14

--- a/solution.py
+++ b/solution.py
@@ -198,7 +198,7 @@
                 post[p, pl.ds(8 + start, 8), :] = after[p]
             post[Q, pl.ds(8 + start, 8), :] = solid[here, :].astype(f32)
 
-    def pack_kernel(post, own, near, far, *outs):
+    def pack_kernel(post, own, far, near, *outs):
         me, odd = position()
         below, above = sides(odd, near, far)
         outs = by_owner(outs, order_in)
@@ -402,7 +402,7 @@
             edge[n] = main[p, pl.ds(8 + start, 8), :]
         copy.wait()
 
-    def finish_kernel(_, edge, near, far, out, patch, sem):
+    def finish_kernel(_, edge, far, near, out, patch, sem):
         below, above = sides(position()[1], near, far)
         for n in range(len(ends)):
             patch[n] = edge[n]
@@ -456,10 +456,8 @@
     def hop(near, far):
         ahead = [(s + 1) % slabs if s % 2 == 0 else (s - 1) % slabs for s in range(slabs)]
         behind = [(s - 1) % slabs if s % 2 == 0 else (s + 1) % slabs for s in range(slabs)]
-        return (
-            lax.ppermute(near, "gy", list(enumerate(ahead))),
-            lax.ppermute(far, "gy", list(enumerate(behind))),
-        )
+        far = lax.ppermute(far, "gy", list(enumerate(behind)))
+        return lax.ppermute(near, "gy", list(enumerate(ahead))), far
 
     def padded(count):
         return shape(count, 8 + WHOLE + 8, LANES)
@@ -504,7 +502,7 @@
             pack_kernel,
             "pack_planes",
             (shape(rows_in, LANES),) * owners,
-            (post, own, near, far),
+            (post, own, far, near),
             large,
         )
         got = exchange(parts, order_in)
@@ -552,7 +550,7 @@
             finish_kernel,
             "finish",
             shape(Q, WHOLE, LANES),
-            (out, edge, near, far),
+            (out, edge, far, near),
             small,
             (pltpu.VMEM((len(ends), 8, LANES), f32), pltpu.SemaphoreType.DMA((len(ends),))),
             spec=(in_place, VMEM_SPEC, VMEM_SPEC, VMEM_SPEC),

time: 48.2 us -> 47.8 us (level)
  waiting for transfers between devices: 11.5 us -> 10.9 us
    ppermute x4, waiting for transfers between devices: 1.99 us -> 1.39 us  [the longest x2 1.29 us: hop(): far = lax.ppermute(far, 'gy', list(enumerate(behind)))]
  transfers between devices with their start and end apart: 18 -> 18, of which waited for: 7 -> 8; matrix products, arithmetic and copies ran while one was open for 0% -> 0% of each run, Pallas kernels for 4% -> 4%
where the time goes in v15:
time: 47.8 us; the launch traced here: 47.7 us
  starting transfers between devices  29.5 us (62%)
  waiting for transfers between devices  10.9 us (23%)
  Pallas kernels  7.22 us (15%)
    ppermute x14, starting transfers between devices, exchange(): lax.ppermute(parts[n], 'gx', [(g, g ^ order[n]) for g in range(owners)])  24.7 us
    ppermute x14, waiting for transfers between devices, exchange(): lax.ppermute(parts[n], 'gx', [(g, g ^ order[n]) for g in range(owners)])  9.49 us
    pallas_call x8, Pallas kernels, call(): pl.pallas_call(kernel, out_shape=out_shape, in_specs=specs, out_specs=out...  7.22 us
    ppermute x2, starting transfers between devices, hop(): far = lax.ppermute(far, 'gy', list(enumerate(behind)))  2.51 us
    ppermute x2, starting transfers between devices, hop(): return (lax.ppermute(near, 'gy', list(enumerate(ahead))), far)  2.3 us
    ppermute x2, waiting for transfers between devices, hop(): far = lax.ppermute(far, 'gy', list(enumerate(behind)))  1.29 us
  transfers between devices with their start and end apart: 18, of which 8 were waited for; matrix products, arithmetic and copies ran while one was open for 0% of the time, Pallas kernels for 4%

profile of v15, /device:TPU:0, one launch (start us, length us, event | category | flops | bytes accessed | tf_op | source)
XLA Modules:
  0.0 47.7 jit_solution(13405637635358201119)
XLA Ops:
  0.0 0.0 copy-start
  0.0 0.0 copy-start.1
  0.0 1.8 %edge_planes.1 = (f32[24,128]{1,0:T(8,128)}, f32[24,128]{1,0:T(8,128)}, f32[8,128]{1,0:T(8,128)}) custom-call(f32[19,64,128]{2,1,0:T(8,128)} %bitcast.26, s32[64,128]{1,0:T(8,128)} %bitcast.28, s32[1,2]{1,0:T(1,128)} %slots.1, s32[2,3]{1,0:T(2,128)} %bitcast.30), custom_call_target="tpu_custom_call" | custom-call | flops 100000 | bytes 100000 | tf_op jit(solution)/shard_map/edge_planes/pallas_call | solution.py:438
  1.8 2.4 %collective-permute-start = (f32[24,128]{1,0:T(8,128)}, f32[24,128]{1,0:T(8,128)S(1)}, u32[]{:S(2)}, u32[]{:S(2)}) collective-permute-start(f32[24,128]{1,0:T(8,128)} %get-tuple-element.29), channel_id=1, source_target_pairs={{0,3},{1,2},{2,1},{3,0},{4,7},{5,6},{6,5},{7,4},{8,11},{9,10},{10,... | collective-permute-start | bytes 36872 | tf_op jit(solution)/shard_map/ppermute | solution.py:459
  4.2 0.7 %collective-permute-start.1 = (f32[24,128]{1,0:T(8,128)}, f32[24,128]{1,0:T(8,128)S(1)}, u32[]{:S(2)}, u32[]{:S(2)}) collective-permute-start(f32[24,128]{1,0:T(8,128)} %get-tuple-element.30), channel_id=1, source_target_pairs={{0,1},{1,0},{2,3},{3,2},{4,5},{5,4},{6,7},{7,6},{8,9},{9,8},{10,11... | collective-permute-start | bytes 36872 | tf_op jit(solution)/shard_map/ppermute | solution.py:460
  4.9 0.0 copy-done
  4.9 0.0 copy-done.1
  4.9 0.2 first_collision.1.post
  5.1 0.7 %collective-permute-done.far = f32[24,128]{1,0:T(8,128)S(1)} collective-permute-done((f32[24,128]{1,0:T(8,128)}, f32[24,128]{1,0:T(8,128)S(1)}, u32[]{:S(2)}, u32[]{:S(2)}) %collective-permute-start) | collective-permute-done | bytes 12320 | tf_op jit(solution)/shard_map/ppermute | solution.py:459
  5.8 0.1 collective-permute-done.1.near
  5.9 0.0 copy-done.2
  5.9 0.2 pack_planes.1
  6.2 3.4 %collective-permute-start.2 = (f32[168,128]{1,0:T(8,128)S(1)}, f32[168,128]{1,0:T(8,128)S(1)}, u32[]{:S(2)}, u32[]{:S(2)}) collective-permute-start(f32[168,128]{1,0:T(8,128)S(1)} %get-tuple-element.32), channel_id=1, source_target_pairs={{0,16},{4,20},{8,24},{12,28},{16,0},{20,4},{24,8},{28,12},{1,17},{... | collective-permute-start | bytes 258056 | tf_op jit(solution)/shard_map/ppermute | solution.py:452
  9.6 1.6 %collective-permute-start.3 = (f32[168,128]{1,0:T(8,128)S(1)}, f32[168,128]{1,0:T(8,128)S(1)}, u32[]{:S(2)}, u32[]{:S(2)}) collective-permute-start(f32[168,128]{1,0:T(8,128)S(1)} %get-tuple-element.33), channel_id=1, source_target_pairs={{0,8},{4,12},{8,0},{12,4},{16,24},{20,28},{24,16},{28,20},{1,9},{5... | collective-permute-start | bytes 258056 | tf_op jit(solution)/shard_map/ppermute | solution.py:452
  11.2 1.4 %collective-permute-start.5 = (f32[168,128]{1,0:T(8,128)S(1)}, f32[168,128]{1,0:T(8,128)S(1)}, u32[]{:S(2)}, u32[]{:S(2)}) collective-permute-start(f32[168,128]{1,0:T(8,128)S(1)} %get-tuple-element.35), channel_id=1, source_target_pairs={{0,12},{4,8},{8,4},{12,0},{16,28},{20,24},{24,20},{28,16},{1,13},{... | collective-permute-start | bytes 258056 | tf_op jit(solution)/shard_map/ppermute | solution.py:452
  12.6 0.0 collective-permute-start.4
  12.6 3.9 %collective-permute-start.6 = (f32[168,128]{1,0:T(8,128)S(1)}, f32[168,128]{1,0:T(8,128)S(1)}, u32[]{:S(2)}, u32[]{:S(2)}) collective-permute-start(f32[168,128]{1,0:T(8,128)S(1)} %get-tuple-element.36), channel_id=1, source_target_pairs={{0,24},{4,28},{8,16},{12,20},{16,8},{20,12},{24,0},{28,4},{1,25},{... | collective-permute-start | bytes 258056 | tf_op jit(solution)/shard_map/ppermute | solution.py:452
  16.5 0.0 collective-permute-done.2.refs_1_
  16.5 2.4 %collective-permute-start.7 = (f32[168,128]{1,0:T(8,128)S(1)}, f32[168,128]{1,0:T(8,128)S(1)}, u32[]{:S(2)}, u32[]{:S(2)}) collective-permute-start(f32[168,128]{1,0:T(8,128)S(1)} %get-tuple-element.37), channel_id=1, source_target_pairs={{0,28},{4,24},{8,20},{12,16},{16,12},{20,8},{24,4},{28,0},{1,29},{... | collective-permute-start | bytes 258056 | tf_op jit(solution)/shard_map/ppermute | solution.py:452
  18.9 0.0 collective-permute-done.3.refs_2_
  18.9 0.5 %collective-permute-start.8 = (f32[168,128]{1,0:T(8,128)S(1)}, f32[168,128]{1,0:T(8,128)S(1)}, u32[]{:S(2)}, u32[]{:S(2)}) collective-permute-start(f32[168,128]{1,0:T(8,128)S(1)} %get-tuple-element.38), channel_id=1, source_target_pairs={{0,4},{4,0},{8,12},{12,8},{16,20},{20,16},{24,28},{28,24},{1,5},{5... | collective-permute-start | bytes 258056 | tf_op jit(solution)/shard_map/ppermute | solution.py:452
  19.4 0.0 collective-permute-done.5.refs_3_.refs_4_
  19.4 0.7 %place_early.1.refs_8_ = f32[20,2,32,128]{3,2,1,0:T(8,128)S(1)} custom-call(f32[168,128]{1,0:T(8,128)S(1)} %get-tuple-element.31.refs_0_, f32[168,128]{1,0:T(8,128)S(1)} %collective-permute-done.2.refs_1_, f32[168,128]{1,0:T(8,128)S(1)} %collective-permute-done.3.refs_2_, f32[168,128]{1,0:T(8,128)S(1)} %collective-permute-done.5.refs_3_.refs_4_), custom_call_target="tpu_custom_call" | custom-call | flops 4000000 | bytes 4000000 | tf_op jit(solution)/shard_map/place_early/pallas_call | solution.py:438
  20.2 4.9 %collective-permute-done.4.refs_3_ = f32[168,128]{1,0:T(8,128)S(1)} collective-permute-done((f32[168,128]{1,0:T(8,128)S(1)}, f32[168,128]{1,0:T(8,128)S(1)}, u32[]{:S(2)}, u32[]{:S(2)}) %collective-permute-start.4) | collective-permute-done | bytes 86048 | tf_op jit(solution)/shard_map/ppermute | solution.py:452
  25.1 0.0 collective-permute-done.6.refs_5_
  25.1 0.0 collective-permute-done.7.refs_6_
  25.1 0.4 collective-permute-done.8.refs_7_
  25.4 2.6 %second_step.1 = (f32[152,128]{1,0:T(8,128)S(1)}, f32[152,128]{1,0:T(8,128)S(1)}, f32[152,128]{1,0:T(8,128)S(1)}, f32[152,128]{1,0:T(8,128)S(1)}, f32[152,128]{1...) custom-call(f32[168,128]{1,0:T(8,128)S(1)} %get-tuple-element.31.ref, ...), custom_call_target="tpu_custom_call", output_to_operand_aliasing={{8}: (8, {})} | custom-call | flops 4000000 | bytes 4000000 | tf_op jit(solution)/shard_map/second_step/pallas_call | solution.py:438
  28.1 3.1 %collective-permute-start.9 = (f32[152,128]{1,0:T(8,128)S(1)}, f32[152,128]{1,0:T(8,128)S(1)}, u32[]{:S(2)}, u32[]{:S(2)}) collective-permute-start(f32[152,128]{1,0:T(8,128)S(1)} %get-tuple-element.40), channel_id=1, source_target_pairs={{0,16},{4,20},{8,24},{12,28},{16,0},{20,4},{24,8},{28,12},{1,17},{... | collective-permute-start | bytes 233480 | tf_op jit(solution)/shard_map/ppermute | solution.py:452
  31.2 0.0 collective-permute-start.10
  31.2 1.8 %collective-permute-start.11 = (f32[152,128]{1,0:T(8,128)S(1)}, f32[152,128]{1,0:T(8,128)S(1)}, u32[]{:S(2)}, u32[]{:S(2)}) collective-permute-start(f32[152,128]{1,0:T(8,128)S(1)} %get-tuple-element.42), channel_id=1, source_target_pairs={{0,20},{4,16},{8,28},{12,24},{16,4},{20,0},{24,12},{28,8},{1,21},{... | collective-permute-start | bytes 233480 | tf_op jit(solution)/shard_map/ppermute | solution.py:452
  33.0 1.2 %collective-permute-start.12 = (f32[152,128]{1,0:T(8,128)S(1)}, f32[152,128]{1,0:T(8,128)S(1)}, u32[]{:S(2)}, u32[]{:S(2)}) collective-permute-start(f32[152,128]{1,0:T(8,128)S(1)} %get-tuple-element.43), channel_id=1, source_target_pairs={{0,12},{4,8},{8,4},{12,0},{16,28},{20,24},{24,20},{28,16},{1,13},{... | collective-permute-start | bytes 233480 | tf_op jit(solution)/shard_map/ppermute | solution.py:452
  34.2 2.3 %collective-permute-start.13 = (f32[152,128]{1,0:T(8,128)S(1)}, f32[152,128]{1,0:T(8,128)S(1)}, u32[]{:S(2)}, u32[]{:S(2)}) collective-permute-start(f32[152,128]{1,0:T(8,128)S(1)} %get-tuple-element.44), channel_id=1, source_target_pairs={{0,24},{4,28},{8,16},{12,20},{16,8},{20,12},{24,0},{28,4},{1,25},{... | collective-permute-start | bytes 233480 | tf_op jit(solution)/shard_map/ppermute | solution.py:452
  36.5 0.0 collective-permute-done.9.refs_1_
  36.5 1.5 %collective-permute-start.14 = (f32[152,128]{1,0:T(8,128)S(1)}, f32[152,128]{1,0:T(8,128)S(1)}, u32[]{:S(2)}, u32[]{:S(2)}) collective-permute-start(f32[152,128]{1,0:T(8,128)S(1)} %get-tuple-element.45), channel_id=1, source_target_pairs={{0,28},{4,24},{8,20},{12,16},{16,12},{20,8},{24,4},{28,0},{1,29},{... | collective-permute-start | bytes 233480 | tf_op jit(solution)/shard_map/ppermute | solution.py:452
  38.0 0.0 collective-permute-done.10.refs_2_
  38.0 1.5 %collective-permute-start.15 = (f32[152,128]{1,0:T(8,128)S(1)}, f32[152,128]{1,0:T(8,128)S(1)}, u32[]{:S(2)}, u32[]{:S(2)}) collective-permute-start(f32[152,128]{1,0:T(8,128)S(1)} %get-tuple-element.46), channel_id=1, source_target_pairs={{0,4},{4,0},{8,12},{12,8},{16,20},{20,16},{24,28},{28,24},{1,5},{5... | collective-permute-start | bytes 233480 | tf_op jit(solution)/shard_map/ppermute | solution.py:452
  39.5 0.7 %collective-permute-done.11.refs_3_ = f32[152,128]{1,0:T(8,128)S(1)} collective-permute-done((f32[152,128]{1,0:T(8,128)S(1)}, f32[152,128]{1,0:T(8,128)S(1)}, u32[]{:S(2)}, u32[]{:S(2)}) %collective-permute-start.11) | collective-permute-done | bytes 77856 | tf_op jit(solution)/shard_map/ppermute | solution.py:452
  40.2 0.0 collective-permute-done.12.refs_4_
  40.2 1.3 %collective-permute-done.13.refs_5_ = f32[152,128]{1,0:T(8,128)S(1)} collective-permute-done((f32[152,128]{1,0:T(8,128)S(1)}, f32[152,128]{1,0:T(8,128)S(1)}, u32[]{:S(2)}, u32[]{:S(2)}) %collective-permute-start.13) | collective-permute-done | bytes 77856 | tf_op jit(solution)/shard_map/ppermute | solution.py:452
  41.5 2.1 %collective-permute-done.14.refs_6_ = f32[152,128]{1,0:T(8,128)S(1)} collective-permute-done((f32[152,128]{1,0:T(8,128)S(1)}, f32[152,128]{1,0:T(8,128)S(1)}, u32[]{:S(2)}, u32[]{:S(2)}) %collective-permute-start.14) | collective-permute-done | bytes 77856 | tf_op jit(solution)/shard_map/ppermute | solution.py:452
  43.7 0.0 collective-permute-done.15.refs_7_
  43.7 0.1 collective-permute-start.16
  43.8 1.6 %collective-permute-start.17 = (f32[24,128]{1,0:T(8,128)S(1)}, f32[24,128]{1,0:T(8,128)S(1)}, u32[]{:S(2)}, u32[]{:S(2)}) collective-permute-start(f32[24,128]{1,0:T(8,128)S(1)} %get-tuple-element.50), channel_id=1, source_target_pairs={{0,1},{1,0},{2,3},{3,2},{4,5},{5,4},{6,7},{7,6},{8,9},{9,8},{10,11... | collective-permute-start | bytes 36872 | tf_op jit(solution)/shard_map/ppermute | solution.py:460
  45.4 0.9 %unpack_planes.1 = (f32[19,64,128]{2,1,0:T(8,128)}, f32[10,8,128]{2,1,0:T(8,128)S(1)}) custom-call(f32[152,128]{1,0:T(8,128)S(1)} %get-tuple-element.39.refs_0_, f32[152,128]{1,0:T(8,128)S(1)} %collective-permute-done.9.refs_1_, f32[152,128]{1,0:T(8,128)S(1)} %collective-permute-done.10.refs_2_, f32[152,128]{1,0:T(8,128)S(1)} %collective-permute-done.11.refs_3_, ...), custom_call_target="tpu_custom_call" | custom-call | flops 4000000 | bytes 4000000 | tf_op jit(solution)/shard_map/unpack_planes/pallas_call | solution.py:438
  46.4 0.6 %collective-permute-done.16.far = f32[24,128]{1,0:T(8,128)S(1)} collective-permute-done((f32[24,128]{1,0:T(8,128)S(1)}, f32[24,128]{1,0:T(8,128)S(1)}, u32[]{:S(2)}, u32[]{:S(2)}) %collective-permute-start.16) | collective-permute-done | bytes 12320 | tf_op jit(solution)/shard_map/ppermute | solution.py:459
  46.9 0.0 collective-permute-done.17.near
  47.0 0.7 %finish.1 = f32[19,64,128]{2,1,0:T(8,128)} custom-call(f32[19,64,128]{2,1,0:T(8,128)} %get-tuple-element.47._, f32[10,8,128]{2,1,0:T(8,128)S(1)} %get-tuple-element.48.edge, f32[24,128]{1,0:T(8,128)S(1)} %collective-permute-done.16.far, f32[24,128]{1,0:T(8,128)S(1)} %collective-permute-done.17.near), custom_call_target="tpu_custom_call", output_to_operand_aliasing={{}: (0, {})} | custom-call | flops 100000 | bytes 100000 | tf_op jit(solution)/shard_map/finish/pallas_call | solution.py:438
  (2 shorter events, 0.0 us)
Async XLA Ops:
  0.0 4.9 %copy-start = (f32[1,2,19,4096]{3,1,2,0:T(2,128)S(1)}, f32[1,2,19,4096]{3,1,2,0:T(2,128)}, u32[]{:S(2)}) copy-start(f32[1,2,19,4096]{3,1,2,0:T(2,128)} %param.4) | copy-start | bytes 1867780
  0.0 4.9 %copy-start.1 = (s32[1,2,4096]{2,1,0:T(2,128)S(1)}, s32[1,2,4096]{2,1,0:T(2,128)}, u32[]{:S(2)}) copy-start(s32[1,2,4096]{2,1,0:T(2,128)} %param.5) | copy-start | bytes 98308
  1.8 4.1 %collective-permute-start = (f32[24,128]{1,0:T(8,128)}, f32[24,128]{1,0:T(8,128)S(1)}, u32[]{:S(2)}, u32[]{:S(2)}) collective-permute-start(f32[24,128]{1,0:T(8,128)} %get-tuple-element.29), channel_id=1, source_target_pairs={{0,3},{1,2},{2,1},{3,0},{4,7},{5,6},{6,5},{7,4},{8,11},{9,10},{10,... | collective-permute-start | bytes 36872 | tf_op jit(solution)/shard_map/ppermute | solution.py:459
  4.2 1.7 %collective-permute-start.1 = (f32[24,128]{1,0:T(8,128)}, f32[24,128]{1,0:T(8,128)S(1)}, u32[]{:S(2)}, u32[]{:S(2)}) collective-permute-start(f32[24,128]{1,0:T(8,128)} %get-tuple-element.30), channel_id=1, source_target_pairs={{0,1},{1,0},{2,3},{3,2},{4,5},{5,4},{6,7},{7,6},{8,9},{9,8},{10,11... | collective-permute-start | bytes 36872 | tf_op jit(solution)/shard_map/ppermute | solution.py:460
  4.9 1.0 %copy-start.2 = (f32[8,128]{1,0:T(8,128)S(1)}, f32[8,128]{1,0:T(8,128)}, u32[]{:S(2)}) copy-start(f32[8,128]{1,0:T(8,128)} %get-tuple-element.28.own) | copy-start | bytes 12292
  6.2 10.3 %collective-permute-start.2 = (f32[168,128]{1,0:T(8,128)S(1)}, f32[168,128]{1,0:T(8,128)S(1)}, u32[]{:S(2)}, u32[]{:S(2)}) collective-permute-start(f32[168,128]{1,0:T(8,128)S(1)} %get-tuple-element.32), channel_id=1, source_target_pairs={{0,16},{4,20},{8,24},{12,28},{16,0},{20,4},{24,8},{28,12},{1,17},{... | collective-permute-start | bytes 258056 | tf_op jit(solution)/shard_map/ppermute | solution.py:452
  9.6 9.3 %collective-permute-start.3 = (f32[168,128]{1,0:T(8,128)S(1)}, f32[168,128]{1,0:T(8,128)S(1)}, u32[]{:S(2)}, u32[]{:S(2)}) collective-permute-start(f32[168,128]{1,0:T(8,128)S(1)} %get-tuple-element.33), channel_id=1, source_target_pairs={{0,8},{4,12},{8,0},{12,4},{16,24},{20,28},{24,16},{28,20},{1,9},{5... | collective-permute-start | bytes 258056 | tf_op jit(solution)/shard_map/ppermute | solution.py:452
  11.2 8.3 %collective-permute-start.5 = (f32[168,128]{1,0:T(8,128)S(1)}, f32[168,128]{1,0:T(8,128)S(1)}, u32[]{:S(2)}, u32[]{:S(2)}) collective-permute-start(f32[168,128]{1,0:T(8,128)S(1)} %get-tuple-element.35), channel_id=1, source_target_pairs={{0,12},{4,8},{8,4},{12,0},{16,28},{20,24},{24,20},{28,16},{1,13},{... | collective-permute-start | bytes 258056 | tf_op jit(solution)/shard_map/ppermute | solution.py:452
  12.6 12.5 %collective-permute-start.4 = (f32[168,128]{1,0:T(8,128)S(1)}, f32[168,128]{1,0:T(8,128)S(1)}, u32[]{:S(2)}, u32[]{:S(2)}) collective-permute-start(f32[168,128]{1,0:T(8,128)S(1)} %get-tuple-element.34), channel_id=1, source_target_pairs={{0,20},{4,16},{8,28},{12,24},{16,4},{20,0},{24,12},{28,8},{1,21},{... | collective-permute-start | bytes 258056 | tf_op jit(solution)/shard_map/ppermute | solution.py:452
  12.6 12.5 %collective-permute-start.6 = (f32[168,128]{1,0:T(8,128)S(1)}, f32[168,128]{1,0:T(8,128)S(1)}, u32[]{:S(2)}, u32[]{:S(2)}) collective-permute-start(f32[168,128]{1,0:T(8,128)S(1)} %get-tuple-element.36), channel_id=1, source_target_pairs={{0,24},{4,28},{8,16},{12,20},{16,8},{20,12},{24,0},{28,4},{1,25},{... | collective-permute-start | bytes 258056 | tf_op jit(solution)/shard_map/ppermute | solution.py:452
  16.5 8.6 %collective-permute-start.7 = (f32[168,128]{1,0:T(8,128)S(1)}, f32[168,128]{1,0:T(8,128)S(1)}, u32[]{:S(2)}, u32[]{:S(2)}) collective-permute-start(f32[168,128]{1,0:T(8,128)S(1)} %get-tuple-element.37), channel_id=1, source_target_pairs={{0,28},{4,24},{8,20},{12,16},{16,12},{20,8},{24,4},{28,0},{1,29},{... | collective-permute-start | bytes 258056 | tf_op jit(solution)/shard_map/ppermute | solution.py:452
  18.9 6.5 %collective-permute-start.8 = (f32[168,128]{1,0:T(8,128)S(1)}, f32[168,128]{1,0:T(8,128)S(1)}, u32[]{:S(2)}, u32[]{:S(2)}) collective-permute-start(f32[168,128]{1,0:T(8,128)S(1)} %get-tuple-element.38), channel_id=1, source_target_pairs={{0,4},{4,0},{8,12},{12,8},{16,20},{20,16},{24,28},{28,24},{1,5},{5... | collective-permute-start | bytes 258056 | tf_op jit(solution)/shard_map/ppermute | solution.py:452
  28.1 8.4 %collective-permute-start.9 = (f32[152,128]{1,0:T(8,128)S(1)}, f32[152,128]{1,0:T(8,128)S(1)}, u32[]{:S(2)}, u32[]{:S(2)}) collective-permute-start(f32[152,128]{1,0:T(8,128)S(1)} %get-tuple-element.40), channel_id=1, source_target_pairs={{0,16},{4,20},{8,24},{12,28},{16,0},{20,4},{24,8},{28,12},{1,17},{... | collective-permute-start | bytes 233480 | tf_op jit(solution)/shard_map/ppermute | solution.py:452
  31.2 6.8 %collective-permute-start.10 = (f32[152,128]{1,0:T(8,128)S(1)}, f32[152,128]{1,0:T(8,128)S(1)}, u32[]{:S(2)}, u32[]{:S(2)}) collective-permute-start(f32[152,128]{1,0:T(8,128)S(1)} %get-tuple-element.41), channel_id=1, source_target_pairs={{0,8},{4,12},{8,0},{12,4},{16,24},{20,28},{24,16},{28,20},{1,9},{5... | collective-permute-start | bytes 233480 | tf_op jit(solution)/shard_map/ppermute | solution.py:452
  31.2 9.0 %collective-permute-start.11 = (f32[152,128]{1,0:T(8,128)S(1)}, f32[152,128]{1,0:T(8,128)S(1)}, u32[]{:S(2)}, u32[]{:S(2)}) collective-permute-start(f32[152,128]{1,0:T(8,128)S(1)} %get-tuple-element.42), channel_id=1, source_target_pairs={{0,20},{4,16},{8,28},{12,24},{16,4},{20,0},{24,12},{28,8},{1,21},{... | collective-permute-start | bytes 233480 | tf_op jit(solution)/shard_map/ppermute | solution.py:452
  33.0 7.3 %collective-permute-start.12 = (f32[152,128]{1,0:T(8,128)S(1)}, f32[152,128]{1,0:T(8,128)S(1)}, u32[]{:S(2)}, u32[]{:S(2)}) collective-permute-start(f32[152,128]{1,0:T(8,128)S(1)} %get-tuple-element.43), channel_id=1, source_target_pairs={{0,12},{4,8},{8,4},{12,0},{16,28},{20,24},{24,20},{28,16},{1,13},{... | collective-permute-start | bytes 233480 | tf_op jit(solution)/shard_map/ppermute | solution.py:452
  34.2 7.4 %collective-permute-start.13 = (f32[152,128]{1,0:T(8,128)S(1)}, f32[152,128]{1,0:T(8,128)S(1)}, u32[]{:S(2)}, u32[]{:S(2)}) collective-permute-start(f32[152,128]{1,0:T(8,128)S(1)} %get-tuple-element.44), channel_id=1, source_target_pairs={{0,24},{4,28},{8,16},{12,20},{16,8},{20,12},{24,0},{28,4},{1,25},{... | collective-permute-start | bytes 233480 | tf_op jit(solution)/shard_map/ppermute | solution.py:452
  36.5 7.2 %collective-permute-start.14 = (f32[152,128]{1,0:T(8,128)S(1)}, f32[152,128]{1,0:T(8,128)S(1)}, u32[]{:S(2)}, u32[]{:S(2)}) collective-permute-start(f32[152,128]{1,0:T(8,128)S(1)} %get-tuple-element.45), channel_id=1, source_target_pairs={{0,28},{4,24},{8,20},{12,16},{16,12},{20,8},{24,4},{28,0},{1,29},{... | collective-permute-start | bytes 233480 | tf_op jit(solution)/shard_map/ppermute | solution.py:452
  38.0 5.7 %collective-permute-start.15 = (f32[152,128]{1,0:T(8,128)S(1)}, f32[152,128]{1,0:T(8,128)S(1)}, u32[]{:S(2)}, u32[]{:S(2)}) collective-permute-start(f32[152,128]{1,0:T(8,128)S(1)} %get-tuple-element.46), channel_id=1, source_target_pairs={{0,4},{4,0},{8,12},{12,8},{16,20},{20,16},{24,28},{28,24},{1,5},{5... | collective-permute-start | bytes 233480 | tf_op jit(solution)/shard_map/ppermute | solution.py:452
  43.7 3.2 %collective-permute-start.16 = (f32[24,128]{1,0:T(8,128)S(1)}, f32[24,128]{1,0:T(8,128)S(1)}, u32[]{:S(2)}, u32[]{:S(2)}) collective-permute-start(f32[24,128]{1,0:T(8,128)S(1)} %get-tuple-element.49), channel_id=1, source_target_pairs={{0,3},{1,2},{2,1},{3,0},{4,7},{5,6},{6,5},{7,4},{8,11},{9,10},{10,... | collective-permute-start | bytes 36872 | tf_op jit(solution)/shard_map/ppermute | solution.py:459
  43.8 3.2 %collective-permute-start.17 = (f32[24,128]{1,0:T(8,128)S(1)}, f32[24,128]{1,0:T(8,128)S(1)}, u32[]{:S(2)}, u32[]{:S(2)}) collective-permute-start(f32[24,128]{1,0:T(8,128)S(1)} %get-tuple-element.50), channel_id=1, source_target_pairs={{0,1},{1,0},{2,3},{3,2},{4,5},{5,4},{6,7},{7,6},{8,9},{9,8},{10,11... | collective-permute-start | bytes 36872 | tf_op jit(solution)/shard_map/ppermute | solution.py:460

commit v16 on v15

--- a/solution.py
+++ b/solution.py
@@ -164,11 +164,10 @@
 
     def edge_kernel(pops, mask, slots, swaps, near, far, own, up, down, cells, solid, held, given, sem):
         ends = (WHOLE - 8, 0)
-        copies = []
+        copies = [(slots, held), (swaps, given)]
         for n, start in enumerate(ends):
             copies.append((pops.at[:, pl.ds(start, 8), :], cells.at[n]))
             copies.append((mask.at[pl.ds(start, 8), :], solid.at[n]))
-        copies += [(slots, held), (swaps, given)]
         copies = [
             pltpu.make_async_copy(source, target, sem.at[n])
             for n, (source, target) in enumerate(copies)
@@ -238,7 +237,7 @@
                     pl.ds(p * share + t, block, stride=NB), :
                 ]
 
-    early = [0, half, 2, 3]
+    early = [0, half, 2]
     late = [d for d in order_in if d not in early]
 
     def early_kernel(*refs):

time: 47.8 us -> 48 us (level)
  starting transfers between devices: 29.5 us -> 30.1 us
  waiting for transfers between devices: 10.9 us -> 10.4 us
    ppermute x14, starting transfers between devices: 24.7 us -> 25.3 us  [exchange(): lax.ppermute(parts[n], 'gx', [(g, g ^ order[n]) for g in range(owners)])]
    ppermute x14, waiting for transfers between devices: 9.49 us -> 8.97 us  [exchange(): lax.ppermute(parts[n], 'gx', [(g, g ^ order[n]) for g in range(owners)])]
  transfers between devices with their start and end apart: 18 -> 18, of which waited for: 8 -> 11; matrix products, arithmetic and copies ran while one was open for 0% -> 0% of each run, Pallas kernels for 4% -> 4%
where the time goes in v16:
time: 48 us; the launch traced here: 47.8 us
  starting transfers between devices  30.1 us (63%)
  waiting for transfers between devices  10.4 us (22%)
  Pallas kernels  7.21 us (15%)
    ppermute x14, starting transfers between devices, exchange(): lax.ppermute(parts[n], 'gx', [(g, g ^ order[n]) for g in range(owners)])  25.3 us
    ppermute x14, waiting for transfers between devices, exchange(): lax.ppermute(parts[n], 'gx', [(g, g ^ order[n]) for g in range(owners)])  8.97 us
    pallas_call x8, Pallas kernels, call(): pl.pallas_call(kernel, out_shape=out_shape, in_specs=specs, out_specs=out...  7.21 us
    ppermute x2, starting transfers between devices, hop(): far = lax.ppermute(far, 'gy', list(enumerate(behind)))  2.51 us
    ppermute x2, starting transfers between devices, hop(): return (lax.ppermute(near, 'gy', list(enumerate(ahead))), far)  2.3 us
    ppermute x2, waiting for transfers between devices, hop(): far = lax.ppermute(far, 'gy', list(enumerate(behind)))  1.29 us
  transfers between devices with their start and end apart: 18, of which 11 were waited for; matrix products, arithmetic and copies ran while one was open for 0% of the time, Pallas kernels for 4%

profile of v16, /device:TPU:0, one launch (start us, length us, event | category | flops | bytes accessed | tf_op | source)
XLA Modules:
  0.0 47.8 jit_solution(8677457631400888987)
XLA Ops:
  0.0 0.0 copy-start
  0.0 0.0 copy-start.1
  0.0 1.8 %edge_planes.1 = (f32[24,128]{1,0:T(8,128)}, f32[24,128]{1,0:T(8,128)}, f32[8,128]{1,0:T(8,128)}) custom-call(f32[19,64,128]{2,1,0:T(8,128)} %bitcast.26, s32[64,128]{1,0:T(8,128)} %bitcast.28, s32[1,2]{1,0:T(1,128)} %slots.1, s32[2,3]{1,0:T(2,128)} %bitcast.30), custom_call_target="tpu_custom_call" | custom-call | flops 100000 | bytes 100000 | tf_op jit(solution)/shard_map/edge_planes/pallas_call | solution.py:437
  1.8 2.4 %collective-permute-start = (f32[24,128]{1,0:T(8,128)}, f32[24,128]{1,0:T(8,128)S(1)}, u32[]{:S(2)}, u32[]{:S(2)}) collective-permute-start(f32[24,128]{1,0:T(8,128)} %get-tuple-element.29), channel_id=1, source_target_pairs={{0,3},{1,2},{2,1},{3,0},{4,7},{5,6},{6,5},{7,4},{8,11},{9,10},{10,... | collective-permute-start | bytes 36872 | tf_op jit(solution)/shard_map/ppermute | solution.py:458
  4.2 0.7 %collective-permute-start.1 = (f32[24,128]{1,0:T(8,128)}, f32[24,128]{1,0:T(8,128)S(1)}, u32[]{:S(2)}, u32[]{:S(2)}) collective-permute-start(f32[24,128]{1,0:T(8,128)} %get-tuple-element.30), channel_id=1, source_target_pairs={{0,1},{1,0},{2,3},{3,2},{4,5},{5,4},{6,7},{7,6},{8,9},{9,8},{10,11... | collective-permute-start | bytes 36872 | tf_op jit(solution)/shard_map/ppermute | solution.py:459
  4.9 0.0 copy-done
  4.9 0.0 copy-done.1
  4.9 0.2 first_collision.1.post
  5.2 0.7 %collective-permute-done.far = f32[24,128]{1,0:T(8,128)S(1)} collective-permute-done((f32[24,128]{1,0:T(8,128)}, f32[24,128]{1,0:T(8,128)S(1)}, u32[]{:S(2)}, u32[]{:S(2)}) %collective-permute-start) | collective-permute-done | bytes 12320 | tf_op jit(solution)/shard_map/ppermute | solution.py:458
  5.9 0.1 collective-permute-done.1.near
  6.0 0.0 copy-done.2
  6.0 0.2 pack_planes.1
  6.2 3.4 %collective-permute-start.2 = (f32[168,128]{1,0:T(8,128)S(1)}, f32[168,128]{1,0:T(8,128)S(1)}, u32[]{:S(2)}, u32[]{:S(2)}) collective-permute-start(f32[168,128]{1,0:T(8,128)S(1)} %get-tuple-element.32), channel_id=1, source_target_pairs={{0,16},{4,20},{8,24},{12,28},{16,0},{20,4},{24,8},{28,12},{1,17},{... | collective-permute-start | bytes 258056 | tf_op jit(solution)/shard_map/ppermute | solution.py:451
  9.6 1.6 %collective-permute-start.3 = (f32[168,128]{1,0:T(8,128)S(1)}, f32[168,128]{1,0:T(8,128)S(1)}, u32[]{:S(2)}, u32[]{:S(2)}) collective-permute-start(f32[168,128]{1,0:T(8,128)S(1)} %get-tuple-element.33), channel_id=1, source_target_pairs={{0,8},{4,12},{8,0},{12,4},{16,24},{20,28},{24,16},{28,20},{1,9},{5... | collective-permute-start | bytes 258056 | tf_op jit(solution)/shard_map/ppermute | solution.py:451
  11.2 1.3 %collective-permute-start.4 = (f32[168,128]{1,0:T(8,128)S(1)}, f32[168,128]{1,0:T(8,128)S(1)}, u32[]{:S(2)}, u32[]{:S(2)}) collective-permute-start(f32[168,128]{1,0:T(8,128)S(1)} %get-tuple-element.34), channel_id=1, source_target_pairs={{0,20},{4,16},{8,28},{12,24},{16,4},{20,0},{24,12},{28,8},{1,21},{... | collective-permute-start | bytes 258056 | tf_op jit(solution)/shard_map/ppermute | solution.py:451
  12.5 0.1 collective-permute-start.5
  12.6 3.9 %collective-permute-start.6 = (f32[168,128]{1,0:T(8,128)S(1)}, f32[168,128]{1,0:T(8,128)S(1)}, u32[]{:S(2)}, u32[]{:S(2)}) collective-permute-start(f32[168,128]{1,0:T(8,128)S(1)} %get-tuple-element.36), channel_id=1, source_target_pairs={{0,24},{4,28},{8,16},{12,20},{16,8},{20,12},{24,0},{28,4},{1,25},{... | collective-permute-start | bytes 258056 | tf_op jit(solution)/shard_map/ppermute | solution.py:451
  16.5 0.0 collective-permute-done.2.refs_1_
  16.5 3.0 %collective-permute-start.7 = (f32[168,128]{1,0:T(8,128)S(1)}, f32[168,128]{1,0:T(8,128)S(1)}, u32[]{:S(2)}, u32[]{:S(2)}) collective-permute-start(f32[168,128]{1,0:T(8,128)S(1)} %get-tuple-element.37), channel_id=1, source_target_pairs={{0,28},{4,24},{8,20},{12,16},{16,12},{20,8},{24,4},{28,0},{1,29},{... | collective-permute-start | bytes 258056 | tf_op jit(solution)/shard_map/ppermute | solution.py:451
  19.5 0.0 collective-permute-done.3.refs_2_
  19.5 0.5 %collective-permute-start.8 = (f32[168,128]{1,0:T(8,128)S(1)}, f32[168,128]{1,0:T(8,128)S(1)}, u32[]{:S(2)}, u32[]{:S(2)}) collective-permute-start(f32[168,128]{1,0:T(8,128)S(1)} %get-tuple-element.38), channel_id=1, source_target_pairs={{0,4},{4,0},{8,12},{12,8},{16,20},{20,16},{24,28},{28,24},{1,5},{5... | collective-permute-start | bytes 258056 | tf_op jit(solution)/shard_map/ppermute | solution.py:451
  20.0 0.7 %place_early.1.refs_8_ = f32[20,2,32,128]{3,2,1,0:T(8,128)S(1)} custom-call(f32[168,128]{1,0:T(8,128)S(1)} %get-tuple-element.31.refs_0_, f32[168,128]{1,0:T(8,128)S(1)} %collective-permute-done.2.refs_1_, f32[168,128]{1,0:T(8,128)S(1)} %collective-permute-done.3.refs_2_), custom_call_target="tpu_custom_call" | custom-call | flops 4000000 | bytes 4000000 | tf_op jit(solution)/shard_map/place_early/pallas_call | solution.py:437
  20.7 0.0 collective-permute-done.4.refs_3_
  20.7 0.0 collective-permute-done.5.refs_4_
  20.7 0.5 %collective-permute-done.6.refs_5_ = f32[168,128]{1,0:T(8,128)S(1)} collective-permute-done((f32[168,128]{1,0:T(8,128)S(1)}, f32[168,128]{1,0:T(8,128)S(1)}, u32[]{:S(2)}, u32[]{:S(2)}) %collective-permute-start.6) | collective-permute-done | bytes 86048 | tf_op jit(solution)/shard_map/ppermute | solution.py:451
  21.2 2.6 %collective-permute-done.7.refs_6_ = f32[168,128]{1,0:T(8,128)S(1)} collective-permute-done((f32[168,128]{1,0:T(8,128)S(1)}, f32[168,128]{1,0:T(8,128)S(1)}, u32[]{:S(2)}, u32[]{:S(2)}) %collective-permute-start.7) | collective-permute-done | bytes 86048 | tf_op jit(solution)/shard_map/ppermute | solution.py:451
  23.8 1.2 %collective-permute-done.8.refs_7_ = f32[168,128]{1,0:T(8,128)S(1)} collective-permute-done((f32[168,128]{1,0:T(8,128)S(1)}, f32[168,128]{1,0:T(8,128)S(1)}, u32[]{:S(2)}, u32[]{:S(2)}) %collective-permute-start.8) | collective-permute-done | bytes 86048 | tf_op jit(solution)/shard_map/ppermute | solution.py:451
  25.0 2.6 %second_step.1 = (f32[152,128]{1,0:T(8,128)S(1)}, f32[152,128]{1,0:T(8,128)S(1)}, f32[152,128]{1,0:T(8,128)S(1)}, f32[152,128]{1,0:T(8,128)S(1)}, f32[152,128]{1...) custom-call(f32[168,128]{1,0:T(8,128)S(1)} %get-tuple-element.31.ref, ...), custom_call_target="tpu_custom_call", output_to_operand_aliasing={{8}: (8, {})} | custom-call | flops 4000000 | bytes 4000000 | tf_op jit(solution)/shard_map/second_step/pallas_call | solution.py:437
  27.7 3.5 %collective-permute-start.9 = (f32[152,128]{1,0:T(8,128)S(1)}, f32[152,128]{1,0:T(8,128)S(1)}, u32[]{:S(2)}, u32[]{:S(2)}) collective-permute-start(f32[152,128]{1,0:T(8,128)S(1)} %get-tuple-element.40), channel_id=1, source_target_pairs={{0,16},{4,20},{8,24},{12,28},{16,0},{20,4},{24,8},{28,12},{1,17},{... | collective-permute-start | bytes 233480 | tf_op jit(solution)/shard_map/ppermute | solution.py:451
  31.2 0.0 collective-permute-start.10
  31.2 1.7 %collective-permute-start.11 = (f32[152,128]{1,0:T(8,128)S(1)}, f32[152,128]{1,0:T(8,128)S(1)}, u32[]{:S(2)}, u32[]{:S(2)}) collective-permute-start(f32[152,128]{1,0:T(8,128)S(1)} %get-tuple-element.42), channel_id=1, source_target_pairs={{0,20},{4,16},{8,28},{12,24},{16,4},{20,0},{24,12},{28,8},{1,21},{... | collective-permute-start | bytes 233480 | tf_op jit(solution)/shard_map/ppermute | solution.py:451
  32.9 1.3 %collective-permute-start.12 = (f32[152,128]{1,0:T(8,128)S(1)}, f32[152,128]{1,0:T(8,128)S(1)}, u32[]{:S(2)}, u32[]{:S(2)}) collective-permute-start(f32[152,128]{1,0:T(8,128)S(1)} %get-tuple-element.43), channel_id=1, source_target_pairs={{0,12},{4,8},{8,4},{12,0},{16,28},{20,24},{24,20},{28,16},{1,13},{... | collective-permute-start | bytes 233480 | tf_op jit(solution)/shard_map/ppermute | solution.py:451
  34.2 2.3 %collective-permute-start.13 = (f32[152,128]{1,0:T(8,128)S(1)}, f32[152,128]{1,0:T(8,128)S(1)}, u32[]{:S(2)}, u32[]{:S(2)}) collective-permute-start(f32[152,128]{1,0:T(8,128)S(1)} %get-tuple-element.44), channel_id=1, source_target_pairs={{0,24},{4,28},{8,16},{12,20},{16,8},{20,12},{24,0},{28,4},{1,25},{... | collective-permute-start | bytes 233480 | tf_op jit(solution)/shard_map/ppermute | solution.py:451
  36.5 0.0 collective-permute-done.9.refs_1_
  36.5 1.5 %collective-permute-start.14 = (f32[152,128]{1,0:T(8,128)S(1)}, f32[152,128]{1,0:T(8,128)S(1)}, u32[]{:S(2)}, u32[]{:S(2)}) collective-permute-start(f32[152,128]{1,0:T(8,128)S(1)} %get-tuple-element.45), channel_id=1, source_target_pairs={{0,28},{4,24},{8,20},{12,16},{16,12},{20,8},{24,4},{28,0},{1,29},{... | collective-permute-start | bytes 233480 | tf_op jit(solution)/shard_map/ppermute | solution.py:451
  38.0 0.3 collective-permute-done.10.refs_2_
  38.2 1.2 %collective-permute-start.15 = (f32[152,128]{1,0:T(8,128)S(1)}, f32[152,128]{1,0:T(8,128)S(1)}, u32[]{:S(2)}, u32[]{:S(2)}) collective-permute-start(f32[152,128]{1,0:T(8,128)S(1)} %get-tuple-element.46), channel_id=1, source_target_pairs={{0,4},{4,0},{8,12},{12,8},{16,20},{20,16},{24,28},{28,24},{1,5},{5... | collective-permute-start | bytes 233480 | tf_op jit(solution)/shard_map/ppermute | solution.py:451
  39.5 1.2 %collective-permute-done.11.refs_3_ = f32[152,128]{1,0:T(8,128)S(1)} collective-permute-done((f32[152,128]{1,0:T(8,128)S(1)}, f32[152,128]{1,0:T(8,128)S(1)}, u32[]{:S(2)}, u32[]{:S(2)}) %collective-permute-start.11) | collective-permute-done | bytes 77856 | tf_op jit(solution)/shard_map/ppermute | solution.py:451
  40.7 0.0 collective-permute-done.12.refs_4_
  40.7 1.0 %collective-permute-done.13.refs_5_ = f32[152,128]{1,0:T(8,128)S(1)} collective-permute-done((f32[152,128]{1,0:T(8,128)S(1)}, f32[152,128]{1,0:T(8,128)S(1)}, u32[]{:S(2)}, u32[]{:S(2)}) %collective-permute-start.13) | collective-permute-done | bytes 77856 | tf_op jit(solution)/shard_map/ppermute | solution.py:451
  41.6 2.0 %collective-permute-done.14.refs_6_ = f32[152,128]{1,0:T(8,128)S(1)} collective-permute-done((f32[152,128]{1,0:T(8,128)S(1)}, f32[152,128]{1,0:T(8,128)S(1)}, u32[]{:S(2)}, u32[]{:S(2)}) %collective-permute-start.14) | collective-permute-done | bytes 77856 | tf_op jit(solution)/shard_map/ppermute | solution.py:451
  43.6 0.2 collective-permute-done.15.refs_7_
  43.9 0.1 collective-permute-start.16
  43.9 1.6 %collective-permute-start.17 = (f32[24,128]{1,0:T(8,128)S(1)}, f32[24,128]{1,0:T(8,128)S(1)}, u32[]{:S(2)}, u32[]{:S(2)}) collective-permute-start(f32[24,128]{1,0:T(8,128)S(1)} %get-tuple-element.50), channel_id=1, source_target_pairs={{0,1},{1,0},{2,3},{3,2},{4,5},{5,4},{6,7},{7,6},{8,9},{9,8},{10,11... | collective-permute-start | bytes 36872 | tf_op jit(solution)/shard_map/ppermute | solution.py:459
  45.6 0.9 %unpack_planes.1 = (f32[19,64,128]{2,1,0:T(8,128)}, f32[10,8,128]{2,1,0:T(8,128)S(1)}) custom-call(f32[152,128]{1,0:T(8,128)S(1)} %get-tuple-element.39.refs_0_, f32[152,128]{1,0:T(8,128)S(1)} %collective-permute-done.9.refs_1_, f32[152,128]{1,0:T(8,128)S(1)} %collective-permute-done.10.refs_2_, f32[152,128]{1,0:T(8,128)S(1)} %collective-permute-done.11.refs_3_, ...), custom_call_target="tpu_custom_call" | custom-call | flops 4000000 | bytes 4000000 | tf_op jit(solution)/shard_map/unpack_planes/pallas_call | solution.py:437
  46.5 0.6 %collective-permute-done.16.far = f32[24,128]{1,0:T(8,128)S(1)} collective-permute-done((f32[24,128]{1,0:T(8,128)S(1)}, f32[24,128]{1,0:T(8,128)S(1)}, u32[]{:S(2)}, u32[]{:S(2)}) %collective-permute-start.16) | collective-permute-done | bytes 12320 | tf_op jit(solution)/shard_map/ppermute | solution.py:458
  47.1 0.0 collective-permute-done.17.near
  47.1 0.7 %finish.1 = f32[19,64,128]{2,1,0:T(8,128)} custom-call(f32[19,64,128]{2,1,0:T(8,128)} %get-tuple-element.47._, f32[10,8,128]{2,1,0:T(8,128)S(1)} %get-tuple-element.48.edge, f32[24,128]{1,0:T(8,128)S(1)} %collective-permute-done.16.far, f32[24,128]{1,0:T(8,128)S(1)} %collective-permute-done.17.near), custom_call_target="tpu_custom_call", output_to_operand_aliasing={{}: (0, {})} | custom-call | flops 100000 | bytes 100000 | tf_op jit(solution)/shard_map/finish/pallas_call | solution.py:437
  (2 shorter events, 0.0 us)
Async XLA Ops:
  0.0 4.9 %copy-start = (f32[1,2,19,4096]{3,1,2,0:T(2,128)S(1)}, f32[1,2,19,4096]{3,1,2,0:T(2,128)}, u32[]{:S(2)}) copy-start(f32[1,2,19,4096]{3,1,2,0:T(2,128)} %param.4) | copy-start | bytes 1867780
  0.0 4.9 %copy-start.1 = (s32[1,2,4096]{2,1,0:T(2,128)S(1)}, s32[1,2,4096]{2,1,0:T(2,128)}, u32[]{:S(2)}) copy-start(s32[1,2,4096]{2,1,0:T(2,128)} %param.5) | copy-start | bytes 98308
  1.8 4.1 %collective-permute-start = (f32[24,128]{1,0:T(8,128)}, f32[24,128]{1,0:T(8,128)S(1)}, u32[]{:S(2)}, u32[]{:S(2)}) collective-permute-start(f32[24,128]{1,0:T(8,128)} %get-tuple-element.29), channel_id=1, source_target_pairs={{0,3},{1,2},{2,1},{3,0},{4,7},{5,6},{6,5},{7,4},{8,11},{9,10},{10,... | collective-permute-start | bytes 36872 | tf_op jit(solution)/shard_map/ppermute | solution.py:458
  4.2 1.7 %collective-permute-start.1 = (f32[24,128]{1,0:T(8,128)}, f32[24,128]{1,0:T(8,128)S(1)}, u32[]{:S(2)}, u32[]{:S(2)}) collective-permute-start(f32[24,128]{1,0:T(8,128)} %get-tuple-element.30), channel_id=1, source_target_pairs={{0,1},{1,0},{2,3},{3,2},{4,5},{5,4},{6,7},{7,6},{8,9},{9,8},{10,11... | collective-permute-start | bytes 36872 | tf_op jit(solution)/shard_map/ppermute | solution.py:459
  4.9 1.0 %copy-start.2 = (f32[8,128]{1,0:T(8,128)S(1)}, f32[8,128]{1,0:T(8,128)}, u32[]{:S(2)}) copy-start(f32[8,128]{1,0:T(8,128)} %get-tuple-element.28.own) | copy-start | bytes 12292
  6.2 10.3 %collective-permute-start.2 = (f32[168,128]{1,0:T(8,128)S(1)}, f32[168,128]{1,0:T(8,128)S(1)}, u32[]{:S(2)}, u32[]{:S(2)}) collective-permute-start(f32[168,128]{1,0:T(8,128)S(1)} %get-tuple-element.32), channel_id=1, source_target_pairs={{0,16},{4,20},{8,24},{12,28},{16,0},{20,4},{24,8},{28,12},{1,17},{... | collective-permute-start | bytes 258056 | tf_op jit(solution)/shard_map/ppermute | solution.py:451
  9.6 9.8 %collective-permute-start.3 = (f32[168,128]{1,0:T(8,128)S(1)}, f32[168,128]{1,0:T(8,128)S(1)}, u32[]{:S(2)}, u32[]{:S(2)}) collective-permute-start(f32[168,128]{1,0:T(8,128)S(1)} %get-tuple-element.33), channel_id=1, source_target_pairs={{0,8},{4,12},{8,0},{12,4},{16,24},{20,28},{24,16},{28,20},{1,9},{5... | collective-permute-start | bytes 258056 | tf_op jit(solution)/shard_map/ppermute | solution.py:451
  11.2 9.5 %collective-permute-start.4 = (f32[168,128]{1,0:T(8,128)S(1)}, f32[168,128]{1,0:T(8,128)S(1)}, u32[]{:S(2)}, u32[]{:S(2)}) collective-permute-start(f32[168,128]{1,0:T(8,128)S(1)} %get-tuple-element.34), channel_id=1, source_target_pairs={{0,20},{4,16},{8,28},{12,24},{16,4},{20,0},{24,12},{28,8},{1,21},{... | collective-permute-start | bytes 258056 | tf_op jit(solution)/shard_map/ppermute | solution.py:451
  12.5 8.2 %collective-permute-start.5 = (f32[168,128]{1,0:T(8,128)S(1)}, f32[168,128]{1,0:T(8,128)S(1)}, u32[]{:S(2)}, u32[]{:S(2)}) collective-permute-start(f32[168,128]{1,0:T(8,128)S(1)} %get-tuple-element.35), channel_id=1, source_target_pairs={{0,12},{4,8},{8,4},{12,0},{16,28},{20,24},{24,20},{28,16},{1,13},{... | collective-permute-start | bytes 258056 | tf_op jit(solution)/shard_map/ppermute | solution.py:451
  12.6 8.6 %collective-permute-start.6 = (f32[168,128]{1,0:T(8,128)S(1)}, f32[168,128]{1,0:T(8,128)S(1)}, u32[]{:S(2)}, u32[]{:S(2)}) collective-permute-start(f32[168,128]{1,0:T(8,128)S(1)} %get-tuple-element.36), channel_id=1, source_target_pairs={{0,24},{4,28},{8,16},{12,20},{16,8},{20,12},{24,0},{28,4},{1,25},{... | collective-permute-start | bytes 258056 | tf_op jit(solution)/shard_map/ppermute | solution.py:451
  16.5 7.3 %collective-permute-start.7 = (f32[168,128]{1,0:T(8,128)S(1)}, f32[168,128]{1,0:T(8,128)S(1)}, u32[]{:S(2)}, u32[]{:S(2)}) collective-permute-start(f32[168,128]{1,0:T(8,128)S(1)} %get-tuple-element.37), channel_id=1, source_target_pairs={{0,28},{4,24},{8,20},{12,16},{16,12},{20,8},{24,4},{28,0},{1,29},{... | collective-permute-start | bytes 258056 | tf_op jit(solution)/shard_map/ppermute | solution.py:451
  19.5 5.6 %collective-permute-start.8 = (f32[168,128]{1,0:T(8,128)S(1)}, f32[168,128]{1,0:T(8,128)S(1)}, u32[]{:S(2)}, u32[]{:S(2)}) collective-permute-start(f32[168,128]{1,0:T(8,128)S(1)} %get-tuple-element.38), channel_id=1, source_target_pairs={{0,4},{4,0},{8,12},{12,8},{16,20},{20,16},{24,28},{28,24},{1,5},{5... | collective-permute-start | bytes 258056 | tf_op jit(solution)/shard_map/ppermute | solution.py:451
  27.7 8.8 %collective-permute-start.9 = (f32[152,128]{1,0:T(8,128)S(1)}, f32[152,128]{1,0:T(8,128)S(1)}, u32[]{:S(2)}, u32[]{:S(2)}) collective-permute-start(f32[152,128]{1,0:T(8,128)S(1)} %get-tuple-element.40), channel_id=1, source_target_pairs={{0,16},{4,20},{8,24},{12,28},{16,0},{20,4},{24,8},{28,12},{1,17},{... | collective-permute-start | bytes 233480 | tf_op jit(solution)/shard_map/ppermute | solution.py:451
  31.2 7.1 %collective-permute-start.10 = (f32[152,128]{1,0:T(8,128)S(1)}, f32[152,128]{1,0:T(8,128)S(1)}, u32[]{:S(2)}, u32[]{:S(2)}) collective-permute-start(f32[152,128]{1,0:T(8,128)S(1)} %get-tuple-element.41), channel_id=1, source_target_pairs={{0,8},{4,12},{8,0},{12,4},{16,24},{20,28},{24,16},{28,20},{1,9},{5... | collective-permute-start | bytes 233480 | tf_op jit(solution)/shard_map/ppermute | solution.py:451
  31.2 9.5 %collective-permute-start.11 = (f32[152,128]{1,0:T(8,128)S(1)}, f32[152,128]{1,0:T(8,128)S(1)}, u32[]{:S(2)}, u32[]{:S(2)}) collective-permute-start(f32[152,128]{1,0:T(8,128)S(1)} %get-tuple-element.42), channel_id=1, source_target_pairs={{0,20},{4,16},{8,28},{12,24},{16,4},{20,0},{24,12},{28,8},{1,21},{... | collective-permute-start | bytes 233480 | tf_op jit(solution)/shard_map/ppermute | solution.py:451
  32.9 7.8 %collective-permute-start.12 = (f32[152,128]{1,0:T(8,128)S(1)}, f32[152,128]{1,0:T(8,128)S(1)}, u32[]{:S(2)}, u32[]{:S(2)}) collective-permute-start(f32[152,128]{1,0:T(8,128)S(1)} %get-tuple-element.43), channel_id=1, source_target_pairs={{0,12},{4,8},{8,4},{12,0},{16,28},{20,24},{24,20},{28,16},{1,13},{... | collective-permute-start | bytes 233480 | tf_op jit(solution)/shard_map/ppermute | solution.py:451
  34.2 7.4 %collective-permute-start.13 = (f32[152,128]{1,0:T(8,128)S(1)}, f32[152,128]{1,0:T(8,128)S(1)}, u32[]{:S(2)}, u32[]{:S(2)}) collective-permute-start(f32[152,128]{1,0:T(8,128)S(1)} %get-tuple-element.44), channel_id=1, source_target_pairs={{0,24},{4,28},{8,16},{12,20},{16,8},{20,12},{24,0},{28,4},{1,25},{... | collective-permute-start | bytes 233480 | tf_op jit(solution)/shard_map/ppermute | solution.py:451
  36.5 7.2 %collective-permute-start.14 = (f32[152,128]{1,0:T(8,128)S(1)}, f32[152,128]{1,0:T(8,128)S(1)}, u32[]{:S(2)}, u32[]{:S(2)}) collective-permute-start(f32[152,128]{1,0:T(8,128)S(1)} %get-tuple-element.45), channel_id=1, source_target_pairs={{0,28},{4,24},{8,20},{12,16},{16,12},{20,8},{24,4},{28,0},{1,29},{... | collective-permute-start | bytes 233480 | tf_op jit(solution)/shard_map/ppermute | solution.py:451
  38.2 5.6 %collective-permute-start.15 = (f32[152,128]{1,0:T(8,128)S(1)}, f32[152,128]{1,0:T(8,128)S(1)}, u32[]{:S(2)}, u32[]{:S(2)}) collective-permute-start(f32[152,128]{1,0:T(8,128)S(1)} %get-tuple-element.46), channel_id=1, source_target_pairs={{0,4},{4,0},{8,12},{12,8},{16,20},{20,16},{24,28},{28,24},{1,5},{5... | collective-permute-start | bytes 233480 | tf_op jit(solution)/shard_map/ppermute | solution.py:451
  43.9 3.2 %collective-permute-start.16 = (f32[24,128]{1,0:T(8,128)S(1)}, f32[24,128]{1,0:T(8,128)S(1)}, u32[]{:S(2)}, u32[]{:S(2)}) collective-permute-start(f32[24,128]{1,0:T(8,128)S(1)} %get-tuple-element.49), channel_id=1, source_target_pairs={{0,3},{1,2},{2,1},{3,0},{4,7},{5,6},{6,5},{7,4},{8,11},{9,10},{10,... | collective-permute-start | bytes 36872 | tf_op jit(solution)/shard_map/ppermute | solution.py:458
  43.9 3.2 %collective-permute-start.17 = (f32[24,128]{1,0:T(8,128)S(1)}, f32[24,128]{1,0:T(8,128)S(1)}, u32[]{:S(2)}, u32[]{:S(2)}) collective-permute-start(f32[24,128]{1,0:T(8,128)S(1)} %get-tuple-element.50), channel_id=1, source_target_pairs={{0,1},{1,0},{2,3},{3,2},{4,5},{5,4},{6,7},{7,6},{8,9},{9,8},{10,11... | collective-permute-start | bytes 36872 | tf_op jit(solution)/shard_map/ppermute | solution.py:459

commit v17 on v15

--- a/solution.py
+++ b/solution.py
@@ -143,7 +143,7 @@
     half = owners // 2
     spare = [*range(half + 2, owners), *range(4, half), 1]
     order_in = [0, half, 2, half + 1, 3, *spare]
-    order_out = [0, half, 2, half + 1, 3, *spare]
+    order_out = [0, half, 2, half + 1, half + 2, 3, *spare[1:]]
 
     def by_owner(refs, order):
         return [refs[order.index(d)] for d in range(owners)]

time: 47.8 us -> 48.2 us (level)
  waiting for transfers between devices: 10.9 us -> 12.1 us
  starting transfers between devices: 29.5 us -> 28.6 us
    ppermute x14, waiting for transfers between devices: 9.49 us -> 10.8 us  [exchange(): lax.ppermute(parts[n], 'gx', [(g, g ^ order[n]) for g in range(owners)])]
    ppermute x14, starting transfers between devices: 24.7 us -> 23.8 us  [exchange(): lax.ppermute(parts[n], 'gx', [(g, g ^ order[n]) for g in range(owners)])]
where the time goes in v17:
time: 48.2 us; the launch traced here: 48 us
  starting transfers between devices  28.6 us (59%)
  waiting for transfers between devices  12.1 us (25%)
  Pallas kernels  7.2 us (15%)
    ppermute x14, starting transfers between devices, exchange(): lax.ppermute(parts[n], 'gx', [(g, g ^ order[n]) for g in range(owners)])  23.8 us
    ppermute x14, waiting for transfers between devices, exchange(): lax.ppermute(parts[n], 'gx', [(g, g ^ order[n]) for g in range(owners)])  10.8 us
    pallas_call x8, Pallas kernels, call(): pl.pallas_call(kernel, out_shape=out_shape, in_specs=specs, out_specs=out...  7.2 us
    ppermute x2, starting transfers between devices, hop(): far = lax.ppermute(far, 'gy', list(enumerate(behind)))  2.51 us
    ppermute x2, starting transfers between devices, hop(): return (lax.ppermute(near, 'gy', list(enumerate(ahead))), far)  2.3 us
    ppermute x2, waiting for transfers between devices, hop(): far = lax.ppermute(far, 'gy', list(enumerate(behind)))  1.29 us
  transfers between devices with their start and end apart: 18, of which 8 were waited for; matrix products, arithmetic and copies ran while one was open for 0% of the time, Pallas kernels for 4%

profile of v17, /device:TPU:0, one launch (start us, length us, event | category | flops | bytes accessed | tf_op | source)
XLA Modules:
  0.0 48.0 jit_solution(7778732825701480820)
XLA Ops:
  0.0 0.0 copy-start
  0.0 0.0 copy-start.1
  0.0 1.8 %edge_planes.1 = (f32[24,128]{1,0:T(8,128)}, f32[24,128]{1,0:T(8,128)}, f32[8,128]{1,0:T(8,128)}) custom-call(f32[19,64,128]{2,1,0:T(8,128)} %bitcast.26, s32[64,128]{1,0:T(8,128)} %bitcast.28, s32[1,2]{1,0:T(1,128)} %slots.1, s32[2,3]{1,0:T(2,128)} %bitcast.30), custom_call_target="tpu_custom_call" | custom-call | flops 100000 | bytes 100000 | tf_op jit(solution)/shard_map/edge_planes/pallas_call | solution.py:438
  1.8 2.4 %collective-permute-start = (f32[24,128]{1,0:T(8,128)}, f32[24,128]{1,0:T(8,128)S(1)}, u32[]{:S(2)}, u32[]{:S(2)}) collective-permute-start(f32[24,128]{1,0:T(8,128)} %get-tuple-element.29), channel_id=1, source_target_pairs={{0,3},{1,2},{2,1},{3,0},{4,7},{5,6},{6,5},{7,4},{8,11},{9,10},{10,... | collective-permute-start | bytes 36872 | tf_op jit(solution)/shard_map/ppermute | solution.py:459
  4.2 0.7 %collective-permute-start.1 = (f32[24,128]{1,0:T(8,128)}, f32[24,128]{1,0:T(8,128)S(1)}, u32[]{:S(2)}, u32[]{:S(2)}) collective-permute-start(f32[24,128]{1,0:T(8,128)} %get-tuple-element.30), channel_id=1, source_target_pairs={{0,1},{1,0},{2,3},{3,2},{4,5},{5,4},{6,7},{7,6},{8,9},{9,8},{10,11... | collective-permute-start | bytes 36872 | tf_op jit(solution)/shard_map/ppermute | solution.py:460
  4.9 0.0 copy-done
  4.9 0.0 copy-done.1
  4.9 0.2 first_collision.1.post
  5.1 0.7 %collective-permute-done.far = f32[24,128]{1,0:T(8,128)S(1)} collective-permute-done((f32[24,128]{1,0:T(8,128)}, f32[24,128]{1,0:T(8,128)S(1)}, u32[]{:S(2)}, u32[]{:S(2)}) %collective-permute-start) | collective-permute-done | bytes 12320 | tf_op jit(solution)/shard_map/ppermute | solution.py:459
  5.8 0.1 collective-permute-done.1.near
  5.9 0.0 copy-done.2
  5.9 0.2 pack_planes.1
  6.2 3.4 %collective-permute-start.2 = (f32[168,128]{1,0:T(8,128)S(1)}, f32[168,128]{1,0:T(8,128)S(1)}, u32[]{:S(2)}, u32[]{:S(2)}) collective-permute-start(f32[168,128]{1,0:T(8,128)S(1)} %get-tuple-element.32), channel_id=1, source_target_pairs={{0,16},{4,20},{8,24},{12,28},{16,0},{20,4},{24,8},{28,12},{1,17},{... | collective-permute-start | bytes 258056 | tf_op jit(solution)/shard_map/ppermute | solution.py:452
  9.6 1.6 %collective-permute-start.3 = (f32[168,128]{1,0:T(8,128)S(1)}, f32[168,128]{1,0:T(8,128)S(1)}, u32[]{:S(2)}, u32[]{:S(2)}) collective-permute-start(f32[168,128]{1,0:T(8,128)S(1)} %get-tuple-element.33), channel_id=1, source_target_pairs={{0,8},{4,12},{8,0},{12,4},{16,24},{20,28},{24,16},{28,20},{1,9},{5... | collective-permute-start | bytes 258056 | tf_op jit(solution)/shard_map/ppermute | solution.py:452
  11.2 1.4 %collective-permute-start.5 = (f32[168,128]{1,0:T(8,128)S(1)}, f32[168,128]{1,0:T(8,128)S(1)}, u32[]{:S(2)}, u32[]{:S(2)}) collective-permute-start(f32[168,128]{1,0:T(8,128)S(1)} %get-tuple-element.35), channel_id=1, source_target_pairs={{0,12},{4,8},{8,4},{12,0},{16,28},{20,24},{24,20},{28,16},{1,13},{... | collective-permute-start | bytes 258056 | tf_op jit(solution)/shard_map/ppermute | solution.py:452
  12.6 0.0 collective-permute-start.4
  12.6 3.9 %collective-permute-start.6 = (f32[168,128]{1,0:T(8,128)S(1)}, f32[168,128]{1,0:T(8,128)S(1)}, u32[]{:S(2)}, u32[]{:S(2)}) collective-permute-start(f32[168,128]{1,0:T(8,128)S(1)} %get-tuple-element.36), channel_id=1, source_target_pairs={{0,24},{4,28},{8,16},{12,20},{16,8},{20,12},{24,0},{28,4},{1,25},{... | collective-permute-start | bytes 258056 | tf_op jit(solution)/shard_map/ppermute | solution.py:452
  16.5 0.0 collective-permute-done.2.refs_1_
  16.5 2.4 %collective-permute-start.7 = (f32[168,128]{1,0:T(8,128)S(1)}, f32[168,128]{1,0:T(8,128)S(1)}, u32[]{:S(2)}, u32[]{:S(2)}) collective-permute-start(f32[168,128]{1,0:T(8,128)S(1)} %get-tuple-element.37), channel_id=1, source_target_pairs={{0,28},{4,24},{8,20},{12,16},{16,12},{20,8},{24,4},{28,0},{1,29},{... | collective-permute-start | bytes 258056 | tf_op jit(solution)/shard_map/ppermute | solution.py:452
  18.9 0.0 collective-permute-done.3.refs_2_
  18.9 0.5 %collective-permute-start.8 = (f32[168,128]{1,0:T(8,128)S(1)}, f32[168,128]{1,0:T(8,128)S(1)}, u32[]{:S(2)}, u32[]{:S(2)}) collective-permute-start(f32[168,128]{1,0:T(8,128)S(1)} %get-tuple-element.38), channel_id=1, source_target_pairs={{0,4},{4,0},{8,12},{12,8},{16,20},{20,16},{24,28},{28,24},{1,5},{5... | collective-permute-start | bytes 258056 | tf_op jit(solution)/shard_map/ppermute | solution.py:452
  19.4 0.0 collective-permute-done.5.refs_3_.refs_4_
  19.4 0.7 %place_early.1.refs_8_ = f32[20,2,32,128]{3,2,1,0:T(8,128)S(1)} custom-call(f32[168,128]{1,0:T(8,128)S(1)} %get-tuple-element.31.refs_0_, f32[168,128]{1,0:T(8,128)S(1)} %collective-permute-done.2.refs_1_, f32[168,128]{1,0:T(8,128)S(1)} %collective-permute-done.3.refs_2_, f32[168,128]{1,0:T(8,128)S(1)} %collective-permute-done.5.refs_3_.refs_4_), custom_call_target="tpu_custom_call" | custom-call | flops 4000000 | bytes 4000000 | tf_op jit(solution)/shard_map/place_early/pallas_call | solution.py:438
  20.2 4.9 %collective-permute-done.4.refs_3_ = f32[168,128]{1,0:T(8,128)S(1)} collective-permute-done((f32[168,128]{1,0:T(8,128)S(1)}, f32[168,128]{1,0:T(8,128)S(1)}, u32[]{:S(2)}, u32[]{:S(2)}) %collective-permute-start.4) | collective-permute-done | bytes 86048 | tf_op jit(solution)/shard_map/ppermute | solution.py:452
  25.1 0.0 collective-permute-done.6.refs_5_
  25.1 0.0 collective-permute-done.7.refs_6_
  25.1 0.4 collective-permute-done.8.refs_7_
  25.4 2.6 %second_step.1 = (f32[152,128]{1,0:T(8,128)S(1)}, f32[152,128]{1,0:T(8,128)S(1)}, f32[152,128]{1,0:T(8,128)S(1)}, f32[152,128]{1,0:T(8,128)S(1)}, f32[152,128]{1...) custom-call(f32[168,128]{1,0:T(8,128)S(1)} %get-tuple-element.31.ref, ...), custom_call_target="tpu_custom_call", output_to_operand_aliasing={{8}: (8, {})} | custom-call | flops 4000000 | bytes 4000000 | tf_op jit(solution)/shard_map/second_step/pallas_call | solution.py:438
  28.1 3.1 %collective-permute-start.9 = (f32[152,128]{1,0:T(8,128)S(1)}, f32[152,128]{1,0:T(8,128)S(1)}, u32[]{:S(2)}, u32[]{:S(2)}) collective-permute-start(f32[152,128]{1,0:T(8,128)S(1)} %get-tuple-element.40), channel_id=1, source_target_pairs={{0,16},{4,20},{8,24},{12,28},{16,0},{20,4},{24,8},{28,12},{1,17},{... | collective-permute-start | bytes 233480 | tf_op jit(solution)/shard_map/ppermute | solution.py:452
  31.2 0.0 collective-permute-start.10
  31.2 1.8 %collective-permute-start.11 = (f32[152,128]{1,0:T(8,128)S(1)}, f32[152,128]{1,0:T(8,128)S(1)}, u32[]{:S(2)}, u32[]{:S(2)}) collective-permute-start(f32[152,128]{1,0:T(8,128)S(1)} %get-tuple-element.42), channel_id=1, source_target_pairs={{0,20},{4,16},{8,28},{12,24},{16,4},{20,0},{24,12},{28,8},{1,21},{... | collective-permute-start | bytes 233480 | tf_op jit(solution)/shard_map/ppermute | solution.py:452
  33.0 2.5 %collective-permute-start.12 = (f32[152,128]{1,0:T(8,128)S(1)}, f32[152,128]{1,0:T(8,128)S(1)}, u32[]{:S(2)}, u32[]{:S(2)}) collective-permute-start(f32[152,128]{1,0:T(8,128)S(1)} %get-tuple-element.43), channel_id=1, source_target_pairs={{0,24},{4,28},{8,16},{12,20},{16,8},{20,12},{24,0},{28,4},{1,25},{... | collective-permute-start | bytes 233480 | tf_op jit(solution)/shard_map/ppermute | solution.py:452
  35.5 0.1 collective-permute-start.13
  35.6 0.0 collective-permute-done.9.refs_1_
  35.6 2.2 %collective-permute-start.14 = (f32[152,128]{1,0:T(8,128)S(1)}, f32[152,128]{1,0:T(8,128)S(1)}, u32[]{:S(2)}, u32[]{:S(2)}) collective-permute-start(f32[152,128]{1,0:T(8,128)S(1)} %get-tuple-element.45), channel_id=1, source_target_pairs={{0,28},{4,24},{8,20},{12,16},{16,12},{20,8},{24,4},{28,0},{1,29},{... | collective-permute-start | bytes 233480 | tf_op jit(solution)/shard_map/ppermute | solution.py:452
  37.7 0.0 collective-permute-done.10.refs_2_
  37.8 0.8 %collective-permute-start.15 = (f32[152,128]{1,0:T(8,128)S(1)}, f32[152,128]{1,0:T(8,128)S(1)}, u32[]{:S(2)}, u32[]{:S(2)}) collective-permute-start(f32[152,128]{1,0:T(8,128)S(1)} %get-tuple-element.46), channel_id=1, source_target_pairs={{0,4},{4,0},{8,12},{12,8},{16,20},{20,16},{24,28},{28,24},{1,5},{5... | collective-permute-start | bytes 233480 | tf_op jit(solution)/shard_map/ppermute | solution.py:452
  38.6 3.4 %collective-permute-done.11.refs_3_ = f32[152,128]{1,0:T(8,128)S(1)} collective-permute-done((f32[152,128]{1,0:T(8,128)S(1)}, f32[152,128]{1,0:T(8,128)S(1)}, u32[]{:S(2)}, u32[]{:S(2)}) %collective-permute-start.11) | collective-permute-done | bytes 77856 | tf_op jit(solution)/shard_map/ppermute | solution.py:452
  42.0 0.0 collective-permute-done.12.refs_4_
  42.0 1.3 %collective-permute-done.13.refs_5_ = f32[152,128]{1,0:T(8,128)S(1)} collective-permute-done((f32[152,128]{1,0:T(8,128)S(1)}, f32[152,128]{1,0:T(8,128)S(1)}, u32[]{:S(2)}, u32[]{:S(2)}) %collective-permute-start.13) | collective-permute-done | bytes 77856 | tf_op jit(solution)/shard_map/ppermute | solution.py:452
  43.3 0.0 collective-permute-done.14.refs_6_
  43.3 0.8 %collective-permute-done.15.refs_7_ = f32[152,128]{1,0:T(8,128)S(1)} collective-permute-done((f32[152,128]{1,0:T(8,128)S(1)}, f32[152,128]{1,0:T(8,128)S(1)}, u32[]{:S(2)}, u32[]{:S(2)}) %collective-permute-start.15) | collective-permute-done | bytes 77856 | tf_op jit(solution)/shard_map/ppermute | solution.py:452
  44.0 0.1 collective-permute-start.16
  44.1 1.6 %collective-permute-start.17 = (f32[24,128]{1,0:T(8,128)S(1)}, f32[24,128]{1,0:T(8,128)S(1)}, u32[]{:S(2)}, u32[]{:S(2)}) collective-permute-start(f32[24,128]{1,0:T(8,128)S(1)} %get-tuple-element.50), channel_id=1, source_target_pairs={{0,1},{1,0},{2,3},{3,2},{4,5},{5,4},{6,7},{7,6},{8,9},{9,8},{10,11... | collective-permute-start | bytes 36872 | tf_op jit(solution)/shard_map/ppermute | solution.py:460
  45.8 0.9 %unpack_planes.1 = (f32[19,64,128]{2,1,0:T(8,128)}, f32[10,8,128]{2,1,0:T(8,128)S(1)}) custom-call(f32[152,128]{1,0:T(8,128)S(1)} %get-tuple-element.39.refs_0_, f32[152,128]{1,0:T(8,128)S(1)} %collective-permute-done.9.refs_1_, f32[152,128]{1,0:T(8,128)S(1)} %collective-permute-done.10.refs_2_, f32[152,128]{1,0:T(8,128)S(1)} %collective-permute-done.11.refs_3_, ...), custom_call_target="tpu_custom_call" | custom-call | flops 4000000 | bytes 4000000 | tf_op jit(solution)/shard_map/unpack_planes/pallas_call | solution.py:438
  46.7 0.6 %collective-permute-done.16.far = f32[24,128]{1,0:T(8,128)S(1)} collective-permute-done((f32[24,128]{1,0:T(8,128)S(1)}, f32[24,128]{1,0:T(8,128)S(1)}, u32[]{:S(2)}, u32[]{:S(2)}) %collective-permute-start.16) | collective-permute-done | bytes 12320 | tf_op jit(solution)/shard_map/ppermute | solution.py:459
  47.3 0.0 collective-permute-done.17.near
  47.3 0.7 %finish.1 = f32[19,64,128]{2,1,0:T(8,128)} custom-call(f32[19,64,128]{2,1,0:T(8,128)} %get-tuple-element.47._, f32[10,8,128]{2,1,0:T(8,128)S(1)} %get-tuple-element.48.edge, f32[24,128]{1,0:T(8,128)S(1)} %collective-permute-done.16.far, f32[24,128]{1,0:T(8,128)S(1)} %collective-permute-done.17.near), custom_call_target="tpu_custom_call", output_to_operand_aliasing={{}: (0, {})} | custom-call | flops 100000 | bytes 100000 | tf_op jit(solution)/shard_map/finish/pallas_call | solution.py:438
  (2 shorter events, 0.0 us)
Async XLA Ops:
  0.0 4.9 %copy-start = (f32[1,2,19,4096]{3,1,2,0:T(2,128)S(1)}, f32[1,2,19,4096]{3,1,2,0:T(2,128)}, u32[]{:S(2)}) copy-start(f32[1,2,19,4096]{3,1,2,0:T(2,128)} %param.4) | copy-start | bytes 1867780
  0.0 4.9 %copy-start.1 = (s32[1,2,4096]{2,1,0:T(2,128)S(1)}, s32[1,2,4096]{2,1,0:T(2,128)}, u32[]{:S(2)}) copy-start(s32[1,2,4096]{2,1,0:T(2,128)} %param.5) | copy-start | bytes 98308
  1.8 4.1 %collective-permute-start = (f32[24,128]{1,0:T(8,128)}, f32[24,128]{1,0:T(8,128)S(1)}, u32[]{:S(2)}, u32[]{:S(2)}) collective-permute-start(f32[24,128]{1,0:T(8,128)} %get-tuple-element.29), channel_id=1, source_target_pairs={{0,3},{1,2},{2,1},{3,0},{4,7},{5,6},{6,5},{7,4},{8,11},{9,10},{10,... | collective-permute-start | bytes 36872 | tf_op jit(solution)/shard_map/ppermute | solution.py:459
  4.2 1.7 %collective-permute-start.1 = (f32[24,128]{1,0:T(8,128)}, f32[24,128]{1,0:T(8,128)S(1)}, u32[]{:S(2)}, u32[]{:S(2)}) collective-permute-start(f32[24,128]{1,0:T(8,128)} %get-tuple-element.30), channel_id=1, source_target_pairs={{0,1},{1,0},{2,3},{3,2},{4,5},{5,4},{6,7},{7,6},{8,9},{9,8},{10,11... | collective-permute-start | bytes 36872 | tf_op jit(solution)/shard_map/ppermute | solution.py:460
  4.9 1.0 %copy-start.2 = (f32[8,128]{1,0:T(8,128)S(1)}, f32[8,128]{1,0:T(8,128)}, u32[]{:S(2)}) copy-start(f32[8,128]{1,0:T(8,128)} %get-tuple-element.28.own) | copy-start | bytes 12292
  6.2 10.3 %collective-permute-start.2 = (f32[168,128]{1,0:T(8,128)S(1)}, f32[168,128]{1,0:T(8,128)S(1)}, u32[]{:S(2)}, u32[]{:S(2)}) collective-permute-start(f32[168,128]{1,0:T(8,128)S(1)} %get-tuple-element.32), channel_id=1, source_target_pairs={{0,16},{4,20},{8,24},{12,28},{16,0},{20,4},{24,8},{28,12},{1,17},{... | collective-permute-start | bytes 258056 | tf_op jit(solution)/shard_map/ppermute | solution.py:452
  9.6 9.3 %collective-permute-start.3 = (f32[168,128]{1,0:T(8,128)S(1)}, f32[168,128]{1,0:T(8,128)S(1)}, u32[]{:S(2)}, u32[]{:S(2)}) collective-permute-start(f32[168,128]{1,0:T(8,128)S(1)} %get-tuple-element.33), channel_id=1, source_target_pairs={{0,8},{4,12},{8,0},{12,4},{16,24},{20,28},{24,16},{28,20},{1,9},{5... | collective-permute-start | bytes 258056 | tf_op jit(solution)/shard_map/ppermute | solution.py:452
  11.2 8.3 %collective-permute-start.5 = (f32[168,128]{1,0:T(8,128)S(1)}, f32[168,128]{1,0:T(8,128)S(1)}, u32[]{:S(2)}, u32[]{:S(2)}) collective-permute-start(f32[168,128]{1,0:T(8,128)S(1)} %get-tuple-element.35), channel_id=1, source_target_pairs={{0,12},{4,8},{8,4},{12,0},{16,28},{20,24},{24,20},{28,16},{1,13},{... | collective-permute-start | bytes 258056 | tf_op jit(solution)/shard_map/ppermute | solution.py:452
  12.6 12.5 %collective-permute-start.4 = (f32[168,128]{1,0:T(8,128)S(1)}, f32[168,128]{1,0:T(8,128)S(1)}, u32[]{:S(2)}, u32[]{:S(2)}) collective-permute-start(f32[168,128]{1,0:T(8,128)S(1)} %get-tuple-element.34), channel_id=1, source_target_pairs={{0,20},{4,16},{8,28},{12,24},{16,4},{20,0},{24,12},{28,8},{1,21},{... | collective-permute-start | bytes 258056 | tf_op jit(solution)/shard_map/ppermute | solution.py:452
  12.6 12.5 %collective-permute-start.6 = (f32[168,128]{1,0:T(8,128)S(1)}, f32[168,128]{1,0:T(8,128)S(1)}, u32[]{:S(2)}, u32[]{:S(2)}) collective-permute-start(f32[168,128]{1,0:T(8,128)S(1)} %get-tuple-element.36), channel_id=1, source_target_pairs={{0,24},{4,28},{8,16},{12,20},{16,8},{20,12},{24,0},{28,4},{1,25},{... | collective-permute-start | bytes 258056 | tf_op jit(solution)/shard_map/ppermute | solution.py:452
  16.5 8.6 %collective-permute-start.7 = (f32[168,128]{1,0:T(8,128)S(1)}, f32[168,128]{1,0:T(8,128)S(1)}, u32[]{:S(2)}, u32[]{:S(2)}) collective-permute-start(f32[168,128]{1,0:T(8,128)S(1)} %get-tuple-element.37), channel_id=1, source_target_pairs={{0,28},{4,24},{8,20},{12,16},{16,12},{20,8},{24,4},{28,0},{1,29},{... | collective-permute-start | bytes 258056 | tf_op jit(solution)/shard_map/ppermute | solution.py:452
  18.9 6.5 %collective-permute-start.8 = (f32[168,128]{1,0:T(8,128)S(1)}, f32[168,128]{1,0:T(8,128)S(1)}, u32[]{:S(2)}, u32[]{:S(2)}) collective-permute-start(f32[168,128]{1,0:T(8,128)S(1)} %get-tuple-element.38), channel_id=1, source_target_pairs={{0,4},{4,0},{8,12},{12,8},{16,20},{20,16},{24,28},{28,24},{1,5},{5... | collective-permute-start | bytes 258056 | tf_op jit(solution)/shard_map/ppermute | solution.py:452
  28.1 7.5 %collective-permute-start.9 = (f32[152,128]{1,0:T(8,128)S(1)}, f32[152,128]{1,0:T(8,128)S(1)}, u32[]{:S(2)}, u32[]{:S(2)}) collective-permute-start(f32[152,128]{1,0:T(8,128)S(1)} %get-tuple-element.40), channel_id=1, source_target_pairs={{0,16},{4,20},{8,24},{12,28},{16,0},{20,4},{24,8},{28,12},{1,17},{... | collective-permute-start | bytes 233480 | tf_op jit(solution)/shard_map/ppermute | solution.py:452
  31.2 6.6 %collective-permute-start.10 = (f32[152,128]{1,0:T(8,128)S(1)}, f32[152,128]{1,0:T(8,128)S(1)}, u32[]{:S(2)}, u32[]{:S(2)}) collective-permute-start(f32[152,128]{1,0:T(8,128)S(1)} %get-tuple-element.41), channel_id=1, source_target_pairs={{0,8},{4,12},{8,0},{12,4},{16,24},{20,28},{24,16},{28,20},{1,9},{5... | collective-permute-start | bytes 233480 | tf_op jit(solution)/shard_map/ppermute | solution.py:452
  31.2 10.8 %collective-permute-start.11 = (f32[152,128]{1,0:T(8,128)S(1)}, f32[152,128]{1,0:T(8,128)S(1)}, u32[]{:S(2)}, u32[]{:S(2)}) collective-permute-start(f32[152,128]{1,0:T(8,128)S(1)} %get-tuple-element.42), channel_id=1, source_target_pairs={{0,20},{4,16},{8,28},{12,24},{16,4},{20,0},{24,12},{28,8},{1,21},{... | collective-permute-start | bytes 233480 | tf_op jit(solution)/shard_map/ppermute | solution.py:452
  33.0 9.0 %collective-permute-start.12 = (f32[152,128]{1,0:T(8,128)S(1)}, f32[152,128]{1,0:T(8,128)S(1)}, u32[]{:S(2)}, u32[]{:S(2)}) collective-permute-start(f32[152,128]{1,0:T(8,128)S(1)} %get-tuple-element.43), channel_id=1, source_target_pairs={{0,24},{4,28},{8,16},{12,20},{16,8},{20,12},{24,0},{28,4},{1,25},{... | collective-permute-start | bytes 233480 | tf_op jit(solution)/shard_map/ppermute | solution.py:452
  35.5 7.7 %collective-permute-start.13 = (f32[152,128]{1,0:T(8,128)S(1)}, f32[152,128]{1,0:T(8,128)S(1)}, u32[]{:S(2)}, u32[]{:S(2)}) collective-permute-start(f32[152,128]{1,0:T(8,128)S(1)} %get-tuple-element.44), channel_id=1, source_target_pairs={{0,12},{4,8},{8,4},{12,0},{16,28},{20,24},{24,20},{28,16},{1,13},{... | collective-permute-start | bytes 233480 | tf_op jit(solution)/shard_map/ppermute | solution.py:452
  35.6 7.7 %collective-permute-start.14 = (f32[152,128]{1,0:T(8,128)S(1)}, f32[152,128]{1,0:T(8,128)S(1)}, u32[]{:S(2)}, u32[]{:S(2)}) collective-permute-start(f32[152,128]{1,0:T(8,128)S(1)} %get-tuple-element.45), channel_id=1, source_target_pairs={{0,28},{4,24},{8,20},{12,16},{16,12},{20,8},{24,4},{28,0},{1,29},{... | collective-permute-start | bytes 233480 | tf_op jit(solution)/shard_map/ppermute | solution.py:452
  37.8 6.3 %collective-permute-start.15 = (f32[152,128]{1,0:T(8,128)S(1)}, f32[152,128]{1,0:T(8,128)S(1)}, u32[]{:S(2)}, u32[]{:S(2)}) collective-permute-start(f32[152,128]{1,0:T(8,128)S(1)} %get-tuple-element.46), channel_id=1, source_target_pairs={{0,4},{4,0},{8,12},{12,8},{16,20},{20,16},{24,28},{28,24},{1,5},{5... | collective-permute-start | bytes 233480 | tf_op jit(solution)/shard_map/ppermute | solution.py:452
  44.0 3.2 %collective-permute-start.16 = (f32[24,128]{1,0:T(8,128)S(1)}, f32[24,128]{1,0:T(8,128)S(1)}, u32[]{:S(2)}, u32[]{:S(2)}) collective-permute-start(f32[24,128]{1,0:T(8,128)S(1)} %get-tuple-element.49), channel_id=1, source_target_pairs={{0,3},{1,2},{2,1},{3,0},{4,7},{5,6},{6,5},{7,4},{8,11},{9,10},{10,... | collective-permute-start | bytes 36872 | tf_op jit(solution)/shard_map/ppermute | solution.py:459
  44.1 3.2 %collective-permute-start.17 = (f32[24,128]{1,0:T(8,128)S(1)}, f32[24,128]{1,0:T(8,128)S(1)}, u32[]{:S(2)}, u32[]{:S(2)}) collective-permute-start(f32[24,128]{1,0:T(8,128)S(1)} %get-tuple-element.50), channel_id=1, source_target_pairs={{0,1},{1,0},{2,3},{3,2},{4,5},{5,4},{6,7},{7,6},{8,9},{9,8},{10,11... | collective-permute-start | bytes 36872 | tf_op jit(solution)/shard_map/ppermute | solution.py:460
